TPU v7x, 32 devices: a whole 2x2x4 slice. The times are simulated.
32 devices in a mesh: dp: 16 (over z, y, x), tensor: 2 (over core).
Axes of the slice: x: 2, y: 2, z: 4, core: 2. Of those that a mesh axis runs over, the one named last changes fastest.
Arguments:
- tokens: bfloat16 [32768, 512], P(('dp', 'tensor')), may hold values from -6 to 6
- lengths: int32 [16, 6], P('dp'), may hold values from 1 to 1024, 2048 in all within a row
- w_qkv: bfloat16 [512, 3, 512], P(None, None, 'tensor'), may hold values from -0.25 to 0.25
- w_attn: bfloat16 [512, 512], P('tensor'), may hold values from -1 to 1
- w_in: bfloat16 [512, 2048], P(None, 'tensor'), may hold values from -0.25 to 0.25
- w_out: bfloat16 [2048, 512], P('tensor'), may hold values from -0.125 to 0.125
- gain_attn: float32 [512], replicated, may hold values from 0.5 to 1.5
- gain_mlp: float32 [512], replicated, may hold values from 0.5 to 1.5
- blend: float32 [2, 8], P(None, 'tensor'), may hold values from 0.5 to 2
- cotangent: bfloat16 [32768, 512], P(('dp', 'tensor')), may hold values from -6 to 6
Outputs:
- output: bfloat16 [32768, 512], P(('dp', 'tensor'))
- grad_input: bfloat16 [32768, 512], P(('dp', 'tensor'))
- grad_w_qkv: float32 [512, 3, 512], P(None, None, 'tensor')
- grad_w_attn: float32 [512, 512], P('tensor')
- grad_w_in: float32 [512, 2048], P(None, 'tensor')
- grad_w_out: float32 [2048, 512], P('tensor')
- grad_gain_attn: float32 [512], replicated
- grad_gain_mlp: float32 [512], replicated
- grad_blend: float32 [2, 8], P(None, 'tensor')
Inputs may be any that keep to these rules, and one draw needn't show every extreme that they name: In every row the 6 lengths sum to 2048, and the longest is exactly 1024.
All inputs are finite; a program needn't handle non-finite values.
Results may differ from a plain program's by a relative error of at most 0.012.
Values may be sent and summed in bfloat16 or wider, within the bound.
No kernel may reach another device: no remote copies, remote signals or barrier semaphores. Data moves between devices by JAX's collectives and lax.ppermute only.
A program may use at most 192 MiB of HBM per device.

v0:
```python
from functools import partial

import jax
import jax.numpy as jnp
from jax import lax
from jax.sharding import PartitionSpec as P

BAND = 30


def rms_scale(values, gain):
    return values * lax.rsqrt(jnp.mean(values * values, axis=-1, keepdims=True) + 1e-06) * gain


def gelu_tanh(values):
    return jax.nn.gelu(values, approximate=True)


def make_kit():

    @jax.custom_vjp
    def round_value(values):
        return lax.optimization_barrier(values.astype(jnp.bfloat16)).astype(jnp.float32)

    @jax.custom_vjp
    def round_grad(values):
        return values

    def value_keep(values):
        return (round_value(values), None)

    def value_pass(kept, grad):
        return (grad,)

    def grad_keep(values):
        return (values, None)

    def grad_round(kept, grad):
        return (round_value(grad),)

    round_value.defvjp(value_keep, value_pass)
    round_grad.defvjp(grad_keep, grad_round)

    @jax.custom_vjp
    def score_product(left, right):
        return jnp.einsum(
            "hqe,hke->hqk",
            left.astype(jnp.bfloat16),
            right.astype(jnp.bfloat16),
            preferred_element_type=jnp.float32,
        )

    def score_keep(left, right):
        return (score_product(left, right), (left.astype(jnp.bfloat16), right.astype(jnp.bfloat16)))

    def score_back(kept, grad):
        left, right = kept
        grad_low = grad.astype(jnp.bfloat16)
        return (
            jnp.einsum("hqk,hke->hqe", grad_low, right, preferred_element_type=jnp.float32),
            jnp.einsum("hqk,hqe->hke", grad_low, left, preferred_element_type=jnp.float32),
        )

    score_product.defvjp(score_keep, score_back)

    @jax.custom_vjp
    def weight_product(weights, values):
        return jnp.einsum(
            "hqk,hke->hqe",
            weights.astype(jnp.bfloat16),
            values.astype(jnp.bfloat16),
            preferred_element_type=jnp.float32,
        )

    def weight_keep(weights, values):
        return (
            weight_product(weights, values),
            (weights.astype(jnp.bfloat16), values.astype(jnp.bfloat16)),
        )

    def weight_back(kept, grad):
        weights, values = kept
        grad_low = grad.astype(jnp.bfloat16)
        return (
            jnp.einsum("hqe,hke->hqk", grad_low, values, preferred_element_type=jnp.float32),
            jnp.einsum("hqk,hqe->hke", weights, grad_low, preferred_element_type=jnp.float32),
        )

    weight_product.defvjp(weight_keep, weight_back)

    def features(values):
        first = round_grad(round_value(jax.nn.elu(values) + 1.0))
        second = round_grad(round_value(jnp.tanh(values)))
        return (first, second)

    def near_part(queries, keys, values, query_segment, key_segment, query_places, key_places):
        behind = query_places[:, None] - key_places[None, :]
        banded = (query_segment[:, None] == key_segment[None, :]) & (behind >= 0) & (behind < BAND)
        scores = round_grad(score_product(queries, keys)) * queries.shape[2] ** (-0.5)
        scores = jnp.where(banded[None], scores, -1e30)
        top = jnp.max(scores, axis=-1, keepdims=True)
        raised = jnp.exp(scores - top)
        weights = round_value(raised / jnp.sum(raised, axis=-1, keepdims=True))
        return round_grad(weight_product(weights, values))

    def far_part(
        query_one,
        query_two,
        key_one,
        key_two,
        values,
        query_segment,
        key_segment,
        query_places,
        key_places,
    ):
        allowed = (
            (query_segment[:, None] == key_segment[None, :])
            & (key_places[None, :] <= query_places[:, None])
        ).astype(jnp.float32)
        first = round_grad(score_product(query_one, key_one)) * allowed
        second = round_grad(score_product(query_two, key_two)) * allowed
        first_sum = weight_product(round_value(first), values)
        second_sum = weight_product(round_value(second), values)
        return (first_sum, jnp.sum(first, axis=-1), second_sum, jnp.sum(allowed, axis=-1))

    def block_mixer(queries, keys, values, blend, segment):
        row_len = queries.shape[1]
        block = min(512, row_len)
        margin = 128
        places = jnp.arange(row_len, dtype=jnp.int32)
        query_one, query_two = features(queries)
        key_one, key_two = features(keys)
        key_pad = jnp.pad(keys, ((0, 0), (margin, 0), (0, 0)))
        value_pad = jnp.pad(values, ((0, 0), (margin, 0), (0, 0)))
        segment_pad = jnp.concatenate([jnp.full((margin,), -1, jnp.int32), segment])
        place_pad = jnp.arange(row_len + margin, dtype=jnp.int32) - margin
        pieces = []
        for index in range(row_len // block):
            first_row = index * block
            last_row = first_row + block
            near = jax.checkpoint(near_part)(
                queries[:, first_row:last_row],
                key_pad[:, first_row : last_row + margin],
                value_pad[:, first_row : last_row + margin],
                segment[first_row:last_row],
                segment_pad[first_row : last_row + margin],
                places[first_row:last_row],
                place_pad[first_row : last_row + margin],
            )
            totals = None
            for other in range(index + 1):
                first_col = other * block
                last_col = first_col + block
                part = jax.checkpoint(far_part)(
                    query_one[:, first_row:last_row],
                    query_two[:, first_row:last_row],
                    key_one[:, first_col:last_col],
                    key_two[:, first_col:last_col],
                    values[:, first_col:last_col],
                    segment[first_row:last_row],
                    segment[first_col:last_col],
                    places[first_row:last_row],
                    places[first_col:last_col],
                )
                totals = (
                    part
                    if totals is None
                    else tuple((older + newer for older, newer in zip(totals, part)))
                )
            far_one = round_grad(totals[0]) / totals[1][:, :, None]
            far_two = round_grad(totals[2]) / totals[3][None, :, None]
            pieces.append(
                near + blend[0][:, None, None] * far_one + blend[1][:, None, None] * far_two
            )
        return jnp.concatenate(pieces, axis=1)

    return (round_value, block_mixer)


def contract_rows(left, right):
    return lax.dot_general(
        left, right, (((0,), (0,)), ((), ())), preferred_element_type=jnp.float32
    )


def contract_cols(left, right):
    return lax.dot_general(
        left, right, (((1,), (1,)), ((), ())), preferred_element_type=jnp.float32
    )


def body(tokens, lengths, w_qkv, w_attn, w_in, w_out, gain_attn, gain_mlp, blend, cotangent):
    round_value, block_mixer = make_kit()
    local_rows, width = tokens.shape
    heads_local = blend.shape[1]
    head_dim = w_qkv.shape[2] // heads_local
    local_x = tokens.astype(jnp.float32)
    normed, norm_back = jax.vjp(rms_scale, local_x, gain_attn)
    gathered = lax.all_gather(normed.astype(jnp.bfloat16), "tensor", axis=0, tiled=True)
    row_len = gathered.shape[0]
    weights_qkv = w_qkv.reshape(width, -1)
    projected = jnp.dot(gathered, weights_qkv, preferred_element_type=jnp.float32).astype(
        jnp.bfloat16
    )
    split = (
        projected.astype(jnp.float32)
        .reshape(row_len, 3, heads_local, head_dim)
        .transpose(1, 2, 0, 3)
    )
    ends = jnp.cumsum(lengths[0]).astype(jnp.int32)
    places = jnp.arange(row_len, dtype=jnp.int32)
    segment = jnp.sum((places[:, None] >= ends[None, :]).astype(jnp.int32), axis=1).astype(
        jnp.int32
    )
    mixed_heads, mixer_back = jax.vjp(
        partial(block_mixer, segment=segment), split[0], split[1], split[2], blend
    )
    mixed_low = (
        mixed_heads.transpose(1, 0, 2).reshape(row_len, heads_local * head_dim).astype(jnp.bfloat16)
    )
    hidden = local_x + lax.psum_scatter(
        jnp.dot(
            lax.slice_in_dim(mixed_low, 0, lax.axis_size("tensor") * local_rows, axis=0),
            w_attn,
            preferred_element_type=jnp.float32,
        ),
        "tensor",
        scatter_dimension=0,
        tiled=True,
    )
    normed_two, norm2_back = jax.vjp(rms_scale, hidden, gain_mlp)
    gathered_two = lax.all_gather(normed_two.astype(jnp.bfloat16), "tensor", axis=0, tiled=True)
    before = jnp.dot(gathered_two, w_in, preferred_element_type=jnp.float32)
    active, gelu_back = jax.vjp(gelu_tanh, before)
    active_low = active.astype(jnp.bfloat16)
    output = (
        hidden
        + lax.psum_scatter(
            jnp.dot(
                lax.slice_in_dim(active_low, 0, local_rows * lax.axis_size("tensor"), axis=0),
                w_out,
                preferred_element_type=jnp.float32,
            ).astype(jnp.bfloat16),
            "tensor",
            scatter_dimension=0,
            tiled=True,
        ).astype(jnp.float32)
    ).astype(jnp.bfloat16)
    grad_full = lax.all_gather(cotangent, "tensor", axis=0, tiled=True)
    grad_w_out = contract_rows(active_low, grad_full)
    grad_active = round_value(contract_cols(grad_full, w_out))
    grad_before = gelu_back(grad_active)[0].astype(jnp.bfloat16)
    grad_w_in = contract_rows(gathered_two, grad_before)
    grad_normed_two = lax.psum_scatter(
        contract_cols(
            lax.slice_in_dim(grad_before, 0, lax.axis_size("tensor") * local_rows, axis=0), w_in
        ),
        "tensor",
        scatter_dimension=0,
        tiled=True,
    )
    grad_hidden_part, grad_gain_mlp = norm2_back(grad_normed_two)
    grad_hidden = cotangent.astype(jnp.float32) + grad_hidden_part
    branch_full = lax.all_gather(grad_hidden.astype(jnp.bfloat16), "tensor", axis=0, tiled=True)
    grad_w_attn = contract_rows(mixed_low, branch_full)
    grad_mixed = round_value(contract_cols(branch_full, w_attn))
    grad_heads = grad_mixed.reshape(row_len, heads_local, head_dim).transpose(1, 0, 2)
    grad_query, grad_key, grad_value, grad_blend = mixer_back(grad_heads)
    grad_projected = jnp.stack([grad_query, grad_key, grad_value]).transpose(2, 0, 1, 3)
    grad_projected = grad_projected.reshape(row_len, 3 * heads_local * head_dim).astype(
        jnp.bfloat16
    )
    grad_w_qkv = contract_rows(gathered, grad_projected).reshape(w_qkv.shape)
    grad_normed = lax.psum_scatter(
        contract_cols(
            lax.slice_in_dim(grad_projected, 0, lax.axis_size("tensor") * local_rows, axis=0),
            weights_qkv,
        ),
        "tensor",
        scatter_dimension=0,
        tiled=True,
    )
    grad_x_part, grad_gain_attn = norm_back(grad_normed)
    grad_input = (grad_hidden + grad_x_part).astype(jnp.bfloat16)
    grad_w_qkv, grad_w_attn, grad_w_in, grad_w_out, grad_blend, grad_gain_attn, grad_gain_mlp = (
        lax.psum(
            (
                grad_w_qkv,
                grad_w_attn,
                grad_w_in,
                grad_w_out,
                grad_blend,
                grad_gain_attn,
                grad_gain_mlp,
            ),
            "dp",
        )
    )
    grad_gain_attn, grad_gain_mlp = lax.psum((grad_gain_attn, grad_gain_mlp), "tensor")
    return (
        output,
        grad_input,
        grad_w_qkv,
        grad_w_attn,
        grad_w_in,
        grad_w_out,
        grad_gain_attn,
        grad_gain_mlp,
        grad_blend,
    )


def solution(mesh):
    return jax.shard_map(
        body,
        mesh=mesh,
        in_specs=(
            P(("dp", "tensor"), None),
            P("dp", None),
            P(None, None, "tensor"),
            P("tensor", None),
            P(None, "tensor"),
            P("tensor", None),
            P(),
            P(),
            P(None, "tensor"),
            P(("dp", "tensor"), None),
        ),
        out_specs=(
            P(("dp", "tensor"), None),
            P(("dp", "tensor"), None),
            P(None, None, "tensor"),
            P("tensor", None),
            P(None, "tensor"),
            P("tensor", None),
            P(),
            P(),
            P(None, "tensor"),
        ),
        check_vma=False,
    )
```

profile of v0, /device:TPU:0, one launch (start us, length us, event | category | flops | bytes accessed | tf_op | source)
XLA Modules:
  0.0 754.3 jit_solution(13191721175408618854)
XLA Ops:
  10.1 2.5 fusion.40
  13.4 2.9 fusion.105
  20.7 5.0 and_convert_fusion.19
  26.1 3.4 convolution_convert_fusion.1
  40.4 2.7 multiply_reduce_fusion.13
  45.2 2.7 multiply_reduce_fusion.10
  47.9 2.2 multiply_convert_fusion.49
  50.1 2.7 multiply_reduce_fusion.8
  54.9 2.7 multiply_reduce_fusion.9
  57.6 2.1 multiply_convert_fusion.52
  59.8 2.7 multiply_reduce_fusion.11
  64.5 3.0 multiply_reduce_fusion.12
  69.6 2.7 multiply_reduce_fusion.6
  74.4 2.7 multiply_reduce_fusion.4
  79.2 2.7 multiply_reduce_fusion.5
  83.9 2.7 multiply_reduce_fusion.7
  87.8 6.4 fusion.529
  94.1 4.4 divide_convert_fusion.6
  98.5 6.2 fusion.538
  104.7 4.4 divide_convert_fusion.7
  109.1 6.5 fusion.520
  115.6 4.4 divide_convert_fusion.5
  120.0 5.5 fusion.511
  125.5 3.1 divide_convert_fusion.4
  161.7 2.9 fusion.547
  165.4 13.7 %reduce-scatter.5.cloned.1.call-done = f32[1024,512]{1,0:T(8,128)} async-done(((f32[2048,512]{1,0:T(8,128)}), f32[1024,512]{1,0:T(8,128)}) %reduce-scatter.5.cloned.1.call-update) | async-done | bytes 2097168 | tf_op jit(solution)/shard_map/reduce_scatter | solution.py:222
  179.1 2.2 multiply_reduce_fusion.16
  182.9 9.8 %all-gather.9.cloned.1.call-done = bf16[2048,512]{1,0:T(8,128)(2,1)} async-done(((bf16[1024,512]{1,0:T(8,128)(2,1)}), bf16[2048,512]{1,0:T(8,128)(2,1)}) %all-gather.9.cloned.1.call-update) | async-done | bytes 2097168 | tf_op jit(solution)/shard_map/all_gather | solution.py:250
  192.7 6.2 convolution_convert_fusion
  198.8 7.7 %all-gather.7.cloned.1.call-done = bf16[2048,512]{1,0:T(8,128)(2,1)} async-done(((bf16[1024,512]{1,0:T(8,128)(2,1)}), bf16[2048,512]{1,0:T(8,128)(2,1)}) %all-gather.7.cloned.1.call-update) | async-done | bytes 2097168 | tf_op jit(solution)/shard_map/all_gather | solution.py:233
  206.5 11.7 %fusion.6 = (bf16[2048,1024]{1,0:T(8,128)(2,1)S(1)}, bf16[2048,1024]{1,0:T(8,128)(2,1)}) fusion(bf16[2048,1024]{1,0:T(8,128)(2,1)} %convolution_convert_fusion, bf16[2048,512]{1,0:T(8,128)(2,1)} %all-gather.7.cloned.1.call-done, bf16[512,1024]{1,0:T(8,128)(2,1)S(1)} %copy-done), kind=kOutput, calls=%fused_computation.10 | convolution fusion | flops 2195718144 | bytes 15728640 | tf_op jit(solution)/shard_map/dot_general | solution.py:234
  220.2 4.5 fusion.548
  224.8 13.3 %reduce-scatter.9.cloned.1.call-done = f32[1024,512]{1,0:T(8,128)} async-done(((f32[2048,512]{1,0:T(8,128)}), f32[1024,512]{1,0:T(8,128)}) %reduce-scatter.9.cloned.1.call-update) | async-done | bytes 2097168 | tf_op jit(solution)/shard_map/reduce_scatter | solution.py:255
  238.1 2.9 multiply_reduce_fusion.14
  243.9 2.8 fusion.506
  246.7 8.0 %all-gather.11.cloned.1.call-done = bf16[2048,512]{1,0:T(8,128)(2,1)} async-done(((bf16[1024,512]{1,0:T(8,128)(2,1)}), bf16[2048,512]{1,0:T(8,128)(2,1)}) %all-gather.11.cloned.1.call-update) | async-done | bytes 2097168 | tf_op jit(solution)/shard_map/all_gather | solution.py:265
  254.7 2.3 convolution_convert_fusion.3
  357.4 2.1 multiply_convert_fusion.10
  363.4 2.4 multiply_convert_fusion.7
  379.4 2.5 multiply_reduce_fusion.3
  381.8 3.7 convert_reduce_fusion.3
  385.5 3.7 multiply_convert_fusion.4
  395.8 2.5 multiply_reduce_fusion
  398.3 3.7 convert_reduce_fusion
  402.0 3.3 multiply_convert_fusion.1
  412.0 2.5 multiply_reduce_fusion.1
  414.5 3.7 convert_reduce_fusion.1
  418.2 3.3 multiply_convert_fusion.2
  428.0 2.5 multiply_reduce_fusion.2
  430.5 4.4 convert_reduce_fusion.2
  434.9 4.7 multiply_convert_fusion.3
  439.6 2.7 fusion.566
  482.1 2.6 fusion.44
  487.4 3.9 fusion.549
  492.5 5.8 convolution_convert_fusion.2
  498.4 7.1 fusion.551
  505.5 3.8 fusion.552
  511.4 3.0 fusion.64
  515.8 2.5 fusion.41
  518.3 45.4 %all-reduce.73 = (f32[512]{0:T(512)S(1)}, f32[512]{0:T(512)S(1)}, f32[2,4]{1,0:T(2,128)}) all-reduce(f32[512]{0:T(512)S(1)} %get-tuple-element.315, f32[512]{0:T(512)S(1)} %copy-done.238, f32[2,4]{1,0:T(2,128)S(1)} %pad_add_fusion.6), channel_id=1, replica_groups=mesh['dp'=16,'tensor'=2] {'dp'}, use_global_device_ids=true, to_apply=%region_67.68 | all-reduce | flops 1032 | bytes 8256 | tf_op jit(solution)/shard_map/psum | solution.py:287
  563.7 3.0 all-reduce.75
  566.8 4.5 fusion.58
  571.3 168.8 %all-reduce.78.cloned.1.call-done = (f32[512,3,256]{2,0,1:T(8,128)}, f32[256,512]{1,0:T(8,128)}, f32[512,1024]{1,0:T(8,128)}, f32[1024,512]{1,0:T(8,128)}) async-done(((f32[512,3,256]{2,0,1:T(8,128)}, f32[256,512]{1,0:T(8,128)}, f32[512,1024]{1,0:T(8,128)}, f32[1024,512]{1,0:T(8,128)}), (f32[512,3,256]{2,0,1:T(8,128)}, f32[256,512]{1,0:T(8,128)}, f32[512,1024]{1,0:T(8,128)}, ...) | async-done | bytes 6291472 | tf_op jit(solution)/shard_map/psum | solution.py:287
  740.0 2.8 copy.133
  (771 shorter events, 262.4 us)
Async XLA Ops:
  7.2 199.3 %copy-start = (bf16[512,1024]{1,0:T(8,128)(2,1)S(1)}, bf16[512,1024]{1,0:T(8,128)(2,1)}, u32[]{:S(2)}) copy-start(bf16[512,1024]{1,0:T(8,128)(2,1)} %param.14) | copy-start | bytes 3145732
  7.2 5.5 copy-start.256
  7.2 5.8 copy-start.181
  7.2 18.8 %all-gather.5.cloned.1.call-start = ((), (), s32[]{:S(2)}) async-start(), calls=%async_computation.4 | async-start | bytes 3145728 | tf_op jit(solution)/shard_map/all_gather | solution.py:200
  10.1 6.7 copy-start.253
  12.6 166.5 %reduce-scatter.5.cloned.1.call-start = ((), (), s32[]{:S(2)}) async-start(), calls=%async_computation.5 | async-start | bytes 6291456 | tf_op jit(solution)/shard_map/reduce_scatter | solution.py:222
  12.7 13.0 %copy-start.193 = (s32[512]{0:T(512)}, s32[512]{0:T(512)S(1)}, u32[]{:S(2)}) copy-start(s32[512]{0:T(512)S(1)} %iota_add_fusion.1) | copy-start | bytes 6148
  13.0 12.7 %copy-start.195 = (s32[512]{0:T(512)}, s32[512]{0:T(512)S(1)}, u32[]{:S(2)}) copy-start(s32[512]{0:T(512)S(1)} %get-tuple-element.210) | copy-start | bytes 6148
  13.0 12.7 %copy-start.197 = (s32[512]{0:T(512)}, s32[512]{0:T(512)S(1)}, u32[]{:S(2)}) copy-start(s32[512]{0:T(512)S(1)} %get-tuple-element.217) | copy-start | bytes 6148
  13.1 12.7 %copy-start.199 = (s32[512]{0:T(512)}, s32[512]{0:T(512)S(1)}, u32[]{:S(2)}) copy-start(s32[512]{0:T(512)S(1)} %get-tuple-element.195) | copy-start | bytes 6148
  13.3 12.7 %copy-start.182 = (bf16[512,3,256]{0,2,1:T(8,128)(2,1)}, bf16[512,3,256]{0,2,1:T(8,128)(2,1)S(1)}, u32[]{:S(2)}) copy-start(bf16[512,3,256]{0,2,1:T(8,128)(2,1)S(1)} %copy.64) | copy-start | bytes 2359300
  17.9 7.8 %copy-start.206 = (s32[640]{0:T(1024)}, s32[640]{0:T(1024)S(1)}, u32[]{:S(2)}) copy-start(s32[640]{0:T(1024)S(1)} %get-tuple-element.170) | copy-start | bytes 7684
  18.0 7.8 %copy-start.208 = (s32[640]{0:T(1024)}, s32[640]{0:T(1024)S(1)}, u32[]{:S(2)}) copy-start(s32[640]{0:T(1024)S(1)} %get-tuple-element.178) | copy-start | bytes 7684
  18.0 7.8 %copy-start.210 = (s32[640]{0:T(1024)}, s32[640]{0:T(1024)S(1)}, u32[]{:S(2)}) copy-start(s32[640]{0:T(1024)S(1)} %get-tuple-element.186) | copy-start | bytes 7684
  18.0 7.8 %copy-start.212 = (s32[640]{0:T(1024)}, s32[640]{0:T(1024)S(1)}, u32[]{:S(2)}) copy-start(s32[640]{0:T(1024)S(1)} %get-tuple-element.162) | copy-start | bytes 7684
  18.0 7.8 %copy-start.214 = (s32[640]{0:T(1024)}, s32[640]{0:T(1024)S(1)}, u32[]{:S(2)}) copy-start(s32[640]{0:T(1024)S(1)} %get-tuple-element.172) | copy-start | bytes 7684
  18.0 7.8 %copy-start.216 = (s32[640]{0:T(1024)}, s32[640]{0:T(1024)S(1)}, u32[]{:S(2)}) copy-start(s32[640]{0:T(1024)S(1)} %get-tuple-element.180) | copy-start | bytes 7684
  18.0 7.8 %copy-start.218 = (s32[640]{0:T(1024)}, s32[640]{0:T(1024)S(1)}, u32[]{:S(2)}) copy-start(s32[640]{0:T(1024)S(1)} %get-tuple-element.188) | copy-start | bytes 7684
  18.0 7.8 %copy-start.220 = (s32[640]{0:T(1024)}, s32[640]{0:T(1024)S(1)}, u32[]{:S(2)}) copy-start(s32[640]{0:T(1024)S(1)} %get-tuple-element.164) | copy-start | bytes 7684
  33.2 53.4 %copy-start.79 = (bf16[4,2048,64]{1,2,0:T(8,128)(2,1)}, bf16[4,2048,64]{1,2,0:T(8,128)(2,1)S(1)}, u32[]{:S(2)}) copy-start(bf16[4,2048,64]{1,2,0:T(8,128)(2,1)S(1)} %get-tuple-element.380) | copy-start | bytes 3145732
  33.2 126.4 %copy-start.17 = (bf16[4,2048,64]{1,2,0:T(8,128)(2,1)}, bf16[4,2048,64]{1,2,0:T(8,128)(2,1)S(1)}, u32[]{:S(2)}) copy-start(bf16[4,2048,64]{1,2,0:T(8,128)(2,1)S(1)} %get-tuple-element.378) | copy-start | bytes 3145732
  36.4 45.5 %copy-start.5 = (bf16[4,512,64]{1,2,0:T(8,128)(2,1)}, bf16[4,512,64]{1,2,0:T(8,128)(2,1)S(1)}, u32[]{:S(2)}) copy-start(bf16[4,512,64]{1,2,0:T(8,128)(2,1)S(1)} %get-tuple-element.435) | copy-start | bytes 786436
  36.4 45.5 %copy-start.9 = (bf16[4,512,64]{1,2,0:T(8,128)(2,1)}, bf16[4,512,64]{1,2,0:T(8,128)(2,1)S(1)}, u32[]{:S(2)}) copy-start(bf16[4,512,64]{1,2,0:T(8,128)(2,1)S(1)} %get-tuple-element.529) | copy-start | bytes 786436
  37.5 46.4 %copy-start.7 = (bf16[4,512,64]{1,2,0:T(8,128)(2,1)}, bf16[4,512,64]{1,2,0:T(8,128)(2,1)S(1)}, u32[]{:S(2)}) copy-start(bf16[4,512,64]{1,2,0:T(8,128)(2,1)S(1)} %get-tuple-element.440) | copy-start | bytes 786436
  37.5 46.4 %copy-start.11 = (bf16[4,512,64]{1,2,0:T(8,128)(2,1)}, bf16[4,512,64]{1,2,0:T(8,128)(2,1)S(1)}, u32[]{:S(2)}) copy-start(bf16[4,512,64]{1,2,0:T(8,128)(2,1)S(1)} %get-tuple-element.536) | copy-start | bytes 786436
  87.8 62.8 %copy-start.19 = (bf16[4,512,64]{1,2,0:T(8,128)(2,1)}, bf16[4,512,64]{1,2,0:T(8,128)(2,1)S(1)}, u32[]{:S(2)}) copy-start(bf16[4,512,64]{1,2,0:T(8,128)(2,1)S(1)} %get-tuple-element.430) | copy-start | bytes 786436
  87.8 64.6 %copy-start.13 = (bf16[4,512,64]{1,2,0:T(8,128)(2,1)}, bf16[4,512,64]{1,2,0:T(8,128)(2,1)S(1)}, u32[]{:S(2)}) copy-start(bf16[4,512,64]{1,2,0:T(8,128)(2,1)S(1)} %get-tuple-element.429) | copy-start | bytes 786436
  130.1 24.6 %copy-start.159 = (f32[4,512,64]{1,2,0:T(8,128)}, f32[4,512,64]{1,2,0:T(8,128)S(1)}, u32[]{:S(2)}) copy-start(f32[4,512,64]{1,2,0:T(8,128)S(1)} %fusion.553) | copy-start | bytes 1572868
  137.5 17.2 %copy-start.184 = (f32[4,512,64]{1,2,0:T(8,128)}, f32[4,512,64]{1,2,0:T(8,128)S(1)}, u32[]{:S(2)}) copy-start(f32[4,512,64]{1,2,0:T(8,128)S(1)} %convolution_divide_fusion) | copy-start | bytes 1572868
  141.6 16.2 %copy-start.161 = (f32[4,512,64]{1,2,0:T(8,128)}, f32[4,512,64]{1,2,0:T(8,128)S(1)}, u32[]{:S(2)}) copy-start(f32[4,512,64]{1,2,0:T(8,128)S(1)} %convolution_add_fusion.25) | copy-start | bytes 1572868
  145.0 11.1 %copy-start.164 = (f32[4,512,64]{1,2,0:T(8,128)}, f32[4,512,64]{1,2,0:T(8,128)S(1)}, u32[]{:S(2)}) copy-start(f32[4,512,64]{1,2,0:T(8,128)S(1)} %convolution_add_fusion.22) | copy-start | bytes 1572868
  150.5 9.2 %copy-start.166 = (f32[4,512,64]{1,2,0:T(8,128)}, f32[4,512,64]{1,2,0:T(8,128)S(1)}, u32[]{:S(2)}) copy-start(f32[4,512,64]{1,2,0:T(8,128)S(1)} %convolution_add_fusion.17) | copy-start | bytes 1572868
  152.2 3.8 copy-start.186
  153.0 4.8 copy-start.188
  154.7 4.9 copy-start.190
  164.6 28.1 %all-gather.9.cloned.1.call-start = ((), (), s32[]{:S(2)}) async-start(), calls=%async_computation.8 | async-start | bytes 3145728 | tf_op jit(solution)/shard_map/all_gather | solution.py:250
  165.4 16.0 %copy-start.235 = (f32[512]{0:T(512)S(1)}, f32[512]{0:T(512)}, u32[]{:S(2)}) copy-start(f32[512]{0:T(512)} %param.17) | copy-start | bytes 6148
  165.4 41.1 %all-gather.7.cloned.1.call-start = ((), (), s32[]{:S(2)}) async-start(), calls=%async_computation.6 | async-start | bytes 3145728 | tf_op jit(solution)/shard_map/all_gather | solution.py:233
  181.3 59.7 %copy-start.2 = (f32[1024,512]{1,0:T(8,128)}, f32[1024,512]{1,0:T(8,128)S(1)}, u32[]{:S(2)}) copy-start(f32[1024,512]{1,0:T(8,128)S(1)} %get-tuple-element.369) | copy-start | bytes 6291460
  181.4 59.6 %copy-start.201 = (f32[1024]{0:T(1024)}, f32[1024]{0:T(1024)S(1)}, u32[]{:S(2)}) copy-start(f32[1024]{0:T(1024)S(1)} %fusion.410) | copy-start | bytes 12292
  182.8 55.3 %reduce-scatter.9.cloned.1.call-start = ((), (), s32[]{:S(2)}) async-start(), calls=%async_computation.9 | async-start | bytes 6291456 | tf_op jit(solution)/shard_map/reduce_scatter | solution.py:255
  224.7 16.3 %copy-start.35 = (bf16[1024,512]{1,0:T(8,128)(2,1)S(1)}, bf16[1024,512]{1,0:T(8,128)(2,1)}, u32[]{:S(2)}) copy-start(bf16[1024,512]{1,0:T(8,128)(2,1)} %param.19) | copy-start | bytes 3145732
  224.7 30.0 %all-gather.11.cloned.1.call-start = ((), (), s32[]{:S(2)}) async-start(), calls=%async_computation.10 | async-start | bytes 3145728 | tf_op jit(solution)/shard_map/all_gather | solution.py:265
  242.7 272.5 %reduce-scatter.11.cloned.1.call-start = ((), (), s32[]{:S(2)}) async-start(), calls=%async_computation.11 | async-start | bytes 6291456 | tf_op jit(solution)/shard_map/reduce_scatter | solution.py:275
  243.9 10.8 %copy-start.180 = (bf16[256,512]{1,0:T(8,128)(2,1)S(1)}, bf16[256,512]{1,0:T(8,128)(2,1)}, u32[]{:S(2)}) copy-start(bf16[256,512]{1,0:T(8,128)(2,1)} %param.13) | copy-start | bytes 786436
  258.3 107.5 %copy-start.76 = (bf16[4,512,64]{1,2,0:T(8,128)(2,1)}, bf16[4,512,64]{1,2,0:T(8,128)(2,1)S(1)}, u32[]{:S(2)}) copy-start(bf16[4,512,64]{1,2,0:T(8,128)(2,1)S(1)} %get-tuple-element.242) | copy-start | bytes 786436
  258.3 113.2 %copy-start.112 = (bf16[4,512,64]{1,2,0:T(8,128)(2,1)}, bf16[4,512,64]{1,2,0:T(8,128)(2,1)S(1)}, u32[]{:S(2)}) copy-start(bf16[4,512,64]{1,2,0:T(8,128)(2,1)S(1)} %get-tuple-element.256) | copy-start | bytes 786436
  259.2 120.2 %copy-start.110 = (bf16[4,512,64]{1,2,0:T(8,128)(2,1)}, bf16[4,512,64]{1,2,0:T(8,128)(2,1)S(1)}, u32[]{:S(2)}) copy-start(bf16[4,512,64]{1,2,0:T(8,128)(2,1)S(1)} %get-tuple-element.165) | copy-start | bytes 786436
  259.2 136.7 %copy-start.108 = (bf16[4,512,64]{1,2,0:T(8,128)(2,1)}, bf16[4,512,64]{1,2,0:T(8,128)(2,1)S(1)}, u32[]{:S(2)}) copy-start(bf16[4,512,64]{1,2,0:T(8,128)(2,1)S(1)} %get-tuple-element.189) | copy-start | bytes 786436
  259.2 152.8 %copy-start.106 = (bf16[4,512,64]{1,2,0:T(8,128)(2,1)}, bf16[4,512,64]{1,2,0:T(8,128)(2,1)S(1)}, u32[]{:S(2)}) copy-start(bf16[4,512,64]{1,2,0:T(8,128)(2,1)S(1)} %get-tuple-element.181) | copy-start | bytes 786436
  262.2 97.5 %copy-start.72 = (bf16[4,512,64]{1,2,0:T(8,128)(2,1)}, bf16[4,512,64]{1,2,0:T(8,128)(2,1)S(1)}, u32[]{:S(2)}) copy-start(bf16[4,512,64]{1,2,0:T(8,128)(2,1)S(1)} %get-tuple-element.285) | copy-start | bytes 786436
  446.3 6.9 copy-start.163
  447.9 5.3 copy-start.156
  474.9 5.9 slice-start
  491.3 75.5 %reduce-scatter.7.cloned.1.call-start = ((), (), s32[]{:S(2)}) async-start(), calls=%async_computation.7 | async-start | bytes 3145728 | tf_op jit(solution)/shard_map/reduce_scatter | solution.py:239
  498.3 7.1 copy-start.169
  498.3 241.7 %all-reduce.78.cloned.1.call-start = ((), (), s32[]{:S(2)}) async-start(), calls=%async_computation.12 | async-start | bytes 12582912 | tf_op jit(solution)/shard_map/psum | solution.py:287
  498.4 7.1 copy-start.78
  505.5 5.3 copy-start.254
  514.5 52.3 %copy-start.223 = (f32[1024]{0:T(1024)S(1)}, f32[1024]{0:T(1024)}, u32[]{:S(2)}) copy-start(f32[1024]{0:T(1024)} %copy-done.222) | copy-start | bytes 12292
  514.5 52.3 %copy-start.3 = (f32[1024,512]{1,0:T(8,128)S(1)}, f32[1024,512]{1,0:T(8,128)}, u32[]{:S(2)}) copy-start(f32[1024,512]{1,0:T(8,128)} %copy-done.2) | copy-start | bytes 6291460
  514.5 52.3 %copy-start.202 = (f32[1024]{0:T(1024)S(1)}, f32[1024]{0:T(1024)}, u32[]{:S(2)}) copy-start(f32[1024]{0:T(1024)} %copy-done.201) | copy-start | bytes 12292
  514.5 52.3 %copy-start.225 = (f32[1024]{0:T(1024)S(1)}, f32[1024]{0:T(1024)}, u32[]{:S(2)}) copy-start(f32[1024]{0:T(1024)} %copy-done.224) | copy-start | bytes 12292
  514.5 52.3 %copy-start.236 = (f32[512]{0:T(512)S(1)}, f32[512]{0:T(512)}, u32[]{:S(2)}) copy-start(f32[512]{0:T(512)} %param.17) | copy-start | bytes 6148
  (205 other events, 351.7 us)
Sparse Core Ops, SparseCore 0:
  12.7 13.2 all-gather.4
  164.7 14.3 reduce-scatter.4
  180.8 11.8 all-gather.8
  194.7 11.7 all-gather.6
  224.9 13.1 reduce-scatter.8
  242.8 11.8 all-gather.10
  491.4 13.2 reduce-scatter.10
  507.5 10.8 reduce-scatter.6
  525.5 214.5 all-reduce.77
where the time goes:
time: 760 us; the launch traced here: 754 us
  matrix products  291 us (38%)
  waiting for transfers between devices  222 us (29%)
  other arithmetic  98.8 us (13%)
  local copies, waits for them, and re-layouts  75.4 us (10%)
  blocking collectives  48.5 us (6%)
  between operations  17.2 us (2%)
    psum x1, waiting for transfers between devices, body(): lax.psum((grad_w_qkv, grad_w_attn, grad_w_in, grad_w_out, grad_blend, gra...  169 us
    dot_general x40, matrix products, far_part(): first = round_grad(score_product(query_one, key_one)) * allowed  76.9 us
    unnamed x525, local copies, waits for them, and re-layouts  65 us
    dot_general x40, matrix products, far_part(): second = round_grad(score_product(query_two, key_two)) * allowed  64.9 us
    psum x1, blocking collectives, body(): lax.psum((grad_w_qkv, grad_w_attn, grad_w_in, grad_w_out, grad_blend, gra...  45.4 us
    sub x4, matrix products, near_part(): raised = jnp.exp(scores - top)  24.5 us
    dot_general x12, matrix products, near_part(): score_product(queries, keys)  18.1 us
    dot_general x30, matrix products, far_part(): second_sum = weight_product(round_value(second), values)  17.7 us
  transfers between devices with their start and end apart: 9, of which 7 were waited for; matrix products, arithmetic and copies ran while one was open for 7% of the time, Pallas kernels for 0%

commit v1 on v0

v1 whole, which is shorter than its diff:
```python
from functools import partial

import jax
import jax.numpy as jnp
from jax import lax
from jax.experimental import pallas as pl
from jax.experimental.pallas import tpu as pltpu
from jax.sharding import PartitionSpec as P

BAND = 30
HALO = 32
BLOCK = 128
EPS = 1e-06
BF = jnp.bfloat16
F32 = jnp.float32
VMEM_BYTES = 60 * 1024 * 1024
GELU_A = 0.7978845608028654
GELU_B = 0.044715


def nn(left, right):
    return lax.dot_general(left, right, (((1,), (0,)), ((), ())), preferred_element_type=F32)


def nt(left, right):
    return lax.dot_general(left, right, (((1,), (1,)), ((), ())), preferred_element_type=F32)


def tn(left, right):
    return lax.dot_general(left, right, (((0,), (0,)), ((), ())), preferred_element_type=F32)


def iota(shape, dim):
    return lax.broadcasted_iota(jnp.int32, shape, dim)


def whole(shape):
    return pl.BlockSpec(shape, lambda *_: (0,) * len(shape))


def params():
    return pltpu.CompilerParams(vmem_limit_bytes=VMEM_BYTES)


def starts_of(ends_ref, places, docs):
    start = jnp.full(places.shape, ends_ref[docs], jnp.int32)
    for doc in range(docs):
        end = ends_ref[doc]
        start = jnp.where(places >= end, jnp.maximum(start, end), start)
    return start


def start_at(ends_ref, place, docs):
    start = ends_ref[docs]
    for doc in range(docs):
        end = ends_ref[doc]
        start = jnp.where(place >= end, jnp.maximum(start, end), start)
    return start


def norm_project_kernel(x_ref, gain_ref, w_ref, normed_ref, out_ref):
    x = x_ref[...].astype(F32)
    r = lax.rsqrt(jnp.mean(x * x, axis=1, keepdims=True) + EPS)
    normed = (x * r * gain_ref[...]).astype(BF)
    normed_ref[...] = normed
    out_ref[...] = nn(normed, w_ref[...]).astype(BF)


def first_feature(values):
    return jnp.where(values > 0, values + 1.0, jnp.exp(jnp.minimum(values, 0.0))).astype(BF)


def second_feature(values):
    return jnp.tanh(values).astype(BF)


def pair_diag(rows, cols):
    row = iota((rows, cols), 0)
    col = iota((rows, cols), 1)
    return ((row // 64) % 2) == ((col // 64) % 2)


def project_state_kernel(docs, ends_ref, normed_ref, w_ref, own_ref, out_ref, state_ref, sum_ref, halo_ref):
    rows = normed_ref.shape[0]
    other = nn(normed_ref[...], w_ref[...]).astype(BF)
    out_ref[...] = other
    member_from = start_at(ends_ref, rows - 1, docs)
    member = iota((rows, 1), 0) >= member_from
    diag = pair_diag(256, 128)
    for pair in range(4):
        src = own_ref if pair < 2 else out_ref
        col = 128 * (pair % 2)
        slot = (pair + 2) % 4
        keys = src[:, 256 + col : 384 + col]
        values = src[:, 512 + col : 640 + col]
        wide = jnp.where(member, keys.astype(F32), 0.0)
        one = jnp.where(member, first_feature(wide).astype(F32), 0.0)
        two = second_feature(wide)
        features = jnp.concatenate([one.astype(BF), two], axis=1)
        state = jnp.where(diag, tn(features, values), 0.0)
        state_ref[slot] = state.astype(BF)
        sum_ref[slot] = jnp.broadcast_to(jnp.sum(one, axis=0, keepdims=True), (8, 128))
        halo_ref[:, 128 * slot : 128 * slot + 128] = keys[rows - HALO :]
        halo_ref[:, 512 + 128 * slot : 640 + 128 * slot] = values[rows - HALO :]


def block_masks(ends_ref, docs, first):
    row_places = first + iota((1, 256), 1) % BLOCK
    start_row = starts_of(ends_ref, row_places, docs)
    window_places = first - HALO + iota((BLOCK + HALO, 256), 0)
    banded = (window_places <= row_places) & (
        window_places >= jnp.maximum(start_row, row_places - (BAND - 1))
    )
    key_places = first + iota((BLOCK, 256), 0)
    causal = (key_places <= row_places) & (key_places >= start_row)
    col_places = first + iota((BLOCK, 1), 0)
    start_col = starts_of(ends_ref, col_places, docs)
    key_lane = first + iota((BLOCK, BLOCK), 1)
    causal_q = ((key_lane <= col_places) & (key_lane >= start_col)).astype(F32).astype(BF)
    count = (col_places - start_col + 1).astype(F32)
    carried = start_col < first
    member_from = start_at(ends_ref, first + BLOCK - 1, docs)
    member = col_places >= member_from
    keep = member_from < first
    return banded, causal, causal_q, count, carried, member, keep


def stack_heads(values):
    lane = iota(values.shape, 1) % 128
    zero = jnp.zeros_like(values)
    return jnp.concatenate(
        [jnp.where(lane < 64, values, zero), jnp.where(lane >= 64, values, zero)], axis=0
    )


def pick_heads(values):
    half = values.shape[0] // 2
    lane = iota((half, values.shape[1]), 1) % 128
    return jnp.where(lane < 64, values[:half], values[half:])


def pair_front(q, k, prev_k, blend_one, blend_two, carry, masks, ones_diag):
    banded, causal, causal_q, count, carried, member, keep = masks
    wide_q = q.astype(F32)
    wide_k = k.astype(F32)
    q_one = first_feature(wide_q)
    q_two = second_feature(wide_q)
    k_one = first_feature(wide_k)
    k_two = second_feature(wide_k)
    sums = nn(causal_q, k_one) + jnp.where(carried, carry, 0.0)
    total = nn((q_one.astype(F32) * sums).astype(BF), ones_diag)
    ratio_one = blend_one / total
    ratio_two = blend_two / count
    q_scaled = jnp.concatenate(
        [
            (q_one.astype(F32) * ratio_one).astype(BF),
            (q_two.astype(F32) * ratio_two).astype(BF),
        ],
        axis=1,
    )
    k_both = jnp.concatenate([k_one, k_two], axis=1)
    q_stack = stack_heads(q)
    s_stack = stack_heads(q_scaled)
    window = jnp.concatenate([prev_k, k], axis=0)
    scores = jnp.where(banded, nt(window, q_stack) * 0.125, -1e30)
    raised = jnp.exp(scores - jnp.max(scores, axis=0, keepdims=True))
    near = raised * (1.0 / jnp.sum(raised, axis=0, keepdims=True))
    far = jnp.where(causal, nt(k_both, s_stack), 0.0)
    weights = jnp.concatenate([near[:HALO], near[HALO:] + far], axis=0).astype(BF)
    return dict(
        q_one=q_one,
        q_two=q_two,
        k_one=k_one,
        k_two=k_two,
        sums=sums,
        total=total,
        ratio_one=ratio_one,
        ratio_two=ratio_two,
        q_scaled=q_scaled,
        k_both=k_both,
        q_stack=q_stack,
        s_stack=s_stack,
        window=window,
        near=near,
        weights=weights,
    )


def ones_diagonal():
    return pair_diag(128, 128).astype(F32).astype(BF)


def mixer_forward_kernel(
    docs,
    ends_ref,
    own_ref,
    other_ref,
    halo_ref,
    state_in_ref,
    sum_in_ref,
    blend_ref,
    mixed_ref,
    state_out_ref,
    sum_out_ref,
    prev_out_ref,
    state_ref,
    sum_ref,
    prev_ref,
):
    index = pl.program_id(0)
    first = index * BLOCK

    @pl.when(index == 0)
    def _():
        state_ref[...] = state_in_ref[...].astype(F32)
        sum_ref[...] = sum_in_ref[...]
        prev_ref[...] = halo_ref[...]

    masks = block_masks(ends_ref, docs, first)
    banded, causal, causal_q, count, carried, member, keep = masks
    diag = pair_diag(256, 128)
    ones_diag = ones_diagonal()
    prev_out_ref[0] = prev_ref[...]
    for pair in range(4):
        src = own_ref if pair < 2 else other_ref
        col = 128 * (pair % 2)
        lanes = slice(128 * pair, 128 * pair + 128)
        value_lanes = slice(512 + 128 * pair, 640 + 128 * pair)
        q = src[:, col : col + 128]
        k = src[:, 256 + col : 384 + col]
        v = src[:, 512 + col : 640 + col]
        state = state_ref[pair]
        carry = sum_ref[pair][0:1]
        state_low = state.astype(BF)
        state_out_ref[0, pair] = state_low
        sum_out_ref[0, pair] = sum_ref[pair]
        front = pair_front(
            q, k, prev_ref[:, lanes], blend_ref[0:1, lanes], blend_ref[1:2, lanes], carry, masks, ones_diag
        )
        v_window = jnp.concatenate([prev_ref[:, value_lanes], v], axis=0)
        out = pick_heads(tn(front["weights"], v_window))
        q_carried = jnp.where(carried, front["q_scaled"], jnp.zeros_like(front["q_scaled"]))
        out = out + nn(q_carried, state_low)
        mixed_ref[:, lanes] = out.astype(BF)
        k_member = jnp.where(member, front["k_both"], jnp.zeros_like(front["k_both"]))
        added = jnp.where(diag, tn(k_member, v), 0.0)
        state_ref[pair] = jnp.where(keep, state, 0.0) + added
        sum_ref[pair] = jnp.broadcast_to(front["sums"][BLOCK - 1 : BLOCK], (8, 128))
        prev_ref[:, lanes] = k[BLOCK - HALO :]
        prev_ref[:, value_lanes] = v[BLOCK - HALO :]


def mixer_backward_kernel(
    docs,
    ends_ref,
    own_ref,
    other_ref,
    prev_ref,
    state_ref,
    sum_ref,
    blend_ref,
    grad_ref,
    gq_ref,
    gk_ref,
    gv_ref,
    halo_ref,
    back_state_ref,
    back_sum_ref,
    blend_out_ref,
    dk_ref,
    dv_ref,
):
    step = pl.program_id(0)
    index = pl.num_programs(0) - 1 - step
    first = index * BLOCK

    @pl.when(step == 0)
    def _():
        back_state_ref[...] = jnp.zeros_like(back_state_ref)
        back_sum_ref[...] = jnp.zeros_like(back_sum_ref)
        blend_out_ref[...] = jnp.zeros_like(blend_out_ref)
        dk_ref[...] = jnp.zeros_like(dk_ref)
        dv_ref[...] = jnp.zeros_like(dv_ref)

    masks = block_masks(ends_ref, docs, first)
    banded, causal, causal_q, count, carried, member, keep = masks
    diag = pair_diag(256, 128)
    ones_diag = ones_diagonal()
    for pair in range(4):
        src = own_ref if pair < 2 else other_ref
        col = 128 * (pair % 2)
        lanes = slice(128 * pair, 128 * pair + 128)
        value_lanes = slice(512 + 128 * pair, 640 + 128 * pair)
        q = src[:, col : col + 128]
        k = src[:, 256 + col : 384 + col]
        v = src[:, 512 + col : 640 + col]
        grad = grad_ref[:, lanes]
        front = pair_front(
            q,
            k,
            prev_ref[0, :, lanes],
            blend_ref[0:1, lanes],
            blend_ref[1:2, lanes],
            sum_ref[0, pair][0:1],
            masks,
            ones_diag,
        )
        state = state_ref[0, pair]
        v_window = jnp.concatenate([prev_ref[0, :, value_lanes], v], axis=0)
        g_stack = stack_heads(grad)
        grad_weights = nt(v_window, g_stack)
        near = front["near"]
        inner = near * grad_weights
        dscores = (
            (inner - near * jnp.sum(inner, axis=0, keepdims=True)) * 0.125
        ).astype(BF)
        far = jnp.where(causal, grad_weights[HALO:], 0.0).astype(BF)
        up = pick_heads(tn(far, front["k_both"]))
        g_carried = jnp.where(carried, grad, jnp.zeros_like(grad))
        up = up + nt(g_carried, state)
        up_one = up[:, :128]
        up_two = up[:, 128:]
        q_one = front["q_one"].astype(F32)
        mean_one = nn((q_one * up_one).astype(BF), ones_diag) / front["total"]
        grad_one = front["ratio_one"] * (up_one - mean_one * front["sums"])
        grad_two = front["ratio_two"] * up_two
        tanh_q = jnp.tanh(q.astype(F32))
        slope_q = jnp.exp(jnp.minimum(q.astype(F32), 0.0))
        gq = pick_heads(tn(dscores, front["window"]))
        gq = gq + grad_one * slope_q + grad_two * (1.0 - tanh_q * tanh_q)
        gq_ref[:, lanes] = gq.astype(BF)
        blend_out_ref[0, pair] += jnp.broadcast_to(
            jnp.sum(mean_one, axis=0, keepdims=True) / 64.0, (8, 128)
        )
        blend_out_ref[1, pair] += jnp.broadcast_to(
            jnp.sum(front["q_two"].astype(F32) * up_two / count, axis=0, keepdims=True), (8, 128)
        )

        back = back_state_ref[pair]
        back_low = back.astype(BF)
        back_sum = back_sum_ref[pair][0:1]
        k_member = jnp.where(member, front["k_both"], jnp.zeros_like(front["k_both"]))
        v_member = jnp.where(member, v, jnp.zeros_like(v))
        dv = nn(front["weights"], g_stack)
        dv_own = dv[HALO:] + nn(k_member, back_low)
        weighted = (mean_one * front["q_scaled"][:, :128].astype(F32)).astype(BF)
        dfeat = nn(far, front["s_stack"]) + nt(v_member, back_low)
        d_one = dfeat[:, :128] - tn(causal_q, weighted) - jnp.where(member, back_sum, 0.0)
        d_two = dfeat[:, 128:]
        dk = nn(dscores, front["q_stack"])
        tanh_k = jnp.tanh(k.astype(F32))
        slope_k = jnp.exp(jnp.minimum(k.astype(F32), 0.0))
        gk = dk[HALO:] + d_one * slope_k + d_two * (1.0 - tanh_k * tanh_k)
        gk_ref[: BLOCK - HALO, lanes] = gk[: BLOCK - HALO].astype(BF)
        gk_ref[BLOCK - HALO :, lanes] = (gk[BLOCK - HALO :] + dk_ref[:, lanes]).astype(BF)
        gv_ref[: BLOCK - HALO, lanes] = dv_own[: BLOCK - HALO].astype(BF)
        gv_ref[BLOCK - HALO :, lanes] = (dv_own[BLOCK - HALO :] + dv_ref[:, lanes]).astype(BF)
        dk_ref[:, lanes] = dk[:HALO]
        dv_ref[:, lanes] = dv[:HALO]
        q_carried = jnp.where(carried, front["q_scaled"], jnp.zeros_like(front["q_scaled"]))
        added = jnp.where(diag, tn(q_carried, grad), 0.0)
        back_state_ref[pair] = jnp.where(keep, back, 0.0) + added
        added_sum = jnp.sum(
            jnp.where(carried, weighted.astype(F32), 0.0), axis=0, keepdims=True
        )
        back_sum_ref[pair] = jnp.broadcast_to(
            jnp.where(keep, back_sum, 0.0) + added_sum, (8, 128)
        )

    @pl.when(index == 0)
    def _():
        halo_ref[:, :512] = dk_ref[...]
        halo_ref[:, 512:] = dv_ref[...]


def feed_kernel(
    mixed_ref,
    x_ref,
    cot_ref,
    gain_ref,
    wa_own_ref,
    wa_other_ref,
    wi_own_ref,
    wi_other_ref,
    wo_own_ref,
    wo_other_ref,
    out_ref,
    normed_ref,
    active_ref,
    gpre_ref,
    ghid_ref,
    branch_ref,
    gmix_ref,
    ggain_ref,
):
    step = pl.program_id(0)
    x = x_ref[...].astype(F32)
    hidden = x + (nn(mixed_ref[:, :256], wa_own_ref[...]) + nn(mixed_ref[:, 256:], wa_other_ref[...]))
    r = lax.rsqrt(jnp.mean(hidden * hidden, axis=1, keepdims=True) + EPS)
    y = hidden * r
    gain = gain_ref[...]
    normed = (y * gain).astype(BF)
    normed_ref[...] = normed
    grad = cot_ref[...]
    total = hidden
    back = None
    for half, (wi_ref, wo_ref) in enumerate(((wi_own_ref, wo_own_ref), (wi_other_ref, wo_other_ref))):
        width = wi_ref.shape[1]
        for part in range(2):
            cols = slice(part * width // 2, (part + 1) * width // 2)
            dest = slice(half * width + part * width // 2, half * width + (part + 1) * width // 2)
            u = nn(normed, wi_ref[:, cols])
            square = u * u
            t = jnp.tanh(u * (GELU_A + (GELU_A * GELU_B) * square))
            gate = 0.5 + 0.5 * t
            active = (u * gate).astype(BF)
            slope = gate + u * (0.5 - 0.5 * t * t) * (GELU_A + (3.0 * GELU_A * GELU_B) * square)
            active_ref[:, dest] = active
            total = total + nn(active, wo_ref[cols, :])
            gact = nt(grad, wo_ref[cols, :])
            gpre = (gact * slope).astype(BF)
            gpre_ref[:, dest] = gpre
            term = nt(gpre, wi_ref[:, cols])
            back = term if back is None else back + term
    out_ref[...] = total.astype(BF)
    scaled = back * gain
    ghid = grad.astype(F32) + r * (scaled - y * jnp.mean(scaled * y, axis=1, keepdims=True))
    ghid_ref[...] = ghid
    branch = ghid.astype(BF)
    branch_ref[...] = branch
    gmix_ref[:, :256] = nt(branch, wa_own_ref[...]).astype(BF)
    gmix_ref[:, 256:] = nt(branch, wa_other_ref[...]).astype(BF)

    @pl.when(step == 0)
    def _():
        ggain_ref[...] = jnp.zeros_like(ggain_ref)

    ggain_ref[0:1] += jnp.sum(back * y, axis=0, keepdims=True)


def weight_grads_kernel(mixed_ref, branch_ref, active_ref, cot_ref, normed_ref, gpre_ref, wo_ref, wi_ref):
    for half in range(2):
        wo_ref[half, 0:1024] = tn(active_ref[:, 1024 * half : 1024 * half + 1024], cot_ref[...]).astype(BF)
        wo_ref[half, 1024:1280] = tn(mixed_ref[:, 256 * half : 256 * half + 256], branch_ref[...]).astype(BF)
        wi_ref[half] = tn(normed_ref[...], gpre_ref[:, 1024 * half : 1024 * half + 1024]).astype(BF)


def finish_kernel(
    docs,
    ends_ref,
    flag_ref,
    own_ref,
    other_ref,
    normed_ref,
    gq_ref,
    gk_ref,
    gv_ref,
    halo_ref,
    back_state_ref,
    back_sum_ref,
    gproj_ref,
    wgrad_ref,
):
    rows = own_ref.shape[0]
    flag = flag_ref[0]
    member_from = start_at(ends_ref, rows - 1, docs)
    member = (iota((rows, 1), 0) >= member_from) & (flag == 0)
    live = flag == 0
    for pair in range(4):
        src = own_ref if pair < 2 else other_ref
        col = 128 * (pair % 2)
        lanes = slice(128 * pair, 128 * pair + 128)
        base = 768 * (pair // 2) + col
        slot = (pair + 2) % 4
        k = src[:, 256 + col : 384 + col].astype(F32)
        v = src[:, 512 + col : 640 + col]
        back = back_state_ref[slot].astype(BF)
        back_sum = back_sum_ref[slot][0:1]
        t = jnp.tanh(k)
        slope = jnp.exp(jnp.minimum(k, 0.0))
        k_both = jnp.concatenate([first_feature(k), t.astype(BF)], axis=1)
        dfeat = nt(v, back)
        extra_k = (dfeat[:, :128] - back_sum) * slope + dfeat[:, 128:] * (1.0 - t * t)
        extra_v = nn(k_both, back)
        gk = gk_ref[:, lanes].astype(F32) + jnp.where(member, extra_k, 0.0)
        gv = gv_ref[:, lanes].astype(F32) + jnp.where(member, extra_v, 0.0)
        other_lanes = slice(128 * slot, 128 * slot + 128)
        other_values = slice(512 + 128 * slot, 640 + 128 * slot)
        halo_k = jnp.where(live, halo_ref[:, other_lanes], 0.0)
        halo_v = jnp.where(live, halo_ref[:, other_values], 0.0)
        cut = rows - HALO
        gproj_ref[:, base : base + 128] = gq_ref[:, lanes]
        gproj_ref[:cut, base + 256 : base + 384] = gk[:cut].astype(BF)
        gproj_ref[cut:, base + 256 : base + 384] = (gk[cut:] + halo_k).astype(BF)
        gproj_ref[:cut, base + 512 : base + 640] = gv[:cut].astype(BF)
        gproj_ref[cut:, base + 512 : base + 640] = (gv[cut:] + halo_v).astype(BF)
    for half in range(2):
        wgrad_ref[half] = tn(normed_ref[...], gproj_ref[:, 768 * half : 768 * half + 768]).astype(BF)


def input_grad_kernel(gproj_ref, x_ref, ghid_ref, gain_ref, w_own_ref, w_other_ref, out_ref, ggain_ref):
    step = pl.program_id(0)
    gnormed = nt(gproj_ref[:, :768], w_own_ref[...]) + nt(gproj_ref[:, 768:], w_other_ref[...])
    x = x_ref[...].astype(F32)
    r = lax.rsqrt(jnp.mean(x * x, axis=1, keepdims=True) + EPS)
    y = x * r
    scaled = gnormed * gain_ref[...]
    grad = ghid_ref[...] + r * (scaled - y * jnp.mean(scaled * y, axis=1, keepdims=True))
    out_ref[...] = grad.astype(BF)

    @pl.when(step == 0)
    def _():
        ggain_ref[...] = jnp.zeros_like(ggain_ref)

    ggain_ref[0:1] += jnp.sum(gnormed * y, axis=0, keepdims=True)


def dp_dims(count):
    dims = []
    stride = 1
    left = count
    for size in (2, 2):
        if left % size == 0 and left > 1:
            dims.append((size, stride))
            stride *= size
            left //= size
    while left > 1:
        size = 4 if left % 4 == 0 else (2 if left % 2 == 0 else left)
        dims.append((size, stride))
        stride *= size
        left //= size
    return dims


def shift_pairs(count, size, stride, offset):
    pairs = []
    for src in range(count):
        place = (src // stride) % size
        pairs.append((src, src + ((place + offset) % size - place) * stride))
    return pairs


def scatter_step(values, count, size, stride):
    place = (lax.axis_index("dp") // stride) % size
    parts = values.reshape((size, values.shape[0] // size) + values.shape[1:])
    total = lax.dynamic_index_in_dim(parts, place, 0, keepdims=False).astype(F32)
    for offset in range(1, size):
        sent = lax.dynamic_index_in_dim(parts, (place + offset) % size, 0, keepdims=False)
        got = lax.ppermute(sent, "dp", shift_pairs(count, size, stride, offset))
        total = total + got.astype(F32)
    return total.astype(values.dtype)


def gather_step(values, count, size, stride):
    place = (lax.axis_index("dp") // stride) % size
    whole_values = jnp.zeros((size,) + values.shape, values.dtype)
    whole_values = lax.dynamic_update_index_in_dim(whole_values, values, place, 0)
    for offset in range(1, size):
        got = lax.ppermute(values, "dp", shift_pairs(count, size, stride, offset))
        whole_values = lax.dynamic_update_index_in_dim(
            whole_values, got, (place - offset) % size, 0
        )
    return whole_values.reshape((size * values.shape[0],) + values.shape[1:])


def reduce_all(values, count):
    dims = dp_dims(count)
    if not dims:
        return values
    orders = [dims]
    if len(dims) > 1:
        orders.append([dims[1], dims[0]] + dims[2:])
    pieces = []
    for part, order in zip(jnp.split(values, len(orders), axis=0), orders):
        for size, stride in order:
            part = scatter_step(part, count, size, stride)
        for size, stride in reversed(order):
            part = gather_step(part, count, size, stride)
        pieces.append(part)
    return jnp.concatenate(pieces, axis=0)


def reduce_small(values, count):
    for size, stride in dp_dims(count):
        total = values
        for offset in range(1, size):
            total = total + lax.ppermute(values, "dp", shift_pairs(count, size, stride, offset))
        values = total
    return values


def swap(values):
    return lax.ppermute(values, "tensor", [(0, 1), (1, 0)])


def body(count, tokens, lengths, w_qkv, w_attn, w_in, w_out, gain_attn, gain_mlp, blend, cotangent):
    rows, width = tokens.shape
    docs = lengths.shape[1]
    half = lax.axis_index("tensor").astype(jnp.int32)
    blocks = rows // BLOCK

    wq_own = w_qkv.reshape(width, -1)
    wq_other = swap(wq_own)
    wa_other, wi_other, wo_other = swap(w_attn), swap(w_in), swap(w_out)
    blend_both = jnp.repeat(jnp.concatenate([blend, swap(blend)], axis=1), 64, axis=1)
    ends = jnp.concatenate([jnp.cumsum(lengths[0]), jnp.zeros((1,), jnp.int32)]).astype(jnp.int32) - half * rows
    flag = half.reshape(1)
    gain_one = gain_attn.reshape(1, width)
    gain_two = gain_mlp.reshape(1, width)
    smem = pl.BlockSpec(memory_space=pltpu.SMEM)

    def row_block(size, cols):
        return pl.BlockSpec((size, cols), lambda i: (i, 0))

    own_cols = wq_own.shape[1]
    normed, own = pl.pallas_call(
        norm_project_kernel,
        grid=(4,),
        in_specs=[row_block(rows // 4, width), whole((1, width)), whole(wq_own.shape)],
        out_specs=[row_block(rows // 4, width), row_block(rows // 4, own_cols)],
        out_shape=[jax.ShapeDtypeStruct((rows, width), BF), jax.ShapeDtypeStruct((rows, own_cols), BF)],
        compiler_params=params(),
        name="norm_project",
    )(tokens, gain_one, wq_own)
    other, state_end, sum_end, halo_end = pl.pallas_call(
        partial(project_state_kernel, docs),
        in_specs=[smem] + [pl.BlockSpec(memory_space=pltpu.VMEM)] * 3,
        out_shape=[
            jax.ShapeDtypeStruct((rows, own_cols), BF),
            jax.ShapeDtypeStruct((4, 256, 128), BF),
            jax.ShapeDtypeStruct((4, 8, 128), F32),
            jax.ShapeDtypeStruct((HALO, 1024), BF),
        ],
        compiler_params=params(),
        name="project_state",
    )(ends, normed, wq_other, own)
    state_in, sum_in, halo_in = swap(state_end), swap(sum_end), swap(halo_end)

    mixed, states, sums, prevs = pl.pallas_call(
        partial(mixer_forward_kernel, docs),
        grid=(blocks,),
        in_specs=[
            smem,
            row_block(BLOCK, own_cols),
            row_block(BLOCK, own_cols),
            whole((HALO, 1024)),
            whole((4, 256, 128)),
            whole((4, 8, 128)),
            whole(blend_both.shape),
        ],
        out_specs=[
            row_block(BLOCK, width),
            pl.BlockSpec((1, 4, 256, 128), lambda i: (i, 0, 0, 0)),
            pl.BlockSpec((1, 4, 8, 128), lambda i: (i, 0, 0, 0)),
            pl.BlockSpec((1, HALO, 1024), lambda i: (i, 0, 0)),
        ],
        out_shape=[
            jax.ShapeDtypeStruct((rows, width), BF),
            jax.ShapeDtypeStruct((blocks, 4, 256, 128), BF),
            jax.ShapeDtypeStruct((blocks, 4, 8, 128), F32),
            jax.ShapeDtypeStruct((blocks, HALO, 1024), BF),
        ],
        scratch_shapes=[
            pltpu.VMEM((4, 256, 128), F32),
            pltpu.VMEM((4, 8, 128), F32),
            pltpu.VMEM((HALO, 1024), BF),
        ],
        compiler_params=params(),
        name="mixer_forward",
    )(ends, own, other, halo_in, state_in, sum_in, blend_both)

    hidden_units = 2 * w_in.shape[1]
    tall = rows // 4
    output, normed_two, active, gpre, ghid, branch, gmix, ggain_mlp = pl.pallas_call(
        feed_kernel,
        grid=(4,),
        in_specs=[
            row_block(tall, width),
            row_block(tall, width),
            row_block(tall, width),
            whole((1, width)),
            whole(w_attn.shape),
            whole(w_attn.shape),
            whole(w_in.shape),
            whole(w_in.shape),
            whole(w_out.shape),
            whole(w_out.shape),
        ],
        out_specs=[
            row_block(tall, width),
            row_block(tall, width),
            row_block(tall, hidden_units),
            row_block(tall, hidden_units),
            row_block(tall, width),
            row_block(tall, width),
            row_block(tall, width),
            whole((8, width)),
        ],
        out_shape=[
            jax.ShapeDtypeStruct((rows, width), BF),
            jax.ShapeDtypeStruct((rows, width), BF),
            jax.ShapeDtypeStruct((rows, hidden_units), BF),
            jax.ShapeDtypeStruct((rows, hidden_units), BF),
            jax.ShapeDtypeStruct((rows, width), F32),
            jax.ShapeDtypeStruct((rows, width), BF),
            jax.ShapeDtypeStruct((rows, width), BF),
            jax.ShapeDtypeStruct((8, width), F32),
        ],
        compiler_params=params(),
        name="feed",
    )(mixed, tokens, cotangent, gain_two, w_attn, wa_other, w_in, wi_other, w_out, wo_other)

    wo_grads, wi_grads = pl.pallas_call(
        weight_grads_kernel,
        out_shape=[
            jax.ShapeDtypeStruct((2, w_out.shape[0] + w_attn.shape[0], width), BF),
            jax.ShapeDtypeStruct((2, width, w_in.shape[1]), BF),
        ],
        compiler_params=params(),
        name="weight_grads",
    )(mixed, branch, active, cotangent, normed_two, gpre)

    def join_halves(pair):
        return (pair[0].astype(F32) + swap(pair[1]).astype(F32)).astype(BF)

    wo_sum = reduce_all(join_halves(wo_grads), count)
    wi_sum = reduce_all(join_halves(wi_grads), count)

    back_block = lambda size, cols: pl.BlockSpec((size, cols), lambda i: (blocks - 1 - i, 0))
    gq, gk, gv, halo_back, back_state, back_sum, gblend = pl.pallas_call(
        partial(mixer_backward_kernel, docs),
        grid=(blocks,),
        in_specs=[
            smem,
            back_block(BLOCK, own_cols),
            back_block(BLOCK, own_cols),
            pl.BlockSpec((1, HALO, 1024), lambda i: (blocks - 1 - i, 0, 0)),
            pl.BlockSpec((1, 4, 256, 128), lambda i: (blocks - 1 - i, 0, 0, 0)),
            pl.BlockSpec((1, 4, 8, 128), lambda i: (blocks - 1 - i, 0, 0, 0)),
            whole(blend_both.shape),
            back_block(BLOCK, width),
        ],
        out_specs=[
            back_block(BLOCK, width),
            back_block(BLOCK, width),
            back_block(BLOCK, width),
            whole((HALO, 1024)),
            whole((4, 256, 128)),
            whole((4, 8, 128)),
            whole((2, 4, 8, 128)),
        ],
        out_shape=[
            jax.ShapeDtypeStruct((rows, width), BF),
            jax.ShapeDtypeStruct((rows, width), BF),
            jax.ShapeDtypeStruct((rows, width), BF),
            jax.ShapeDtypeStruct((HALO, 1024), F32),
            jax.ShapeDtypeStruct((4, 256, 128), F32),
            jax.ShapeDtypeStruct((4, 8, 128), F32),
            jax.ShapeDtypeStruct((2, 4, 8, 128), F32),
        ],
        scratch_shapes=[pltpu.VMEM((HALO, 512), F32), pltpu.VMEM((HALO, 512), F32)],
        compiler_params=params(),
        name="mixer_backward",
    )(ends, own, other, prevs, states, sums, blend_both, gmix)
    halo_got, back_state_got, back_sum_got = swap(halo_back), swap(back_state), swap(back_sum)

    gproj, wq_grads = pl.pallas_call(
        partial(finish_kernel, docs),
        in_specs=[smem, smem] + [pl.BlockSpec(memory_space=pltpu.VMEM)] * 9,
        out_shape=[
            jax.ShapeDtypeStruct((rows, 2 * own_cols), BF),
            jax.ShapeDtypeStruct((2, width, own_cols), BF),
        ],
        compiler_params=params(),
        name="finish",
    )(ends, flag, own, other, normed, gq, gk, gv, halo_got, back_state_got, back_sum_got)
    wq_sum = reduce_all(join_halves(wq_grads), count)

    grad_input, ggain_attn = pl.pallas_call(
        input_grad_kernel,
        grid=(4,),
        in_specs=[
            row_block(tall, 2 * own_cols),
            row_block(tall, width),
            row_block(tall, width),
            whole((1, width)),
            whole(wq_own.shape),
            whole(wq_own.shape),
        ],
        out_specs=[row_block(tall, width), whole((8, width))],
        out_shape=[jax.ShapeDtypeStruct((rows, width), BF), jax.ShapeDtypeStruct((8, width), F32)],
        compiler_params=params(),
        name="input_grad",
    )(gproj, tokens, ghid, gain_one, wq_own, wq_other)

    gblend_heads = jnp.sum(gblend[:, :, 0].reshape(2, 8, 64), axis=2)
    gblend_own = gblend_heads[:, :4] + swap(gblend_heads[:, 4:])
    gains = jnp.concatenate([ggain_attn[:1], ggain_mlp[:1]], axis=0)
    gains = gains + swap(gains)
    small = jnp.concatenate([gains, jnp.pad(gblend_own.reshape(1, 8), ((0, 0), (0, width - 8)))], axis=0)
    small = reduce_small(small, count)

    units = w_out.shape[0]
    return (
        output,
        grad_input,
        wq_sum.astype(F32).reshape(w_qkv.shape),
        wo_sum[units:].astype(F32),
        wi_sum.astype(F32),
        wo_sum[:units].astype(F32),
        small[0],
        small[1],
        small[2, :8].reshape(2, 4),
    )


def solution(mesh):
    return jax.shard_map(
        partial(body, mesh.shape["dp"]),
        mesh=mesh,
        in_specs=(
            P(("dp", "tensor"), None),
            P("dp", None),
            P(None, None, "tensor"),
            P("tensor", None),
            P(None, "tensor"),
            P("tensor", None),
            P(),
            P(),
            P(None, "tensor"),
            P(("dp", "tensor"), None),
        ),
        out_specs=(
            P(("dp", "tensor"), None),
            P(("dp", "tensor"), None),
            P(None, None, "tensor"),
            P("tensor", None),
            P(None, "tensor"),
            P("tensor", None),
            P(),
            P(),
            P(None, "tensor"),
        ),
        check_vma=False,
    )
```

time: 760 us -> 345 us (0.45)
  matrix products: 291 us -> 0 us
  waiting for transfers between devices: 222 us -> 70.4 us
  Pallas kernels: 0 us -> 104 us
  other arithmetic: 98.8 us -> 14 us
  starting transfers between devices: 0.62 us -> 78.8 us
  blocking collectives: 48.5 us -> 0 us
  between operations: 17.2 us -> 1.49 us
    dot_general x176 -> x0, matrix products: 267 us -> none  [the longest x40 76.9 us: far_part(): first = round_grad(score_product(query_one, key_one)) * allowed]
    psum x1 -> x0, waiting for transfers between devices: 169 us -> none  [body(): lax.psum((grad_w_qkv, grad_w_attn, grad_w_in, grad_w_out, grad_blend, gra...]
    pallas_call x0 -> x8, Pallas kernels: none -> 104 us  [the longest x1 27.1 us: body(): pl.pallas_call(partial(mixer_backward_kernel, docs), grid=(blocks,), in_s...]
    ppermute x0 -> x81, starting transfers between devices: none -> 78.8 us  [the longest x30 37.8 us: scatter_step(): got = lax.ppermute(sent, 'dp', shift_pairs(count, size, stride, offset))]
    ppermute x0 -> x81, waiting for transfers between devices: none -> 70.4 us  [the longest x30 46.1 us: gather_step(): got = lax.ppermute(values, 'dp', shift_pairs(count, size, stride, offset))]
    unnamed x525 -> x38, local copies, waits for them, and re-layouts: 65 us -> 6.27 us
    dynamic_update_slice x0 -> x42, local copies, waits for them, and re-layouts: none -> 51.4 us  [the longest x30 26.7 us: gather_step(): lax.dynamic_update_index_in_dim(whole_values, got, (place - offset) % siz...]
    psum x2 -> x0, blocking collectives: 48.5 us -> none  [the longest x1 45.4 us: body(): lax.psum((grad_w_qkv, grad_w_attn, grad_w_in, grad_w_out, grad_blend, gra...]
  transfers between devices with their start and end apart: 9 -> 81, of which waited for: 7 -> 31; matrix products, arithmetic and copies ran while one was open for 7% -> 24% of each run, Pallas kernels for 0% -> 16%
where the time goes in v1:
time: 345 us; the launch traced here: 344 us
  Pallas kernels  104 us (30%)
  starting transfers between devices  78.8 us (23%)
  local copies, waits for them, and re-layouts  75.1 us (22%)
  waiting for transfers between devices  70.4 us (20%)
  other arithmetic  14 us (4%)
    ppermute x30, waiting for transfers between devices, gather_step(): got = lax.ppermute(values, 'dp', shift_pairs(count, size, stride, offset))  46.1 us
    ppermute x30, starting transfers between devices, scatter_step(): got = lax.ppermute(sent, 'dp', shift_pairs(count, size, stride, offset))  37.8 us
    pallas_call x1, Pallas kernels, body(): pl.pallas_call(partial(mixer_backward_kernel, docs), grid=(blocks,), in_s...  27.1 us
    ppermute x30, starting transfers between devices, gather_step(): got = lax.ppermute(values, 'dp', shift_pairs(count, size, stride, offset))  26.9 us
    dynamic_update_slice x30, local copies, waits for them, and re-layouts, gather_step(): lax.dynamic_update_index_in_dim(whole_values, got, (place - offset) % siz...  26.7 us
    dynamic_update_slice x12, local copies, waits for them, and re-layouts, gather_step(): lax.dynamic_update_index_in_dim(whole_values, values, place, 0)  24.8 us
    pallas_call x1, Pallas kernels, body(): pl.pallas_call(feed_kernel, grid=(4,), in_specs=[row_block(tall, width),...  21 us
    pallas_call x1, Pallas kernels, body(): pl.pallas_call(partial(mixer_forward_kernel, docs), grid=(blocks,), in_sp...  20.9 us
  transfers between devices with their start and end apart: 81, of which 31 were waited for; matrix products, arithmetic and copies ran while one was open for 24% of the time, Pallas kernels for 16%

profile of v1, /device:TPU:0, one launch (start us, length us, event | category | flops | bytes accessed | tf_op | source)
XLA Modules:
  0.0 343.9 jit_solution(16690813809728456199)
XLA Ops:
  0.7 1.5 copy.39
  3.5 4.6 %norm_project.1 = (bf16[1024,512]{1,0:T(8,128)(2,1)}, bf16[1024,768]{1,0:T(8,128)(2,1)}) custom-call(bf16[1024,512]{1,0:T(8,128)(2,1)} %x_ref.5, f32[1,512]{1,0:T(1,128)} %bitcast.341, bf16[512,768]{1,0:T(8,128)(2,1)} %copy-done), custom_call_target="tpu_custom_call" | custom-call | tf_op jit(solution)/shard_map/norm_project/pallas_call | solution.py:616
  9.7 4.9 %project_state.1 = (bf16[1024,768]{1,0:T(8,128)(2,1)}, bf16[4,256,128]{2,1,0:T(8,128)(2,1)}, f32[4,8,128]{2,1,0:T(8,128)}, bf16[32,1024]{1,0:T(8,128)(2,1)}) custom-call(s32[7]{0:T(128)} %add_subtract_fusion.ends_ref, bf16[1024,512]{1,0:T(8,128)(2,1)} %get-tuple-element.41.normed_ref, bf16[512,768]{1,0:T(8,128)(2,1)} %copy-done.1, ...), custom_call_target="tpu_custom_call" | custom-call | tf_op jit(solution)/shard_map/project_state/pallas_call | solution.py:625
  20.1 20.9 %mixer_forward.1 = (bf16[1024,512]{1,0:T(8,128)(2,1)}, bf16[8,4,256,128]{3,2,1,0:T(8,128)(2,1)}, f32[8,4,8,128]{3,2,1,0:T(8,128)}, bf16[8,32,1024]{2,1,0:T(8,128)(2,1)}) custom-call(s32[7]{0:T(128)} %add_subtract_fusion.ends_ref, bf16[1024,768]{1,0:T(8,128)(2,1)} %get-tuple-element.40.own_ref, bf16[1024,768]{1,0:T(8,128)(2,1)} %get-tuple-element.42.other_ref, ...), custom_call_target="tpu_custom_call" | custom-call | tf_op jit(solution)/shard_map/mixer_forward/pallas_call | solution.py:639
  41.7 21.0 %feed.1 = (bf16[1024,512]{1,0:T(8,128)(2,1)}, bf16[1024,512]{1,0:T(8,128)(2,1)}, bf16[1024,2048]{1,0:T(8,128)(2,1)}, bf16[1024,2048]{1,0:T(8,128)(2,1)}, f32[102...) custom-call(bf16[1024,512]{1,0:T(8,128)(2,1)} %get-tuple-element.46.mixed_ref, ...), custom_call_target="tpu_custom_call" | custom-call | tf_op jit(solution)/shard_map/feed/pallas_call | solution.py:674
  62.7 27.1 %mixer_backward.1 = (bf16[1024,512]{1,0:T(8,128)(2,1)}, bf16[1024,512]{1,0:T(8,128)(2,1)}, bf16[1024,512]{1,0:T(8,128)(2,1)}, f32[32,1024]{1,0:T(8,128)}, f32[4,...) custom-call(s32[7]{0:T(128)} %add_subtract_fusion.ends_ref, ...), custom_call_target="tpu_custom_call" | custom-call | tf_op jit(solution)/shard_map/mixer_backward/pallas_call | solution.py:730
  92.7 11.0 %weight_grads.1 = (bf16[2,1280,512]{2,1,0:T(8,128)(2,1)}, bf16[2,512,1024]{2,1,0:T(8,128)(2,1)}) custom-call(bf16[1024,512]{1,0:T(8,128)(2,1)} %get-tuple-element.46.mixed_ref, bf16[1024,512]{1,0:T(8,128)(2,1)} %get-tuple-element.62.branch_ref, bf16[1024,2048]{1,0:T(8,128)(2,1)} %get-tuple-element.63.active_ref, bf16[1024,512]{1,0:T(8,128)(2,1)} %cot_ref.3, ...), custom_call_target="tpu_custom_call" | custom-call | tf_op jit(solution)/shard_map/weight_grads/pallas_call | solution.py:713
  104.6 8.0 %finish.1 = (bf16[1024,1536]{1,0:T(8,128)(2,1)}, bf16[2,512,768]{2,1,0:T(8,128)(2,1)}) custom-call(s32[7]{0:T(128)} %add_subtract_fusion.ends_ref, s32[1]{0:T(128)} %bitcast.5.flag_ref, bf16[1024,768]{1,0:T(8,128)(2,1)} %get-tuple-element.40.own_ref, bf16[1024,768]{1,0:T(8,128)(2,1)} %get-tuple-element.42.other_ref, ...), custom_call_target="tpu_custom_call" | custom-call | tf_op jit(solution)/shard_map/finish/pallas_call | solution.py:767
  112.6 6.6 %input_grad.1 = (bf16[1024,512]{1,0:T(8,128)(2,1)}, f32[8,512]{1,0:T(8,128)}) custom-call(bf16[1024,1536]{1,0:T(8,128)(2,1)} %get-tuple-element.58.gproj_ref, bf16[1024,512]{1,0:T(8,128)(2,1)} %x_ref.5, f32[1024,512]{1,0:T(8,128)} %get-tuple-element.59.ghid_ref, f32[1,512]{1,0:T(1,128)} %bitcast.342, bf16[512,768]{1,0:T(8,128)(2,1)} %copy-done, ...), custom_call_target="tpu_custom_call" | custom-call | tf_op jit(solution)/shard_map/input_grad/pallas_call | solution.py:779
  121.2 2.8 collective-permute-start.76
  124.0 2.4 slice_bitcast_fusion.1
  126.4 1.6 collective-permute-start.77
  130.2 1.6 collective-permute-start.78
  131.7 2.6 collective-permute-start.79
  134.3 1.4 collective-permute-start.80
  136.3 1.7 collective-permute-done.80
  139.2 1.9 fusion.1
  141.3 1.3 collective-permute-start.44
  142.6 1.6 collective-permute-start.54
  144.2 1.7 fusion
  147.5 1.8 collective-permute-done.44
  149.4 2.7 collective-permute-start.45
  152.2 1.5 collective-permute-start.55
  153.7 1.3 fusion.2
  155.2 3.7 %collective-permute-done.45 = bf16[64,1024]{1,0:T(8,128)(2,1)S(1)} collective-permute-done((bf16[64,1024]{1,0:T(8,128)(2,1)S(1)}, bf16[64,1024]{1,0:T(8,128)(2,1)S(1)}, u32[]{:S(2)}, u32[]{:S(2)}) %collective-permute-start.45) | collective-permute-done | bytes 131104 | tf_op jit(solution)/shard_map/ppermute | solution.py:549
  159.6 3.1 collective-permute-start.47
  162.9 1.9 collective-permute-done.46
  165.5 2.4 collective-permute-start.57
  167.8 1.3 collective-permute-start.58
  169.2 1.5 collective-permute-done.56
  171.3 1.5 collective-permute-start.22
  173.6 2.8 collective-permute-done.12
  177.0 2.5 collective-permute-start.51
  179.7 5.7 %collective-permute-done.59 = bf16[16,1024]{1,0:T(8,128)(2,1)S(1)} collective-permute-done((bf16[16,1024]{1,0:T(8,128)(2,1)S(1)}, bf16[16,1024]{1,0:T(8,128)(2,1)S(1)}, u32[]{:S(2)}, u32[]{:S(2)}) %collective-permute-start.59) | collective-permute-done | bytes 32800 | tf_op jit(solution)/shard_map/ppermute | solution.py:559
  186.2 3.9 %collective-permute-done.60 = bf16[16,1024]{1,0:T(8,128)(2,1)S(1)} collective-permute-done((bf16[16,1024]{1,0:T(8,128)(2,1)S(1)}, bf16[16,1024]{1,0:T(8,128)(2,1)S(1)}, u32[]{:S(2)}, u32[]{:S(2)}) %collective-permute-start.60) | collective-permute-done | bytes 32800 | tf_op jit(solution)/shard_map/ppermute | solution.py:559
  190.2 1.3 collective-permute-start.13
  196.2 2.8 collective-permute-start.16
  199.1 1.7 collective-permute-done.14
  201.4 3.5 %collective-permute-start.26 = (bf16[16,768]{1,0:T(8,128)(2,1)S(1)}, bf16[16,768]{1,0:T(8,128)(2,1)S(1)}, u32[]{:S(2)}, u32[]{:S(2)}) collective-permute-start(bf16[16,768]{1,0:T(8,128)(2,1)S(1)} %get-tuple-element.123), channel_id=1, source_target_pairs={{0,24},{2,26},{4,28},{6,30},{8,0},{10,2},{12,4},{14,6},{16,8},{18,... | collective-permute-start | bytes 73736 | tf_op jit(solution)/shard_map/ppermute | solution.py:549
  204.9 1.5 collective-permute-done.24
  209.3 2.1 collective-permute-start.18
  219.6 3.0 collective-permute-start.29
  222.5 1.5 collective-permute-start.65
  224.6 1.5 collective-permute-start.53
  226.7 1.6 collective-permute-start.20
  229.6 4.1 %collective-permute-done.20 = bf16[64,768]{1,0:T(8,128)(2,1)S(1)} collective-permute-done((bf16[64,768]{1,0:T(8,128)(2,1)S(1)}, bf16[64,768]{1,0:T(8,128)(2,1)S(1)}, u32[]{:S(2)}, u32[]{:S(2)}) %collective-permute-start.20) | collective-permute-done | bytes 98336 | tf_op jit(solution)/shard_map/ppermute | solution.py:559
  234.7 3.7 %collective-permute-done.30 = bf16[64,768]{1,0:T(8,128)(2,1)S(1)} collective-permute-done((bf16[64,768]{1,0:T(8,128)(2,1)S(1)}, bf16[64,768]{1,0:T(8,128)(2,1)S(1)}, u32[]{:S(2)}, u32[]{:S(2)}) %collective-permute-start.30) | collective-permute-done | bytes 98336 | tf_op jit(solution)/shard_map/ppermute | solution.py:559
  240.5 9.5 %dynamic_update_slice.159 = bf16[2,128,768]{1,0,2:T(2,128)(2,1)S(1)} dynamic-update-slice(bf16[2,128,768]{1,0,2:T(2,128)(2,1)S(1)} %broadcast.45.clone.1, bf16[1,128,768]{1,0,2:T(2,128)(2,1)S(1)} %copy.43, s32[]{:T(128)S(6)} %select_n.403, s32[]{:T(128)} %constant.578.clone.1, s32[]{:T(128)} %constant.578.clone.1) | dynamic-update-slice | bytes 393220 | tf_op jit(solution)/shard_map/jit(dynamic_update_index_in_dim)/dynamic_update_slice | solution.py:557
  250.2 9.5 %dynamic_update_slice.167 = bf16[2,128,768]{1,0,2:T(2,128)(2,1)S(1)} dynamic-update-slice(bf16[2,128,768]{1,0,2:T(2,128)(2,1)S(1)} %broadcast.45.clone, bf16[1,128,768]{1,0,2:T(2,128)(2,1)S(1)} %copy.45, s32[]{:T(128)S(6)} %select_n.408, s32[]{:T(128)} %constant.578.clone.1, s32[]{:T(128)} %constant.578.clone.1) | dynamic-update-slice | bytes 393220 | tf_op jit(solution)/shard_map/jit(dynamic_update_index_in_dim)/dynamic_update_slice | solution.py:557
  261.7 2.8 collective-permute-start.68
  267.7 2.8 collective-permute-start.37
  276.6 3.5 %collective-permute-done.69 = bf16[40,512]{1,0:T(8,128)(2,1)S(1)} collective-permute-done((bf16[40,512]{1,0:T(8,128)(2,1)S(1)}, bf16[40,512]{1,0:T(8,128)(2,1)S(1)}, u32[]{:S(2)}, u32[]{:S(2)}) %collective-permute-start.69) | collective-permute-done | bytes 40992 | tf_op jit(solution)/shard_map/ppermute | solution.py:559
  280.8 4.3 %collective-permute-done.70 = bf16[40,512]{1,0:T(8,128)(2,1)S(1)} collective-permute-done((bf16[40,512]{1,0:T(8,128)(2,1)S(1)}, bf16[40,512]{1,0:T(8,128)(2,1)S(1)}, u32[]{:S(2)}, u32[]{:S(2)}) %collective-permute-start.70) | collective-permute-done | bytes 40992 | tf_op jit(solution)/shard_map/ppermute | solution.py:559
  285.9 3.2 collective-permute-done.71
  289.7 5.2 %collective-permute-done.38 = bf16[40,512]{1,0:T(8,128)(2,1)S(1)} collective-permute-done((bf16[40,512]{1,0:T(8,128)(2,1)S(1)}, bf16[40,512]{1,0:T(8,128)(2,1)S(1)}, u32[]{:S(2)}, u32[]{:S(2)}) %collective-permute-start.38) | collective-permute-done | bytes 40992 | tf_op jit(solution)/shard_map/ppermute | solution.py:559
  295.5 4.3 %collective-permute-done.39 = bf16[40,512]{1,0:T(8,128)(2,1)S(1)} collective-permute-done((bf16[40,512]{1,0:T(8,128)(2,1)S(1)}, bf16[40,512]{1,0:T(8,128)(2,1)S(1)}, u32[]{:S(2)}, u32[]{:S(2)}) %collective-permute-start.39) | collective-permute-done | bytes 40992 | tf_op jit(solution)/shard_map/ppermute | solution.py:559
  300.6 3.2 collective-permute-done.40
  307.2 1.4 collective-permute-start.41
  310.5 1.6 maximum_convert_fusion
  312.5 9.5 %dynamic_update_slice.160 = bf16[2,128,768]{1,0,2:T(2,128)(2,1)S(1)} dynamic-update-slice(bf16[2,128,768]{1,0,2:T(2,128)(2,1)S(1)} %dynamic_update_slice.159, bf16[1,128,768]{1,0,2:T(2,128)(2,1)S(1)} %copy.44, s32[]{:T(128)S(6)} %select_n.429, s32[]{:T(128)} %constant.578.clone.1, s32[]{:T(128)} %constant.578.clone.1) | dynamic-update-slice | bytes 393220 | tf_op jit(solution)/shard_map/jit(dynamic_update_index_in_dim)/dynamic_update_slice | solution.py:560
  322.7 9.5 %dynamic_update_slice.168 = bf16[2,128,768]{1,0,2:T(2,128)(2,1)S(1)} dynamic-update-slice(bf16[2,128,768]{1,0,2:T(2,128)(2,1)S(1)} %dynamic_update_slice.167, bf16[1,128,768]{1,0,2:T(2,128)(2,1)S(1)} %copy.46, s32[]{:T(128)S(6)} %select_n.427, s32[]{:T(128)} %constant.578.clone.1, s32[]{:T(128)} %constant.578.clone.1) | dynamic-update-slice | bytes 393220 | tf_op jit(solution)/shard_map/jit(dynamic_update_index_in_dim)/dynamic_update_slice | solution.py:560
  332.6 1.6 copy.47
  336.4 4.9 %collective-permute-done.42 = bf16[320,512]{1,0:T(8,128)(2,1)S(1)} collective-permute-done((bf16[320,512]{1,0:T(8,128)(2,1)S(1)}, bf16[320,512]{1,0:T(8,128)(2,1)S(1)}, u32[]{:S(2)}, u32[]{:S(2)}) %collective-permute-start.42) | collective-permute-done | bytes 327712 | tf_op jit(solution)/shard_map/ppermute | solution.py:559
  342.3 1.6 fusion.3
  (282 shorter events, 72.0 us)
Async XLA Ops:
  2.5 6.4 %collective-permute-start = (bf16[512,768]{1,0:T(8,128)(2,1)S(1)}, bf16[512,768]{1,0:T(8,128)(2,1)S(1)}, u32[]{:S(2)}, u32[]{:S(2)}) collective-permute-start(bf16[512,768]{1,0:T(8,128)(2,1)S(1)} %copy.40.w_ref.w_own_ref), channel_id=1, source_target_pairs={{0,1},{1,0},{2,3},{3,2},{4,5},{5,4},{6,7},{7,6},{8,9},{9,8},{10,11... | collective-permute-start | bytes 2359304 | tf_op jit(solution)/shard_map/ppermute | solution.py:593
  3.0 38.1 %collective-permute-start.6 = (bf16[512,1024]{1,0:T(8,128)(2,1)S(1)}, bf16[512,1024]{1,0:T(8,128)(2,1)}, u32[]{:S(2)}, u32[]{:S(2)}) collective-permute-start(bf16[512,1024]{1,0:T(8,128)(2,1)S(1)} %copy-done.5), channel_id=1, source_target_pairs={{0,1},{1,0},{2,3},{3,2},{4,5},{5,4},{6,7},{7,6},{8,9},{9,8},{10,11... | collective-permute-start | bytes 3145736 | tf_op jit(solution)/shard_map/ppermute | solution.py:593
  3.1 38.0 %collective-permute-start.7 = (bf16[1024,512]{1,0:T(8,128)(2,1)}, bf16[1024,512]{1,0:T(8,128)(2,1)}, u32[]{:S(2)}, u32[]{:S(2)}) collective-permute-start(bf16[1024,512]{1,0:T(8,128)(2,1)} %wo_own_ref.1), channel_id=1, source_target_pairs={{0,1},{1,0},{2,3},{3,2},{4,5},{5,4},{6,7},{7,6},{8,9},{9,8},{10,11... | collective-permute-start | bytes 3145736 | tf_op jit(solution)/shard_map/ppermute | solution.py:593
  14.9 26.1 %collective-permute-start.5 = (bf16[256,512]{1,0:T(8,128)(2,1)S(1)}, bf16[256,512]{1,0:T(8,128)(2,1)S(1)}, u32[]{:S(2)}, u32[]{:S(2)}) collective-permute-start(bf16[256,512]{1,0:T(8,128)(2,1)S(1)} %copy-done.9), channel_id=1, source_target_pairs={{0,1},{1,0},{2,3},{3,2},{4,5},{5,4},{6,7},{7,6},{8,9},{9,8},{10,11... | collective-permute-start | bytes 786440 | tf_op jit(solution)/shard_map/ppermute | solution.py:593
  89.8 13.9 %collective-permute-start.9 = (f32[4,256,128]{2,1,0:T(8,128)}, f32[4,256,128]{2,1,0:T(8,128)S(1)}, u32[]{:S(2)}, u32[]{:S(2)}) collective-permute-start(f32[4,256,128]{2,1,0:T(8,128)} %get-tuple-element.56), channel_id=1, source_target_pairs={{0,1},{1,0},{2,3},{3,2},{4,5},{5,4},{6,7},{7,6},{8,9},{9,8},{10,11... | collective-permute-start | bytes 1572872 | tf_op jit(solution)/shard_map/ppermute | solution.py:593
  90.2 13.5 %collective-permute-start.8 = (f32[32,1024]{1,0:T(8,128)}, f32[32,1024]{1,0:T(8,128)S(1)}, u32[]{:S(2)}, u32[]{:S(2)}) collective-permute-start(f32[32,1024]{1,0:T(8,128)} %get-tuple-element.55), channel_id=1, source_target_pairs={{0,1},{1,0},{2,3},{3,2},{4,5},{5,4},{6,7},{7,6},{8,9},{9,8},{10,11... | collective-permute-start | bytes 393224 | tf_op jit(solution)/shard_map/ppermute | solution.py:593
  90.4 13.3 %collective-permute-start.10 = (f32[4,8,128]{2,1,0:T(8,128)}, f32[4,8,128]{2,1,0:T(8,128)S(1)}, u32[]{:S(2)}, u32[]{:S(2)}) collective-permute-start(f32[4,8,128]{2,1,0:T(8,128)} %get-tuple-element.57), channel_id=1, source_target_pairs={{0,1},{1,0},{2,3},{3,2},{4,5},{5,4},{6,7},{7,6},{8,9},{9,8},{10,11... | collective-permute-start | bytes 49160 | tf_op jit(solution)/shard_map/ppermute | solution.py:593
  92.4 27.8 %collective-permute-start.75 = (f32[2,4]{1,0:T(2,128)S(1)}, f32[2,4]{1,0:T(2,128)S(1)}, u32[]{:S(2)}, u32[]{:S(2)}) collective-permute-start(f32[2,4]{1,0:T(2,128)S(1)} %slice.60), channel_id=1, source_target_pairs={{0,1},{1,0},{2,3},{3,2},{4,5},{5,4},{6,7},{7,6},{8,9},{9,8},{10,11... | collective-permute-start | bytes 104 | tf_op jit(solution)/shard_map/ppermute | solution.py:593
  121.2 5.2 %collective-permute-start.76 = (f32[3,512]{1,0:T(4,128)S(1)}, f32[3,512]{1,0:T(4,128)S(1)}, u32[]{:S(2)}, u32[]{:S(2)}) collective-permute-start(f32[3,512]{1,0:T(4,128)S(1)} %select_maximum_fusion), channel_id=1, source_target_pairs={{0,2},{2,0},{4,6},{6,4},{8,10},{10,8},{12,14},{14,12},{16,18},{18,... | collective-permute-start | bytes 18440 | tf_op jit(solution)/shard_map/ppermute | solution.py:587
  126.4 12.8 %collective-permute-start.43 = (bf16[512,1024]{1,0:T(8,128)(2,1)}, bf16[512,1024]{1,0:T(8,128)(2,1)}, u32[]{:S(2)}, u32[]{:S(2)}) collective-permute-start(bf16[512,1024]{1,0:T(8,128)(2,1)} %slice_bitcast_fusion.1), channel_id=1, source_target_pairs={{0,1},{1,0},{2,3},{3,2},{4,5},{5,4},{6,7},{7,6},{8,9},{9,8},{10,11... | collective-permute-start | bytes 3145736 | tf_op jit(solution)/shard_map/ppermute | solution.py:593
  129.2 15.1 %collective-permute-start.32 = (bf16[1280,512]{1,0:T(8,128)(2,1)}, bf16[1280,512]{1,0:T(8,128)(2,1)}, u32[]{:S(2)}, u32[]{:S(2)}) collective-permute-start(bf16[1280,512]{1,0:T(8,128)(2,1)} %slice_bitcast_fusion), channel_id=1, source_target_pairs={{0,1},{1,0},{2,3},{3,2},{4,5},{5,4},{6,7},{7,6},{8,9},{9,8},{10,11... | collective-permute-start | bytes 3932168 | tf_op jit(solution)/shard_map/ppermute | solution.py:593
  130.2 5.6 %collective-permute-start.78 = (f32[3,512]{1,0:T(4,128)S(1)}, f32[3,512]{1,0:T(4,128)S(1)}, u32[]{:S(2)}, u32[]{:S(2)}) collective-permute-start(f32[3,512]{1,0:T(4,128)S(1)} %add.500), channel_id=1, source_target_pairs={{0,8},{2,10},{4,12},{6,14},{8,16},{10,18},{12,20},{14,22},{16,24},... | collective-permute-start | bytes 18440 | tf_op jit(solution)/shard_map/ppermute | solution.py:587
  135.8 18.0 %collective-permute-start.11 = (bf16[512,768]{1,0:T(8,128)(2,1)S(1)}, bf16[512,768]{1,0:T(8,128)(2,1)}, u32[]{:S(2)}, u32[]{:S(2)}) collective-permute-start(bf16[512,768]{1,0:T(8,128)(2,1)S(1)} %slice_bitcast_fusion.2), channel_id=1, source_target_pairs={{0,1},{1,0},{2,3},{3,2},{4,5},{5,4},{6,7},{7,6},{8,9},{9,8},{10,11... | collective-permute-start | bytes 2359304 | tf_op jit(solution)/shard_map/ppermute | solution.py:593
  141.3 8.0 %collective-permute-start.44 = (bf16[128,1024]{1,0:T(8,128)(2,1)S(1)}, bf16[128,1024]{1,0:T(8,128)(2,1)S(1)}, u32[]{:S(2)}, u32[]{:S(2)}) collective-permute-start(bf16[128,1024]{1,0:T(8,128)(2,1)S(1)} %dynamic-slice_bitcast_fusion.3), channel_id=1, source_target_pairs={{0,2},{2,0},{4,6},{6,4},{8,10},{10,8},{12,14},{14,12},{16,18},{18,... | collective-permute-start | bytes 786440 | tf_op jit(solution)/shard_map/ppermute | solution.py:549
  142.6 9.4 %collective-permute-start.54 = (bf16[128,1024]{1,0:T(8,128)(2,1)S(1)}, bf16[128,1024]{1,0:T(8,128)(2,1)S(1)}, u32[]{:S(2)}, u32[]{:S(2)}) collective-permute-start(bf16[128,1024]{1,0:T(8,128)(2,1)S(1)} %dynamic-slice_bitcast_fusion.2), channel_id=1, source_target_pairs={{0,4},{2,6},{4,0},{6,2},{8,12},{10,14},{12,8},{14,10},{16,20},{18,... | collective-permute-start | bytes 786440 | tf_op jit(solution)/shard_map/ppermute | solution.py:549
  146.1 63.2 %collective-permute-start.64 = (bf16[320,512]{1,0:T(8,128)(2,1)S(1)}, bf16[320,512]{1,0:T(8,128)(2,1)S(1)}, u32[]{:S(2)}, u32[]{:S(2)}) collective-permute-start(bf16[320,512]{1,0:T(8,128)(2,1)S(1)} %dynamic-slice_bitcast_fusion), channel_id=1, source_target_pairs={{0,2},{2,0},{4,6},{6,4},{8,10},{10,8},{12,14},{14,12},{16,18},{18,... | collective-permute-start | bytes 983048 | tf_op jit(solution)/shard_map/ppermute | solution.py:549
  146.9 64.6 %collective-permute-start.33 = (bf16[320,512]{1,0:T(8,128)(2,1)S(1)}, bf16[320,512]{1,0:T(8,128)(2,1)S(1)}, u32[]{:S(2)}, u32[]{:S(2)}) collective-permute-start(bf16[320,512]{1,0:T(8,128)(2,1)S(1)} %dynamic-slice_bitcast_fusion.1), channel_id=1, source_target_pairs={{0,4},{2,6},{4,0},{6,2},{8,12},{10,14},{12,8},{14,10},{16,20},{18,... | collective-permute-start | bytes 983048 | tf_op jit(solution)/shard_map/ppermute | solution.py:549
  149.4 9.5 %collective-permute-start.45 = (bf16[64,1024]{1,0:T(8,128)(2,1)S(1)}, bf16[64,1024]{1,0:T(8,128)(2,1)S(1)}, u32[]{:S(2)}, u32[]{:S(2)}) collective-permute-start(bf16[64,1024]{1,0:T(8,128)(2,1)S(1)} %dynamic-slice_bitcast_fusion.9), channel_id=1, source_target_pairs={{0,4},{2,6},{4,0},{6,2},{8,12},{10,14},{12,8},{14,10},{16,20},{18,... | collective-permute-start | bytes 393224 | tf_op jit(solution)/shard_map/ppermute | solution.py:549
  152.2 10.6 %collective-permute-start.55 = (bf16[64,1024]{1,0:T(8,128)(2,1)S(1)}, bf16[64,1024]{1,0:T(8,128)(2,1)S(1)}, u32[]{:S(2)}, u32[]{:S(2)}) collective-permute-start(bf16[64,1024]{1,0:T(8,128)(2,1)S(1)} %dynamic-slice_bitcast_fusion.8), channel_id=1, source_target_pairs={{0,2},{2,0},{4,6},{6,4},{8,10},{10,8},{12,14},{14,12},{16,18},{18,... | collective-permute-start | bytes 393224 | tf_op jit(solution)/shard_map/ppermute | solution.py:549
  159.0 5.9 %collective-permute-start.46 = (bf16[16,1024]{1,0:T(8,128)(2,1)S(1)}, bf16[16,1024]{1,0:T(8,128)(2,1)S(1)}, u32[]{:S(2)}, u32[]{:S(2)}) collective-permute-start(bf16[16,1024]{1,0:T(8,128)(2,1)S(1)} %get-tuple-element.113), channel_id=1, source_target_pairs={{0,8},{2,10},{4,12},{6,14},{8,16},{10,18},{12,20},{14,22},{16,24},... | collective-permute-start | bytes 98312 | tf_op jit(solution)/shard_map/ppermute | solution.py:549
  159.6 5.9 %collective-permute-start.47 = (bf16[16,1024]{1,0:T(8,128)(2,1)S(1)}, bf16[16,1024]{1,0:T(8,128)(2,1)S(1)}, u32[]{:S(2)}, u32[]{:S(2)}) collective-permute-start(bf16[16,1024]{1,0:T(8,128)(2,1)S(1)} %get-tuple-element.115), channel_id=1, source_target_pairs={{0,16},{2,18},{4,20},{6,22},{8,24},{10,26},{12,28},{14,30},{16,0},... | collective-permute-start | bytes 98312 | tf_op jit(solution)/shard_map/ppermute | solution.py:549
  162.8 5.1 %collective-permute-start.48 = (bf16[16,1024]{1,0:T(8,128)(2,1)S(1)}, bf16[16,1024]{1,0:T(8,128)(2,1)S(1)}, u32[]{:S(2)}, u32[]{:S(2)}) collective-permute-start(bf16[16,1024]{1,0:T(8,128)(2,1)S(1)} %get-tuple-element.114), channel_id=1, source_target_pairs={{0,24},{2,26},{4,28},{6,30},{8,0},{10,2},{12,4},{14,6},{16,8},{18,... | collective-permute-start | bytes 98312 | tf_op jit(solution)/shard_map/ppermute | solution.py:549
  164.8 5.8 %collective-permute-start.56 = (bf16[16,1024]{1,0:T(8,128)(2,1)S(1)}, bf16[16,1024]{1,0:T(8,128)(2,1)S(1)}, u32[]{:S(2)}, u32[]{:S(2)}) collective-permute-start(bf16[16,1024]{1,0:T(8,128)(2,1)S(1)} %get-tuple-element.116), channel_id=1, source_target_pairs={{0,8},{2,10},{4,12},{6,14},{8,16},{10,18},{12,20},{14,22},{16,24},... | collective-permute-start | bytes 98312 | tf_op jit(solution)/shard_map/ppermute | solution.py:549
  165.5 5.8 %collective-permute-start.57 = (bf16[16,1024]{1,0:T(8,128)(2,1)S(1)}, bf16[16,1024]{1,0:T(8,128)(2,1)S(1)}, u32[]{:S(2)}, u32[]{:S(2)}) collective-permute-start(bf16[16,1024]{1,0:T(8,128)(2,1)S(1)} %get-tuple-element.118), channel_id=1, source_target_pairs={{0,16},{2,18},{4,20},{6,22},{8,24},{10,26},{12,28},{14,30},{16,0},... | collective-permute-start | bytes 98312 | tf_op jit(solution)/shard_map/ppermute | solution.py:549
  170.7 5.7 %collective-permute-start.12 = (bf16[128,768]{1,0:T(8,128)(2,1)S(1)}, bf16[128,768]{1,0:T(8,128)(2,1)S(1)}, u32[]{:S(2)}, u32[]{:S(2)}) collective-permute-start(bf16[128,768]{1,0:T(8,128)(2,1)S(1)} %dynamic-slice_bitcast_fusion.5), channel_id=1, source_target_pairs={{0,2},{2,0},{4,6},{6,4},{8,10},{10,8},{12,14},{14,12},{16,18},{18,... | collective-permute-start | bytes 589832 | tf_op jit(solution)/shard_map/ppermute | solution.py:549
  171.3 5.7 %collective-permute-start.22 = (bf16[128,768]{1,0:T(8,128)(2,1)S(1)}, bf16[128,768]{1,0:T(8,128)(2,1)S(1)}, u32[]{:S(2)}, u32[]{:S(2)}) collective-permute-start(bf16[128,768]{1,0:T(8,128)(2,1)S(1)} %dynamic-slice_bitcast_fusion.4), channel_id=1, source_target_pairs={{0,4},{2,6},{4,0},{6,2},{8,12},{10,14},{12,8},{14,10},{16,20},{18,... | collective-permute-start | bytes 589832 | tf_op jit(solution)/shard_map/ppermute | solution.py:549
  172.8 6.8 %collective-permute-start.49 = (bf16[16,1024]{1,0:T(8,128)(2,1)S(1)}, bf16[16,1024]{1,0:T(8,128)(2,1)S(1)}, u32[]{:S(2)}, u32[]{:S(2)}) collective-permute-start(bf16[16,1024]{1,0:T(8,128)(2,1)S(1)} %get-tuple-element.92), channel_id=1, source_target_pairs={{0,8},{2,10},{4,12},{6,14},{8,16},{10,18},{12,20},{14,22},{16,24},... | collective-permute-start | bytes 98312 | tf_op jit(solution)/shard_map/ppermute | solution.py:559
  176.3 9.0 %collective-permute-start.50 = (bf16[16,1024]{1,0:T(8,128)(2,1)S(1)}, bf16[16,1024]{1,0:T(8,128)(2,1)S(1)}, u32[]{:S(2)}, u32[]{:S(2)}) collective-permute-start(bf16[16,1024]{1,0:T(8,128)(2,1)S(1)} %get-tuple-element.92), channel_id=1, source_target_pairs={{0,16},{2,18},{4,20},{6,22},{8,24},{10,26},{12,28},{14,30},{16,0},... | collective-permute-start | bytes 98312 | tf_op jit(solution)/shard_map/ppermute | solution.py:559
  177.0 14.5 %collective-permute-start.51 = (bf16[16,1024]{1,0:T(8,128)(2,1)S(1)}, bf16[16,1024]{1,0:T(8,128)(2,1)S(1)}, u32[]{:S(2)}, u32[]{:S(2)}) collective-permute-start(bf16[16,1024]{1,0:T(8,128)(2,1)S(1)} %get-tuple-element.92), channel_id=1, source_target_pairs={{0,24},{2,26},{4,28},{6,30},{8,0},{10,2},{12,4},{14,6},{16,8},{18,... | collective-permute-start | bytes 98312 | tf_op jit(solution)/shard_map/ppermute | solution.py:559
  179.6 5.8 %collective-permute-start.59 = (bf16[16,1024]{1,0:T(8,128)(2,1)S(1)}, bf16[16,1024]{1,0:T(8,128)(2,1)S(1)}, u32[]{:S(2)}, u32[]{:S(2)}) collective-permute-start(bf16[16,1024]{1,0:T(8,128)(2,1)S(1)} %get-tuple-element.94), channel_id=1, source_target_pairs={{0,8},{2,10},{4,12},{6,14},{8,16},{10,18},{12,20},{14,22},{16,24},... | collective-permute-start | bytes 98312 | tf_op jit(solution)/shard_map/ppermute | solution.py:559
  185.4 8.3 %collective-permute-start.61 = (bf16[16,1024]{1,0:T(8,128)(2,1)S(1)}, bf16[16,1024]{1,0:T(8,128)(2,1)S(1)}, u32[]{:S(2)}, u32[]{:S(2)}) collective-permute-start(bf16[16,1024]{1,0:T(8,128)(2,1)S(1)} %get-tuple-element.94), channel_id=1, source_target_pairs={{0,24},{2,26},{4,28},{6,30},{8,0},{10,2},{12,4},{14,6},{16,8},{18,... | collective-permute-start | bytes 98312 | tf_op jit(solution)/shard_map/ppermute | solution.py:559
  195.1 5.7 %collective-permute-start.14 = (bf16[16,768]{1,0:T(8,128)(2,1)S(1)}, bf16[16,768]{1,0:T(8,128)(2,1)S(1)}, u32[]{:S(2)}, u32[]{:S(2)}) collective-permute-start(bf16[16,768]{1,0:T(8,128)(2,1)S(1)} %get-tuple-element.119), channel_id=1, source_target_pairs={{0,8},{2,10},{4,12},{6,14},{8,16},{10,18},{12,20},{14,22},{16,24},... | collective-permute-start | bytes 73736 | tf_op jit(solution)/shard_map/ppermute | solution.py:549
  195.2 5.6 %collective-permute-start.15 = (bf16[16,768]{1,0:T(8,128)(2,1)S(1)}, bf16[16,768]{1,0:T(8,128)(2,1)S(1)}, u32[]{:S(2)}, u32[]{:S(2)}) collective-permute-start(bf16[16,768]{1,0:T(8,128)(2,1)S(1)} %get-tuple-element.121), channel_id=1, source_target_pairs={{0,16},{2,18},{4,20},{6,22},{8,24},{10,26},{12,28},{14,30},{16,0},... | collective-permute-start | bytes 73736 | tf_op jit(solution)/shard_map/ppermute | solution.py:549
  196.2 5.2 %collective-permute-start.16 = (bf16[16,768]{1,0:T(8,128)(2,1)S(1)}, bf16[16,768]{1,0:T(8,128)(2,1)S(1)}, u32[]{:S(2)}, u32[]{:S(2)}) collective-permute-start(bf16[16,768]{1,0:T(8,128)(2,1)S(1)} %get-tuple-element.120), channel_id=1, source_target_pairs={{0,24},{2,26},{4,28},{6,30},{8,0},{10,2},{12,4},{14,6},{16,8},{18,... | collective-permute-start | bytes 73736 | tf_op jit(solution)/shard_map/ppermute | solution.py:549
  200.8 5.6 %collective-permute-start.24 = (bf16[16,768]{1,0:T(8,128)(2,1)S(1)}, bf16[16,768]{1,0:T(8,128)(2,1)S(1)}, u32[]{:S(2)}, u32[]{:S(2)}) collective-permute-start(bf16[16,768]{1,0:T(8,128)(2,1)S(1)} %get-tuple-element.122), channel_id=1, source_target_pairs={{0,8},{2,10},{4,12},{6,14},{8,16},{10,18},{12,20},{14,22},{16,24},... | collective-permute-start | bytes 73736 | tf_op jit(solution)/shard_map/ppermute | solution.py:549
  200.8 6.6 %collective-permute-start.25 = (bf16[16,768]{1,0:T(8,128)(2,1)S(1)}, bf16[16,768]{1,0:T(8,128)(2,1)S(1)}, u32[]{:S(2)}, u32[]{:S(2)}) collective-permute-start(bf16[16,768]{1,0:T(8,128)(2,1)S(1)} %get-tuple-element.124), channel_id=1, source_target_pairs={{0,16},{2,18},{4,20},{6,22},{8,24},{10,26},{12,28},{14,30},{16,0},... | collective-permute-start | bytes 73736 | tf_op jit(solution)/shard_map/ppermute | solution.py:549
  201.4 7.1 %collective-permute-start.26 = (bf16[16,768]{1,0:T(8,128)(2,1)S(1)}, bf16[16,768]{1,0:T(8,128)(2,1)S(1)}, u32[]{:S(2)}, u32[]{:S(2)}) collective-permute-start(bf16[16,768]{1,0:T(8,128)(2,1)S(1)} %get-tuple-element.123), channel_id=1, source_target_pairs={{0,24},{2,26},{4,28},{6,30},{8,0},{10,2},{12,4},{14,6},{16,8},{18,... | collective-permute-start | bytes 73736 | tf_op jit(solution)/shard_map/ppermute | solution.py:549
  206.4 7.6 %collective-permute-start.52 = (bf16[64,1024]{1,0:T(8,128)(2,1)S(1)}, bf16[64,1024]{1,0:T(8,128)(2,1)S(1)}, u32[]{:S(2)}, u32[]{:S(2)}) collective-permute-start(bf16[64,1024]{1,0:T(8,128)(2,1)S(1)} %bitcast.328), channel_id=1, source_target_pairs={{0,4},{2,6},{4,0},{6,2},{8,12},{10,14},{12,8},{14,10},{16,20},{18,... | collective-permute-start | bytes 393224 | tf_op jit(solution)/shard_map/ppermute | solution.py:559
  207.5 9.3 %collective-permute-start.62 = (bf16[64,1024]{1,0:T(8,128)(2,1)S(1)}, bf16[64,1024]{1,0:T(8,128)(2,1)S(1)}, u32[]{:S(2)}, u32[]{:S(2)}) collective-permute-start(bf16[64,1024]{1,0:T(8,128)(2,1)S(1)} %bitcast.330), channel_id=1, source_target_pairs={{0,2},{2,0},{4,6},{6,4},{8,10},{10,8},{12,14},{14,12},{16,18},{18,... | collective-permute-start | bytes 393224 | tf_op jit(solution)/shard_map/ppermute | solution.py:559
  208.5 11.1 %collective-permute-start.17 = (bf16[16,768]{1,0:T(8,128)(2,1)S(1)}, bf16[16,768]{1,0:T(8,128)(2,1)S(1)}, u32[]{:S(2)}, u32[]{:S(2)}) collective-permute-start(bf16[16,768]{1,0:T(8,128)(2,1)S(1)} %get-tuple-element.98), channel_id=1, source_target_pairs={{0,8},{2,10},{4,12},{6,14},{8,16},{10,18},{12,20},{14,22},{16,24},... | collective-permute-start | bytes 73736 | tf_op jit(solution)/shard_map/ppermute | solution.py:559
  209.3 13.2 %collective-permute-start.18 = (bf16[16,768]{1,0:T(8,128)(2,1)S(1)}, bf16[16,768]{1,0:T(8,128)(2,1)S(1)}, u32[]{:S(2)}, u32[]{:S(2)}) collective-permute-start(bf16[16,768]{1,0:T(8,128)(2,1)S(1)} %get-tuple-element.98), channel_id=1, source_target_pairs={{0,16},{2,18},{4,20},{6,22},{8,24},{10,26},{12,28},{14,30},{16,0},... | collective-permute-start | bytes 73736 | tf_op jit(solution)/shard_map/ppermute | solution.py:559
  211.5 12.6 %collective-permute-start.19 = (bf16[16,768]{1,0:T(8,128)(2,1)S(1)}, bf16[16,768]{1,0:T(8,128)(2,1)S(1)}, u32[]{:S(2)}, u32[]{:S(2)}) collective-permute-start(bf16[16,768]{1,0:T(8,128)(2,1)S(1)} %get-tuple-element.98), channel_id=1, source_target_pairs={{0,24},{2,26},{4,28},{6,30},{8,0},{10,2},{12,4},{14,6},{16,8},{18,... | collective-permute-start | bytes 73736 | tf_op jit(solution)/shard_map/ppermute | solution.py:559
  214.1 10.5 %collective-permute-start.27 = (bf16[16,768]{1,0:T(8,128)(2,1)S(1)}, bf16[16,768]{1,0:T(8,128)(2,1)S(1)}, u32[]{:S(2)}, u32[]{:S(2)}) collective-permute-start(bf16[16,768]{1,0:T(8,128)(2,1)S(1)} %get-tuple-element.100), channel_id=1, source_target_pairs={{0,8},{2,10},{4,12},{6,14},{8,16},{10,18},{12,20},{14,22},{16,24},... | collective-permute-start | bytes 73736 | tf_op jit(solution)/shard_map/ppermute | solution.py:559
  216.7 9.4 %collective-permute-start.28 = (bf16[16,768]{1,0:T(8,128)(2,1)S(1)}, bf16[16,768]{1,0:T(8,128)(2,1)S(1)}, u32[]{:S(2)}, u32[]{:S(2)}) collective-permute-start(bf16[16,768]{1,0:T(8,128)(2,1)S(1)} %get-tuple-element.100), channel_id=1, source_target_pairs={{0,16},{2,18},{4,20},{6,22},{8,24},{10,26},{12,28},{14,30},{16,0},... | collective-permute-start | bytes 73736 | tf_op jit(solution)/shard_map/ppermute | solution.py:559
  219.6 7.1 %collective-permute-start.29 = (bf16[16,768]{1,0:T(8,128)(2,1)S(1)}, bf16[16,768]{1,0:T(8,128)(2,1)S(1)}, u32[]{:S(2)}, u32[]{:S(2)}) collective-permute-start(bf16[16,768]{1,0:T(8,128)(2,1)S(1)} %get-tuple-element.100), channel_id=1, source_target_pairs={{0,24},{2,26},{4,28},{6,30},{8,0},{10,2},{12,4},{14,6},{16,8},{18,... | collective-permute-start | bytes 73736 | tf_op jit(solution)/shard_map/ppermute | solution.py:559
  222.5 37.1 %collective-permute-start.65 = (bf16[160,512]{1,0:T(8,128)(2,1)}, bf16[160,512]{1,0:T(8,128)(2,1)}, u32[]{:S(2)}, u32[]{:S(2)}) collective-permute-start(bf16[160,512]{1,0:T(8,128)(2,1)} %dynamic-slice_bitcast_fusion.6), channel_id=1, source_target_pairs={{0,4},{2,6},{4,0},{6,2},{8,12},{10,14},{12,8},{14,10},{16,20},{18,... | collective-permute-start | bytes 491528 | tf_op jit(solution)/shard_map/ppermute | solution.py:549
  224.0 37.6 %collective-permute-start.34 = (bf16[160,512]{1,0:T(8,128)(2,1)}, bf16[160,512]{1,0:T(8,128)(2,1)}, u32[]{:S(2)}, u32[]{:S(2)}) collective-permute-start(bf16[160,512]{1,0:T(8,128)(2,1)} %dynamic-slice_bitcast_fusion.7), channel_id=1, source_target_pairs={{0,2},{2,0},{4,6},{6,4},{8,10},{10,8},{12,14},{14,12},{16,18},{18,... | collective-permute-start | bytes 491528 | tf_op jit(solution)/shard_map/ppermute | solution.py:549
  224.6 82.6 %collective-permute-start.53 = (bf16[128,1024]{1,0:T(8,128)(2,1)}, bf16[128,1024]{1,0:T(8,128)(2,1)}, u32[]{:S(2)}, u32[]{:S(2)}) collective-permute-start(bf16[128,1024]{1,0:T(8,128)(2,1)} %bitcast.95), channel_id=1, source_target_pairs={{0,2},{2,0},{4,6},{6,4},{8,10},{10,8},{12,14},{14,12},{16,18},{18,... | collective-permute-start | bytes 786440 | tf_op jit(solution)/shard_map/ppermute | solution.py:559
  226.1 83.4 %collective-permute-start.63 = (bf16[128,1024]{1,0:T(8,128)(2,1)}, bf16[128,1024]{1,0:T(8,128)(2,1)}, u32[]{:S(2)}, u32[]{:S(2)}) collective-permute-start(bf16[128,1024]{1,0:T(8,128)(2,1)} %bitcast.117), channel_id=1, source_target_pairs={{0,4},{2,6},{4,0},{6,2},{8,12},{10,14},{12,8},{14,10},{16,20},{18,... | collective-permute-start | bytes 786440 | tf_op jit(solution)/shard_map/ppermute | solution.py:559
  226.7 7.1 %collective-permute-start.20 = (bf16[64,768]{1,0:T(8,128)(2,1)S(1)}, bf16[64,768]{1,0:T(8,128)(2,1)S(1)}, u32[]{:S(2)}, u32[]{:S(2)}) collective-permute-start(bf16[64,768]{1,0:T(8,128)(2,1)S(1)} %bitcast.332), channel_id=1, source_target_pairs={{0,4},{2,6},{4,0},{6,2},{8,12},{10,14},{12,8},{14,10},{16,20},{18,... | collective-permute-start | bytes 294920 | tf_op jit(solution)/shard_map/ppermute | solution.py:559
  260.6 6.0 %collective-permute-start.66 = (bf16[40,512]{1,0:T(8,128)(2,1)S(1)}, bf16[40,512]{1,0:T(8,128)(2,1)S(1)}, u32[]{:S(2)}, u32[]{:S(2)}) collective-permute-start(bf16[40,512]{1,0:T(8,128)(2,1)S(1)} %get-tuple-element.107), channel_id=1, source_target_pairs={{0,8},{2,10},{4,12},{6,14},{8,16},{10,18},{12,20},{14,22},{16,24},... | collective-permute-start | bytes 122888 | tf_op jit(solution)/shard_map/ppermute | solution.py:549
  260.7 5.9 %collective-permute-start.67 = (bf16[40,512]{1,0:T(8,128)(2,1)S(1)}, bf16[40,512]{1,0:T(8,128)(2,1)S(1)}, u32[]{:S(2)}, u32[]{:S(2)}) collective-permute-start(bf16[40,512]{1,0:T(8,128)(2,1)S(1)} %get-tuple-element.109), channel_id=1, source_target_pairs={{0,16},{2,18},{4,20},{6,22},{8,24},{10,26},{12,28},{14,30},{16,0},... | collective-permute-start | bytes 122888 | tf_op jit(solution)/shard_map/ppermute | solution.py:549
  261.7 6.0 %collective-permute-start.68 = (bf16[40,512]{1,0:T(8,128)(2,1)S(1)}, bf16[40,512]{1,0:T(8,128)(2,1)S(1)}, u32[]{:S(2)}, u32[]{:S(2)}) collective-permute-start(bf16[40,512]{1,0:T(8,128)(2,1)S(1)} %get-tuple-element.108), channel_id=1, source_target_pairs={{0,24},{2,26},{4,28},{6,30},{8,0},{10,2},{12,4},{14,6},{16,8},{18,... | collective-permute-start | bytes 122888 | tf_op jit(solution)/shard_map/ppermute | solution.py:549
  266.6 5.8 %collective-permute-start.35 = (bf16[40,512]{1,0:T(8,128)(2,1)S(1)}, bf16[40,512]{1,0:T(8,128)(2,1)S(1)}, u32[]{:S(2)}, u32[]{:S(2)}) collective-permute-start(bf16[40,512]{1,0:T(8,128)(2,1)S(1)} %get-tuple-element.110), channel_id=1, source_target_pairs={{0,8},{2,10},{4,12},{6,14},{8,16},{10,18},{12,20},{14,22},{16,24},... | collective-permute-start | bytes 122888 | tf_op jit(solution)/shard_map/ppermute | solution.py:549
  266.6 6.6 %collective-permute-start.36 = (bf16[40,512]{1,0:T(8,128)(2,1)S(1)}, bf16[40,512]{1,0:T(8,128)(2,1)S(1)}, u32[]{:S(2)}, u32[]{:S(2)}) collective-permute-start(bf16[40,512]{1,0:T(8,128)(2,1)S(1)} %get-tuple-element.112), channel_id=1, source_target_pairs={{0,16},{2,18},{4,20},{6,22},{8,24},{10,26},{12,28},{14,30},{16,0},... | collective-permute-start | bytes 122888 | tf_op jit(solution)/shard_map/ppermute | solution.py:549
  267.7 6.7 %collective-permute-start.37 = (bf16[40,512]{1,0:T(8,128)(2,1)S(1)}, bf16[40,512]{1,0:T(8,128)(2,1)S(1)}, u32[]{:S(2)}, u32[]{:S(2)}) collective-permute-start(bf16[40,512]{1,0:T(8,128)(2,1)S(1)} %get-tuple-element.111), channel_id=1, source_target_pairs={{0,24},{2,26},{4,28},{6,30},{8,0},{10,2},{12,4},{14,6},{16,8},{18,... | collective-permute-start | bytes 122888 | tf_op jit(solution)/shard_map/ppermute | solution.py:549
  272.5 39.6 %collective-permute-start.21 = (bf16[128,768]{1,0:T(8,128)(2,1)S(1)}, bf16[128,768]{1,0:T(8,128)(2,1)S(1)}, u32[]{:S(2)}, u32[]{:S(2)}) collective-permute-start(bf16[128,768]{1,0:T(8,128)(2,1)S(1)} %bitcast.314), channel_id=1, source_target_pairs={{0,2},{2,0},{4,6},{6,4},{8,10},{10,8},{12,14},{14,12},{16,18},{18,... | collective-permute-start | bytes 589832 | tf_op jit(solution)/shard_map/ppermute | solution.py:559
  273.2 49.0 %collective-permute-start.31 = (bf16[128,768]{1,0:T(8,128)(2,1)}, bf16[128,768]{1,0:T(8,128)(2,1)S(1)}, u32[]{:S(2)}, u32[]{:S(2)}) collective-permute-start(bf16[128,768]{1,0:T(8,128)(2,1)} %bitcast.48), channel_id=1, source_target_pairs={{0,4},{2,6},{4,0},{6,2},{8,12},{10,14},{12,8},{14,10},{16,20},{18,... | collective-permute-start | bytes 589832 | tf_op jit(solution)/shard_map/ppermute | solution.py:559
  274.3 5.8 %collective-permute-start.69 = (bf16[40,512]{1,0:T(8,128)(2,1)S(1)}, bf16[40,512]{1,0:T(8,128)(2,1)S(1)}, u32[]{:S(2)}, u32[]{:S(2)}) collective-permute-start(bf16[40,512]{1,0:T(8,128)(2,1)S(1)} %get-tuple-element.90), channel_id=1, source_target_pairs={{0,8},{2,10},{4,12},{6,14},{8,16},{10,18},{12,20},{14,22},{16,24},... | collective-permute-start | bytes 122888 | tf_op jit(solution)/shard_map/ppermute | solution.py:559
  289.1 5.8 %collective-permute-start.38 = (bf16[40,512]{1,0:T(8,128)(2,1)S(1)}, bf16[40,512]{1,0:T(8,128)(2,1)S(1)}, u32[]{:S(2)}, u32[]{:S(2)}) collective-permute-start(bf16[40,512]{1,0:T(8,128)(2,1)S(1)} %get-tuple-element.96), channel_id=1, source_target_pairs={{0,8},{2,10},{4,12},{6,14},{8,16},{10,18},{12,20},{14,22},{16,24},... | collective-permute-start | bytes 122888 | tf_op jit(solution)/shard_map/ppermute | solution.py:559
  303.8 31.2 %collective-permute-start.72 = (bf16[160,512]{1,0:T(8,128)(2,1)}, bf16[160,512]{1,0:T(8,128)(2,1)S(1)}, u32[]{:S(2)}, u32[]{:S(2)}) collective-permute-start(bf16[160,512]{1,0:T(8,128)(2,1)} %bitcast.136), channel_id=1, source_target_pairs={{0,4},{2,6},{4,0},{6,2},{8,12},{10,14},{12,8},{14,10},{16,20},{18,... | collective-permute-start | bytes 491528 | tf_op jit(solution)/shard_map/ppermute | solution.py:559
  307.2 27.0 %collective-permute-start.41 = (bf16[160,512]{1,0:T(8,128)(2,1)}, bf16[160,512]{1,0:T(8,128)(2,1)S(1)}, u32[]{:S(2)}, u32[]{:S(2)}) collective-permute-start(bf16[160,512]{1,0:T(8,128)(2,1)} %bitcast.68), channel_id=1, source_target_pairs={{0,2},{2,0},{4,6},{6,4},{8,10},{10,8},{12,14},{14,12},{16,18},{18,... | collective-permute-start | bytes 491528 | tf_op jit(solution)/shard_map/ppermute | solution.py:559
  334.2 7.1 %collective-permute-start.42 = (bf16[320,512]{1,0:T(8,128)(2,1)S(1)}, bf16[320,512]{1,0:T(8,128)(2,1)S(1)}, u32[]{:S(2)}, u32[]{:S(2)}) collective-permute-start(bf16[320,512]{1,0:T(8,128)(2,1)S(1)} %bitcast.307), channel_id=1, source_target_pairs={{0,4},{2,6},{4,0},{6,2},{8,12},{10,14},{12,8},{14,10},{16,20},{18,... | collective-permute-start | bytes 983048 | tf_op jit(solution)/shard_map/ppermute | solution.py:559
  335.0 7.2 %collective-permute-start.73 = (bf16[320,512]{1,0:T(8,128)(2,1)S(1)}, bf16[320,512]{1,0:T(8,128)(2,1)S(1)}, u32[]{:S(2)}, u32[]{:S(2)}) collective-permute-start(bf16[320,512]{1,0:T(8,128)(2,1)S(1)} %bitcast.305), channel_id=1, source_target_pairs={{0,2},{2,0},{4,6},{6,4},{8,10},{10,8},{12,14},{14,12},{16,18},{18,... | collective-permute-start | bytes 983048 | tf_op jit(solution)/shard_map/ppermute | solution.py:559
  (35 other events, 155.8 us)

commit v2 on v1

--- a/solution.py
+++ b/solution.py
@@ -9,6 +9,7 @@
 
 BAND = 30
 HALO = 32
+EXTRA = 64
 BLOCK = 128
 EPS = 1e-06
 BF = jnp.bfloat16
@@ -42,6 +43,14 @@
     return pltpu.CompilerParams(vmem_limit_bytes=VMEM_BYTES)
 
 
+def cost(micros):
+    return pl.CostEstimate(flops=int(micros * 1e7), bytes_accessed=1 << 20, transcendentals=0)
+
+
+def tie(*values):
+    return lax.optimization_barrier(values)
+
+
 def starts_of(ends_ref, places, docs):
     start = jnp.full(places.shape, ends_ref[docs], jnp.int32)
     for doc in range(docs):
@@ -63,7 +72,41 @@
     r = lax.rsqrt(jnp.mean(x * x, axis=1, keepdims=True) + EPS)
     normed = (x * r * gain_ref[...]).astype(BF)
     normed_ref[...] = normed
-    out_ref[...] = nn(normed, w_ref[...]).astype(BF)
+    project(normed, w_ref, out_ref)
+
+
+def project(normed, w_ref, out_ref):
+    cols = w_ref.shape[2]
+    for kind in range(3):
+        out_ref[:, cols * kind : cols * kind + cols] = nn(normed, w_ref[kind]).astype(BF)
+
+
+PACKET = 4 * (128 + 16) + 8 * HALO
+
+
+def pack(packet_ref, pair, state, total):
+    base = 144 * pair
+    packet_ref[base : base + 64] = (state[:64] + state[64:128]).astype(BF)
+    packet_ref[base + 64 : base + 128] = (state[128:192] + state[192:]).astype(BF)
+    packet_ref[base + 128 : base + 144] = jnp.broadcast_to(total, (16, 128)).astype(BF)
+
+
+def pack_halo(packet_ref, kind, pair, rows):
+    base = 576 + HALO * (4 * kind + pair)
+    packet_ref[base : base + HALO] = rows
+
+
+def unpack(packet_ref, pair, diag):
+    base = 144 * pair
+    one = packet_ref[base : base + 64].astype(F32)
+    two = packet_ref[base + 64 : base + 128].astype(F32)
+    state = jnp.where(diag, jnp.concatenate([one, one, two, two], axis=0), 0.0)
+    return state, packet_ref[base + 128 : base + 136].astype(F32)
+
+
+def unpack_halo(packet_ref, kind, pair):
+    base = 576 + HALO * (4 * kind + pair)
+    return packet_ref[base : base + HALO]
 
 
 def first_feature(values):
@@ -80,10 +123,9 @@
     return ((row // 64) % 2) == ((col // 64) % 2)
 
 
-def project_state_kernel(docs, ends_ref, normed_ref, w_ref, own_ref, out_ref, state_ref, sum_ref, halo_ref):
+def project_state_kernel(docs, ends_ref, normed_ref, w_ref, own_ref, out_ref, packet_ref):
     rows = normed_ref.shape[0]
-    other = nn(normed_ref[...], w_ref[...]).astype(BF)
-    out_ref[...] = other
+    project(normed_ref[...], w_ref, out_ref)
     member_from = start_at(ends_ref, rows - 1, docs)
     member = iota((rows, 1), 0) >= member_from
     diag = pair_diag(256, 128)
@@ -98,10 +140,9 @@
         two = second_feature(wide)
         features = jnp.concatenate([one.astype(BF), two], axis=1)
         state = jnp.where(diag, tn(features, values), 0.0)
-        state_ref[slot] = state.astype(BF)
-        sum_ref[slot] = jnp.broadcast_to(jnp.sum(one, axis=0, keepdims=True), (8, 128))
-        halo_ref[:, 128 * slot : 128 * slot + 128] = keys[rows - HALO :]
-        halo_ref[:, 512 + 128 * slot : 640 + 128 * slot] = values[rows - HALO :]
+        pack(packet_ref, slot, state, jnp.sum(one, axis=0, keepdims=True))
+        pack_halo(packet_ref, 0, slot, keys[rows - HALO :])
+        pack_halo(packet_ref, 1, slot, values[rows - HALO :])
 
 
 def block_masks(ends_ref, docs, first):
@@ -195,9 +236,7 @@
     ends_ref,
     own_ref,
     other_ref,
-    halo_ref,
-    state_in_ref,
-    sum_in_ref,
+    packet_ref,
     blend_ref,
     mixed_ref,
     state_out_ref,
@@ -212,9 +251,11 @@
 
     @pl.when(index == 0)
     def _():
-        state_ref[...] = state_in_ref[...].astype(F32)
-        sum_ref[...] = sum_in_ref[...]
-        prev_ref[...] = halo_ref[...]
+        for pair in range(4):
+            state_ref[pair], sum_ref[pair] = unpack(packet_ref, pair, pair_diag(256, 128))
+            for kind in range(2):
+                lane = 512 * kind + 128 * pair
+                prev_ref[:, lane : lane + 128] = unpack_halo(packet_ref, kind, pair)
 
     masks = block_masks(ends_ref, docs, first)
     banded, causal, causal_q, count, carried, member, keep = masks
@@ -252,6 +293,8 @@
 
 def mixer_backward_kernel(
     docs,
+    top,
+    resumed,
     ends_ref,
     own_ref,
     other_ref,
@@ -260,27 +303,17 @@
     sum_ref,
     blend_ref,
     grad_ref,
-    gq_ref,
-    gk_ref,
-    gv_ref,
-    halo_ref,
-    back_state_ref,
-    back_sum_ref,
-    blend_out_ref,
-    dk_ref,
-    dv_ref,
+    *refs,
 ):
+    carried_in = refs[:4] if resumed else None
+    gq_ref, gk_ref, gv_ref, halo_ref, back_state_ref, back_sum_ref, blend_out_ref, packet_ref = refs[-8:]
     step = pl.program_id(0)
-    index = pl.num_programs(0) - 1 - step
-    first = index * BLOCK
+    first = (top - step) * BLOCK
 
     @pl.when(step == 0)
     def _():
-        back_state_ref[...] = jnp.zeros_like(back_state_ref)
-        back_sum_ref[...] = jnp.zeros_like(back_sum_ref)
-        blend_out_ref[...] = jnp.zeros_like(blend_out_ref)
-        dk_ref[...] = jnp.zeros_like(dk_ref)
-        dv_ref[...] = jnp.zeros_like(dv_ref)
+        for place, ref in enumerate((halo_ref, back_state_ref, back_sum_ref, blend_out_ref)):
+            ref[...] = carried_in[place][...] if resumed else jnp.zeros_like(ref)
 
     masks = block_masks(ends_ref, docs, first)
     banded, causal, causal_q, count, carried, member, keep = masks
@@ -352,11 +385,11 @@
         slope_k = jnp.exp(jnp.minimum(k.astype(F32), 0.0))
         gk = dk[HALO:] + d_one * slope_k + d_two * (1.0 - tanh_k * tanh_k)
         gk_ref[: BLOCK - HALO, lanes] = gk[: BLOCK - HALO].astype(BF)
-        gk_ref[BLOCK - HALO :, lanes] = (gk[BLOCK - HALO :] + dk_ref[:, lanes]).astype(BF)
+        gk_ref[BLOCK - HALO :, lanes] = (gk[BLOCK - HALO :] + halo_ref[:, lanes]).astype(BF)
         gv_ref[: BLOCK - HALO, lanes] = dv_own[: BLOCK - HALO].astype(BF)
-        gv_ref[BLOCK - HALO :, lanes] = (dv_own[BLOCK - HALO :] + dv_ref[:, lanes]).astype(BF)
-        dk_ref[:, lanes] = dk[:HALO]
-        dv_ref[:, lanes] = dv[:HALO]
+        gv_ref[BLOCK - HALO :, lanes] = (dv_own[BLOCK - HALO :] + halo_ref[:, value_lanes]).astype(BF)
+        halo_ref[:, lanes] = dk[:HALO]
+        halo_ref[:, value_lanes] = dv[:HALO]
         q_carried = jnp.where(carried, front["q_scaled"], jnp.zeros_like(front["q_scaled"]))
         added = jnp.where(diag, tn(q_carried, grad), 0.0)
         back_state_ref[pair] = jnp.where(keep, back, 0.0) + added
@@ -367,10 +400,14 @@
             jnp.where(keep, back_sum, 0.0) + added_sum, (8, 128)
         )
 
-    @pl.when(index == 0)
+    @pl.when(first == 0)
     def _():
-        halo_ref[:, :512] = dk_ref[...]
-        halo_ref[:, 512:] = dv_ref[...]
+        for pair in range(4):
+            slot = (pair + 2) % 4
+            pack(packet_ref, slot, back_state_ref[pair], back_sum_ref[pair][0:1])
+            for kind in range(2):
+                lane = 512 * kind + 128 * pair
+                pack_halo(packet_ref, kind, slot, halo_ref[:, lane : lane + 128].astype(BF))
 
 
 def feed_kernel(
@@ -393,7 +430,6 @@
     gmix_ref,
     ggain_ref,
 ):
-    step = pl.program_id(0)
     x = x_ref[...].astype(F32)
     hidden = x + (nn(mixed_ref[:, :256], wa_own_ref[...]) + nn(mixed_ref[:, 256:], wa_other_ref[...]))
     r = lax.rsqrt(jnp.mean(hidden * hidden, axis=1, keepdims=True) + EPS)
@@ -431,18 +467,34 @@
     gmix_ref[:, :256] = nt(branch, wa_own_ref[...]).astype(BF)
     gmix_ref[:, 256:] = nt(branch, wa_other_ref[...]).astype(BF)
 
-    @pl.when(step == 0)
+    @pl.when(pl.program_id(0) == 0)
     def _():
         ggain_ref[...] = jnp.zeros_like(ggain_ref)
 
     ggain_ref[0:1] += jnp.sum(back * y, axis=0, keepdims=True)
 
 
-def weight_grads_kernel(mixed_ref, branch_ref, active_ref, cot_ref, normed_ref, gpre_ref, wo_ref, wi_ref):
-    for half in range(2):
-        wo_ref[half, 0:1024] = tn(active_ref[:, 1024 * half : 1024 * half + 1024], cot_ref[...]).astype(BF)
-        wo_ref[half, 1024:1280] = tn(mixed_ref[:, 256 * half : 256 * half + 256], branch_ref[...]).astype(BF)
-        wi_ref[half] = tn(normed_ref[...], gpre_ref[:, 1024 * half : 1024 * half + 1024]).astype(BF)
+def out_grads_kernel(mixed_ref, branch_ref, active_ref, cot_ref, *grad_refs):
+    units = active_ref.shape[1] // 2
+    heads = mixed_ref.shape[1] // 2
+    for half, grad_ref in enumerate(grad_refs):
+        active = active_ref[:, units * half : units * (half + 1)]
+        mixed = mixed_ref[:, heads * half : heads * half + heads // 2]
+        grad_ref[:units] = tn(active, cot_ref[...]).astype(BF)
+        grad_ref[units:] = tn(mixed, branch_ref[...]).astype(BF)
+
+
+def in_grads_kernel(mixed_ref, branch_ref, normed_ref, gpre_ref, *grad_refs):
+    units = gpre_ref.shape[1] // 2
+    heads = mixed_ref.shape[1] // 2
+    width = normed_ref.shape[1]
+    for half, grad_ref in enumerate(grad_refs):
+        mixed = mixed_ref[:, heads * half + heads // 2 : heads * (half + 1)]
+        grad_ref[: heads // 2] = tn(mixed, branch_ref[...]).astype(BF)
+        for part in range(2):
+            first = units * half + part * units // 2
+            row = heads // 2 + width * part
+            grad_ref[row : row + width] = tn(normed_ref[...], gpre_ref[:, first : first + units // 2]).astype(BF)
 
 
 def finish_kernel(
@@ -452,55 +504,116 @@
     own_ref,
     other_ref,
     normed_ref,
-    gq_ref,
-    gk_ref,
-    gv_ref,
-    halo_ref,
-    back_state_ref,
-    back_sum_ref,
-    gproj_ref,
-    wgrad_ref,
+    packet_ref,
+    gblend_ref,
+    ggain_ref,
+    gain_ref,
+    w_own_ref,
+    w_other_ref,
+    *refs,
 ):
+    *grad_refs, gproj_ref, wgrad_own_ref, wgrad_sent_ref = refs
+
+    def grad_rows(kind, lanes):
+        parts = [ref[:, lanes] for ref in grad_refs[kind::3]]
+        return jnp.concatenate(parts, axis=0)
+
     rows = own_ref.shape[0]
     flag = flag_ref[0]
     member_from = start_at(ends_ref, rows - 1, docs)
     member = (iota((rows, 1), 0) >= member_from) & (flag == 0)
     live = flag == 0
+    diag = pair_diag(256, 128)
     for pair in range(4):
         src = own_ref if pair < 2 else other_ref
         col = 128 * (pair % 2)
         lanes = slice(128 * pair, 128 * pair + 128)
         base = 768 * (pair // 2) + col
-        slot = (pair + 2) % 4
         k = src[:, 256 + col : 384 + col].astype(F32)
         v = src[:, 512 + col : 640 + col]
-        back = back_state_ref[slot].astype(BF)
-        back_sum = back_sum_ref[slot][0:1]
+        back, back_sum = unpack(packet_ref, pair, diag)
+        back, back_sum = back.astype(BF), back_sum[0:1]
         t = jnp.tanh(k)
         slope = jnp.exp(jnp.minimum(k, 0.0))
         k_both = jnp.concatenate([first_feature(k), t.astype(BF)], axis=1)
         dfeat = nt(v, back)
         extra_k = (dfeat[:, :128] - back_sum) * slope + dfeat[:, 128:] * (1.0 - t * t)
         extra_v = nn(k_both, back)
-        gk = gk_ref[:, lanes].astype(F32) + jnp.where(member, extra_k, 0.0)
-        gv = gv_ref[:, lanes].astype(F32) + jnp.where(member, extra_v, 0.0)
-        other_lanes = slice(128 * slot, 128 * slot + 128)
-        other_values = slice(512 + 128 * slot, 640 + 128 * slot)
-        halo_k = jnp.where(live, halo_ref[:, other_lanes], 0.0)
-        halo_v = jnp.where(live, halo_ref[:, other_values], 0.0)
+        gk = grad_rows(1, lanes).astype(F32) + jnp.where(member, extra_k, 0.0)
+        gv = grad_rows(2, lanes).astype(F32) + jnp.where(member, extra_v, 0.0)
+        halo_k = jnp.where(live, unpack_halo(packet_ref, 0, pair).astype(F32), 0.0)
+        halo_v = jnp.where(live, unpack_halo(packet_ref, 1, pair).astype(F32), 0.0)
         cut = rows - HALO
-        gproj_ref[:, base : base + 128] = gq_ref[:, lanes]
+        gproj_ref[:, base : base + 128] = grad_rows(0, lanes)
         gproj_ref[:cut, base + 256 : base + 384] = gk[:cut].astype(BF)
         gproj_ref[cut:, base + 256 : base + 384] = (gk[cut:] + halo_k).astype(BF)
         gproj_ref[:cut, base + 512 : base + 640] = gv[:cut].astype(BF)
         gproj_ref[cut:, base + 512 : base + 640] = (gv[cut:] + halo_v).astype(BF)
-    for half in range(2):
-        wgrad_ref[half] = tn(normed_ref[...], gproj_ref[:, 768 * half : 768 * half + 768]).astype(BF)
-
-
-def input_grad_kernel(gproj_ref, x_ref, ghid_ref, gain_ref, w_own_ref, w_other_ref, out_ref, ggain_ref):
-    step = pl.program_id(0)
-    gnormed = nt(gproj_ref[:, :768], w_own_ref[...]) + nt(gproj_ref[:, 768:], w_other_ref[...])
+    width = normed_ref.shape[1]
+    cols = w_own_ref.shape[2]
+    normed = normed_ref[...]
+    ones = jnp.ones((1, cols), F32)
+    gain_grad = jnp.zeros((1, width), F32)
+    for half, (wgrad_ref, w_ref) in enumerate(((wgrad_own_ref, w_own_ref), (wgrad_sent_ref, w_other_ref))):
+        for kind in range(3):
+            first = 3 * cols * half + cols * kind
+            wgrad = tn(normed, gproj_ref[:, first : first + cols])
+            wgrad_ref[width * kind : width * kind + width] = wgrad.astype(BF)
+            products = wgrad * w_ref[kind].astype(F32)
+            high = products.astype(BF)
+            low = (products - high.astype(F32)).astype(BF)
+            gain_grad = gain_grad + nt(ones.astype(BF), high) + nt(ones.astype(BF), low)
+    gain_grad = gain_grad / gain_ref[...]
+    for half, wgrad_ref in enumerate((wgrad_own_ref, wgrad_sent_ref)):
+        blends = [
+            jnp.concatenate([gblend_ref[kind, 2 * half + pair][0:1] for pair in range(2)], axis=1)
+            for kind in range(2)
+        ]
+        gains = [gain_grad[:, :256], gain_grad[:, 256:], ggain_ref[0:1, :256], ggain_ref[0:1, 256:]]
+        extra = jnp.concatenate(blends + gains + [jnp.zeros((10, 256), F32)], axis=0)
+        wgrad_ref[3 * width : 3 * width + 16] = extra.astype(BF)
+        wgrad_ref[3 * width + 16 :] = jnp.zeros((EXTRA - 16, 256), BF)
+
+
+def merged(low, mine, got):
+    return jnp.where(low, mine, got), jnp.where(low, got, mine)
+
+
+def feed_output_kernel(bits_ref, out_mine_ref, out_got_ref, in_mine_ref, in_got_ref, wo_ref, wa_ref, wi_ref):
+    units, width = wo_ref.shape
+    rows = out_mine_ref.shape[0]
+    quarter = wa_ref.shape[0] // 2
+    first, second = merged(bits_ref[0] == 0, out_mine_ref[...], out_got_ref[...])
+    wo_ref[:rows] = first.astype(F32)
+    wo_ref[rows:] = second[: units - rows].astype(F32)
+    wa_ref[:quarter] = second[units - rows :].astype(F32)
+    first, second = merged(bits_ref[1] == 0, in_mine_ref[...], in_got_ref[...])
+    wa_ref[quarter:] = first[:quarter].astype(F32)
+    upper = rows - quarter
+    wi_ref[:upper, : units // 2] = first[quarter:].astype(F32)
+    wi_ref[upper:, : units // 2] = second[: width - upper].astype(F32)
+    wi_ref[:, units // 2 :] = second[width - upper :].astype(F32)
+
+
+def qkv_output_kernel(bits_ref, a_mine_ref, a_got_ref, b_mine_ref, b_got_ref, wq_ref, rest_ref):
+    rows = a_mine_ref.shape[0]
+    top, upper = merged(bits_ref[0] == 0, a_mine_ref[...], a_got_ref[...])
+    wq_ref[:rows] = top.astype(F32)
+    wq_ref[rows : 2 * rows] = upper.astype(F32)
+    lower, bottom = merged(bits_ref[1] == 0, b_mine_ref[...], b_got_ref[...])
+    wq_ref[2 * rows : 3 * rows] = lower.astype(F32)
+    wq_ref[3 * rows :] = bottom[: rows - EXTRA].astype(F32)
+    rest_ref[...] = bottom[rows - EXTRA : rows - EXTRA + 8].astype(F32)
+
+
+def input_grad_kernel(gproj_ref, x_ref, ghid_ref, gain_ref, w_own_ref, w_other_ref, out_ref):
+    cols = w_own_ref.shape[2]
+    gnormed = None
+    for half, w_ref in enumerate((w_own_ref, w_other_ref)):
+        for kind in range(3):
+            first = 3 * cols * half + cols * kind
+            term = nt(gproj_ref[:, first : first + cols], w_ref[kind])
+            gnormed = term if gnormed is None else gnormed + term
     x = x_ref[...].astype(F32)
     r = lax.rsqrt(jnp.mean(x * x, axis=1, keepdims=True) + EPS)
     y = x * r
@@ -508,85 +621,113 @@
     grad = ghid_ref[...] + r * (scaled - y * jnp.mean(scaled * y, axis=1, keepdims=True))
     out_ref[...] = grad.astype(BF)
 
-    @pl.when(step == 0)
-    def _():
-        ggain_ref[...] = jnp.zeros_like(ggain_ref)
-
-    ggain_ref[0:1] += jnp.sum(gnormed * y, axis=0, keepdims=True)
-
-
-def dp_dims(count):
-    dims = []
+
+def flip(values, count, stride):
+    return lax.ppermute(values, "dp", [(src, src ^ stride) for src in range(count)])
+
+
+def strides_of(count):
+    strides = []
     stride = 1
-    left = count
-    for size in (2, 2):
-        if left % size == 0 and left > 1:
-            dims.append((size, stride))
-            stride *= size
-            left //= size
-    while left > 1:
-        size = 4 if left % 4 == 0 else (2 if left % 2 == 0 else left)
-        dims.append((size, stride))
-        stride *= size
-        left //= size
-    return dims
-
-
-def shift_pairs(count, size, stride, offset):
-    pairs = []
-    for src in range(count):
-        place = (src // stride) % size
-        pairs.append((src, src + ((place + offset) % size - place) * stride))
-    return pairs
-
-
-def scatter_step(values, count, size, stride):
-    place = (lax.axis_index("dp") // stride) % size
-    parts = values.reshape((size, values.shape[0] // size) + values.shape[1:])
-    total = lax.dynamic_index_in_dim(parts, place, 0, keepdims=False).astype(F32)
-    for offset in range(1, size):
-        sent = lax.dynamic_index_in_dim(parts, (place + offset) % size, 0, keepdims=False)
-        got = lax.ppermute(sent, "dp", shift_pairs(count, size, stride, offset))
-        total = total + got.astype(F32)
-    return total.astype(values.dtype)
-
-
-def gather_step(values, count, size, stride):
-    place = (lax.axis_index("dp") // stride) % size
-    whole_values = jnp.zeros((size,) + values.shape, values.dtype)
-    whole_values = lax.dynamic_update_index_in_dim(whole_values, values, place, 0)
-    for offset in range(1, size):
-        got = lax.ppermute(values, "dp", shift_pairs(count, size, stride, offset))
-        whole_values = lax.dynamic_update_index_in_dim(
-            whole_values, got, (place - offset) % size, 0
-        )
-    return whole_values.reshape((size * values.shape[0],) + values.shape[1:])
-
-
-def reduce_all(values, count):
-    dims = dp_dims(count)
-    if not dims:
-        return values
-    orders = [dims]
-    if len(dims) > 1:
-        orders.append([dims[1], dims[0]] + dims[2:])
-    pieces = []
-    for part, order in zip(jnp.split(values, len(orders), axis=0), orders):
-        for size, stride in order:
-            part = scatter_step(part, count, size, stride)
-        for size, stride in reversed(order):
-            part = gather_step(part, count, size, stride)
-        pieces.append(part)
-    return jnp.concatenate(pieces, axis=0)
-
-
-def reduce_small(values, count):
-    for size, stride in dp_dims(count):
-        total = values
-        for offset in range(1, size):
-            total = total + lax.ppermute(values, "dp", shift_pairs(count, size, stride, offset))
-        values = total
-    return values
+    while stride < count:
+        strides.append(stride)
+        stride *= 2
+    return strides
+
+
+class Reduction:
+    def __init__(self, stacks, count, whole_late=False):
+        self.stacks = [[(term, 0) for term in terms] for terms in stacks]
+        self.rows = [terms[0].shape[0] for terms in stacks]
+        self.count = count
+        strides = strides_of(count)
+        self.orders = [strides, strides[1::-1] + strides[2:]]
+        self.steps = len(strides)
+        self.taken = 0
+        self.halved = min(2, self.steps) if whole_late else self.steps
+        self.place = lax.axis_index("dp")
+        self.held = None
+
+    def bit(self, stride):
+        return (self.place // stride) % 2
+
+    def after(self, *tokens):
+        if self.held is not None:
+            *self.gots, first, second = tie(*self.gots, *self.held)
+            self.held = [first, second]
+            return tokens
+        news = [terms[-1][0] for terms in self.stacks]
+        if news[0] is news[1]:
+            news = news[:1]
+        tied = tie(*news, *tokens)
+        for stack in range(2):
+            offset = self.stacks[stack][-1][1]
+            self.stacks[stack][-1] = (tied[min(stack, len(news) - 1)], offset)
+        return tied[len(news) :]
+
+    def cut(self, stack, rows, skip):
+        total = None
+        for term, offset in self.stacks[stack]:
+            part = lax.dynamic_slice_in_dim(term, offset + skip, rows, 0).astype(F32)
+            total = part if total is None else total + part
+        return total.astype(BF)
+
+    def outgoing(self):
+        cuts = []
+        for stack in range(2):
+            if self.taken < self.halved:
+                self.rows[stack] //= 2
+                bit = self.bit(self.orders[stack][self.taken])
+                cuts.append(self.cut(stack, self.rows[stack], (1 - bit) * self.rows[stack]))
+            else:
+                cuts.append(self.cut(stack, self.rows[stack], 0))
+        return cuts if self.taken < 2 else [jnp.concatenate(cuts, axis=0)]
+
+    def send(self, cuts):
+        gots = [flip(cut, self.count, self.orders[stack][self.taken]) for stack, cut in enumerate(cuts)]
+        for stack in range(2):
+            skip = self.rows[0] if stack == 1 and len(cuts) == 1 else 0
+            got = gots[min(stack, len(cuts) - 1)]
+            if self.taken < self.halved:
+                bit = self.bit(self.orders[stack][self.taken])
+                kept = [(term, offset + bit * self.rows[stack]) for term, offset in self.stacks[stack]]
+            else:
+                kept = [(cuts[0], skip)]
+            self.stacks[stack] = kept + [(got, skip)]
+        self.taken += 1
+
+    def start_gather(self):
+        self.held = [self.cut(stack, self.rows[stack], 0) for stack in range(2)]
+
+    def gather_outgoing(self):
+        return list(self.held) if self.halved <= 2 else [jnp.concatenate(self.held, axis=0)]
+
+    def gather_send(self, cuts):
+        step = self.halved - 1
+        gots = [flip(cut, self.count, self.orders[stack][step]) for stack, cut in enumerate(cuts)]
+        if len(gots) == 1:
+            first = self.held[0].shape[0]
+            gots = [gots[0][:first], gots[0][first:]]
+        self.gots = gots
+        self.halved = step
+
+    def last_bits(self):
+        return jnp.stack([self.bit(order[0]) if order else 0 * self.place for order in self.orders])
+
+    def parts(self):
+        if self.steps > 0:
+            return [self.held[0], self.gots[0], self.held[1], self.gots[1]]
+        halves = []
+        for held in self.held:
+            middle = held.shape[0] // 2
+            halves += [held[:middle], held[middle:]]
+        return halves
+
+    def gather_take(self):
+        for stack in range(2):
+            low = self.bit(self.orders[stack][self.halved]) == 0
+            mine, got = self.held[stack], self.gots[stack]
+            self.held[stack] = jnp.concatenate([jnp.where(low, mine, got), jnp.where(low, got, mine)], axis=0)
 
 
 def swap(values):
@@ -599,7 +740,7 @@
     half = lax.axis_index("tensor").astype(jnp.int32)
     blocks = rows // BLOCK
 
-    wq_own = w_qkv.reshape(width, -1)
+    wq_own = w_qkv.transpose(1, 0, 2)
     wq_other = swap(wq_own)
     wa_other, wi_other, wo_other = swap(w_attn), swap(w_in), swap(w_out)
     blend_both = jnp.repeat(jnp.concatenate([blend, swap(blend)], axis=1), 64, axis=1)
@@ -612,7 +753,7 @@
     def row_block(size, cols):
         return pl.BlockSpec((size, cols), lambda i: (i, 0))
 
-    own_cols = wq_own.shape[1]
+    own_cols = 3 * wq_own.shape[2]
     normed, own = pl.pallas_call(
         norm_project_kernel,
         grid=(4,),
@@ -620,21 +761,21 @@
         out_specs=[row_block(rows // 4, width), row_block(rows // 4, own_cols)],
         out_shape=[jax.ShapeDtypeStruct((rows, width), BF), jax.ShapeDtypeStruct((rows, own_cols), BF)],
         compiler_params=params(),
+        cost_estimate=cost(5),
         name="norm_project",
     )(tokens, gain_one, wq_own)
-    other, state_end, sum_end, halo_end = pl.pallas_call(
+    other, packet = pl.pallas_call(
         partial(project_state_kernel, docs),
         in_specs=[smem] + [pl.BlockSpec(memory_space=pltpu.VMEM)] * 3,
         out_shape=[
             jax.ShapeDtypeStruct((rows, own_cols), BF),
-            jax.ShapeDtypeStruct((4, 256, 128), BF),
-            jax.ShapeDtypeStruct((4, 8, 128), F32),
-            jax.ShapeDtypeStruct((HALO, 1024), BF),
+            jax.ShapeDtypeStruct((PACKET, 128), BF),
         ],
         compiler_params=params(),
+        cost_estimate=cost(5),
         name="project_state",
     )(ends, normed, wq_other, own)
-    state_in, sum_in, halo_in = swap(state_end), swap(sum_end), swap(halo_end)
+    packet = swap(packet)
 
     mixed, states, sums, prevs = pl.pallas_call(
         partial(mixer_forward_kernel, docs),
@@ -643,9 +784,7 @@
             smem,
             row_block(BLOCK, own_cols),
             row_block(BLOCK, own_cols),
-            whole((HALO, 1024)),
-            whole((4, 256, 128)),
-            whole((4, 8, 128)),
+            whole((PACKET, 128)),
             whole(blend_both.shape),
         ],
         out_specs=[
@@ -666,8 +805,9 @@
             pltpu.VMEM((HALO, 1024), BF),
         ],
         compiler_params=params(),
+        cost_estimate=cost(20),
         name="mixer_forward",
-    )(ends, own, other, halo_in, state_in, sum_in, blend_both)
+    )(ends, own, other, packet, blend_both)
 
     hidden_units = 2 * w_in.shape[1]
     tall = rows // 4
@@ -707,110 +847,199 @@
             jax.ShapeDtypeStruct((8, width), F32),
         ],
         compiler_params=params(),
+        cost_estimate=cost(20),
         name="feed",
     )(mixed, tokens, cotangent, gain_two, w_attn, wa_other, w_in, wi_other, w_out, wo_other)
 
-    wo_grads, wi_grads = pl.pallas_call(
-        weight_grads_kernel,
-        out_shape=[
-            jax.ShapeDtypeStruct((2, w_out.shape[0] + w_attn.shape[0], width), BF),
-            jax.ShapeDtypeStruct((2, width, w_in.shape[1]), BF),
-        ],
+    units = w_out.shape[0]
+    quarter = w_attn.shape[0] // 2
+    out_shape = jax.ShapeDtypeStruct((units + quarter, width), BF)
+    out_own, out_sent = pl.pallas_call(
+        out_grads_kernel,
+        out_shape=[out_shape, out_shape],
         compiler_params=params(),
-        name="weight_grads",
-    )(mixed, branch, active, cotangent, normed_two, gpre)
-
-    def join_halves(pair):
-        return (pair[0].astype(F32) + swap(pair[1]).astype(F32)).astype(BF)
-
-    wo_sum = reduce_all(join_halves(wo_grads), count)
-    wi_sum = reduce_all(join_halves(wi_grads), count)
-
-    back_block = lambda size, cols: pl.BlockSpec((size, cols), lambda i: (blocks - 1 - i, 0))
-    gq, gk, gv, halo_back, back_state, back_sum, gblend = pl.pallas_call(
-        partial(mixer_backward_kernel, docs),
-        grid=(blocks,),
-        in_specs=[
-            smem,
-            back_block(BLOCK, own_cols),
-            back_block(BLOCK, own_cols),
-            pl.BlockSpec((1, HALO, 1024), lambda i: (blocks - 1 - i, 0, 0)),
-            pl.BlockSpec((1, 4, 256, 128), lambda i: (blocks - 1 - i, 0, 0, 0)),
-            pl.BlockSpec((1, 4, 8, 128), lambda i: (blocks - 1 - i, 0, 0, 0)),
-            whole(blend_both.shape),
-            back_block(BLOCK, width),
-        ],
-        out_specs=[
-            back_block(BLOCK, width),
-            back_block(BLOCK, width),
-            back_block(BLOCK, width),
-            whole((HALO, 1024)),
-            whole((4, 256, 128)),
-            whole((4, 8, 128)),
-            whole((2, 4, 8, 128)),
-        ],
-        out_shape=[
-            jax.ShapeDtypeStruct((rows, width), BF),
-            jax.ShapeDtypeStruct((rows, width), BF),
-            jax.ShapeDtypeStruct((rows, width), BF),
-            jax.ShapeDtypeStruct((HALO, 1024), F32),
-            jax.ShapeDtypeStruct((4, 256, 128), F32),
-            jax.ShapeDtypeStruct((4, 8, 128), F32),
-            jax.ShapeDtypeStruct((2, 4, 8, 128), F32),
-        ],
-        scratch_shapes=[pltpu.VMEM((HALO, 512), F32), pltpu.VMEM((HALO, 512), F32)],
+        cost_estimate=cost(6),
+        name="out_grads",
+    )(mixed, branch, active, cotangent)
+    normed_two, gpre, out_sent = tie(normed_two, gpre, out_sent)
+    in_shape = jax.ShapeDtypeStruct((quarter + units, width), BF)
+    in_own, in_sent = pl.pallas_call(
+        in_grads_kernel,
+        out_shape=[in_shape, in_shape],
         compiler_params=params(),
-        name="mixer_backward",
-    )(ends, own, other, prevs, states, sums, blend_both, gmix)
-    halo_got, back_state_got, back_sum_got = swap(halo_back), swap(back_state), swap(back_sum)
-
-    gproj, wq_grads = pl.pallas_call(
+        cost_estimate=cost(6),
+        name="in_grads",
+    )(mixed, branch, normed_two, gpre)
+    feed_sum = Reduction([[out_own, swap(out_sent)], [in_own, swap(in_sent)]], count)
+    wanted = feed_sum.steps
+    if wanted > 0:
+        cuts = feed_sum.outgoing()
+        gmix, *cuts = tie(gmix, *cuts)
+        feed_sum.send(cuts)
+
+    def mixer_backward(first_block, per_call, grads, carried):
+        top = first_block + per_call - 1
+
+        def back_block(*shape):
+            return pl.BlockSpec(shape, lambda i: (top - i,) + (0,) * (len(shape) - 1))
+
+        def call_block(*shape):
+            return pl.BlockSpec(shape, lambda i: (per_call - 1 - i,) + (0,) * (len(shape) - 1))
+
+        carry_shapes = ((HALO, 1024), (4, 256, 128), (4, 8, 128), (2, 4, 8, 128))
+        return pl.pallas_call(
+            partial(mixer_backward_kernel, docs, top, len(carried) > 0),
+            grid=(per_call,),
+            in_specs=[
+                smem,
+                back_block(BLOCK, own_cols),
+                back_block(BLOCK, own_cols),
+                back_block(1, HALO, 1024),
+                back_block(1, 4, 256, 128),
+                back_block(1, 4, 8, 128),
+                whole(blend_both.shape),
+                back_block(BLOCK, width),
+            ]
+            + [whole(c.shape) for c in carried],
+            out_specs=[call_block(BLOCK, width)] * 3 + [whole(shape) for shape in carry_shapes] + [whole((PACKET, 128))],
+            out_shape=[jax.ShapeDtypeStruct((per_call * BLOCK, width), BF)] * 3
+            + [jax.ShapeDtypeStruct(shape, F32) for shape in carry_shapes]
+            + [jax.ShapeDtypeStruct((PACKET, 128), BF)],
+            compiler_params=params(),
+            cost_estimate=cost(3 * per_call),
+            name="mixer_backward",
+        )(ends, own, other, prevs, states, sums, blend_both, grads, *carried)
+
+    sizes = (blocks // 2, blocks // 4, blocks // 4)
+    left = blocks
+    grads = []
+    carried = ()
+    for call, size in enumerate(sizes):
+        left -= size
+        *parts, halo_back, back_state, back_sum, gblend, packet_back = mixer_backward(left, size, gmix, carried)
+        grads.insert(0, parts)
+        if wanted > call + 1:
+            back_state, packet_back = feed_sum.after(back_state, packet_back)
+            cuts = feed_sum.outgoing()
+            back_state, packet_back, *cuts = tie(back_state, packet_back, *cuts)
+            feed_sum.send(cuts)
+        carried = (halo_back, back_state, back_sum, gblend)
+    packet_got = swap(packet_back)
+
+    gproj, wq_mine, wq_sent = pl.pallas_call(
         partial(finish_kernel, docs),
-        in_specs=[smem, smem] + [pl.BlockSpec(memory_space=pltpu.VMEM)] * 9,
+        in_specs=[smem, smem] + [pl.BlockSpec(memory_space=pltpu.VMEM)] * (9 + 3 * len(sizes)),
         out_shape=[
             jax.ShapeDtypeStruct((rows, 2 * own_cols), BF),
-            jax.ShapeDtypeStruct((2, width, own_cols), BF),
+            jax.ShapeDtypeStruct((3 * width + EXTRA, own_cols // 3), BF),
+            jax.ShapeDtypeStruct((3 * width + EXTRA, own_cols // 3), BF),
         ],
         compiler_params=params(),
+        cost_estimate=cost(8),
         name="finish",
-    )(ends, flag, own, other, normed, gq, gk, gv, halo_got, back_state_got, back_sum_got)
-    wq_sum = reduce_all(join_halves(wq_grads), count)
-
-    grad_input, ggain_attn = pl.pallas_call(
-        input_grad_kernel,
-        grid=(4,),
-        in_specs=[
-            row_block(tall, 2 * own_cols),
-            row_block(tall, width),
-            row_block(tall, width),
-            whole((1, width)),
-            whole(wq_own.shape),
-            whole(wq_own.shape),
-        ],
-        out_specs=[row_block(tall, width), whole((8, width))],
-        out_shape=[jax.ShapeDtypeStruct((rows, width), BF), jax.ShapeDtypeStruct((8, width), F32)],
+    )(
+        ends,
+        flag,
+        own,
+        other,
+        normed,
+        packet_got,
+        gblend,
+        ggain_mlp,
+        gain_one,
+        wq_own,
+        wq_other,
+        *[grad for parts in grads for grad in parts],
+    )
+    def input_gradient(gproj):
+        return pl.pallas_call(
+            input_grad_kernel,
+            grid=(4,),
+            in_specs=[
+                row_block(tall, 2 * own_cols),
+                row_block(tall, width),
+                row_block(tall, width),
+                whole((1, width)),
+                whole(wq_own.shape),
+                whole(wq_own.shape),
+            ],
+            out_specs=row_block(tall, width),
+            out_shape=jax.ShapeDtypeStruct((rows, width), BF),
+            compiler_params=params(),
+            cost_estimate=cost(7),
+            name="input_grad",
+        )(gproj, tokens, ghid, gain_one, wq_own, wq_other)
+
+    if wanted > 0:
+        (wq_sent,) = feed_sum.after(wq_sent)
+    while feed_sum.taken < wanted:
+        feed_sum.send(feed_sum.outgoing())
+    wq_got = swap(wq_sent)
+    cut = wq_got.shape[0] // 2
+    wq_sums = Reduction([[wq_mine[:cut], wq_got[:cut]], [wq_mine[cut:], wq_got[cut:]]], count, True)
+    feed_sum.start_gather()
+    first_round = True
+    while feed_sum.halved > 0:
+        feed_cuts = feed_sum.gather_outgoing()
+        wq_cuts = wq_sums.outgoing() if wq_sums.taken < wanted else []
+        gproj, *cuts = tie(gproj, *wq_cuts, *feed_cuts)
+        wq_cuts, feed_cuts = cuts[: len(wq_cuts)], cuts[len(wq_cuts) :]
+        if wq_cuts:
+            wq_sums.send(wq_cuts)
+        feed_sum.gather_send(feed_cuts)
+        if first_round:
+            first_round = False
+            grad_input = input_gradient(gproj)
+            (grad_input,) = wq_sums.after(grad_input)
+        if feed_sum.halved > 0:
+            feed_sum.gather_take()
+    if first_round:
+        grad_input = input_gradient(gproj)
+    while wq_sums.taken < wanted:
+        wq_sums.send(wq_sums.outgoing())
+    wq_sums.start_gather()
+    feed_parts = feed_sum.parts()
+    if wanted > 1:
+        *feed_parts, first, second = tie(*feed_parts, *wq_sums.held)
+        wq_sums.held = [first, second]
+    wo_grad, wa_grad, wi_grad = pl.pallas_call(
+        feed_output_kernel,
+        in_specs=[smem] + [pl.BlockSpec(memory_space=pltpu.VMEM)] * 4,
+        out_shape=[
+            jax.ShapeDtypeStruct(w_out.shape, F32),
+            jax.ShapeDtypeStruct(w_attn.shape, F32),
+            jax.ShapeDtypeStruct(w_in.shape, F32),
+        ],
         compiler_params=params(),
-        name="input_grad",
-    )(gproj, tokens, ghid, gain_one, wq_own, wq_other)
-
-    gblend_heads = jnp.sum(gblend[:, :, 0].reshape(2, 8, 64), axis=2)
-    gblend_own = gblend_heads[:, :4] + swap(gblend_heads[:, 4:])
-    gains = jnp.concatenate([ggain_attn[:1], ggain_mlp[:1]], axis=0)
-    gains = gains + swap(gains)
-    small = jnp.concatenate([gains, jnp.pad(gblend_own.reshape(1, 8), ((0, 0), (0, width - 8)))], axis=0)
-    small = reduce_small(small, count)
-
-    units = w_out.shape[0]
+        cost_estimate=cost(3),
+        name="feed_output",
+    )(feed_sum.last_bits(), *feed_parts)
+    while wq_sums.halved > 0:
+        wq_sums.gather_send(wq_sums.gather_outgoing())
+        if wq_sums.halved > 0:
+            wq_sums.gather_take()
+    wq_grad, rest = pl.pallas_call(
+        qkv_output_kernel,
+        in_specs=[smem] + [pl.BlockSpec(memory_space=pltpu.VMEM)] * 4,
+        out_shape=[
+            jax.ShapeDtypeStruct((3 * width, own_cols // 3), F32),
+            jax.ShapeDtypeStruct((8, own_cols // 3), F32),
+        ],
+        compiler_params=params(),
+        cost_estimate=cost(3),
+        name="qkv_output",
+    )(wq_sums.last_bits(), *wq_sums.parts())
+
     return (
         output,
         grad_input,
-        wq_sum.astype(F32).reshape(w_qkv.shape),
-        wo_sum[units:].astype(F32),
-        wi_sum.astype(F32),
-        wo_sum[:units].astype(F32),
-        small[0],
-        small[1],
-        small[2, :8].reshape(2, 4),
+        wq_grad.reshape(wq_own.shape).transpose(1, 0, 2),
+        wa_grad,
+        wi_grad,
+        wo_grad,
+        rest[2:4].reshape(width),
+        rest[4:6].reshape(width),
+        jnp.sum(rest[:2].reshape(2, 4, 64), axis=2),
     )
 
 

time: 345 us -> 207 us (0.60)
  local copies, waits for them, and re-layouts: 75.1 us -> 9.47 us
  starting transfers between devices: 78.8 us -> 26.2 us
  waiting for transfers between devices: 70.4 us -> 33.8 us
  Pallas kernels: 104 us -> 121 us
    dynamic_update_slice x42 -> x0, local copies, waits for them, and re-layouts: 51.4 us -> none  [the longest x30 26.7 us: gather_step(): lax.dynamic_update_index_in_dim(whole_values, got, (place - offset) % siz...]
    ppermute x65 -> x22, starting transfers between devices: 74.6 us -> 23.8 us  [flip(): lax.ppermute(values, 'dp', [(src, src ^ stride) for src in range(count)])]
    ppermute x65 -> x22, waiting for transfers between devices: 67 us -> 29.7 us  [flip(): lax.ppermute(values, 'dp', [(src, src ^ stride) for src in range(count)])]
    pallas_call x3 -> x8, Pallas kernels: 44.8 us -> 59.2 us  [the longest x3 32.8 us: mixer_backward(): pl.pallas_call(partial(mixer_backward_kernel, docs, top, len(carried) > 0...]
    squeeze x21 -> x0, local copies, waits for them, and re-layouts: 5.23 us -> none  [the longest x3 3.57 us: join_halves(): return (pair[0].astype(F32) + swap(pair[1]).astype(F32)).astype(BF)]
    another operation x20 -> x0, local copies, waits for them, and re-layouts: 4.93 us -> none
    convert_element_type x19 -> x15, other arithmetic: 11.7 us -> 10.7 us  [cut(): return total.astype(BF)]
  transfers between devices with their start and end apart: 81 -> 32, of which waited for: 31 -> 15; matrix products, arithmetic and copies ran while one was open for 24% -> 3% of each run, Pallas kernels for 16% -> 40%
where the time goes in v2:
time: 207 us; the launch traced here: 206 us
  Pallas kernels  121 us (58%)
  waiting for transfers between devices  33.8 us (16%)
  starting transfers between devices  26.2 us (13%)
  other arithmetic  14.7 us (7%)
  local copies, waits for them, and re-layouts  9.47 us (5%)
    pallas_call x3, Pallas kernels, mixer_backward(): pl.pallas_call(partial(mixer_backward_kernel, docs, top, len(carried) > 0...  32.8 us
    ppermute x22, waiting for transfers between devices, flip(): lax.ppermute(values, 'dp', [(src, src ^ stride) for src in range(count)])  29.7 us
    ppermute x22, starting transfers between devices, flip(): lax.ppermute(values, 'dp', [(src, src ^ stride) for src in range(count)])  23.8 us
    pallas_call x1, Pallas kernels, body(): pl.pallas_call(feed_kernel, grid=(4,), in_specs=[row_block(tall, width),...  21.2 us
    pallas_call x1, Pallas kernels, body(): pl.pallas_call(partial(mixer_forward_kernel, docs), grid=(blocks,), in_sp...  20.9 us
    convert_element_type x15, other arithmetic, cut(): return total.astype(BF)  10.7 us
    pallas_call x1, Pallas kernels, body(): pl.pallas_call(partial(finish_kernel, docs), in_specs=[smem, smem] + [pl....  9.92 us
    pallas_call x1, Pallas kernels, body(): pl.pallas_call(out_grads_kernel, out_shape=[out_shape, out_shape], compil...  6.81 us
  transfers between devices with their start and end apart: 32, of which 15 were waited for; matrix products, arithmetic and copies ran while one was open for 3% of the time, Pallas kernels for 40%

profile of v2, /device:TPU:0, one launch (start us, length us, event | category | flops | bytes accessed | tf_op | source)
XLA Modules:
  0.0 205.9 jit_solution(17280172669316153769)
XLA Ops:
  1.8 0.8 reduce-window.9
  2.6 0.6 add_subtract_fusion.ends_ref
  3.2 4.6 %norm_project.1 = (bf16[1024,512]{1,0:T(8,128)(2,1)}, bf16[1024,768]{1,0:T(8,128)(2,1)}) custom-call(bf16[1024,512]{1,0:T(8,128)(2,1)} %x_ref.5, f32[1,512]{1,0:T(1,128)} %bitcast.21, bf16[3,512,256]{2,1,0:T(8,128)(2,1)} %bitcast.18), custom_call_target="tpu_custom_call" | custom-call | flops 50000000 | bytes 1048576 | tf_op jit(solution)/shard_map/norm_project/pallas_call | solution.py:757
  7.7 0.9 copy-done
  8.6 4.8 %project_state.1 = (bf16[1024,768]{1,0:T(8,128)(2,1)}, bf16[832,128]{1,0:T(8,128)(2,1)}) custom-call(s32[7]{0:T(128)} %add_subtract_fusion.ends_ref, bf16[1024,512]{1,0:T(8,128)(2,1)} %get-tuple-element.102.normed_ref, bf16[3,512,256]{2,1,0:T(8,128)(2,1)} %copy-done, bf16[1024,768]{1,0:T(8,128)(2,1)} %get-tuple-element.101.own_ref), custom_call_target="tpu_custom_call" | custom-call | flops 50000000 | bytes 1048576 | tf_op jit(solution)/shard_map/project_state/pallas_call | solution.py:767
  14.0 1.1 collective-permute-done.2
  15.2 0.7 reshape.72.blend_ref
  15.9 0.7 copy-done.18
  16.6 20.9 %mixer_forward.1 = (bf16[1024,512]{1,0:T(8,128)(2,1)}, bf16[8,4,256,128]{3,2,1,0:T(8,128)(2,1)}, f32[8,4,8,128]{3,2,1,0:T(8,128)}, bf16[8,32,1024]{2,1,0:T(8,128)(2,1)}) custom-call(s32[7]{0:T(128)} %add_subtract_fusion.ends_ref, bf16[1024,768]{1,0:T(8,128)(2,1)} %get-tuple-element.101.own_ref, bf16[1024,768]{1,0:T(8,128)(2,1)} %get-tuple-element.103.other_ref, ...), custom_call_target="tpu_custom_call" | custom-call | flops 200000000 | bytes 1048576 | tf_op jit(solution)/shard_map/mixer_forward/pallas_call | solution.py:780
  37.5 0.7 copy-done.17
  39.0 21.2 %feed.1 = (bf16[1024,512]{1,0:T(8,128)(2,1)}, bf16[1024,512]{1,0:T(8,128)(2,1)}, bf16[1024,2048]{1,0:T(8,128)(2,1)}, bf16[1024,2048]{1,0:T(8,128)(2,1)}, f32[102...) custom-call(bf16[1024,512]{1,0:T(8,128)(2,1)} %get-tuple-element.105.mixed_ref, ...), custom_call_target="tpu_custom_call" | custom-call | flops 200000000 | bytes 1048576 | tf_op jit(solution)/shard_map/feed/pallas_call | solution.py:814
  60.1 6.8 %out_grads.1 = (bf16[1152,512]{1,0:T(8,128)(2,1)}, bf16[1152,512]{1,0:T(8,128)(2,1)}) custom-call(bf16[1024,512]{1,0:T(8,128)(2,1)} %get-tuple-element.105.mixed_ref, bf16[1024,512]{1,0:T(8,128)(2,1)} %get-tuple-element.108.branch_ref, bf16[1024,2048]{1,0:T(8,128)(2,1)} %get-tuple-element.109.active_ref, bf16[1024,512]{1,0:T(8,128)(2,1)} %cot_ref.3), custom_call_target="tpu_custom_call" | custom-call | flops 60000000 | bytes 1048576 | tf_op jit(solution)/shard_map/out_grads/pallas_call | solution.py:857
  66.9 6.8 %in_grads.1 = (bf16[1152,512]{1,0:T(8,128)(2,1)}, bf16[1152,512]{1,0:T(8,128)(2,1)}) custom-call(bf16[1024,512]{1,0:T(8,128)(2,1)} %get-tuple-element.105.mixed_ref, bf16[1024,512]{1,0:T(8,128)(2,1)} %get-tuple-element.108.branch_ref, bf16[1024,512]{1,0:T(8,128)(2,1)} %get-tuple-element.115.normed_ref, bf16[1024,2048]{1,0:T(8,128)(2,1)} %get-tuple-element.116.gpre_ref), custom_call_target="tpu_custom_call" | custom-call | flops 60000000 | bytes 1048576 | tf_op jit(solution)/shard_map/in_grads/pallas_call | solution.py:866
  74.2 2.5 %collective-permute-done.7 = bf16[1152,512]{1,0:T(8,128)(2,1)S(1)} collective-permute-done((bf16[1152,512]{1,0:T(8,128)(2,1)}, bf16[1152,512]{1,0:T(8,128)(2,1)S(1)}, u32[]{:S(2)}, u32[]{:S(2)}) %collective-permute-start.7) | collective-permute-done | bytes 1179680 | tf_op jit(solution)/shard_map/ppermute | solution.py:734
  76.8 2.1 add_convert_fusion
  78.8 1.1 add_convert_fusion.1
  80.0 2.8 %collective-permute-start.8 = (bf16[576,512]{1,0:T(8,128)(2,1)}, bf16[576,512]{1,0:T(8,128)(2,1)}, u32[]{:S(2)}, u32[]{:S(2)}) collective-permute-start(bf16[576,512]{1,0:T(8,128)(2,1)} %add_convert_fusion.1), channel_id=1, source_target_pairs={{0,2},{2,0},{4,6},{6,4},{8,10},{10,8},{12,14},{14,12},{16,18},{18,... | collective-permute-start | bytes 1769480 | tf_op jit(solution)/shard_map/ppermute | solution.py:626
  82.8 1.5 collective-permute-start.9
  84.3 14.7 %mixer_backward.3 = (bf16[512,512]{1,0:T(8,128)(2,1)}, bf16[512,512]{1,0:T(8,128)(2,1)}, bf16[512,512]{1,0:T(8,128)(2,1)}, f32[32,1024]{1,0:T(8,128)}, f32[4,256...) custom-call(s32[7]{0:T(128)} %add_subtract_fusion.ends_ref, ...), custom_call_target="tpu_custom_call" | custom-call | flops 120000000 | bytes 1048576 | tf_op jit(solution)/shard_map/mixer_backward/pallas_call | solution.py:890
  99.0 2.2 %add_convert_fusion.2 = (bf16[288,512]{1,0:T(8,128)(2,1)}, bf16[288,512]{1,0:T(8,128)(2,1)}) fusion(bf16[576,512]{1,0:T(8,128)(2,1)} %collective-permute-done.9, s32[]{:T(128)S(6)} %select_n.342, bf16[1152,512]{1,0:T(8,128)(2,1)S(1)} %collective-permute-done.7, s32[]{:T(128)S(6)} %select_n.341, bf16[1152,512]{1,0:T(8,128)(2,1)S(1)} %copy-done.4, ...), kind=kLoop, calls=%fused_computation.4 | loop fusion | flops 1769472 | bytes 2359312 | tf_op jit(solution)/shard_map/convert_element_type | solution.py:673
  101.3 0.7 collective-permute-start.10
  101.9 0.5 collective-permute-start.11
  102.5 8.9 %mixer_backward.4 = (bf16[256,512]{1,0:T(8,128)(2,1)}, bf16[256,512]{1,0:T(8,128)(2,1)}, bf16[256,512]{1,0:T(8,128)(2,1)}, f32[32,1024]{1,0:T(8,128)}, f32[4,256...) custom-call(s32[7]{0:T(128)} %add_subtract_fusion.ends_ref, ...), custom_call_target="tpu_custom_call" | custom-call | flops 60000000 | bytes 1048576 | tf_op jit(solution)/shard_map/mixer_backward/pallas_call | solution.py:890
  111.4 1.1 add_convert_fusion.7
  112.6 1.1 add_convert_fusion.6
  113.6 0.7 pad_maximum_fusion.2
  114.4 1.6 collective-permute-start.12
  116.0 9.1 %mixer_backward.5 = (bf16[256,512]{1,0:T(8,128)(2,1)}, bf16[256,512]{1,0:T(8,128)(2,1)}, bf16[256,512]{1,0:T(8,128)(2,1)}, f32[32,1024]{1,0:T(8,128)}, f32[4,256...) custom-call(s32[7]{0:T(128)} %add_subtract_fusion.ends_ref, ...), custom_call_target="tpu_custom_call" | custom-call | flops 60000000 | bytes 1048576 | tf_op jit(solution)/shard_map/mixer_backward/pallas_call | solution.py:890
  125.1 1.3 add_convert_fusion.19
  126.5 2.6 %collective-permute-start.14 = (bf16[144,512]{1,0:T(8,128)(2,1)S(1)}, bf16[144,512]{1,0:T(8,128)(2,1)}, u32[]{:S(2)}, u32[]{:S(2)}) collective-permute-start(bf16[144,512]{1,0:T(8,128)(2,1)S(1)} %pad_maximum_fusion.10), channel_id=1, source_target_pairs={{0,16},{2,18},{4,20},{6,22},{8,24},{10,26},{12,28},{14,30},{16,0},... | collective-permute-start | bytes 442376 | tf_op jit(solution)/shard_map/ppermute | solution.py:626
  129.2 0.7 copy-done.19
  129.9 9.9 %finish.1 = (bf16[1024,1536]{1,0:T(8,128)(2,1)}, bf16[1600,256]{1,0:T(8,128)(2,1)}, bf16[1600,256]{1,0:T(8,128)(2,1)}) custom-call(s32[7]{0:T(128)} %add_subtract_fusion.ends_ref, s32[1]{0:T(128)} %bitcast.5.flag_ref, bf16[1024,768]{1,0:T(8,128)(2,1)} %get-tuple-element.101.own_ref, bf16[1024,768]{1,0:T(8,128)(2,1)} %get-tuple-element.103.other_ref, ...), custom_call_target="tpu_custom_call" | custom-call | flops 80000000 | bytes 1048576 | tf_op jit(solution)/shard_map/finish/pallas_call | solution.py:929
  140.0 1.4 add_convert_fusion.17
  141.4 0.6 copy-done.11
  142.5 1.2 fusion.1
  143.8 1.4 collective-permute-start.18
  145.3 1.5 collective-permute-start.16
  146.8 1.3 collective-permute-start.17
  148.1 6.4 %input_grad.1 = bf16[1024,512]{1,0:T(8,128)(2,1)} custom-call(bf16[1024,1536]{1,0:T(8,128)(2,1)} %get-tuple-element.167.gproj_ref, bf16[1024,512]{1,0:T(8,128)(2,1)} %x_ref.5, f32[1024,512]{1,0:T(8,128)} %get-tuple-element.168.ghid_ref, f32[1,512]{1,0:T(1,128)} %bitcast.23, bf16[3,512,256]{2,1,0:T(8,128)(2,1)} %bitcast.20, bf16[3,512,256]{2,1,0:T(8,128)(2,1)} %copy-done), custom_call_target="tpu_custom_call" | custom-call | flops 70000000 | bytes 1048576 | tf_op jit(solution)/shard_map/input_grad/pallas_call | solution.py:955
  154.8 0.8 collective-permute-start.20
  156.0 0.9 collective-permute-start.21
  156.9 2.7 %collective-permute-done.20 = bf16[200,256]{1,0:T(8,128)(2,1)S(1)} collective-permute-done((bf16[200,256]{1,0:T(8,128)(2,1)S(1)}, bf16[200,256]{1,0:T(8,128)(2,1)S(1)}, u32[]{:S(2)}, u32[]{:S(2)}) %collective-permute-start.20) | collective-permute-done | bytes 102432 | tf_op jit(solution)/shard_map/ppermute | solution.py:626
  159.6 1.1 collective-permute-done.21
  160.7 3.3 %collective-permute-done.19 = bf16[288,512]{1,0:T(8,128)(2,1)S(1)} collective-permute-done((bf16[288,512]{1,0:T(8,128)(2,1)S(1)}, bf16[288,512]{1,0:T(8,128)(2,1)S(1)}, u32[]{:S(2)}, u32[]{:S(2)}) %collective-permute-start.19) | collective-permute-done | bytes 294944 | tf_op jit(solution)/shard_map/ppermute | solution.py:626
  164.6 1.5 collective-permute-start.24
  166.0 0.7 collective-permute-start.22
  166.7 3.3 %collective-permute-done.23 = bf16[400,256]{1,0:T(8,128)(2,1)S(1)} collective-permute-done((bf16[400,256]{1,0:T(8,128)(2,1)S(1)}, bf16[400,256]{1,0:T(8,128)(2,1)S(1)}, u32[]{:S(2)}, u32[]{:S(2)}) %collective-permute-start.23) | collective-permute-done | bytes 204832 | tf_op jit(solution)/shard_map/ppermute | solution.py:626
  170.1 2.0 collective-permute-done.24
  172.3 1.3 collective-permute-done.22
  174.7 1.4 collective-permute-start.27
  176.2 8.1 %collective-permute-done.27 = bf16[400,256]{1,0:T(8,128)(2,1)S(1)} collective-permute-done((bf16[400,256]{1,0:T(8,128)(2,1)S(1)}, bf16[400,256]{1,0:T(8,128)(2,1)S(1)}, u32[]{:S(2)}, u32[]{:S(2)}) %collective-permute-start.27) | collective-permute-done | bytes 204832 | tf_op jit(solution)/shard_map/ppermute | solution.py:626
  184.3 2.5 %collective-permute-done.25.out_got_ref = bf16[576,512]{1,0:T(8,128)(2,1)S(1)} collective-permute-done((bf16[576,512]{1,0:T(8,128)(2,1)S(1)}, bf16[576,512]{1,0:T(8,128)(2,1)S(1)}, u32[]{:S(2)}, u32[]{:S(2)}) %collective-permute-start.25) | collective-permute-done | bytes 589856 | tf_op jit(solution)/shard_map/ppermute | solution.py:626
  187.2 1.4 collective-permute-start.30
  188.8 4.0 %collective-permute-done.30 = bf16[200,256]{1,0:T(8,128)(2,1)S(1)} collective-permute-done((bf16[200,256]{1,0:T(8,128)(2,1)S(1)}, bf16[200,256]{1,0:T(8,128)(2,1)S(1)}, u32[]{:S(2)}, u32[]{:S(2)}) %collective-permute-start.30) | collective-permute-done | bytes 102432 | tf_op jit(solution)/shard_map/ppermute | solution.py:626
  192.9 0.8 collective-permute-done.28
  193.8 1.1 collective-permute-start.29
  194.9 0.6 pad_add_fusion.bits_ref
  195.4 3.8 %feed_output.1 = (f32[1024,512]{1,0:T(8,128)}, f32[256,512]{1,0:T(8,128)}, f32[512,1024]{1,0:T(8,128)}) custom-call(s32[2]{0:T(128)} %pad_add_fusion.bits_ref, bf16[576,512]{1,0:T(8,128)(2,1)} %copy-done.2, bf16[576,512]{1,0:T(8,128)(2,1)} %copy-done.15, bf16[576,512]{1,0:T(8,128)(2,1)} %copy-done.1, bf16[576,512]{1,0:T(8,128)(2,1)} %copy-done.16), custom_call_target="tpu_custom_call" | custom-call | flops 30000000 | bytes 1048576 | tf_op jit(solution)/shard_map/feed_output/pallas_call | solution.py:1005
  200.0 0.7 copy-done.21
  200.6 2.5 %qkv_output.1 = (f32[1536,256]{1,0:T(8,128)}, f32[8,256]{1,0:T(8,128)}) custom-call(s32[2]{0:T(128)} %pad_add_fusion.bits_ref, bf16[400,256]{1,0:T(8,128)(2,1)} %copy-done.10, bf16[400,256]{1,0:T(8,128)(2,1)} %copy-done.21, bf16[400,256]{1,0:T(8,128)(2,1)} %copy-done.9, bf16[400,256]{1,0:T(8,128)(2,1)} %copy-done.20), custom_call_target="tpu_custom_call" | custom-call | flops 30000000 | bytes 1048576 | tf_op jit(solution)/shard_map/qkv_output/pallas_call | solution.py:1021
  203.2 0.8 fusion.2
  204.1 0.6 copy.19
  204.6 0.6 copy.20
  205.2 0.6 reduce_sum.9
  (107 shorter events, 8.1 us)
Async XLA Ops:
  0.6 36.8 %collective-permute-start.4 = (bf16[512,1024]{1,0:T(8,128)(2,1)}, bf16[512,1024]{1,0:T(8,128)(2,1)S(1)}, u32[]{:S(2)}, u32[]{:S(2)}) collective-permute-start(bf16[512,1024]{1,0:T(8,128)(2,1)} %wi_own_ref.1), channel_id=1, source_target_pairs={{0,1},{1,0},{2,3},{3,2},{4,5},{5,4},{6,7},{7,6},{8,9},{9,8},{10,11... | collective-permute-start | bytes 3145736 | tf_op jit(solution)/shard_map/ppermute | solution.py:734
  1.2 36.3 %collective-permute-start.5 = (bf16[1024,512]{1,0:T(8,128)(2,1)}, bf16[1024,512]{1,0:T(8,128)(2,1)S(1)}, u32[]{:S(2)}, u32[]{:S(2)}) collective-permute-start(bf16[1024,512]{1,0:T(8,128)(2,1)} %wo_own_ref.1), channel_id=1, source_target_pairs={{0,1},{1,0},{2,3},{3,2},{4,5},{5,4},{6,7},{7,6},{8,9},{9,8},{10,11... | collective-permute-start | bytes 3145736 | tf_op jit(solution)/shard_map/ppermute | solution.py:734
  1.2 6.5 %collective-permute-start = (bf16[3,512,256]{2,1,0:T(8,128)(2,1)}, bf16[3,512,256]{2,1,0:T(8,128)(2,1)S(1)}, u32[]{:S(2)}, u32[]{:S(2)}) collective-permute-start(bf16[3,512,256]{2,1,0:T(8,128)(2,1)} %bitcast.17), channel_id=1, source_target_pairs={{0,1},{1,0},{2,3},{3,2},{4,5},{5,4},{6,7},{7,6},{8,9},{9,8},{10,11... | collective-permute-start | bytes 2359304 | tf_op jit(solution)/shard_map/ppermute | solution.py:734
  1.7 35.8 %collective-permute-start.3 = (bf16[256,512]{1,0:T(8,128)(2,1)}, bf16[256,512]{1,0:T(8,128)(2,1)S(1)}, u32[]{:S(2)}, u32[]{:S(2)}) collective-permute-start(bf16[256,512]{1,0:T(8,128)(2,1)} %wa_own_ref.1), channel_id=1, source_target_pairs={{0,1},{1,0},{2,3},{3,2},{4,5},{5,4},{6,7},{7,6},{8,9},{9,8},{10,11... | collective-permute-start | bytes 786440 | tf_op jit(solution)/shard_map/ppermute | solution.py:734
  7.7 0.9 copy-start
  8.6 5.3 %copy-start.22 = (f32[2,4]{1,0:T(2,128)S(1)}, f32[2,4]{1,0:T(2,128)}, u32[]{:S(2)}) copy-start(f32[2,4]{1,0:T(2,128)} %param.18) | copy-start | bytes 100
  13.5 2.4 %collective-permute-start.1 = (bf16[832,128]{1,0:T(8,128)(2,1)}, bf16[832,128]{1,0:T(8,128)(2,1)S(1)}, u32[]{:S(2)}, u32[]{:S(2)}) collective-permute-start(bf16[832,128]{1,0:T(8,128)(2,1)} %get-tuple-element.104), channel_id=1, source_target_pairs={{0,1},{1,0},{2,3},{3,2},{4,5},{5,4},{6,7},{7,6},{8,9},{9,8},{10,11... | collective-permute-start | bytes 638984 | tf_op jit(solution)/shard_map/ppermute | solution.py:734
  13.9 1.1 collective-permute-start.2
  15.9 0.7 copy-start.18
  37.5 0.7 copy-start.17
  37.5 1.1 copy-start.6
  37.5 1.4 copy-start.7
  73.7 5.1 %copy-start.3 = (bf16[1152,512]{1,0:T(8,128)(2,1)S(1)}, bf16[1152,512]{1,0:T(8,128)(2,1)}, u32[]{:S(2)}) copy-start(bf16[1152,512]{1,0:T(8,128)(2,1)} %get-tuple-element.110) | copy-start | bytes 3538948
  73.7 3.1 %collective-permute-start.7 = (bf16[1152,512]{1,0:T(8,128)(2,1)}, bf16[1152,512]{1,0:T(8,128)(2,1)S(1)}, u32[]{:S(2)}, u32[]{:S(2)}) collective-permute-start(bf16[1152,512]{1,0:T(8,128)(2,1)} %get-tuple-element.118), channel_id=1, source_target_pairs={{0,1},{1,0},{2,3},{3,2},{4,5},{5,4},{6,7},{7,6},{8,9},{9,8},{10,11... | collective-permute-start | bytes 3538952 | tf_op jit(solution)/shard_map/ppermute | solution.py:734
  74.0 4.8 %collective-permute-start.6 = (bf16[1152,512]{1,0:T(8,128)(2,1)}, bf16[1152,512]{1,0:T(8,128)(2,1)S(1)}, u32[]{:S(2)}, u32[]{:S(2)}) collective-permute-start(bf16[1152,512]{1,0:T(8,128)(2,1)} %get-tuple-element.114), channel_id=1, source_target_pairs={{0,1},{1,0},{2,3},{3,2},{4,5},{5,4},{6,7},{7,6},{8,9},{9,8},{10,11... | collective-permute-start | bytes 3538952 | tf_op jit(solution)/shard_map/ppermute | solution.py:734
  78.8 5.4 %copy-start.5 = (bf16[1152,512]{1,0:T(8,128)(2,1)}, bf16[1152,512]{1,0:T(8,128)(2,1)S(1)}, u32[]{:S(2)}) copy-start(bf16[1152,512]{1,0:T(8,128)(2,1)S(1)} %collective-permute-done.6) | copy-start | bytes 3538948
  80.0 19.1 %collective-permute-start.8 = (bf16[576,512]{1,0:T(8,128)(2,1)}, bf16[576,512]{1,0:T(8,128)(2,1)}, u32[]{:S(2)}, u32[]{:S(2)}) collective-permute-start(bf16[576,512]{1,0:T(8,128)(2,1)} %add_convert_fusion.1), channel_id=1, source_target_pairs={{0,2},{2,0},{4,6},{6,4},{8,10},{10,8},{12,14},{14,12},{16,18},{18,... | collective-permute-start | bytes 1769480 | tf_op jit(solution)/shard_map/ppermute | solution.py:626
  82.8 16.3 %collective-permute-start.9 = (bf16[576,512]{1,0:T(8,128)(2,1)}, bf16[576,512]{1,0:T(8,128)(2,1)}, u32[]{:S(2)}, u32[]{:S(2)}) collective-permute-start(bf16[576,512]{1,0:T(8,128)(2,1)} %add_convert_fusion), channel_id=1, source_target_pairs={{0,4},{2,6},{4,0},{6,2},{8,12},{10,14},{12,8},{14,10},{16,20},{18,... | collective-permute-start | bytes 1769480 | tf_op jit(solution)/shard_map/ppermute | solution.py:626
  84.3 14.8 %copy-start.4 = (bf16[1152,512]{1,0:T(8,128)(2,1)S(1)}, bf16[1152,512]{1,0:T(8,128)(2,1)}, u32[]{:S(2)}) copy-start(bf16[1152,512]{1,0:T(8,128)(2,1)} %get-tuple-element.117) | copy-start | bytes 3538948
  101.3 10.2 %collective-permute-start.10 = (bf16[288,512]{1,0:T(8,128)(2,1)}, bf16[288,512]{1,0:T(8,128)(2,1)}, u32[]{:S(2)}, u32[]{:S(2)}) collective-permute-start(bf16[288,512]{1,0:T(8,128)(2,1)} %get-tuple-element.129), channel_id=1, source_target_pairs={{0,4},{2,6},{4,0},{6,2},{8,12},{10,14},{12,8},{14,10},{16,20},{18,... | collective-permute-start | bytes 884744 | tf_op jit(solution)/shard_map/ppermute | solution.py:626
  101.9 9.5 %collective-permute-start.11 = (bf16[288,512]{1,0:T(8,128)(2,1)}, bf16[288,512]{1,0:T(8,128)(2,1)}, u32[]{:S(2)}, u32[]{:S(2)}) collective-permute-start(bf16[288,512]{1,0:T(8,128)(2,1)} %get-tuple-element.130), channel_id=1, source_target_pairs={{0,2},{2,0},{4,6},{6,4},{8,10},{10,8},{12,14},{14,12},{16,18},{18,... | collective-permute-start | bytes 884744 | tf_op jit(solution)/shard_map/ppermute | solution.py:626
  114.4 10.7 %collective-permute-start.12 = (bf16[288,512]{1,0:T(8,128)(2,1)}, bf16[288,512]{1,0:T(8,128)(2,1)}, u32[]{:S(2)}, u32[]{:S(2)}) collective-permute-start(bf16[288,512]{1,0:T(8,128)(2,1)} %pad_maximum_fusion.2), channel_id=1, source_target_pairs={{0,8},{2,10},{4,12},{6,14},{8,0},{10,2},{12,4},{14,6},{16,24},{18,... | collective-permute-start | bytes 884744 | tf_op jit(solution)/shard_map/ppermute | solution.py:626
  125.1 1.3 copy-start.23
  126.4 2.7 %collective-permute-start.13 = (bf16[832,128]{1,0:T(8,128)(2,1)S(1)}, bf16[832,128]{1,0:T(8,128)(2,1)S(1)}, u32[]{:S(2)}, u32[]{:S(2)}) collective-permute-start(bf16[832,128]{1,0:T(8,128)(2,1)S(1)} %copy-done.23), channel_id=1, source_target_pairs={{0,1},{1,0},{2,3},{3,2},{4,5},{5,4},{6,7},{7,6},{8,9},{9,8},{10,11... | collective-permute-start | bytes 638984 | tf_op jit(solution)/shard_map/ppermute | solution.py:734
  126.5 13.2 %collective-permute-start.14 = (bf16[144,512]{1,0:T(8,128)(2,1)S(1)}, bf16[144,512]{1,0:T(8,128)(2,1)}, u32[]{:S(2)}, u32[]{:S(2)}) collective-permute-start(bf16[144,512]{1,0:T(8,128)(2,1)S(1)} %pad_maximum_fusion.10), channel_id=1, source_target_pairs={{0,16},{2,18},{4,20},{6,22},{8,24},{10,26},{12,28},{14,30},{16,0},... | collective-permute-start | bytes 442376 | tf_op jit(solution)/shard_map/ppermute | solution.py:626
  129.2 0.7 copy-start.19
  139.8 2.7 %collective-permute-start.15 = (bf16[1600,256]{1,0:T(8,128)(2,1)}, bf16[1600,256]{1,0:T(8,128)(2,1)}, u32[]{:S(2)}, u32[]{:S(2)}) collective-permute-start(bf16[1600,256]{1,0:T(8,128)(2,1)} %get-tuple-element.163), channel_id=1, source_target_pairs={{0,1},{1,0},{2,3},{3,2},{4,5},{5,4},{6,7},{7,6},{8,9},{9,8},{10,11... | collective-permute-start | bytes 2457608 | tf_op jit(solution)/shard_map/ppermute | solution.py:734
  140.0 2.0 copy-start.8
  141.4 0.6 copy-start.11
  141.4 0.6 copy-start.13
  143.8 10.7 %collective-permute-start.18 = (bf16[144,512]{1,0:T(8,128)(2,1)S(1)}, bf16[144,512]{1,0:T(8,128)(2,1)S(1)}, u32[]{:S(2)}, u32[]{:S(2)}) collective-permute-start(bf16[144,512]{1,0:T(8,128)(2,1)S(1)} %pad_maximum_fusion.11), channel_id=1, source_target_pairs={{0,16},{2,18},{4,20},{6,22},{8,24},{10,26},{12,28},{14,30},{16,0},... | collective-permute-start | bytes 442376 | tf_op jit(solution)/shard_map/ppermute | solution.py:626
  145.3 9.4 %collective-permute-start.16 = (bf16[400,256]{1,0:T(8,128)(2,1)S(1)}, bf16[400,256]{1,0:T(8,128)(2,1)S(1)}, u32[]{:S(2)}, u32[]{:S(2)}) collective-permute-start(bf16[400,256]{1,0:T(8,128)(2,1)S(1)} %add_convert_fusion.5), channel_id=1, source_target_pairs={{0,2},{2,0},{4,6},{6,4},{8,10},{10,8},{12,14},{14,12},{16,18},{18,... | collective-permute-start | bytes 614408 | tf_op jit(solution)/shard_map/ppermute | solution.py:626
  146.8 7.9 %collective-permute-start.17 = (bf16[400,256]{1,0:T(8,128)(2,1)S(1)}, bf16[400,256]{1,0:T(8,128)(2,1)S(1)}, u32[]{:S(2)}, u32[]{:S(2)}) collective-permute-start(bf16[400,256]{1,0:T(8,128)(2,1)S(1)} %add_convert_fusion.4), channel_id=1, source_target_pairs={{0,4},{2,6},{4,0},{6,2},{8,12},{10,14},{12,8},{14,10},{16,20},{18,... | collective-permute-start | bytes 614408 | tf_op jit(solution)/shard_map/ppermute | solution.py:626
  148.1 6.5 %copy-start.12 = (bf16[72,512]{1,0:T(8,128)(2,1)S(1)}, bf16[72,512]{1,0:T(8,128)(2,1)}, u32[]{:S(2)}) copy-start(bf16[72,512]{1,0:T(8,128)(2,1)} %copy-done.11) | copy-start | bytes 221188
  148.1 6.5 %copy-start.14 = (bf16[72,512]{1,0:T(8,128)(2,1)S(1)}, bf16[72,512]{1,0:T(8,128)(2,1)}, u32[]{:S(2)}) copy-start(bf16[72,512]{1,0:T(8,128)(2,1)} %copy-done.13) | copy-start | bytes 221188
  154.8 4.7 %collective-permute-start.20 = (bf16[200,256]{1,0:T(8,128)(2,1)S(1)}, bf16[200,256]{1,0:T(8,128)(2,1)S(1)}, u32[]{:S(2)}, u32[]{:S(2)}) collective-permute-start(bf16[200,256]{1,0:T(8,128)(2,1)S(1)} %add_convert_fusion.15), channel_id=1, source_target_pairs={{0,4},{2,6},{4,0},{6,2},{8,12},{10,14},{12,8},{14,10},{16,20},{18,... | collective-permute-start | bytes 307208 | tf_op jit(solution)/shard_map/ppermute | solution.py:626
  155.5 8.5 %collective-permute-start.19 = (bf16[288,512]{1,0:T(8,128)(2,1)S(1)}, bf16[288,512]{1,0:T(8,128)(2,1)S(1)}, u32[]{:S(2)}, u32[]{:S(2)}) collective-permute-start(bf16[288,512]{1,0:T(8,128)(2,1)S(1)} %pad_maximum_fusion.3), channel_id=1, source_target_pairs={{0,8},{2,10},{4,12},{6,14},{8,0},{10,2},{12,4},{14,6},{16,24},{18,... | collective-permute-start | bytes 884744 | tf_op jit(solution)/shard_map/ppermute | solution.py:626
  156.0 4.7 %collective-permute-start.21 = (bf16[200,256]{1,0:T(8,128)(2,1)S(1)}, bf16[200,256]{1,0:T(8,128)(2,1)S(1)}, u32[]{:S(2)}, u32[]{:S(2)}) collective-permute-start(bf16[200,256]{1,0:T(8,128)(2,1)S(1)} %add_convert_fusion.14), channel_id=1, source_target_pairs={{0,2},{2,0},{4,6},{6,4},{8,10},{10,8},{12,14},{14,12},{16,18},{18,... | collective-permute-start | bytes 307208 | tf_op jit(solution)/shard_map/ppermute | solution.py:626
  164.2 5.8 %collective-permute-start.23 = (bf16[400,256]{1,0:T(8,128)(2,1)S(1)}, bf16[400,256]{1,0:T(8,128)(2,1)S(1)}, u32[]{:S(2)}, u32[]{:S(2)}) collective-permute-start(bf16[400,256]{1,0:T(8,128)(2,1)S(1)} %pad_maximum_fusion.6), channel_id=1, source_target_pairs={{0,8},{2,10},{4,12},{6,14},{8,0},{10,2},{12,4},{14,6},{16,24},{18,... | collective-permute-start | bytes 614408 | tf_op jit(solution)/shard_map/ppermute | solution.py:626
  164.6 7.6 %collective-permute-start.24 = (bf16[288,512]{1,0:T(8,128)(2,1)S(1)}, bf16[288,512]{1,0:T(8,128)(2,1)S(1)}, u32[]{:S(2)}, u32[]{:S(2)}) collective-permute-start(bf16[288,512]{1,0:T(8,128)(2,1)S(1)} %pad_maximum_fusion.5), channel_id=1, source_target_pairs={{0,2},{2,0},{4,6},{6,4},{8,10},{10,8},{12,14},{14,12},{16,18},{18,... | collective-permute-start | bytes 884744 | tf_op jit(solution)/shard_map/ppermute | solution.py:626
  166.0 7.5 %collective-permute-start.22 = (bf16[288,512]{1,0:T(8,128)(2,1)S(1)}, bf16[288,512]{1,0:T(8,128)(2,1)S(1)}, u32[]{:S(2)}, u32[]{:S(2)}) collective-permute-start(bf16[288,512]{1,0:T(8,128)(2,1)S(1)} %pad_maximum_fusion.4), channel_id=1, source_target_pairs={{0,4},{2,6},{4,0},{6,2},{8,12},{10,14},{12,8},{14,10},{16,20},{18,... | collective-permute-start | bytes 884744 | tf_op jit(solution)/shard_map/ppermute | solution.py:626
  172.3 2.0 copy-start.1
  173.7 21.7 %copy-start.2 = (bf16[576,512]{1,0:T(8,128)(2,1)}, bf16[576,512]{1,0:T(8,128)(2,1)S(1)}, u32[]{:S(2)}) copy-start(bf16[576,512]{1,0:T(8,128)(2,1)S(1)} %pad_maximum_fusion.out_mine_ref) | copy-start | bytes 1769476
  173.8 13.1 %collective-permute-start.25 = (bf16[576,512]{1,0:T(8,128)(2,1)S(1)}, bf16[576,512]{1,0:T(8,128)(2,1)S(1)}, u32[]{:S(2)}, u32[]{:S(2)}) collective-permute-start(bf16[576,512]{1,0:T(8,128)(2,1)S(1)} %pad_maximum_fusion.out_mine_ref), channel_id=1, source_target_pairs={{0,2},{2,0},{4,6},{6,4},{8,10},{10,8},{12,14},{14,12},{16,18},{18,... | collective-permute-start | bytes 1769480 | tf_op jit(solution)/shard_map/ppermute | solution.py:626
  174.3 12.9 %collective-permute-start.26 = (bf16[576,512]{1,0:T(8,128)(2,1)S(1)}, bf16[576,512]{1,0:T(8,128)(2,1)S(1)}, u32[]{:S(2)}, u32[]{:S(2)}) collective-permute-start(bf16[576,512]{1,0:T(8,128)(2,1)S(1)} %pad_maximum_fusion.1.in_mine_ref), channel_id=1, source_target_pairs={{0,4},{2,6},{4,0},{6,2},{8,12},{10,14},{12,8},{14,10},{16,20},{18,... | collective-permute-start | bytes 1769480 | tf_op jit(solution)/shard_map/ppermute | solution.py:626
  174.7 9.5 %collective-permute-start.27 = (bf16[400,256]{1,0:T(8,128)(2,1)S(1)}, bf16[400,256]{1,0:T(8,128)(2,1)S(1)}, u32[]{:S(2)}, u32[]{:S(2)}) collective-permute-start(bf16[400,256]{1,0:T(8,128)(2,1)S(1)} %pad_maximum_fusion.7), channel_id=1, source_target_pairs={{0,16},{2,18},{4,20},{6,22},{8,24},{10,26},{12,28},{14,30},{16,0},... | collective-permute-start | bytes 614408 | tf_op jit(solution)/shard_map/ppermute | solution.py:626
  186.9 8.6 %copy-start.15 = (bf16[576,512]{1,0:T(8,128)(2,1)}, bf16[576,512]{1,0:T(8,128)(2,1)S(1)}, u32[]{:S(2)}) copy-start(bf16[576,512]{1,0:T(8,128)(2,1)S(1)} %collective-permute-done.25.out_got_ref) | copy-start | bytes 1769476
  187.2 8.2 %copy-start.16 = (bf16[576,512]{1,0:T(8,128)(2,1)}, bf16[576,512]{1,0:T(8,128)(2,1)S(1)}, u32[]{:S(2)}) copy-start(bf16[576,512]{1,0:T(8,128)(2,1)S(1)} %collective-permute-done.26.in_got_ref) | copy-start | bytes 1769476
  187.2 5.6 %collective-permute-start.30 = (bf16[200,256]{1,0:T(8,128)(2,1)S(1)}, bf16[200,256]{1,0:T(8,128)(2,1)S(1)}, u32[]{:S(2)}, u32[]{:S(2)}) collective-permute-start(bf16[200,256]{1,0:T(8,128)(2,1)S(1)} %get-tuple-element.183), channel_id=1, source_target_pairs={{0,2},{2,0},{4,6},{6,4},{8,10},{10,8},{12,14},{14,12},{16,18},{18,... | collective-permute-start | bytes 307208 | tf_op jit(solution)/shard_map/ppermute | solution.py:626
  188.6 5.1 %collective-permute-start.28 = (bf16[200,256]{1,0:T(8,128)(2,1)S(1)}, bf16[200,256]{1,0:T(8,128)(2,1)S(1)}, u32[]{:S(2)}, u32[]{:S(2)}) collective-permute-start(bf16[200,256]{1,0:T(8,128)(2,1)S(1)} %get-tuple-element.182), channel_id=1, source_target_pairs={{0,4},{2,6},{4,0},{6,2},{8,12},{10,14},{12,8},{14,10},{16,20},{18,... | collective-permute-start | bytes 307208 | tf_op jit(solution)/shard_map/ppermute | solution.py:626
  192.9 6.4 %copy-start.9 = (bf16[400,256]{1,0:T(8,128)(2,1)}, bf16[400,256]{1,0:T(8,128)(2,1)S(1)}, u32[]{:S(2)}) copy-start(bf16[400,256]{1,0:T(8,128)(2,1)S(1)} %pad_maximum_fusion.9.b_mine_ref) | copy-start | bytes 614404
  192.9 6.4 %collective-permute-start.31 = (bf16[400,256]{1,0:T(8,128)(2,1)S(1)}, bf16[400,256]{1,0:T(8,128)(2,1)S(1)}, u32[]{:S(2)}, u32[]{:S(2)}) collective-permute-start(bf16[400,256]{1,0:T(8,128)(2,1)S(1)} %pad_maximum_fusion.9.b_mine_ref), channel_id=1, source_target_pairs={{0,4},{2,6},{4,0},{6,2},{8,12},{10,14},{12,8},{14,10},{16,20},{18,... | collective-permute-start | bytes 614408 | tf_op jit(solution)/shard_map/ppermute | solution.py:626
  193.7 5.5 %copy-start.10 = (bf16[400,256]{1,0:T(8,128)(2,1)}, bf16[400,256]{1,0:T(8,128)(2,1)S(1)}, u32[]{:S(2)}) copy-start(bf16[400,256]{1,0:T(8,128)(2,1)S(1)} %pad_maximum_fusion.8.a_mine_ref) | copy-start | bytes 614404
  193.8 5.8 %collective-permute-start.29 = (bf16[400,256]{1,0:T(8,128)(2,1)S(1)}, bf16[400,256]{1,0:T(8,128)(2,1)S(1)}, u32[]{:S(2)}, u32[]{:S(2)}) collective-permute-start(bf16[400,256]{1,0:T(8,128)(2,1)S(1)} %pad_maximum_fusion.8.a_mine_ref), channel_id=1, source_target_pairs={{0,2},{2,0},{4,6},{6,4},{8,10},{10,8},{12,14},{14,12},{16,18},{18,... | collective-permute-start | bytes 614408 | tf_op jit(solution)/shard_map/ppermute | solution.py:626
  199.3 0.7 copy-start.20
  200.0 0.7 copy-start.21

commit v3 on v2

v3 whole, which is shorter than its diff:
```python
from functools import partial

import jax
import jax.numpy as jnp
from jax import lax
from jax.experimental import pallas as pl
from jax.experimental.pallas import tpu as pltpu
from jax.sharding import PartitionSpec as P

BAND = 30
HALO = 32
EXTRA = 64
BLOCK = 128
EPS = 1e-06
BF = jnp.bfloat16
F32 = jnp.float32
GELU_A = 0.7978845608028654
GELU_B = 0.044715


def nn(left, right):
    return lax.dot_general(left, right, (((1,), (0,)), ((), ())), preferred_element_type=F32)


def nt(left, right):
    return lax.dot_general(left, right, (((1,), (1,)), ((), ())), preferred_element_type=F32)


def tn(left, right):
    return lax.dot_general(left, right, (((0,), (0,)), ((), ())), preferred_element_type=F32)


def iota(shape, dim):
    return lax.broadcasted_iota(jnp.int32, shape, dim)


def whole(shape):
    return pl.BlockSpec(shape, lambda *_: (0,) * len(shape))


def params(mebibytes):
    return pltpu.CompilerParams(vmem_limit_bytes=mebibytes << 20)


def cost(micros):
    return pl.CostEstimate(flops=int(micros * 1e7), bytes_accessed=1 << 20, transcendentals=0)


def tie(*values):
    return lax.optimization_barrier(values)


def document_ends(lengths_ref, rows):
    end = -lax.axis_index("tensor") * rows
    ends = [end]
    for doc in range(lengths_ref.shape[1]):
        end = end + lengths_ref[0, doc]
        ends.append(end)
    return ends[1:] + ends[:1]


def starts_of(ends, places):
    start = jnp.full(places.shape, ends[-1], jnp.int32)
    for end in ends[:-1]:
        start = jnp.where(places >= end, jnp.maximum(start, end), start)
    return start


def start_at(ends, place):
    start = ends[-1]
    for end in ends[:-1]:
        start = jnp.where(place >= end, jnp.maximum(start, end), start)
    return start


def norm_project_kernel(x_ref, gain_ref, w_ref, normed_ref, out_ref):
    x = x_ref[...].astype(F32)
    r = lax.rsqrt(jnp.mean(x * x, axis=1, keepdims=True) + EPS)
    normed = (x * r * gain_ref[...]).astype(BF)
    normed_ref[...] = normed
    project(normed, w_ref, out_ref)


def project(normed, w_ref, out_ref):
    cols = w_ref.shape[2]
    for kind in range(3):
        out_ref[:, cols * kind : cols * kind + cols] = nn(normed, w_ref[kind]).astype(BF)


PACKET = 4 * (128 + 16) + 8 * HALO


def pack(packet_ref, pair, state, total):
    base = 144 * pair
    packet_ref[base : base + 64] = (state[:64] + state[64:128]).astype(BF)
    packet_ref[base + 64 : base + 128] = (state[128:192] + state[192:]).astype(BF)
    packet_ref[base + 128 : base + 144] = jnp.broadcast_to(total, (16, 128)).astype(BF)


def pack_halo(packet_ref, kind, pair, rows):
    base = 576 + HALO * (4 * kind + pair)
    packet_ref[base : base + HALO] = rows


def unpack(packet_ref, pair, diag):
    base = 144 * pair
    one = packet_ref[base : base + 64].astype(F32)
    two = packet_ref[base + 64 : base + 128].astype(F32)
    state = jnp.where(diag, jnp.concatenate([one, one, two, two], axis=0), 0.0)
    return state, packet_ref[base + 128 : base + 136].astype(F32)


def unpack_halo(packet_ref, kind, pair):
    base = 576 + HALO * (4 * kind + pair)
    return packet_ref[base : base + HALO]


def first_feature(values):
    return jnp.where(values > 0, values + 1.0, jnp.exp(jnp.minimum(values, 0.0))).astype(BF)


def second_feature(values):
    return jnp.tanh(values).astype(BF)


def pair_diag(rows, cols):
    row = iota((rows, cols), 0)
    col = iota((rows, cols), 1)
    return ((row // 64) % 2) == ((col // 64) % 2)


def project_state_kernel(lengths_ref, normed_ref, w_ref, own_ref, out_ref, packet_ref):
    rows = normed_ref.shape[0]
    project(normed_ref[...], w_ref, out_ref)
    member_from = start_at(document_ends(lengths_ref, rows), rows - 1)
    member = iota((rows, 1), 0) >= member_from
    diag = pair_diag(256, 128)
    for pair in range(4):
        src = own_ref if pair < 2 else out_ref
        col = 128 * (pair % 2)
        slot = (pair + 2) % 4
        keys = src[:, 256 + col : 384 + col]
        values = src[:, 512 + col : 640 + col]
        wide = jnp.where(member, keys.astype(F32), 0.0)
        one = jnp.where(member, first_feature(wide).astype(F32), 0.0)
        two = second_feature(wide)
        features = jnp.concatenate([one.astype(BF), two], axis=1)
        state = jnp.where(diag, tn(features, values), 0.0)
        pack(packet_ref, slot, state, jnp.sum(one, axis=0, keepdims=True))
        pack_halo(packet_ref, 0, slot, keys[rows - HALO :])
        pack_halo(packet_ref, 1, slot, values[rows - HALO :])


def block_masks(ends, first):
    row_places = first + iota((1, 256), 1) % BLOCK
    start_row = starts_of(ends, row_places)
    window_places = first - HALO + iota((BLOCK + HALO, 256), 0)
    banded = (window_places <= row_places) & (
        window_places >= jnp.maximum(start_row, row_places - (BAND - 1))
    )
    key_places = first + iota((BLOCK, 256), 0)
    causal = (key_places <= row_places) & (key_places >= start_row)
    col_places = first + iota((BLOCK, 1), 0)
    start_col = starts_of(ends, col_places)
    key_lane = first + iota((BLOCK, BLOCK), 1)
    causal_q = ((key_lane <= col_places) & (key_lane >= start_col)).astype(F32).astype(BF)
    count = (col_places - start_col + 1).astype(F32)
    carried = start_col < first
    member_from = start_at(ends, first + BLOCK - 1)
    member = col_places >= member_from
    keep = member_from < first
    return banded, causal, causal_q, count, carried, member, keep


def stack_heads(values):
    lane = iota(values.shape, 1) % 128
    zero = jnp.zeros_like(values)
    return jnp.concatenate(
        [jnp.where(lane < 64, values, zero), jnp.where(lane >= 64, values, zero)], axis=0
    )


def pick_heads(values):
    half = values.shape[0] // 2
    lane = iota((half, values.shape[1]), 1) % 128
    return jnp.where(lane < 64, values[:half], values[half:])


def ones_diagonal():
    return pair_diag(128, 128).astype(F32).astype(BF)


def only(mask, values):
    return jnp.where(mask, values, jnp.zeros_like(values))


def each(function, *lists):
    return [function(*values) for values in zip(*lists)]


class Front:
    def __init__(self, qs, ks, prev_ks, blends, carries, masks, ones_diag):
        banded, causal, causal_q, count, carried, member, keep = masks
        self.q_stack = each(lambda q: stack_heads(q * 0.125), qs)
        self.window = each(lambda prev, k: jnp.concatenate([prev, k], axis=0), prev_ks, ks)
        scores = each(nt, self.window, self.q_stack)
        self.k_one = each(lambda k: first_feature(k.astype(F32)), ks)
        products = each(lambda k_one: nn(causal_q, k_one), self.k_one)
        self.q_one = each(lambda q: first_feature(q.astype(F32)), qs)
        self.sums = each(lambda product, carry: product + jnp.where(carried, carry, 0.0), products, carries)
        self.total = each(
            lambda q_one, sums: nn((q_one.astype(F32) * sums).astype(BF), ones_diag), self.q_one, self.sums
        )
        self.q_two = each(lambda q: second_feature(q.astype(F32)), qs)
        self.k_both = each(
            lambda k_one, k: jnp.concatenate([k_one, second_feature(k.astype(F32))], axis=1), self.k_one, ks
        )
        scores = each(lambda score: jnp.where(banded, score, -1e30), scores)
        raised = each(lambda score: jnp.exp(score - jnp.max(score, axis=0, keepdims=True)), scores)
        self.near = each(lambda r: r * (1.0 / jnp.sum(r, axis=0, keepdims=True)), raised)
        inverse = 1.0 / count
        self.ratio_one = each(lambda blend, total: blend[0] / total, blends, self.total)
        self.ratio_two = each(lambda blend: blend[1] * inverse, blends)
        self.q_scaled = each(
            lambda q_one, q_two, one, two: jnp.concatenate(
                [(q_one.astype(F32) * one).astype(BF), (q_two.astype(F32) * two).astype(BF)], axis=1
            ),
            self.q_one,
            self.q_two,
            self.ratio_one,
            self.ratio_two,
        )
        self.s_stack = each(stack_heads, self.q_scaled)
        far = each(nt, self.k_both, self.s_stack)
        self.weights = each(
            lambda near, far: jnp.concatenate(
                [near[:HALO].astype(BF), (near[HALO:] + jnp.where(causal, far, 0.0)).astype(BF)], axis=0
            ),
            self.near,
            far,
        )


PAIRS = range(4)


def pair_lanes(pair):
    return slice(128 * pair, 128 * pair + 128)


def value_lanes(pair):
    return slice(512 + 128 * pair, 640 + 128 * pair)


def heads_of(own_ref, other_ref, kind):
    first = own_ref.shape[1] // 3 * kind
    return [
        (own_ref if pair < 2 else other_ref)[:, first + 128 * (pair % 2) : first + 128 * (pair % 2) + 128]
        for pair in PAIRS
    ]


def pair_blends(own_ref, other_ref):
    first_head = iota((1, 128), 1) < 64
    rows = []
    for pair in PAIRS:
        ref = own_ref if pair < 2 else other_ref
        head = 2 * (pair % 2)
        rows.append([jnp.where(first_head, ref[kind, head], ref[kind, head + 1]) for kind in range(2)])
    return rows


def mixer_forward_block(
    index,
    total_rows,
    lengths_ref,
    own_ref,
    other_ref,
    packet_ref,
    blend_own_ref,
    blend_other_ref,
    state_out_ref,
    prev_out_ref,
    near_ref,
    weights_ref,
    features_ref,
    sums_ref,
    total_ref,
    state_ref,
    sum_ref,
    prev_ref,
):
    first = index * BLOCK

    @pl.when(index == 0)
    def _():
        for pair in PAIRS:
            state_ref[pair], sum_ref[pair] = unpack(packet_ref, pair, pair_diag(256, 128))
            prev_ref[:, pair_lanes(pair)] = unpack_halo(packet_ref, 0, pair)
            prev_ref[:, value_lanes(pair)] = unpack_halo(packet_ref, 1, pair)

    masks = block_masks(document_ends(lengths_ref, total_rows), first)
    banded, causal, causal_q, count, carried, member, keep = masks
    diag = pair_diag(256, 128)
    qs, ks, vs = [heads_of(own_ref, other_ref, kind) for kind in range(3)]
    prev = prev_ref[...]
    states = [state_ref[pair] for pair in PAIRS]
    sums_in = [sum_ref[pair] for pair in PAIRS]
    blends = pair_blends(blend_own_ref, blend_other_ref)
    front = Front(
        qs,
        ks,
        [prev[:, pair_lanes(pair)] for pair in PAIRS],
        blends,
        [total[0:1] for total in sums_in],
        masks,
        ones_diagonal(),
    )
    state_low = each(lambda state: state.astype(BF), states)
    inter = each(lambda q, state: nn(only(carried, q), state), front.q_scaled, state_low)
    added = each(lambda k, v: tn(only(member, k), v), front.k_both, vs)
    outs = [
        tn(front.weights[pair], jnp.concatenate([prev[:, value_lanes(pair)], vs[pair]], axis=0))
        for pair in PAIRS
    ]
    outs = each(lambda out, term: pick_heads(out) + term, outs, inter)
    for pair in PAIRS:
        state_out_ref[0, pair] = state_low[pair]
        near_ref[0, pair] = front.near[pair].astype(BF)
        weights_ref[0, pair] = front.weights[pair][HALO:]
        features_ref[0, pair, 0] = front.q_scaled[pair]
        features_ref[0, pair, 1] = front.k_both[pair]
        sums_ref[:, pair_lanes(pair)] = front.sums[pair]
        total_ref[:, pair_lanes(pair)] = 1.0 / front.total[pair]
        state_ref[pair] = jnp.where(keep, states[pair], 0.0) + jnp.where(diag, added[pair], 0.0)
        sum_ref[pair] = jnp.broadcast_to(front.sums[pair][BLOCK - 1 : BLOCK], (8, 128))
        prev_ref[:, pair_lanes(pair)] = ks[pair][BLOCK - HALO :]
        prev_ref[:, value_lanes(pair)] = vs[pair][BLOCK - HALO :]
    prev_out_ref[0] = prev
    return jnp.concatenate(outs, axis=1).astype(BF)


def mixer_backward_kernel(
    total_rows,
    lengths_ref,
    own_ref,
    other_ref,
    state_ref,
    prev_ref,
    near_ref,
    weights_ref,
    features_ref,
    sums_ref,
    total_ref,
    blend_own_ref,
    blend_other_ref,
    grad_ref,
    gq_ref,
    gk_ref,
    gv_ref,
    packet_ref,
    blend_out_ref,
    halo_ref,
    back_state_ref,
    back_sum_ref,
):
    step = pl.program_id(0)
    first = (pl.num_programs(0) - 1 - step) * BLOCK

    @pl.when(step == 0)
    def _():
        for ref in (halo_ref, back_state_ref, back_sum_ref, blend_out_ref):
            ref[...] = jnp.zeros_like(ref)

    ends = document_ends(lengths_ref, total_rows)
    blends = pair_blends(blend_own_ref, blend_other_ref)
    row_places = first + iota((1, 256), 1) % BLOCK
    key_places = first + iota((BLOCK, 256), 0)
    causal = (key_places <= row_places) & (key_places >= starts_of(ends, row_places))
    causal_k = causal[:, :BLOCK].astype(F32).astype(BF)
    col_places = first + iota((BLOCK, 1), 0)
    start_col = starts_of(ends, col_places)
    inverse = 1.0 / (col_places - start_col + 1).astype(F32)
    carried = start_col < first
    member_from = start_at(ends, first + BLOCK - 1)
    member = col_places >= member_from
    keep = member_from < first
    diag = pair_diag(256, 128)
    ones_diag = ones_diagonal()
    qs, ks, vs = [heads_of(own_ref, other_ref, kind) for kind in range(3)]
    prev = prev_ref[0]
    grads = [grad_ref[:, pair_lanes(pair)] for pair in PAIRS]
    states = [state_ref[0, pair] for pair in PAIRS]
    backs = [back_state_ref[pair] for pair in PAIRS]
    back_sums = [back_sum_ref[pair][0:1] for pair in PAIRS]
    nears = [near_ref[0, pair] for pair in PAIRS]
    q_scaled = [features_ref[0, pair, 0] for pair in PAIRS]
    k_both = [features_ref[0, pair, 1] for pair in PAIRS]
    g_stack = each(stack_heads, grads)
    v_window = [jnp.concatenate([prev[:, value_lanes(pair)], vs[pair]], axis=0) for pair in PAIRS]
    grad_weights = each(nt, v_window, g_stack)
    dv = [
        nn(jnp.concatenate([nears[pair][:HALO], weights_ref[0, pair]], axis=0), g_stack[pair]) for pair in PAIRS
    ]
    up_inter = each(lambda grad, state: nt(only(carried, grad), state), grads, states)
    far = each(lambda gw: jnp.where(causal, gw[HALO:], 0.0).astype(BF), grad_weights)
    up = each(tn, far, k_both)
    s_stack = each(stack_heads, q_scaled)
    dfeat = each(nn, far, s_stack)
    near_wide = each(lambda near: near.astype(F32), nears)
    inner = each(lambda near, gw: near * gw, near_wide, grad_weights)
    dscores = each(
        lambda near, inner: (inner - near * jnp.sum(inner, axis=0, keepdims=True)).astype(BF),
        near_wide,
        inner,
    )
    up = each(lambda up, inter: pick_heads(up) + inter, up, up_inter)
    q_first = each(lambda q: jnp.where(q > 0, q + 1.0, jnp.exp(jnp.minimum(q, 0.0))), [q.astype(F32) for q in qs])
    inverse_total = [total_ref[:, pair_lanes(pair)] for pair in PAIRS]
    mean_one = each(
        lambda q, up, total: nn((q.astype(BF).astype(F32) * up[:, :128]).astype(BF), ones_diag) * total,
        q_first,
        up,
        inverse_total,
    )
    window = [jnp.concatenate([prev[:, pair_lanes(pair)], ks[pair]], axis=0) for pair in PAIRS]
    q_stack = each(lambda q: stack_heads(q * 0.125), qs)
    gq_near = each(tn, dscores, window)
    dk = each(nn, dscores, q_stack)
    back_low = each(lambda back: back.astype(BF), backs)
    dv_far = each(lambda k, back: nn(only(member, k), back), k_both, back_low)
    dfeat_far = each(lambda v, back: nt(only(member, v), back), vs, back_low)
    added = each(lambda q, grad: tn(only(carried, q), grad), q_scaled, grads)
    weighted = each(lambda mean, q: (mean * q[:, :128].astype(F32)).astype(BF), mean_one, q_scaled)
    mean_back = each(lambda weight: nn(causal_k, weight), weighted)
    for pair in PAIRS:
        lanes, values = pair_lanes(pair), value_lanes(pair)
        up_one, up_two = up[pair][:, :128], up[pair][:, 128:]
        tanh_q = jnp.tanh(qs[pair].astype(F32))
        slope_q = jnp.minimum(q_first[pair], 1.0)
        up_two = up_two * inverse
        grad_one = blends[pair][0] * inverse_total[pair] * (up_one - mean_one[pair] * sums_ref[:, lanes])
        grad_two = blends[pair][1] * up_two
        gq = pick_heads(gq_near[pair]) * 0.125 + grad_one * slope_q + grad_two * (1.0 - tanh_q * tanh_q)
        gq_ref[:, lanes] = gq.astype(BF)
        blend_out_ref[0, pair] += jnp.broadcast_to(
            jnp.sum(mean_one[pair], axis=0, keepdims=True) / 64.0, (8, 128)
        )
        blend_out_ref[1, pair] += jnp.broadcast_to(jnp.sum(tanh_q * up_two, axis=0, keepdims=True), (8, 128))
        dv_own = dv[pair][HALO:] + dv_far[pair]
        dfeat_all = dfeat[pair] + dfeat_far[pair]
        d_one = dfeat_all[:, :128] - mean_back[pair] - jnp.where(member, back_sums[pair], 0.0)
        d_two = dfeat_all[:, 128:]
        wide_k = ks[pair].astype(F32)
        tanh_k = jnp.tanh(wide_k)
        slope_k = jnp.exp(jnp.minimum(wide_k, 0.0))
        gk = dk[pair][HALO:] + d_one * slope_k + d_two * (1.0 - tanh_k * tanh_k)
        gk_ref[: BLOCK - HALO, lanes] = gk[: BLOCK - HALO].astype(BF)
        gk_ref[BLOCK - HALO :, lanes] = (gk[BLOCK - HALO :] + halo_ref[:, lanes]).astype(BF)
        gv_ref[: BLOCK - HALO, lanes] = dv_own[: BLOCK - HALO].astype(BF)
        gv_ref[BLOCK - HALO :, lanes] = (dv_own[BLOCK - HALO :] + halo_ref[:, values]).astype(BF)
        halo_ref[:, lanes] = dk[pair][:HALO]
        halo_ref[:, values] = dv[pair][:HALO]
        back_state_ref[pair] = jnp.where(keep, backs[pair], 0.0) + jnp.where(diag, added[pair], 0.0)
        added_sum = jnp.sum(only(carried, weighted[pair].astype(F32)), axis=0, keepdims=True)
        back_sum_ref[pair] = jnp.broadcast_to(
            jnp.where(keep, back_sums[pair], 0.0) + added_sum, (8, 128)
        )

    @pl.when(first == 0)
    def _():
        for pair in PAIRS:
            slot = (pair + 2) % 4
            pack(packet_ref, slot, back_state_ref[pair], back_sum_ref[pair][0:1])
            pack_halo(packet_ref, 0, slot, halo_ref[:, pair_lanes(pair)].astype(BF))
            pack_halo(packet_ref, 1, slot, halo_ref[:, value_lanes(pair)].astype(BF))


LANES = 256


def layer_kernel(
    blocks,
    parts,
    lengths_ref,
    own_ref,
    other_ref,
    packet_ref,
    blend_own_ref,
    blend_other_ref,
    x_ref,
    cot_ref,
    gain_ref,
    wa_own_ref,
    wa_other_ref,
    wi_own_ref,
    wi_other_ref,
    wo_own_ref,
    wo_other_ref,
    mixed_out_ref,
    state_out_ref,
    prev_out_ref,
    near_ref,
    weights_ref,
    features_ref,
    sums_ref,
    total_ref,
    active_ref,
    branch_ref,
    gmix_ref,
    ggain_ref,
    attn_own_ref,
    attn_sent_ref,
    out_own_ref,
    in_own_ref,
    out_sent_ref,
    in_sent_ref,
    state_ref,
    sum_ref,
    prev_ref,
    mixed_ref,
    y_ref,
    r_ref,
    normed_ref,
    normed_turned_ref,
    grad_ref,
    grad_turned_ref,
    back_ref,
    wi_ref,
    wo_ref,
    stack_ref,
    load_sems,
    store_sems,
):
    step = pl.program_id(0)
    width = x_ref.shape[1]
    heads = wa_own_ref.shape[0]
    units = wo_ref.shape[1]
    chunk_units = units // parts
    loads = [
        pltpu.make_async_copy(source, target, load_sems.at[place])
        for place, (source, target) in enumerate(
            (
                (wi_own_ref, wi_ref.at[0]),
                (wo_own_ref, wo_ref.at[0]),
                (wi_other_ref, wi_ref.at[1]),
                (wo_other_ref, wo_ref.at[1]),
            )
        )
    ]

    @pl.when(step == 0)
    def _():
        for load in loads:
            load.start()
        back_ref[...] = jnp.zeros_like(back_ref)

    @pl.when(step < blocks)
    def _():
        mixed = mixer_forward_block(
            step,
            blocks * BLOCK,
            lengths_ref,
            own_ref,
            other_ref,
            packet_ref,
            blend_own_ref,
            blend_other_ref,
            state_out_ref,
            prev_out_ref,
            near_ref,
            weights_ref,
            features_ref,
            sums_ref,
            total_ref,
            state_ref,
            sum_ref,
            prev_ref,
        )
        here = pl.ds(pl.multiple_of(step * BLOCK, BLOCK), BLOCK)
        mixed_out_ref[...] = mixed
        mixed_ref[here, :] = mixed
        hidden = x_ref[...].astype(F32)
        hidden = hidden + nn(mixed[:, :heads], wa_own_ref[...]) + nn(mixed[:, heads:], wa_other_ref[...])
        r = lax.rsqrt(jnp.mean(hidden * hidden, axis=1, keepdims=True) + EPS)
        y = hidden * r
        y_ref[here, :] = y
        r_ref[here, :] = jnp.broadcast_to(r, (BLOCK, r_ref.shape[1]))
        normed = (y * gain_ref[...]).astype(BF)
        normed_ref[here, :] = normed
        normed_turned_ref[:, here] = normed.T
        grad_ref[here, :] = cot_ref[...]
        grad_turned_ref[:, here] = cot_ref[...].T

    @pl.when(step == blocks)
    def _():
        for load in loads:
            load.wait()

    @pl.when(step >= blocks)
    def _():
        half = (step - blocks) // parts
        place = (step - blocks) % parts
        normed = normed_ref[...]
        grad = grad_ref[...]
        first = pl.multiple_of(place * chunk_units, chunk_units)
        wi = wi_ref[half, :, pl.ds(first, chunk_units)]
        wo = wo_ref[half, pl.ds(first, chunk_units), :]
        spans = [slice(LANES * piece, LANES * piece + LANES) for piece in range(chunk_units // LANES)]
        us = [nn(normed, wi[:, span]) for span in spans]
        gacts = [nt(grad, wo[span, :]) for span in spans]
        gpres = []
        for piece, span in enumerate(spans):
            u = us[piece]
            square = u * u
            t = jnp.tanh(u * (GELU_A + (GELU_A * GELU_B) * square))
            gate = 0.5 + 0.5 * t
            active = (u * gate).astype(BF)
            active_ref[:, span] = active
            slope = gate + (u * (0.5 - 0.5 * t * t)) * (GELU_A + (3.0 * GELU_A * GELU_B) * square)
            gpre = (gacts[piece] * slope).astype(BF)
            gpres.append(gpre)
            gout = nn(grad_turned_ref[...], active).astype(BF).T
            spot = len(spans) * place + piece
            for side in range(width // LANES):
                row = pl.multiple_of(units * side + LANES * spot, LANES)
                stack_ref[half, 0, pl.ds(row, LANES), :] = gout[:, LANES * side : LANES * side + LANES]
            row = pl.multiple_of(width * spot, LANES)
            stack_ref[half, 1, pl.ds(row, width), :] = nn(normed_turned_ref[...], gpre).astype(BF)
        back_ref[...] += nt(jnp.concatenate(gpres, axis=1), wi)

    stores = []
    for late in range(2 * parts):
        half, place = late // parts, late % parts
        out_target, in_target = ((out_own_ref, in_own_ref), (out_sent_ref, in_sent_ref))[half]
        spots = [(0, out_target, units * side + chunk_units * place, chunk_units) for side in range(width // LANES)]
        rows = width * chunk_units // LANES
        spots.append((1, in_target, rows * place, rows))
        stores.append(
            [
                pltpu.make_async_copy(
                    stack_ref.at[half, kind, pl.ds(row, count), :],
                    target.at[pl.ds(row, count), :],
                    store_sems.at[late, number],
                )
                for number, (kind, target, row, count) in enumerate(spots)
            ]
        )

    for late in range(2 * parts):

        @pl.when(step == blocks + late)
        def _(late=late):
            for store in stores[late]:
                store.start()

    @pl.when(step == blocks + 2 * parts - 1)
    def _():
        back, y = back_ref[...], y_ref[...]
        scaled = back * gain_ref[...]
        mean = jnp.mean(scaled * y, axis=1, keepdims=True)
        ghid = grad_ref[...].astype(F32) + r_ref[:, :1] * (scaled - y * mean)
        branch = ghid.astype(BF)
        branch_ref[...] = branch
        gmix_ref[:, :heads] = nt(branch, wa_own_ref[...]).astype(BF)
        gmix_ref[:, heads:] = nt(branch, wa_other_ref[...]).astype(BF)
        ggain_ref[...] = jnp.broadcast_to(jnp.sum(back * y, axis=0, keepdims=True), ggain_ref.shape)
        gattn = tn(mixed_ref[...], branch).astype(BF)
        for half, ref in enumerate((attn_own_ref, attn_sent_ref)):
            for side in range(width // LANES):
                lanes = slice(LANES * side, LANES * side + LANES)
                ref[heads * side : heads * side + heads] = gattn[heads * half : heads * half + heads, lanes]
        for some in stores:
            for store in some:
                store.wait()


def output_kernel(x_ref, mixed_ref, active_ref, wa_own_ref, wa_other_ref, wo_own_ref, wo_other_ref, out_ref):
    heads = wa_own_ref.shape[0]
    units = wo_own_ref.shape[0]
    total = x_ref[...].astype(F32)
    total = total + (nn(mixed_ref[:, :heads], wa_own_ref[...]) + nn(mixed_ref[:, heads:], wa_other_ref[...]))
    total = total + (nn(active_ref[:, :units], wo_own_ref[...]) + nn(active_ref[:, units:], wo_other_ref[...]))
    out_ref[...] = total.astype(BF)


def finish_kernel(
    lengths_ref,
    own_ref,
    other_ref,
    normed_ref,
    packet_ref,
    gblend_ref,
    ggain_ref,
    gain_ref,
    w_own_ref,
    w_other_ref,
    attn_own_ref,
    attn_sent_ref,
    *refs,
):
    gq_ref, gk_ref, gv_ref, gproj_ref, wgrad_own_ref, wgrad_sent_ref = refs

    rows = own_ref.shape[0]
    live = lax.axis_index("tensor") == 0
    member_from = start_at(document_ends(lengths_ref, rows), rows - 1)
    member = (iota((rows, 1), 0) >= member_from) & live
    diag = pair_diag(256, 128)
    for pair in range(4):
        src = own_ref if pair < 2 else other_ref
        col = 128 * (pair % 2)
        lanes = slice(128 * pair, 128 * pair + 128)
        base = 768 * (pair // 2) + col
        k = src[:, 256 + col : 384 + col].astype(F32)
        v = src[:, 512 + col : 640 + col]
        back, back_sum = unpack(packet_ref, pair, diag)
        back, back_sum = back.astype(BF), back_sum[0:1]
        t = jnp.tanh(k)
        slope = jnp.exp(jnp.minimum(k, 0.0))
        k_both = jnp.concatenate([first_feature(k), t.astype(BF)], axis=1)
        dfeat = nt(v, back)
        extra_k = (dfeat[:, :128] - back_sum) * slope + dfeat[:, 128:] * (1.0 - t * t)
        extra_v = nn(k_both, back)
        gk = gk_ref[:, lanes].astype(F32) + jnp.where(member, extra_k, 0.0)
        gv = gv_ref[:, lanes].astype(F32) + jnp.where(member, extra_v, 0.0)
        halo_k = jnp.where(live, unpack_halo(packet_ref, 0, pair).astype(F32), 0.0)
        halo_v = jnp.where(live, unpack_halo(packet_ref, 1, pair).astype(F32), 0.0)
        cut = rows - HALO
        gproj_ref[:, base : base + 128] = gq_ref[:, lanes]
        gproj_ref[:cut, base + 256 : base + 384] = gk[:cut].astype(BF)
        gproj_ref[cut:, base + 256 : base + 384] = (gk[cut:] + halo_k).astype(BF)
        gproj_ref[:cut, base + 512 : base + 640] = gv[:cut].astype(BF)
        gproj_ref[cut:, base + 512 : base + 640] = (gv[cut:] + halo_v).astype(BF)
    width = normed_ref.shape[1]
    cols = w_own_ref.shape[2]
    normed = normed_ref[...]
    ones = jnp.ones((1, cols), F32)
    gain_grad = jnp.zeros((1, width), F32)
    for half, (wgrad_ref, w_ref) in enumerate(((wgrad_own_ref, w_own_ref), (wgrad_sent_ref, w_other_ref))):
        for kind in range(3):
            first = 3 * cols * half + cols * kind
            wgrad = tn(normed, gproj_ref[:, first : first + cols])
            wgrad_ref[width * kind : width * kind + width] = wgrad.astype(BF)
            products = wgrad * w_ref[kind].astype(F32)
            high = products.astype(BF)
            low = (products - high.astype(F32)).astype(BF)
            gain_grad = gain_grad + nt(ones.astype(BF), high) + nt(ones.astype(BF), low)
    gain_grad = gain_grad / gain_ref[...]
    for half, wgrad_ref in enumerate((wgrad_own_ref, wgrad_sent_ref)):
        blends = [
            jnp.concatenate([gblend_ref[kind, 2 * half + pair][0:1] for pair in range(2)], axis=1)
            for kind in range(2)
        ]
        gains = [gain_grad[:, :256], gain_grad[:, 256:], ggain_ref[0:1, :256], ggain_ref[0:1, 256:]]
        extra = jnp.concatenate(blends + gains + [jnp.zeros((10, 256), F32)], axis=0)
        attn_ref = (attn_own_ref, attn_sent_ref)[half]
        wgrad_ref[3 * width : 3 * width + attn_ref.shape[0]] = attn_ref[...]
        base = 3 * width + attn_ref.shape[0]
        wgrad_ref[base : base + 16] = extra.astype(BF)
        wgrad_ref[base + 16 :] = jnp.zeros((EXTRA - 16, 256), BF)


def input_grad_kernel(gproj_ref, x_ref, branch_ref, gain_ref, w_own_ref, w_other_ref, out_ref):
    cols = w_own_ref.shape[2]
    gnormed = None
    for half, w_ref in enumerate((w_own_ref, w_other_ref)):
        for kind in range(3):
            first = 3 * cols * half + cols * kind
            term = nt(gproj_ref[:, first : first + cols], w_ref[kind])
            gnormed = term if gnormed is None else gnormed + term
    x = x_ref[...].astype(F32)
    r = lax.rsqrt(jnp.mean(x * x, axis=1, keepdims=True) + EPS)
    y = x * r
    scaled = gnormed * gain_ref[...]
    grad = branch_ref[...].astype(F32) + r * (scaled - y * jnp.mean(scaled * y, axis=1, keepdims=True))
    out_ref[...] = grad.astype(BF)


def merged(low, mine, got):
    return jnp.where(low, mine, got), jnp.where(low, got, mine)


def put_rows(ref, first_row, lane, parts, first, count):
    rows = parts[0].shape[0]
    lanes = parts[0].shape[1]
    for place, part in enumerate(parts):
        low, high = max(first, rows * place), min(first + count, rows * place + rows)
        if low < high:
            values = part[low - rows * place : high - rows * place].astype(F32)
            ref[first_row + low - first : first_row + high - first, lane : lane + lanes] = values


def feed_output_kernel(bits_ref, out_mine_ref, out_got_ref, in_mine_ref, in_got_ref, wo_ref, wi_ref):
    units, width = wo_ref.shape
    outs = merged(bits_ref[0] == 0, out_mine_ref[...], out_got_ref[...])
    for side in range(width // LANES):
        put_rows(wo_ref, 0, LANES * side, outs, units * side, units)
    ins = merged(bits_ref[1] == 0, in_mine_ref[...], in_got_ref[...])
    for place in range(units // LANES):
        put_rows(wi_ref, 0, LANES * place, ins, width * place, width)


def attention_output_kernel(
    bits_ref, a_mine_ref, a_got_ref, b_mine_ref, b_got_ref, wq_ref, wa_ref, gain_one_ref, gain_two_ref, blend_ref
):
    heads, width = wa_ref.shape
    parts = merged(bits_ref[0] == 0, a_mine_ref[...], a_got_ref[...])
    parts += merged(bits_ref[1] == 0, b_mine_ref[...], b_got_ref[...])
    rows = a_mine_ref.shape[0]
    put_rows(wq_ref, 0, 0, parts, 0, 3 * width)
    for side in range(width // LANES):
        put_rows(wa_ref, 0, LANES * side, parts, 3 * width + heads * side, heads)
    rest = parts[3][rows - EXTRA : rows - EXTRA + 16].astype(F32)
    gain_one_ref[...] = jnp.concatenate([rest[2:3], rest[3:4]], axis=1)
    gain_two_ref[...] = jnp.concatenate([rest[4:5], rest[5:6]], axis=1)
    sums = [jnp.sum(rest[:2, 64 * head : 64 * head + 64], axis=1, keepdims=True) for head in range(4)]
    blend_ref[...] = jnp.concatenate(sums, axis=1)


def flip(values, count, stride):
    return lax.ppermute(values, "dp", [(src, src ^ stride) for src in range(count)])


def strides_of(count):
    strides = []
    stride = 1
    while stride < count:
        strides.append(stride)
        stride *= 2
    return strides


class Reduction:
    def __init__(self, stacks, count, whole_late=False):
        self.stacks = [[(term, 0) for term in terms] for terms in stacks]
        self.rows = [terms[0].shape[0] for terms in stacks]
        self.count = count
        strides = strides_of(count)
        self.orders = [strides, strides[1::-1] + strides[2:]]
        self.steps = len(strides)
        self.taken = 0
        self.halved = min(2, self.steps) if whole_late else self.steps
        self.place = lax.axis_index("dp")
        self.held = None

    def bit(self, stride):
        return (self.place // stride) % 2

    def after(self, *tokens):
        if self.held is not None:
            *self.gots, first, second = tie(*self.gots, *self.held)
            self.held = [first, second]
            return tokens
        news = [terms[-1][0] for terms in self.stacks]
        if news[0] is news[1]:
            news = news[:1]
        tied = tie(*news, *tokens)
        for stack in range(2):
            offset = self.stacks[stack][-1][1]
            self.stacks[stack][-1] = (tied[min(stack, len(news) - 1)], offset)
        return tied[len(news) :]

    def cut(self, stack, rows, skip):
        total = None
        for term, offset in self.stacks[stack]:
            part = lax.dynamic_slice_in_dim(term, offset + skip, rows, 0).astype(F32)
            total = part if total is None else total + part
        return total.astype(BF)

    def outgoing(self):
        cuts = []
        for stack in range(2):
            if self.taken < self.halved:
                self.rows[stack] //= 2
                bit = self.bit(self.orders[stack][self.taken])
                cuts.append(self.cut(stack, self.rows[stack], (1 - bit) * self.rows[stack]))
            else:
                cuts.append(self.cut(stack, self.rows[stack], 0))
        return cuts if self.taken < 2 else [jnp.concatenate(cuts, axis=0)]

    def send(self, cuts):
        gots = [flip(cut, self.count, self.orders[stack][self.taken]) for stack, cut in enumerate(cuts)]
        for stack in range(2):
            skip = self.rows[0] if stack == 1 and len(cuts) == 1 else 0
            got = gots[min(stack, len(cuts) - 1)]
            if self.taken < self.halved:
                bit = self.bit(self.orders[stack][self.taken])
                kept = [(term, offset + bit * self.rows[stack]) for term, offset in self.stacks[stack]]
            else:
                kept = [(cuts[0], skip)]
            self.stacks[stack] = kept + [(got, skip)]
        self.taken += 1

    def start_gather(self):
        self.held = [self.cut(stack, self.rows[stack], 0) for stack in range(2)]

    def gather_outgoing(self):
        return list(self.held) if self.halved <= 2 else [jnp.concatenate(self.held, axis=0)]

    def gather_send(self, cuts):
        step = self.halved - 1
        gots = [flip(cut, self.count, self.orders[stack][step]) for stack, cut in enumerate(cuts)]
        if len(gots) == 1:
            first = self.held[0].shape[0]
            gots = [gots[0][:first], gots[0][first:]]
        self.gots = gots
        self.halved = step

    def finished(self):
        return self.taken == self.steps and (self.steps == 0 or (self.held is not None and self.halved == 0))

    def next_cuts(self):
        if self.taken < self.steps:
            return self.outgoing()
        if self.held is None:
            self.start_gather()
        return self.gather_outgoing()

    def next_send(self, cuts):
        if self.held is None:
            self.send(cuts)
        else:
            self.gather_send(cuts)

    def next_take(self):
        if self.held is not None and self.halved > 0:
            self.gather_take()

    def last_bits(self):
        return jnp.stack([self.bit(order[0]) if order else 0 * self.place for order in self.orders])

    def parts(self):
        if self.steps > 0:
            return [self.held[0], self.gots[0], self.held[1], self.gots[1]]
        halves = []
        for held in [self.cut(stack, self.rows[stack], 0) for stack in range(2)]:
            middle = held.shape[0] // 2
            halves += [held[:middle], held[middle:]]
        return halves

    def gather_take(self):
        for stack in range(2):
            low = self.bit(self.orders[stack][self.halved]) == 0
            mine, got = self.held[stack], self.gots[stack]
            self.held[stack] = jnp.concatenate([jnp.where(low, mine, got), jnp.where(low, got, mine)], axis=0)


def swap(values):
    return lax.ppermute(values, "tensor", [(0, 1), (1, 0)])


def body(count, tokens, lengths, w_qkv, w_attn, w_in, w_out, gain_attn, gain_mlp, blend, cotangent):
    rows, width = tokens.shape
    blocks = rows // BLOCK

    wq_own = w_qkv.transpose(1, 0, 2)
    wq_other = swap(wq_own)
    wa_other, wi_other, wo_other = swap(w_attn), swap(w_in), swap(w_out)
    blend_other = swap(blend)
    gain_one = gain_attn.reshape(1, width)
    gain_two = gain_mlp.reshape(1, width)
    smem = pl.BlockSpec(memory_space=pltpu.SMEM)

    def row_block(size, cols):
        return pl.BlockSpec((size, cols), lambda i: (i, 0))

    own_cols = 3 * wq_own.shape[2]
    normed, own = pl.pallas_call(
        norm_project_kernel,
        grid=(4,),
        in_specs=[row_block(rows // 4, width), whole((1, width)), whole(wq_own.shape)],
        out_specs=[row_block(rows // 4, width), row_block(rows // 4, own_cols)],
        out_shape=[jax.ShapeDtypeStruct((rows, width), BF), jax.ShapeDtypeStruct((rows, own_cols), BF)],
        compiler_params=params(60),
        cost_estimate=cost(5),
        name="norm_project",
    )(tokens, gain_one, wq_own)
    other, packet = pl.pallas_call(
        project_state_kernel,
        in_specs=[smem] + [pl.BlockSpec(memory_space=pltpu.VMEM)] * 3,
        out_shape=[
            jax.ShapeDtypeStruct((rows, own_cols), BF),
            jax.ShapeDtypeStruct((PACKET, 128), BF),
        ],
        compiler_params=params(60),
        cost_estimate=cost(5),
        name="project_state",
    )(lengths, normed, wq_other, own)
    packet = swap(packet)

    units = w_out.shape[0]
    tall = rows // 4
    parts = units // (2 * LANES)
    vmem = pl.BlockSpec(memory_space=pltpu.VMEM)
    stack_rows = units * width // LANES
    attn_rows = w_attn.shape[0] * width // LANES
    anywhere = pl.BlockSpec(memory_space=pl.ANY)

    def early(*shape):
        return pl.BlockSpec(shape, lambda i: (jnp.minimum(i, blocks - 1),) + (0,) * (len(shape) - 1))

    kept_blocks = [
        ((blocks, 4, 256, 128), BF),
        ((blocks, HALO, 1024), BF),
        ((blocks, 4, BLOCK + HALO, 256), BF),
        ((blocks, 4, BLOCK, 256), BF),
        ((blocks, 4, 2, BLOCK, 256), BF),
    ]
    mixed, *outs = pl.pallas_call(
        partial(layer_kernel, blocks, parts),
        grid=(blocks + 2 * parts,),
        in_specs=[
            smem,
            early(BLOCK, own_cols),
            early(BLOCK, own_cols),
            whole((PACKET, 128)),
            smem,
            smem,
            early(BLOCK, width),
            early(BLOCK, width),
            whole((1, width)),
            whole(w_attn.shape),
            whole(w_attn.shape),
        ]
        + [anywhere] * 4,
        out_specs=[early(BLOCK, width)]
        + [early(1, *shape[1:]) for shape, _ in kept_blocks]
        + [early(BLOCK, width)] * 2
        + [
            pl.BlockSpec((rows, units // parts), lambda i: (0, jnp.maximum(i - blocks, 0))),
            whole((rows, width)),
            whole((rows, width)),
            whole((8, width)),
            whole((attn_rows, LANES)),
            whole((attn_rows, LANES)),
        ]
        + [anywhere] * 4,
        out_shape=[jax.ShapeDtypeStruct((rows, width), BF)]
        + [jax.ShapeDtypeStruct(shape, kind) for shape, kind in kept_blocks]
        + [jax.ShapeDtypeStruct((rows, width), F32)] * 2
        + [
            jax.ShapeDtypeStruct((rows, 2 * units), BF),
            jax.ShapeDtypeStruct((rows, width), BF),
            jax.ShapeDtypeStruct((rows, width), BF),
            jax.ShapeDtypeStruct((8, width), F32),
            jax.ShapeDtypeStruct((attn_rows, LANES), BF),
            jax.ShapeDtypeStruct((attn_rows, LANES), BF),
        ]
        + [jax.ShapeDtypeStruct((stack_rows, LANES), BF)] * 4,
        scratch_shapes=[
            pltpu.VMEM((4, 256, 128), F32),
            pltpu.VMEM((4, 8, 128), F32),
            pltpu.VMEM((HALO, 1024), BF),
            pltpu.VMEM((rows, width), BF),
            pltpu.VMEM((rows, width), F32),
            pltpu.VMEM((rows, 128), F32),
            pltpu.VMEM((rows, width), BF),
            pltpu.VMEM((width, rows), BF),
            pltpu.VMEM((rows, width), BF),
            pltpu.VMEM((width, rows), BF),
            pltpu.VMEM((rows, width), F32),
            pltpu.VMEM((2,) + w_in.shape, BF),
            pltpu.VMEM((2,) + w_out.shape, BF),
            pltpu.VMEM((2, 2, stack_rows, LANES), BF),
            pltpu.SemaphoreType.DMA((4,)),
            pltpu.SemaphoreType.DMA((2 * parts, 1 + width // LANES)),
        ],
        compiler_params=params(60),
        cost_estimate=cost(30),
        name="layer",
    )(
        lengths,
        own,
        other,
        packet,
        blend,
        blend_other,
        tokens,
        cotangent,
        gain_two,
        w_attn,
        wa_other,
        w_in,
        wi_other,
        w_out,
        wo_other,
    )
    kept, outs = outs[:7], outs[7:]
    active, branch, gmix, ggain_mlp, *attn_grads = outs[:6]
    out_own, in_own, out_sent, in_sent = outs[6:]

    feed_sum = Reduction([[out_own, swap(out_sent)], [in_own, swap(in_sent)]], count)
    wanted = feed_sum.steps
    if wanted > 0:
        cuts = feed_sum.outgoing()
        gmix, *cuts = tie(gmix, *cuts)
        feed_sum.send(cuts)

    def back_block(*shape):
        return pl.BlockSpec(shape, lambda i: (blocks - 1 - i,) + (0,) * (len(shape) - 1))

    gq, gk, gv, packet_back, gblend = pl.pallas_call(
        partial(mixer_backward_kernel, rows),
        grid=(blocks,),
        in_specs=[
            smem,
            back_block(BLOCK, own_cols),
            back_block(BLOCK, own_cols),
            back_block(1, 4, 256, 128),
            back_block(1, HALO, 1024),
            back_block(1, 4, BLOCK + HALO, 256),
            back_block(1, 4, BLOCK, 256),
            back_block(1, 4, 2, BLOCK, 256),
            back_block(BLOCK, width),
            back_block(BLOCK, width),
            smem,
            smem,
            back_block(BLOCK, width),
        ],
        out_specs=[back_block(BLOCK, width)] * 3 + [whole((PACKET, 128)), whole((2, 4, 8, 128))],
        out_shape=[jax.ShapeDtypeStruct((rows, width), BF)] * 3
        + [jax.ShapeDtypeStruct((PACKET, 128), BF), jax.ShapeDtypeStruct((2, 4, 8, 128), F32)],
        scratch_shapes=[
            pltpu.VMEM((HALO, 1024), F32),
            pltpu.VMEM((4, 256, 128), F32),
            pltpu.VMEM((4, 8, 128), F32),
        ],
        compiler_params=params(60),
        cost_estimate=cost(20),
        name="mixer_backward",
    )(lengths, own, other, *kept, blend, blend_other, gmix)
    if wanted > 1:
        (packet_back,) = feed_sum.after(packet_back)
    packet_got = swap(packet_back)
    if wanted > 1:
        cuts = feed_sum.outgoing()
        packet_got, *cuts = tie(packet_got, *cuts)
        feed_sum.send(cuts)

    gproj, wq_mine, wq_sent = pl.pallas_call(
        finish_kernel,
        in_specs=[smem] + [pl.BlockSpec(memory_space=pltpu.VMEM)] * 14,
        out_shape=[
            jax.ShapeDtypeStruct((rows, 2 * own_cols), BF),
            jax.ShapeDtypeStruct((3 * width + attn_rows + EXTRA, own_cols // 3), BF),
            jax.ShapeDtypeStruct((3 * width + attn_rows + EXTRA, own_cols // 3), BF),
        ],
        compiler_params=params(60),
        cost_estimate=cost(8),
        name="finish",
    )(
        lengths,
        own,
        other,
        normed,
        packet_got,
        gblend,
        ggain_mlp,
        gain_one,
        wq_own,
        wq_other,
        *attn_grads,
        gq,
        gk,
        gv,
    )
    def layer_output(active):
        return pl.pallas_call(
            output_kernel,
            grid=(4,),
            in_specs=[row_block(tall, width), row_block(tall, width), row_block(tall, 2 * units)]
            + [whole(w_attn.shape)] * 2
            + [whole(w_out.shape)] * 2,
            out_specs=row_block(tall, width),
            out_shape=jax.ShapeDtypeStruct((rows, width), BF),
            compiler_params=params(60),
            cost_estimate=cost(5),
            name="layer_output",
        )(tokens, mixed, active, w_attn, wa_other, w_out, wo_other)

    def input_gradient(gproj):
        return pl.pallas_call(
            input_grad_kernel,
            grid=(4,),
            in_specs=[
                row_block(tall, 2 * own_cols),
                row_block(tall, width),
                row_block(tall, width),
                whole((1, width)),
                whole(wq_own.shape),
                whole(wq_own.shape),
            ],
            out_specs=row_block(tall, width),
            out_shape=jax.ShapeDtypeStruct((rows, width), BF),
            compiler_params=params(60),
            cost_estimate=cost(7),
            name="input_grad",
        )(gproj, tokens, branch, gain_one, wq_own, wq_other)

    if wanted > 1:
        (wq_sent,) = feed_sum.after(wq_sent)
    wq_got = swap(wq_sent)
    cut = wq_got.shape[0] // 2
    wq_sum = Reduction([[wq_mine[:cut], wq_got[:cut]], [wq_mine[cut:], wq_got[cut:]]], count, True)
    beside = {0: lambda: input_gradient(gproj), 3: lambda: layer_output(active)}
    done = {}
    step = 0
    while not (feed_sum.finished() and wq_sum.finished()):
        running = [reduction for reduction in (wq_sum, feed_sum) if not reduction.finished()]
        cuts = [reduction.next_cuts() for reduction in running]
        flat = list(tie(*[cut for some in cuts for cut in some], gproj, active))
        active, gproj = flat.pop(), flat.pop()
        for reduction, some in zip(running, cuts):
            reduction.next_send([flat.pop(0) for _ in some])
        if step in beside:
            done[step] = beside[step]()
            for reduction in running:
                (done[step],) = reduction.after(done[step])
        for reduction in running:
            reduction.next_take()
        step += 1
    for step in beside:
        if step not in done:
            done[step] = beside[step]()
    grad_input, output = done[0], done[3]

    wo_grad, wi_grad = pl.pallas_call(
        feed_output_kernel,
        in_specs=[smem] + [vmem] * 4,
        out_shape=[jax.ShapeDtypeStruct(w_out.shape, F32), jax.ShapeDtypeStruct(w_in.shape, F32)],
        compiler_params=params(60),
        cost_estimate=cost(3),
        name="feed_output",
    )(feed_sum.last_bits(), *feed_sum.parts())
    wq_grad, wa_grad, ggain_one, ggain_two, gblend_all = pl.pallas_call(
        attention_output_kernel,
        in_specs=[smem] + [vmem] * 4,
        out_shape=[
            jax.ShapeDtypeStruct((3 * width, own_cols // 3), F32),
            jax.ShapeDtypeStruct(w_attn.shape, F32),
            jax.ShapeDtypeStruct((1, width), F32),
            jax.ShapeDtypeStruct((1, width), F32),
            jax.ShapeDtypeStruct(blend.shape, F32),
        ],
        compiler_params=params(60),
        cost_estimate=cost(3),
        name="attention_output",
    )(wq_sum.last_bits(), *wq_sum.parts())

    return (
        output,
        grad_input,
        wq_grad.reshape(wq_own.shape).transpose(1, 0, 2),
        wa_grad,
        wi_grad,
        wo_grad,
        ggain_one.reshape(width),
        ggain_two.reshape(width),
        gblend_all,
    )


def solution(mesh):
    return jax.shard_map(
        partial(body, mesh.shape["dp"]),
        mesh=mesh,
        in_specs=(
            P(("dp", "tensor"), None),
            P("dp", None),
            P(None, None, "tensor"),
            P("tensor", None),
            P(None, "tensor"),
            P("tensor", None),
            P(),
            P(),
            P(None, "tensor"),
            P(("dp", "tensor"), None),
        ),
        out_specs=(
            P(("dp", "tensor"), None),
            P(("dp", "tensor"), None),
            P(None, None, "tensor"),
            P("tensor", None),
            P(None, "tensor"),
            P("tensor", None),
            P(),
            P(),
            P(None, "tensor"),
        ),
        check_vma=False,
    )
```

time: 207 us -> 180 us (0.87)
  Pallas kernels: 121 us -> 88.9 us
  starting transfers between devices: 26.2 us -> 32.1 us
  other arithmetic: 14.7 us -> 11.5 us
  waiting for transfers between devices: 33.8 us -> 36.7 us
    pallas_call x11 -> x7, Pallas kernels: 110 us -> 78 us  [the longest x1 33.5 us: body(): pl.pallas_call(partial(layer_kernel, blocks, parts), grid=(blocks + 2 * p...]
    ppermute x22, starting transfers between devices: 23.8 us -> 29.8 us  [flip(): lax.ppermute(values, 'dp', [(src, src ^ stride) for src in range(count)])]
    ppermute x22, waiting for transfers between devices: 29.7 us -> 32.9 us  [flip(): lax.ppermute(values, 'dp', [(src, src ^ stride) for src in range(count)])]
    unnamed x50 -> x44, local copies, waits for them, and re-layouts: 6.6 us -> 6.76 us
  transfers between devices with their start and end apart: 32 -> 32, of which waited for: 15 -> 15; matrix products, arithmetic and copies ran while one was open for 3% -> 5% of each run, Pallas kernels for 40% -> 29%
where the time goes in v3:
time: 180 us; the launch traced here: 179 us
  Pallas kernels  88.9 us (49%)
  waiting for transfers between devices  36.7 us (20%)
  starting transfers between devices  32.1 us (18%)
  other arithmetic  11.5 us (6%)
  local copies, waits for them, and re-layouts  8.17 us (5%)
    pallas_call x1, Pallas kernels, body(): pl.pallas_call(partial(layer_kernel, blocks, parts), grid=(blocks + 2 * p...  33.5 us
    ppermute x22, waiting for transfers between devices, flip(): lax.ppermute(values, 'dp', [(src, src ^ stride) for src in range(count)])  32.9 us
    ppermute x22, starting transfers between devices, flip(): lax.ppermute(values, 'dp', [(src, src ^ stride) for src in range(count)])  29.8 us
    pallas_call x1, Pallas kernels, body(): pl.pallas_call(partial(mixer_backward_kernel, rows), grid=(blocks,), in_s...  16 us
    pallas_call x1, Pallas kernels, body(): pl.pallas_call(finish_kernel, in_specs=[smem] + [pl.BlockSpec(memory_spac...  10.2 us
    convert_element_type x15, other arithmetic, cut(): return total.astype(BF)  9.61 us
    pallas_call x1, Pallas kernels, layer_output(): pl.pallas_call(output_kernel, grid=(4,), in_specs=[row_block(tall, width)...  7.1 us
    unnamed x44, local copies, waits for them, and re-layouts  6.76 us
  transfers between devices with their start and end apart: 32, of which 15 were waited for; matrix products, arithmetic and copies ran while one was open for 5% of the time, Pallas kernels for 29%

profile of v3, /device:TPU:0, one launch (start us, length us, event | category | flops | bytes accessed | tf_op | source)
XLA Modules:
  0.0 178.5 jit_solution(5961541293372606911)
XLA Ops:
  0.6 0.5 collective-permute-start.4
  1.2 0.4 collective-permute-start
  1.8 4.6 %norm_project.1 = (bf16[1024,512]{1,0:T(8,128)(2,1)}, bf16[1024,768]{1,0:T(8,128)(2,1)}) custom-call(bf16[1024,512]{1,0:T(8,128)(2,1)} %x_ref.7, f32[1,512]{1,0:T(1,128)} %bitcast.14, bf16[3,512,256]{2,1,0:T(8,128)(2,1)} %bitcast.11), custom_call_target="tpu_custom_call" | custom-call | flops 50000000 | bytes 1048576 | tf_op jit(solution)/shard_map/norm_project/pallas_call | solution.py:968
  6.3 0.9 copy-done
  7.2 4.8 %project_state.1 = (bf16[1024,768]{1,0:T(8,128)(2,1)}, bf16[832,128]{1,0:T(8,128)(2,1)}) custom-call(s32[1,6]{1,0:T(1,128)} %lengths_ref.7, bf16[1024,512]{1,0:T(8,128)(2,1)} %get-tuple-element.93.normed_ref, bf16[3,512,256]{2,1,0:T(8,128)(2,1)} %copy-done, bf16[1024,768]{1,0:T(8,128)(2,1)} %get-tuple-element.92.own_ref), custom_call_target="tpu_custom_call" | custom-call | flops 50000000 | bytes 1048576 | tf_op jit(solution)/shard_map/project_state/pallas_call | solution.py:978
  12.1 0.4 collective-permute-start.1
  12.6 1.1 collective-permute-done.2.blend_other_ref
  13.8 0.4 copy-done.21
  15.2 33.5 %layer.1 = (bf16[1024,512]{1,0:T(8,128)(2,1)}, bf16[8,4,256,128]{3,2,1,0:T(8,128)(2,1)}, bf16[8,32,1024]{2,1,0:T(8,128)(2,1)}, bf16[8,4,160,256]{3,2,1,0:T(8,128...) custom-call(s32[1,6]{1,0:T(1,128)} %lengths_ref.7, ...), custom_call_target="tpu_custom_call" | custom-call | flops 300000000 | bytes 1048576 | tf_op jit(solution)/shard_map/layer/pallas_call | solution.py:1009
  48.7 0.4 collective-permute-start.6
  49.3 2.4 %collective-permute-done.6 = bf16[2048,256]{1,0:T(8,128)(2,1)S(1)} collective-permute-done((bf16[2048,256]{1,0:T(8,128)(2,1)}, bf16[2048,256]{1,0:T(8,128)(2,1)S(1)}, u32[]{:S(2)}, u32[]{:S(2)}) %collective-permute-start.6) | collective-permute-done | bytes 1048608 | tf_op jit(solution)/shard_map/ppermute | solution.py:949
  51.7 1.5 add_convert_fusion.1
  53.2 1.6 add_convert_fusion
  54.8 2.9 %collective-permute-start.8 = (bf16[1024,256]{1,0:T(8,128)(2,1)S(1)}, bf16[1024,256]{1,0:T(8,128)(2,1)S(1)}, u32[]{:S(2)}, u32[]{:S(2)}) collective-permute-start(bf16[1024,256]{1,0:T(8,128)(2,1)S(1)} %add_convert_fusion.1), channel_id=1, source_target_pairs={{0,2},{2,0},{4,6},{6,4},{8,10},{10,8},{12,14},{14,12},{16,18},{18,... | collective-permute-start | bytes 1572872 | tf_op jit(solution)/shard_map/ppermute | solution.py:821
  57.7 1.5 collective-permute-start.9
  59.2 16.0 %mixer_backward.1 = (bf16[1024,512]{1,0:T(8,128)(2,1)}, bf16[1024,512]{1,0:T(8,128)(2,1)}, bf16[1024,512]{1,0:T(8,128)(2,1)}, bf16[832,128]{1,0:T(8,128)(2,1)}, f32[2,4,8,128]{3,2,1,0:T(8,128)}) custom-call(s32[1,6]{1,0:T(1,128)} %lengths_ref.7, bf16[1024,768]{1,0:T(8,128)(2,1)} %get-tuple-element.92.own_ref, bf16[1024,768]{1,0:T(8,128)(2,1)} %get-tuple-element.94.other_ref, ...), custom_call_target="tpu_custom_call" | custom-call | flops 200000000 | bytes 1048576 | tf_op jit(solution)/shard_map/mixer_backward/pallas_call | solution.py:1102
  75.4 1.4 add_convert_fusion.4
  77.0 0.7 copy-done.18
  77.7 0.5 collective-permute-start.11
  78.3 10.2 %finish.1 = (bf16[1024,1536]{1,0:T(8,128)(2,1)}, bf16[2112,256]{1,0:T(8,128)(2,1)}, bf16[2112,256]{1,0:T(8,128)(2,1)}) custom-call(s32[1,6]{1,0:T(1,128)} %lengths_ref.7, bf16[1024,768]{1,0:T(8,128)(2,1)} %get-tuple-element.92.own_ref, bf16[1024,768]{1,0:T(8,128)(2,1)} %get-tuple-element.94.other_ref, bf16[1024,512]{1,0:T(8,128)(2,1)} %get-tuple-element.93.normed_ref, ...), custom_call_target="tpu_custom_call" | custom-call | flops 80000000 | bytes 1048576 | tf_op jit(solution)/shard_map/finish/pallas_call | solution.py:1140
  88.5 0.8 copy-done.16
  89.3 1.3 fusion
  90.7 1.1 add_convert_fusion.14
  91.8 1.0 add_convert_fusion.15
  92.8 0.7 pad_maximum_fusion.6
  93.8 2.0 %collective-permute-start.14 = (bf16[528,256]{1,0:T(8,128)(2,1)S(1)}, bf16[528,256]{1,0:T(8,128)(2,1)S(1)}, u32[]{:S(2)}, u32[]{:S(2)}) collective-permute-start(bf16[528,256]{1,0:T(8,128)(2,1)S(1)} %add_convert_fusion.3), channel_id=1, source_target_pairs={{0,2},{2,0},{4,6},{6,4},{8,10},{10,8},{12,14},{14,12},{16,18},{18,... | collective-permute-start | bytes 811016 | tf_op jit(solution)/shard_map/ppermute | solution.py:821
  95.8 1.5 collective-permute-start.15
  97.3 1.6 collective-permute-start.16
  98.9 6.2 %input_grad.1 = bf16[1024,512]{1,0:T(8,128)(2,1)} custom-call(bf16[1024,1536]{1,0:T(8,128)(2,1)} %get-tuple-element.134.gproj_ref, bf16[1024,512]{1,0:T(8,128)(2,1)} %x_ref.7, bf16[1024,512]{1,0:T(8,128)(2,1)} %get-tuple-element.135.branch_ref, f32[1,512]{1,0:T(1,128)} %bitcast.16, bf16[3,512,256]{2,1,0:T(8,128)(2,1)} %bitcast.13, bf16[3,512,256]{2,1,0:T(8,128)(2,1)} %copy-done), custom_call_target="tpu_custom_call" | custom-call | flops 70000000 | bytes 1048576 | tf_op jit(solution)/shard_map/input_grad/pallas_call | solution.py:1182
  105.2 0.6 collective-permute-done.16
  105.8 1.2 add_convert_fusion.19
  107.2 2.7 %collective-permute-start.19 = (bf16[256,256]{1,0:T(8,128)(2,1)S(1)}, bf16[256,256]{1,0:T(8,128)(2,1)S(1)}, u32[]{:S(2)}, u32[]{:S(2)}) collective-permute-start(bf16[256,256]{1,0:T(8,128)(2,1)S(1)} %pad_maximum_fusion.10), channel_id=1, source_target_pairs={{0,16},{2,18},{4,20},{6,22},{8,24},{10,26},{12,28},{14,30},{16,0},... | collective-permute-start | bytes 393224 | tf_op jit(solution)/shard_map/ppermute | solution.py:821
  109.8 0.5 collective-permute-start.18
  110.4 0.5 collective-permute-start.17
  110.9 4.6 %collective-permute-done.19 = bf16[256,256]{1,0:T(8,128)(2,1)S(1)} collective-permute-done((bf16[256,256]{1,0:T(8,128)(2,1)S(1)}, bf16[256,256]{1,0:T(8,128)(2,1)S(1)}, u32[]{:S(2)}, u32[]{:S(2)}) %collective-permute-start.19) | collective-permute-done | bytes 131104 | tf_op jit(solution)/shard_map/ppermute | solution.py:821
  115.4 1.2 add_convert_fusion.17
  117.2 3.8 %collective-permute-start.20 = (bf16[528,256]{1,0:T(8,128)(2,1)S(1)}, bf16[528,256]{1,0:T(8,128)(2,1)S(1)}, u32[]{:S(2)}, u32[]{:S(2)}) collective-permute-start(bf16[528,256]{1,0:T(8,128)(2,1)S(1)} %pad_maximum_fusion.2), channel_id=1, source_target_pairs={{0,8},{2,10},{4,12},{6,14},{8,0},{10,2},{12,4},{14,6},{16,24},{18,... | collective-permute-start | bytes 811016 | tf_op jit(solution)/shard_map/ppermute | solution.py:821
  121.0 4.2 %collective-permute-done.21 = bf16[256,256]{1,0:T(8,128)(2,1)S(1)} collective-permute-done((bf16[256,256]{1,0:T(8,128)(2,1)S(1)}, bf16[256,256]{1,0:T(8,128)(2,1)S(1)}, u32[]{:S(2)}, u32[]{:S(2)}) %collective-permute-start.21) | collective-permute-done | bytes 131104 | tf_op jit(solution)/shard_map/ppermute | solution.py:821
  125.3 3.1 %collective-permute-done.20 = bf16[528,256]{1,0:T(8,128)(2,1)S(1)} collective-permute-done((bf16[528,256]{1,0:T(8,128)(2,1)S(1)}, bf16[528,256]{1,0:T(8,128)(2,1)S(1)}, u32[]{:S(2)}, u32[]{:S(2)}) %collective-permute-start.20) | collective-permute-done | bytes 270368 | tf_op jit(solution)/shard_map/ppermute | solution.py:821
  128.5 0.4 collective-permute-start.23
  128.9 3.2 %collective-permute-start.22 = (bf16[528,256]{1,0:T(8,128)(2,1)S(1)}, bf16[528,256]{1,0:T(8,128)(2,1)S(1)}, u32[]{:S(2)}, u32[]{:S(2)}) collective-permute-start(bf16[528,256]{1,0:T(8,128)(2,1)S(1)} %pad_maximum_fusion.3), channel_id=1, source_target_pairs={{0,16},{2,18},{4,20},{6,22},{8,24},{10,26},{12,28},{14,30},{16,0},... | collective-permute-start | bytes 811016 | tf_op jit(solution)/shard_map/ppermute | solution.py:821
  132.1 7.1 %layer_output.1 = bf16[1024,512]{1,0:T(8,128)(2,1)} custom-call(bf16[1024,512]{1,0:T(8,128)(2,1)} %x_ref.7, bf16[1024,512]{1,0:T(8,128)(2,1)} %get-tuple-element.150.mixed_ref, bf16[1024,2048]{1,0:T(8,128)(2,1)} %get-tuple-element.151.active_ref, bf16[256,512]{1,0:T(8,128)(2,1)} %wa_own_ref.3, bf16[256,512]{1,0:T(8,128)(2,1)} %copy-done.7, ...), custom_call_target="tpu_custom_call" | custom-call | flops 50000000 | bytes 1048576 | tf_op jit(solution)/shard_map/layer_output/pallas_call | solution.py:1168
  139.2 1.7 collective-permute-done.23
  141.1 2.0 %collective-permute-done.22 = bf16[528,256]{1,0:T(8,128)(2,1)S(1)} collective-permute-done((bf16[528,256]{1,0:T(8,128)(2,1)S(1)}, bf16[528,256]{1,0:T(8,128)(2,1)S(1)}, u32[]{:S(2)}, u32[]{:S(2)}) %collective-permute-start.22) | collective-permute-done | bytes 270368 | tf_op jit(solution)/shard_map/ppermute | solution.py:821
  143.1 0.8 collective-permute-start.24
  143.9 1.0 collective-permute-start.25
  144.9 0.9 collective-permute-start.26
  145.8 1.5 collective-permute-start.27
  147.3 1.0 collective-permute-done.24
  148.2 0.7 collective-permute-done.25
  149.0 2.5 %collective-permute-done.26 = bf16[512,256]{1,0:T(8,128)(2,1)S(1)} collective-permute-done((bf16[512,256]{1,0:T(8,128)(2,1)S(1)}, bf16[512,256]{1,0:T(8,128)(2,1)S(1)}, u32[]{:S(2)}, u32[]{:S(2)}) %collective-permute-start.26) | collective-permute-done | bytes 262176 | tf_op jit(solution)/shard_map/ppermute | solution.py:821
  151.7 2.9 %collective-permute-done.27 = bf16[512,256]{1,0:T(8,128)(2,1)S(1)} collective-permute-done((bf16[512,256]{1,0:T(8,128)(2,1)S(1)}, bf16[512,256]{1,0:T(8,128)(2,1)S(1)}, u32[]{:S(2)}, u32[]{:S(2)}) %collective-permute-start.27) | collective-permute-done | bytes 262176 | tf_op jit(solution)/shard_map/ppermute | solution.py:821
  154.7 1.7 collective-permute-start.30
  156.4 0.7 collective-permute-start.31
  157.1 0.6 collective-permute-start.28
  157.7 1.1 collective-permute-start.29
  158.8 0.6 pad_add_fusion.bits_ref
  159.5 9.7 %collective-permute-done.28.a_got_ref = bf16[528,256]{1,0:T(8,128)(2,1)S(1)} collective-permute-done((bf16[528,256]{1,0:T(8,128)(2,1)S(1)}, bf16[528,256]{1,0:T(8,128)(2,1)S(1)}, u32[]{:S(2)}, u32[]{:S(2)}) %collective-permute-start.28) | collective-permute-done | bytes 270368 | tf_op jit(solution)/shard_map/ppermute | solution.py:821
  169.2 0.7 copy-done.13
  169.9 0.7 copy-done.14
  170.6 2.7 %attention_output.1 = (f32[1536,256]{1,0:T(8,128)}, f32[256,512]{1,0:T(8,128)}, f32[1,512]{1,0:T(1,128)}, f32[1,512]{1,0:T(1,128)}, f32[2,4]{1,0:T(2,128)}) custom-call(s32[2]{0:T(128)} %pad_add_fusion.bits_ref, bf16[528,256]{1,0:T(8,128)(2,1)} %copy-done.4, bf16[528,256]{1,0:T(8,128)(2,1)} %copy-done.13, bf16[528,256]{1,0:T(8,128)(2,1)} %copy-done.5, ...), custom_call_target="tpu_custom_call" | custom-call | flops 30000000 | bytes 1048576 | tf_op jit(solution)/shard_map/attention_output/pallas_call | solution.py:1235
  173.3 0.8 copy-done.10
  174.0 0.8 copy-done.11
  174.8 3.7 %feed_output.1 = (f32[1024,512]{1,0:T(8,128)}, f32[512,1024]{1,0:T(8,128)}) custom-call(s32[2]{0:T(128)} %pad_add_fusion.bits_ref, bf16[1024,256]{1,0:T(8,128)(2,1)} %copy-done.2, bf16[1024,256]{1,0:T(8,128)(2,1)} %copy-done.10, bf16[1024,256]{1,0:T(8,128)(2,1)} %copy-done.3, bf16[1024,256]{1,0:T(8,128)(2,1)} %copy-done.11), custom_call_target="tpu_custom_call" | custom-call | flops 30000000 | bytes 1048576 | tf_op jit(solution)/shard_map/feed_output/pallas_call | solution.py:1227
  (93 shorter events, 3.6 us)
Async XLA Ops:
  0.6 13.2 %collective-permute-start.4 = (bf16[512,1024]{1,0:T(8,128)(2,1)}, bf16[512,1024]{1,0:T(8,128)(2,1)S(1)}, u32[]{:S(2)}, u32[]{:S(2)}) collective-permute-start(bf16[512,1024]{1,0:T(8,128)(2,1)} %wi_own_ref.1), channel_id=1, source_target_pairs={{0,1},{1,0},{2,3},{3,2},{4,5},{5,4},{6,7},{7,6},{8,9},{9,8},{10,11... | collective-permute-start | bytes 3145736 | tf_op jit(solution)/shard_map/ppermute | solution.py:949
  1.2 12.6 %collective-permute-start.5 = (bf16[1024,512]{1,0:T(8,128)(2,1)}, bf16[1024,512]{1,0:T(8,128)(2,1)S(1)}, u32[]{:S(2)}, u32[]{:S(2)}) collective-permute-start(bf16[1024,512]{1,0:T(8,128)(2,1)} %wo_own_ref.3), channel_id=1, source_target_pairs={{0,1},{1,0},{2,3},{3,2},{4,5},{5,4},{6,7},{7,6},{8,9},{9,8},{10,11... | collective-permute-start | bytes 3145736 | tf_op jit(solution)/shard_map/ppermute | solution.py:949
  1.2 5.1 %collective-permute-start = (bf16[3,512,256]{2,1,0:T(8,128)(2,1)}, bf16[3,512,256]{2,1,0:T(8,128)(2,1)S(1)}, u32[]{:S(2)}, u32[]{:S(2)}) collective-permute-start(bf16[3,512,256]{2,1,0:T(8,128)(2,1)} %bitcast.10), channel_id=1, source_target_pairs={{0,1},{1,0},{2,3},{3,2},{4,5},{5,4},{6,7},{7,6},{8,9},{9,8},{10,11... | collective-permute-start | bytes 2359304 | tf_op jit(solution)/shard_map/ppermute | solution.py:949
  1.7 12.0 %collective-permute-start.3 = (bf16[256,512]{1,0:T(8,128)(2,1)}, bf16[256,512]{1,0:T(8,128)(2,1)S(1)}, u32[]{:S(2)}, u32[]{:S(2)}) collective-permute-start(bf16[256,512]{1,0:T(8,128)(2,1)} %wa_own_ref.3), channel_id=1, source_target_pairs={{0,1},{1,0},{2,3},{3,2},{4,5},{5,4},{6,7},{7,6},{8,9},{9,8},{10,11... | collective-permute-start | bytes 786440 | tf_op jit(solution)/shard_map/ppermute | solution.py:949
  6.3 6.2 %copy-start.20 = (f32[2,4]{1,0:T(2,128)S(1)}, f32[2,4]{1,0:T(2,128)}, u32[]{:S(2)}) copy-start(f32[2,4]{1,0:T(2,128)} %blend_own_ref.3) | copy-start | bytes 100
  6.3 0.9 copy-start
  12.1 1.7 collective-permute-start.1
  12.5 1.1 collective-permute-start.2
  13.6 0.6 copy-start.21
  13.6 0.7 copy-start.7
  13.8 0.7 copy-start.19
  13.8 1.0 copy-start.6
  13.8 1.4 copy-start.1
  48.7 2.9 %collective-permute-start.6 = (bf16[2048,256]{1,0:T(8,128)(2,1)}, bf16[2048,256]{1,0:T(8,128)(2,1)S(1)}, u32[]{:S(2)}, u32[]{:S(2)}) collective-permute-start(bf16[2048,256]{1,0:T(8,128)(2,1)} %get-tuple-element.98), channel_id=1, source_target_pairs={{0,1},{1,0},{2,3},{3,2},{4,5},{5,4},{6,7},{7,6},{8,9},{9,8},{10,11... | collective-permute-start | bytes 3145736 | tf_op jit(solution)/shard_map/ppermute | solution.py:949
  49.2 4.0 %collective-permute-start.7 = (bf16[2048,256]{1,0:T(8,128)(2,1)}, bf16[2048,256]{1,0:T(8,128)(2,1)S(1)}, u32[]{:S(2)}, u32[]{:S(2)}) collective-permute-start(bf16[2048,256]{1,0:T(8,128)(2,1)} %get-tuple-element.100), channel_id=1, source_target_pairs={{0,1},{1,0},{2,3},{3,2},{4,5},{5,4},{6,7},{7,6},{8,9},{9,8},{10,11... | collective-permute-start | bytes 3145736 | tf_op jit(solution)/shard_map/ppermute | solution.py:949
  51.7 40.1 %copy-start.8 = (bf16[2048,256]{1,0:T(8,128)(2,1)}, bf16[2048,256]{1,0:T(8,128)(2,1)S(1)}, u32[]{:S(2)}) copy-start(bf16[2048,256]{1,0:T(8,128)(2,1)S(1)} %collective-permute-done.6) | copy-start | bytes 3145732
  53.2 22.2 %copy-start.9 = (bf16[2048,256]{1,0:T(8,128)(2,1)}, bf16[2048,256]{1,0:T(8,128)(2,1)S(1)}, u32[]{:S(2)}) copy-start(bf16[2048,256]{1,0:T(8,128)(2,1)S(1)} %collective-permute-done.7) | copy-start | bytes 3145732
  54.8 20.5 %collective-permute-start.8 = (bf16[1024,256]{1,0:T(8,128)(2,1)S(1)}, bf16[1024,256]{1,0:T(8,128)(2,1)S(1)}, u32[]{:S(2)}, u32[]{:S(2)}) collective-permute-start(bf16[1024,256]{1,0:T(8,128)(2,1)S(1)} %add_convert_fusion.1), channel_id=1, source_target_pairs={{0,2},{2,0},{4,6},{6,4},{8,10},{10,8},{12,14},{14,12},{16,18},{18,... | collective-permute-start | bytes 1572872 | tf_op jit(solution)/shard_map/ppermute | solution.py:821
  57.7 17.5 %collective-permute-start.9 = (bf16[1024,256]{1,0:T(8,128)(2,1)S(1)}, bf16[1024,256]{1,0:T(8,128)(2,1)}, u32[]{:S(2)}, u32[]{:S(2)}) collective-permute-start(bf16[1024,256]{1,0:T(8,128)(2,1)S(1)} %add_convert_fusion), channel_id=1, source_target_pairs={{0,4},{2,6},{4,0},{6,2},{8,12},{10,14},{12,8},{14,10},{16,20},{18,... | collective-permute-start | bytes 1572872 | tf_op jit(solution)/shard_map/ppermute | solution.py:821
  75.2 13.3 %copy-start.12 = (bf16[1024,256]{1,0:T(8,128)(2,1)}, bf16[1024,256]{1,0:T(8,128)(2,1)S(1)}, u32[]{:S(2)}) copy-start(bf16[1024,256]{1,0:T(8,128)(2,1)S(1)} %collective-permute-done.8) | copy-start | bytes 1572868
  75.3 1.7 collective-permute-start.10
  77.0 0.7 copy-start.18
  77.7 10.8 %collective-permute-start.11 = (bf16[512,256]{1,0:T(8,128)(2,1)S(1)}, bf16[512,256]{1,0:T(8,128)(2,1)S(1)}, u32[]{:S(2)}, u32[]{:S(2)}) collective-permute-start(bf16[512,256]{1,0:T(8,128)(2,1)S(1)} %get-tuple-element.124), channel_id=1, source_target_pairs={{0,4},{2,6},{4,0},{6,2},{8,12},{10,14},{12,8},{14,10},{16,20},{18,... | collective-permute-start | bytes 786440 | tf_op jit(solution)/shard_map/ppermute | solution.py:821
  78.2 10.3 %collective-permute-start.12 = (bf16[512,256]{1,0:T(8,128)(2,1)S(1)}, bf16[512,256]{1,0:T(8,128)(2,1)S(1)}, u32[]{:S(2)}, u32[]{:S(2)}) collective-permute-start(bf16[512,256]{1,0:T(8,128)(2,1)S(1)} %get-tuple-element.125), channel_id=1, source_target_pairs={{0,2},{2,0},{4,6},{6,4},{8,10},{10,8},{12,14},{14,12},{16,18},{18,... | collective-permute-start | bytes 786440 | tf_op jit(solution)/shard_map/ppermute | solution.py:821
  88.5 5.1 %copy-start.15 = (bf16[512,256]{1,0:T(8,128)(2,1)}, bf16[512,256]{1,0:T(8,128)(2,1)S(1)}, u32[]{:S(2)}) copy-start(bf16[512,256]{1,0:T(8,128)(2,1)S(1)} %collective-permute-done.11) | copy-start | bytes 786436
  88.5 0.8 copy-start.16
  89.3 4.2 %collective-permute-start.13 = (bf16[2112,256]{1,0:T(8,128)(2,1)}, bf16[2112,256]{1,0:T(8,128)(2,1)S(1)}, u32[]{:S(2)}, u32[]{:S(2)}) collective-permute-start(bf16[2112,256]{1,0:T(8,128)(2,1)} %get-tuple-element.127), channel_id=1, source_target_pairs={{0,1},{1,0},{2,3},{3,2},{4,5},{5,4},{6,7},{7,6},{8,9},{9,8},{10,11... | collective-permute-start | bytes 3244040 | tf_op jit(solution)/shard_map/ppermute | solution.py:949
  89.3 1.3 copy-start.17
  93.8 11.4 %collective-permute-start.14 = (bf16[528,256]{1,0:T(8,128)(2,1)S(1)}, bf16[528,256]{1,0:T(8,128)(2,1)S(1)}, u32[]{:S(2)}, u32[]{:S(2)}) collective-permute-start(bf16[528,256]{1,0:T(8,128)(2,1)S(1)} %add_convert_fusion.3), channel_id=1, source_target_pairs={{0,2},{2,0},{4,6},{6,4},{8,10},{10,8},{12,14},{14,12},{16,18},{18,... | collective-permute-start | bytes 811016 | tf_op jit(solution)/shard_map/ppermute | solution.py:821
  95.8 9.4 %collective-permute-start.15 = (bf16[528,256]{1,0:T(8,128)(2,1)S(1)}, bf16[528,256]{1,0:T(8,128)(2,1)S(1)}, u32[]{:S(2)}, u32[]{:S(2)}) collective-permute-start(bf16[528,256]{1,0:T(8,128)(2,1)S(1)} %add_convert_fusion.2), channel_id=1, source_target_pairs={{0,4},{2,6},{4,0},{6,2},{8,12},{10,14},{12,8},{14,10},{16,20},{18,... | collective-permute-start | bytes 811016 | tf_op jit(solution)/shard_map/ppermute | solution.py:821
  97.3 8.5 %collective-permute-start.16 = (bf16[512,256]{1,0:T(8,128)(2,1)}, bf16[512,256]{1,0:T(8,128)(2,1)}, u32[]{:S(2)}, u32[]{:S(2)}) collective-permute-start(bf16[512,256]{1,0:T(8,128)(2,1)} %pad_maximum_fusion.6), channel_id=1, source_target_pairs={{0,8},{2,10},{4,12},{6,14},{8,0},{10,2},{12,4},{14,6},{16,24},{18,... | collective-permute-start | bytes 786440 | tf_op jit(solution)/shard_map/ppermute | solution.py:821
  107.2 8.3 %collective-permute-start.19 = (bf16[256,256]{1,0:T(8,128)(2,1)S(1)}, bf16[256,256]{1,0:T(8,128)(2,1)S(1)}, u32[]{:S(2)}, u32[]{:S(2)}) collective-permute-start(bf16[256,256]{1,0:T(8,128)(2,1)S(1)} %pad_maximum_fusion.10), channel_id=1, source_target_pairs={{0,16},{2,18},{4,20},{6,22},{8,24},{10,26},{12,28},{14,30},{16,0},... | collective-permute-start | bytes 393224 | tf_op jit(solution)/shard_map/ppermute | solution.py:821
  109.8 6.9 %collective-permute-start.18 = (bf16[264,256]{1,0:T(8,128)(2,1)S(1)}, bf16[264,256]{1,0:T(8,128)(2,1)S(1)}, u32[]{:S(2)}, u32[]{:S(2)}) collective-permute-start(bf16[264,256]{1,0:T(8,128)(2,1)S(1)} %add_convert_fusion.12), channel_id=1, source_target_pairs={{0,2},{2,0},{4,6},{6,4},{8,10},{10,8},{12,14},{14,12},{16,18},{18,... | collective-permute-start | bytes 405512 | tf_op jit(solution)/shard_map/ppermute | solution.py:821
  110.4 6.4 %collective-permute-start.17 = (bf16[264,256]{1,0:T(8,128)(2,1)S(1)}, bf16[264,256]{1,0:T(8,128)(2,1)S(1)}, u32[]{:S(2)}, u32[]{:S(2)}) collective-permute-start(bf16[264,256]{1,0:T(8,128)(2,1)S(1)} %add_convert_fusion.13), channel_id=1, source_target_pairs={{0,4},{2,6},{4,0},{6,2},{8,12},{10,14},{12,8},{14,10},{16,20},{18,... | collective-permute-start | bytes 405512 | tf_op jit(solution)/shard_map/ppermute | solution.py:821
  116.9 8.3 %collective-permute-start.21 = (bf16[256,256]{1,0:T(8,128)(2,1)S(1)}, bf16[256,256]{1,0:T(8,128)(2,1)S(1)}, u32[]{:S(2)}, u32[]{:S(2)}) collective-permute-start(bf16[256,256]{1,0:T(8,128)(2,1)S(1)} %pad_maximum_fusion.11), channel_id=1, source_target_pairs={{0,16},{2,18},{4,20},{6,22},{8,24},{10,26},{12,28},{14,30},{16,0},... | collective-permute-start | bytes 393224 | tf_op jit(solution)/shard_map/ppermute | solution.py:821
  117.2 11.1 %collective-permute-start.20 = (bf16[528,256]{1,0:T(8,128)(2,1)S(1)}, bf16[528,256]{1,0:T(8,128)(2,1)S(1)}, u32[]{:S(2)}, u32[]{:S(2)}) collective-permute-start(bf16[528,256]{1,0:T(8,128)(2,1)S(1)} %pad_maximum_fusion.2), channel_id=1, source_target_pairs={{0,8},{2,10},{4,12},{6,14},{8,0},{10,2},{12,4},{14,6},{16,24},{18,... | collective-permute-start | bytes 811016 | tf_op jit(solution)/shard_map/ppermute | solution.py:821
  128.5 12.5 %collective-permute-start.23 = (bf16[512,256]{1,0:T(8,128)(2,1)S(1)}, bf16[512,256]{1,0:T(8,128)(2,1)S(1)}, u32[]{:S(2)}, u32[]{:S(2)}) collective-permute-start(bf16[512,256]{1,0:T(8,128)(2,1)S(1)} %pad_maximum_fusion.7), channel_id=1, source_target_pairs={{0,8},{2,10},{4,12},{6,14},{8,0},{10,2},{12,4},{14,6},{16,24},{18,... | collective-permute-start | bytes 786440 | tf_op jit(solution)/shard_map/ppermute | solution.py:821
  128.9 14.2 %collective-permute-start.22 = (bf16[528,256]{1,0:T(8,128)(2,1)S(1)}, bf16[528,256]{1,0:T(8,128)(2,1)S(1)}, u32[]{:S(2)}, u32[]{:S(2)}) collective-permute-start(bf16[528,256]{1,0:T(8,128)(2,1)S(1)} %pad_maximum_fusion.3), channel_id=1, source_target_pairs={{0,16},{2,18},{4,20},{6,22},{8,24},{10,26},{12,28},{14,30},{16,0},... | collective-permute-start | bytes 811016 | tf_op jit(solution)/shard_map/ppermute | solution.py:821
  143.1 5.1 %collective-permute-start.24 = (bf16[264,256]{1,0:T(8,128)(2,1)S(1)}, bf16[264,256]{1,0:T(8,128)(2,1)S(1)}, u32[]{:S(2)}, u32[]{:S(2)}) collective-permute-start(bf16[264,256]{1,0:T(8,128)(2,1)S(1)} %get-tuple-element.160), channel_id=1, source_target_pairs={{0,4},{2,6},{4,0},{6,2},{8,12},{10,14},{12,8},{14,10},{16,20},{18,... | collective-permute-start | bytes 405512 | tf_op jit(solution)/shard_map/ppermute | solution.py:821
  143.9 5.0 %collective-permute-start.25 = (bf16[264,256]{1,0:T(8,128)(2,1)S(1)}, bf16[264,256]{1,0:T(8,128)(2,1)S(1)}, u32[]{:S(2)}, u32[]{:S(2)}) collective-permute-start(bf16[264,256]{1,0:T(8,128)(2,1)S(1)} %get-tuple-element.161), channel_id=1, source_target_pairs={{0,2},{2,0},{4,6},{6,4},{8,10},{10,8},{12,14},{14,12},{16,18},{18,... | collective-permute-start | bytes 405512 | tf_op jit(solution)/shard_map/ppermute | solution.py:821
  144.9 6.6 %collective-permute-start.26 = (bf16[512,256]{1,0:T(8,128)(2,1)S(1)}, bf16[512,256]{1,0:T(8,128)(2,1)S(1)}, u32[]{:S(2)}, u32[]{:S(2)}) collective-permute-start(bf16[512,256]{1,0:T(8,128)(2,1)S(1)} %pad_maximum_fusion.8), channel_id=1, source_target_pairs={{0,4},{2,6},{4,0},{6,2},{8,12},{10,14},{12,8},{14,10},{16,20},{18,... | collective-permute-start | bytes 786440 | tf_op jit(solution)/shard_map/ppermute | solution.py:821
  145.8 8.8 %collective-permute-start.27 = (bf16[512,256]{1,0:T(8,128)(2,1)S(1)}, bf16[512,256]{1,0:T(8,128)(2,1)S(1)}, u32[]{:S(2)}, u32[]{:S(2)}) collective-permute-start(bf16[512,256]{1,0:T(8,128)(2,1)S(1)} %pad_maximum_fusion.9), channel_id=1, source_target_pairs={{0,2},{2,0},{4,6},{6,4},{8,10},{10,8},{12,14},{14,12},{16,18},{18,... | collective-permute-start | bytes 786440 | tf_op jit(solution)/shard_map/ppermute | solution.py:821
  149.0 8.1 %copy-start.4 = (bf16[528,256]{1,0:T(8,128)(2,1)}, bf16[528,256]{1,0:T(8,128)(2,1)S(1)}, u32[]{:S(2)}) copy-start(bf16[528,256]{1,0:T(8,128)(2,1)S(1)} %pad_maximum_fusion.4.a_mine_ref) | copy-start | bytes 811012
  149.0 8.7 %copy-start.5 = (bf16[528,256]{1,0:T(8,128)(2,1)}, bf16[528,256]{1,0:T(8,128)(2,1)S(1)}, u32[]{:S(2)}) copy-start(bf16[528,256]{1,0:T(8,128)(2,1)S(1)} %pad_maximum_fusion.5.b_mine_ref) | copy-start | bytes 811012
  151.7 21.6 %copy-start.2 = (bf16[1024,256]{1,0:T(8,128)(2,1)}, bf16[1024,256]{1,0:T(8,128)(2,1)S(1)}, u32[]{:S(2)}) copy-start(bf16[1024,256]{1,0:T(8,128)(2,1)S(1)} %pad_maximum_fusion.out_mine_ref) | copy-start | bytes 1572868
  154.7 18.6 %copy-start.3 = (bf16[1024,256]{1,0:T(8,128)(2,1)}, bf16[1024,256]{1,0:T(8,128)(2,1)S(1)}, u32[]{:S(2)}) copy-start(bf16[1024,256]{1,0:T(8,128)(2,1)S(1)} %pad_maximum_fusion.1.in_mine_ref) | copy-start | bytes 1572868
  154.7 18.6 %collective-permute-start.30 = (bf16[1024,256]{1,0:T(8,128)(2,1)S(1)}, bf16[1024,256]{1,0:T(8,128)(2,1)S(1)}, u32[]{:S(2)}, u32[]{:S(2)}) collective-permute-start(bf16[1024,256]{1,0:T(8,128)(2,1)S(1)} %pad_maximum_fusion.out_mine_ref), channel_id=1, source_target_pairs={{0,2},{2,0},{4,6},{6,4},{8,10},{10,8},{12,14},{14,12},{16,18},{18,... | collective-permute-start | bytes 1572872 | tf_op jit(solution)/shard_map/ppermute | solution.py:821
  156.4 16.9 %collective-permute-start.31 = (bf16[1024,256]{1,0:T(8,128)(2,1)S(1)}, bf16[1024,256]{1,0:T(8,128)(2,1)S(1)}, u32[]{:S(2)}, u32[]{:S(2)}) collective-permute-start(bf16[1024,256]{1,0:T(8,128)(2,1)S(1)} %pad_maximum_fusion.1.in_mine_ref), channel_id=1, source_target_pairs={{0,4},{2,6},{4,0},{6,2},{8,12},{10,14},{12,8},{14,10},{16,20},{18,... | collective-permute-start | bytes 1572872 | tf_op jit(solution)/shard_map/ppermute | solution.py:821
  157.1 12.1 %collective-permute-start.28 = (bf16[528,256]{1,0:T(8,128)(2,1)S(1)}, bf16[528,256]{1,0:T(8,128)(2,1)S(1)}, u32[]{:S(2)}, u32[]{:S(2)}) collective-permute-start(bf16[528,256]{1,0:T(8,128)(2,1)S(1)} %pad_maximum_fusion.4.a_mine_ref), channel_id=1, source_target_pairs={{0,2},{2,0},{4,6},{6,4},{8,10},{10,8},{12,14},{14,12},{16,18},{18,... | collective-permute-start | bytes 811016 | tf_op jit(solution)/shard_map/ppermute | solution.py:821
  157.7 11.5 %collective-permute-start.29 = (bf16[528,256]{1,0:T(8,128)(2,1)S(1)}, bf16[528,256]{1,0:T(8,128)(2,1)S(1)}, u32[]{:S(2)}, u32[]{:S(2)}) collective-permute-start(bf16[528,256]{1,0:T(8,128)(2,1)S(1)} %pad_maximum_fusion.5.b_mine_ref), channel_id=1, source_target_pairs={{0,4},{2,6},{4,0},{6,2},{8,12},{10,14},{12,8},{14,10},{16,20},{18,... | collective-permute-start | bytes 811016 | tf_op jit(solution)/shard_map/ppermute | solution.py:821
  169.2 0.7 copy-start.13
  169.9 0.7 copy-start.14
  173.2 0.8 copy-start.10
  174.0 0.8 copy-start.11

commit v4 on v3

--- a/solution.py
+++ b/solution.py
@@ -50,6 +50,16 @@
     return lax.optimization_barrier(values)
 
 
+class Copies:
+    def __init__(self, sems):
+        self.sems = sems
+        self.used = 0
+
+    def make(self, source, target):
+        self.used += 1
+        return pltpu.make_async_copy(source, target, self.sems.at[self.used - 1])
+
+
 def document_ends(lengths_ref, rows):
     end = -lax.axis_index("tensor") * rows
     ends = [end]
@@ -90,10 +100,19 @@
 PACKET = 4 * (128 + 16) + 8 * HALO
 
 
+def packed_state(state):
+    return jnp.concatenate([state[:64] + state[64:128], state[128:192] + state[192:]], axis=0).astype(BF)
+
+
+def unpacked_state(packed, diag):
+    one, two = packed[:64], packed[64:]
+    state = jnp.concatenate([one, one, two, two], axis=0)
+    return jnp.where(diag, state, jnp.zeros_like(state))
+
+
 def pack(packet_ref, pair, state, total):
     base = 144 * pair
-    packet_ref[base : base + 64] = (state[:64] + state[64:128]).astype(BF)
-    packet_ref[base + 64 : base + 128] = (state[128:192] + state[192:]).astype(BF)
+    packet_ref[base : base + 128] = packed_state(state)
     packet_ref[base + 128 : base + 144] = jnp.broadcast_to(total, (16, 128)).astype(BF)
 
 
@@ -104,9 +123,7 @@
 
 def unpack(packet_ref, pair, diag):
     base = 144 * pair
-    one = packet_ref[base : base + 64].astype(F32)
-    two = packet_ref[base + 64 : base + 128].astype(F32)
-    state = jnp.where(diag, jnp.concatenate([one, one, two, two], axis=0), 0.0)
+    state = unpacked_state(packet_ref[base : base + 128].astype(F32), diag)
     return state, packet_ref[base + 128 : base + 136].astype(F32)
 
 
@@ -134,21 +151,17 @@
     project(normed_ref[...], w_ref, out_ref)
     member_from = start_at(document_ends(lengths_ref, rows), rows - 1)
     member = iota((rows, 1), 0) >= member_from
+    ks, vs = [heads_of(own_ref, out_ref, kind) for kind in (1, 2)]
+    wide = [jnp.where(member, k.astype(F32), 0.0) for k in ks]
+    ones = [jnp.where(member, first_feature(k).astype(F32), 0.0) for k in wide]
+    features = each(lambda k, one: jnp.concatenate([one.astype(BF), second_feature(k)], axis=1), wide, ones)
+    states = each(tn, features, vs)
     diag = pair_diag(256, 128)
-    for pair in range(4):
-        src = own_ref if pair < 2 else out_ref
-        col = 128 * (pair % 2)
+    for pair in PAIRS:
         slot = (pair + 2) % 4
-        keys = src[:, 256 + col : 384 + col]
-        values = src[:, 512 + col : 640 + col]
-        wide = jnp.where(member, keys.astype(F32), 0.0)
-        one = jnp.where(member, first_feature(wide).astype(F32), 0.0)
-        two = second_feature(wide)
-        features = jnp.concatenate([one.astype(BF), two], axis=1)
-        state = jnp.where(diag, tn(features, values), 0.0)
-        pack(packet_ref, slot, state, jnp.sum(one, axis=0, keepdims=True))
-        pack_halo(packet_ref, 0, slot, keys[rows - HALO :])
-        pack_halo(packet_ref, 1, slot, values[rows - HALO :])
+        pack(packet_ref, slot, jnp.where(diag, states[pair], 0.0), jnp.sum(ones[pair], axis=0, keepdims=True))
+        pack_halo(packet_ref, 0, slot, ks[pair][rows - HALO :])
+        pack_halo(packet_ref, 1, slot, vs[pair][rows - HALO :])
 
 
 def block_masks(ends, first):
@@ -276,14 +289,12 @@
     lengths_ref,
     own_ref,
     other_ref,
-    packet_ref,
     blend_own_ref,
     blend_other_ref,
     state_out_ref,
     prev_out_ref,
     near_ref,
     weights_ref,
-    features_ref,
     sums_ref,
     total_ref,
     state_ref,
@@ -291,13 +302,6 @@
     prev_ref,
 ):
     first = index * BLOCK
-
-    @pl.when(index == 0)
-    def _():
-        for pair in PAIRS:
-            state_ref[pair], sum_ref[pair] = unpack(packet_ref, pair, pair_diag(256, 128))
-            prev_ref[:, pair_lanes(pair)] = unpack_halo(packet_ref, 0, pair)
-            prev_ref[:, value_lanes(pair)] = unpack_halo(packet_ref, 1, pair)
 
     masks = block_masks(document_ends(lengths_ref, total_rows), first)
     banded, causal, causal_q, count, carried, member, keep = masks
@@ -325,13 +329,11 @@
     ]
     outs = each(lambda out, term: pick_heads(out) + term, outs, inter)
     for pair in PAIRS:
-        state_out_ref[0, pair] = state_low[pair]
+        state_out_ref[0, pair] = packed_state(states[pair])
         near_ref[0, pair] = front.near[pair].astype(BF)
         weights_ref[0, pair] = front.weights[pair][HALO:]
-        features_ref[0, pair, 0] = front.q_scaled[pair]
-        features_ref[0, pair, 1] = front.k_both[pair]
-        sums_ref[:, pair_lanes(pair)] = front.sums[pair]
-        total_ref[:, pair_lanes(pair)] = 1.0 / front.total[pair]
+        sums_ref[:, pair_lanes(pair)] = front.sums[pair].astype(BF)
+        total_ref[:, pair_lanes(pair)] = (1.0 / front.total[pair]).astype(BF)
         state_ref[pair] = jnp.where(keep, states[pair], 0.0) + jnp.where(diag, added[pair], 0.0)
         sum_ref[pair] = jnp.broadcast_to(front.sums[pair][BLOCK - 1 : BLOCK], (8, 128))
         prev_ref[:, pair_lanes(pair)] = ks[pair][BLOCK - HALO :]
@@ -340,38 +342,30 @@
     return jnp.concatenate(outs, axis=1).astype(BF)
 
 
-def mixer_backward_kernel(
+def mixer_backward_block(
+    index,
     total_rows,
     lengths_ref,
+    blend_own_ref,
+    blend_other_ref,
     own_ref,
     other_ref,
     state_ref,
     prev_ref,
     near_ref,
     weights_ref,
-    features_ref,
     sums_ref,
     total_ref,
-    blend_own_ref,
-    blend_other_ref,
     grad_ref,
     gq_ref,
     gk_ref,
     gv_ref,
-    packet_ref,
     blend_out_ref,
     halo_ref,
     back_state_ref,
     back_sum_ref,
 ):
-    step = pl.program_id(0)
-    first = (pl.num_programs(0) - 1 - step) * BLOCK
-
-    @pl.when(step == 0)
-    def _():
-        for ref in (halo_ref, back_state_ref, back_sum_ref, blend_out_ref):
-            ref[...] = jnp.zeros_like(ref)
-
+    first = index * BLOCK
     ends = document_ends(lengths_ref, total_rows)
     blends = pair_blends(blend_own_ref, blend_other_ref)
     row_places = first + iota((1, 256), 1) % BLOCK
@@ -390,12 +384,37 @@
     qs, ks, vs = [heads_of(own_ref, other_ref, kind) for kind in range(3)]
     prev = prev_ref[0]
     grads = [grad_ref[:, pair_lanes(pair)] for pair in PAIRS]
-    states = [state_ref[0, pair] for pair in PAIRS]
+    states = [unpacked_state(state_ref[0, pair], diag) for pair in PAIRS]
     backs = [back_state_ref[pair] for pair in PAIRS]
     back_sums = [back_sum_ref[pair][0:1] for pair in PAIRS]
     nears = [near_ref[0, pair] for pair in PAIRS]
-    q_scaled = [features_ref[0, pair, 0] for pair in PAIRS]
-    k_both = [features_ref[0, pair, 1] for pair in PAIRS]
+    wide_ks = [k.astype(F32) for k in ks]
+    wide_qs = [q.astype(F32) for q in qs]
+    raised_k = [jnp.exp(jnp.minimum(k, 0.0)) for k in wide_ks]
+    raised_q = [jnp.exp(jnp.minimum(q, 0.0)) for q in wide_qs]
+    tanh_ks = [jnp.tanh(k) for k in wide_ks]
+    tanh_qs = [jnp.tanh(q) for q in wide_qs]
+    k_both = each(
+        lambda k, raised, t: jnp.concatenate(
+            [jnp.where(k > 0, k + 1.0, raised).astype(BF), t.astype(BF)], axis=1
+        ),
+        wide_ks,
+        raised_k,
+        tanh_ks,
+    )
+    q_one = each(lambda q, raised: jnp.where(q > 0, q + 1.0, raised).astype(BF).astype(F32), wide_qs, raised_q)
+    inverse_total = [total_ref[:, pair_lanes(pair)].astype(F32) for pair in PAIRS]
+    ratio_one = each(lambda blend, total: blend[0] * total, blends, inverse_total)
+    ratio_two = [blend[1] * inverse for blend in blends]
+    q_scaled = each(
+        lambda one, ratio, t, other: jnp.concatenate(
+            [(one * ratio).astype(BF), (t.astype(BF).astype(F32) * other).astype(BF)], axis=1
+        ),
+        q_one,
+        ratio_one,
+        tanh_qs,
+        ratio_two,
+    )
     g_stack = each(stack_heads, grads)
     v_window = [jnp.concatenate([prev[:, value_lanes(pair)], vs[pair]], axis=0) for pair in PAIRS]
     grad_weights = each(nt, v_window, g_stack)
@@ -415,11 +434,9 @@
         inner,
     )
     up = each(lambda up, inter: pick_heads(up) + inter, up, up_inter)
-    q_first = each(lambda q: jnp.where(q > 0, q + 1.0, jnp.exp(jnp.minimum(q, 0.0))), [q.astype(F32) for q in qs])
-    inverse_total = [total_ref[:, pair_lanes(pair)] for pair in PAIRS]
     mean_one = each(
-        lambda q, up, total: nn((q.astype(BF).astype(F32) * up[:, :128]).astype(BF), ones_diag) * total,
-        q_first,
+        lambda q, up, total: nn((q * up[:, :128]).astype(BF), ones_diag) * total,
+        q_one,
         up,
         inverse_total,
     )
@@ -436,10 +453,9 @@
     for pair in PAIRS:
         lanes, values = pair_lanes(pair), value_lanes(pair)
         up_one, up_two = up[pair][:, :128], up[pair][:, 128:]
-        tanh_q = jnp.tanh(qs[pair].astype(F32))
-        slope_q = jnp.minimum(q_first[pair], 1.0)
+        tanh_q, slope_q = tanh_qs[pair], raised_q[pair]
         up_two = up_two * inverse
-        grad_one = blends[pair][0] * inverse_total[pair] * (up_one - mean_one[pair] * sums_ref[:, lanes])
+        grad_one = ratio_one[pair] * (up_one - mean_one[pair] * sums_ref[:, lanes].astype(F32))
         grad_two = blends[pair][1] * up_two
         gq = pick_heads(gq_near[pair]) * 0.125 + grad_one * slope_q + grad_two * (1.0 - tanh_q * tanh_q)
         gq_ref[:, lanes] = gq.astype(BF)
@@ -451,9 +467,7 @@
         dfeat_all = dfeat[pair] + dfeat_far[pair]
         d_one = dfeat_all[:, :128] - mean_back[pair] - jnp.where(member, back_sums[pair], 0.0)
         d_two = dfeat_all[:, 128:]
-        wide_k = ks[pair].astype(F32)
-        tanh_k = jnp.tanh(wide_k)
-        slope_k = jnp.exp(jnp.minimum(wide_k, 0.0))
+        tanh_k, slope_k = tanh_ks[pair], raised_k[pair]
         gk = dk[pair][HALO:] + d_one * slope_k + d_two * (1.0 - tanh_k * tanh_k)
         gk_ref[: BLOCK - HALO, lanes] = gk[: BLOCK - HALO].astype(BF)
         gk_ref[BLOCK - HALO :, lanes] = (gk[BLOCK - HALO :] + halo_ref[:, lanes]).astype(BF)
@@ -467,7 +481,40 @@
             jnp.where(keep, back_sums[pair], 0.0) + added_sum, (8, 128)
         )
 
-    @pl.when(first == 0)
+
+STEP_BLOCKS = 2
+
+
+def mixer_backward_kernel(lengths_ref, blend_own_ref, blend_other_ref, *refs):
+    inputs, outputs = refs[:9], refs[9:12]
+    packet_ref, blend_out_ref, halo_ref, back_state_ref, back_sum_ref = refs[12:]
+    step = pl.program_id(0)
+    steps = pl.num_programs(0)
+
+    @pl.when(step == 0)
+    def _():
+        for ref in (halo_ref, back_state_ref, back_sum_ref, blend_out_ref):
+            ref[...] = jnp.zeros_like(ref)
+
+    for sub in reversed(range(STEP_BLOCKS)):
+        views = []
+        for ref in inputs + outputs:
+            unit = ref.shape[0] // STEP_BLOCKS
+            views.append(ref.at[sub * unit : sub * unit + unit])
+        mixer_backward_block(
+            (steps - 1 - step) * STEP_BLOCKS + sub,
+            steps * STEP_BLOCKS * BLOCK,
+            lengths_ref,
+            blend_own_ref,
+            blend_other_ref,
+            *views,
+            blend_out_ref,
+            halo_ref,
+            back_state_ref,
+            back_sum_ref,
+        )
+
+    @pl.when(step == steps - 1)
     def _():
         for pair in PAIRS:
             slot = (pair + 2) % 4
@@ -483,104 +530,118 @@
     blocks,
     parts,
     lengths_ref,
-    own_ref,
-    other_ref,
-    packet_ref,
     blend_own_ref,
     blend_other_ref,
-    x_ref,
-    cot_ref,
+    packet_ref,
     gain_ref,
     wa_own_ref,
     wa_other_ref,
-    wi_own_ref,
-    wi_other_ref,
-    wo_own_ref,
-    wo_other_ref,
-    mixed_out_ref,
-    state_out_ref,
-    prev_out_ref,
-    near_ref,
-    weights_ref,
-    features_ref,
-    sums_ref,
-    total_ref,
-    active_ref,
+    own_hbm,
+    other_hbm,
+    x_hbm,
+    cot_hbm,
+    wi_own_hbm,
+    wi_other_hbm,
+    wo_own_hbm,
+    wo_other_hbm,
     branch_ref,
     gmix_ref,
     ggain_ref,
     attn_own_ref,
     attn_sent_ref,
-    out_own_ref,
-    in_own_ref,
-    out_sent_ref,
-    in_sent_ref,
+    mixed_hbm,
+    state_hbm,
+    prev_hbm,
+    near_hbm,
+    weights_hbm,
+    sums_hbm,
+    total_hbm,
+    active_hbm,
+    out_own_hbm,
+    in_own_hbm,
+    out_sent_hbm,
+    in_sent_hbm,
+    own_ref,
+    other_ref,
+    x_ref,
+    grad_ref,
+    wi_ref,
+    wo_ref,
+    mixed_ref,
+    state_out_ref,
+    prev_out_ref,
+    near_ref,
+    weights_ref,
+    sums_ref,
+    total_ref,
+    active_ref,
+    stack_ref,
     state_ref,
     sum_ref,
     prev_ref,
-    mixed_ref,
     y_ref,
     r_ref,
     normed_ref,
     normed_turned_ref,
-    grad_ref,
     grad_turned_ref,
     back_ref,
-    wi_ref,
-    wo_ref,
-    stack_ref,
-    load_sems,
-    store_sems,
+    sems,
 ):
-    step = pl.program_id(0)
-    width = x_ref.shape[1]
+    copies = Copies(sems)
+    rows, width = x_ref.shape
     heads = wa_own_ref.shape[0]
     units = wo_ref.shape[1]
     chunk_units = units // parts
-    loads = [
-        pltpu.make_async_copy(source, target, load_sems.at[place])
-        for place, (source, target) in enumerate(
-            (
-                (wi_own_ref, wi_ref.at[0]),
-                (wo_own_ref, wo_ref.at[0]),
-                (wi_other_ref, wi_ref.at[1]),
-                (wo_other_ref, wo_ref.at[1]),
-            )
+    tokens = ((own_hbm, own_ref), (other_hbm, other_ref), (x_hbm, x_ref), (cot_hbm, grad_ref))
+    first_loads = [copies.make(source.at[:BLOCK], target.at[:BLOCK]) for source, target in tokens]
+    later_loads = [copies.make(source.at[BLOCK:], target.at[BLOCK:]) for source, target in tokens]
+    weight_loads = [
+        copies.make(source, target)
+        for source, target in (
+            (wi_own_hbm, wi_ref.at[0]),
+            (wo_own_hbm, wo_ref.at[0]),
+            (wi_other_hbm, wi_ref.at[1]),
+            (wo_other_hbm, wo_ref.at[1]),
         )
     ]
-
-    @pl.when(step == 0)
-    def _():
-        for load in loads:
-            load.start()
-        back_ref[...] = jnp.zeros_like(back_ref)
-
-    @pl.when(step < blocks)
-    def _():
+    for load in first_loads + later_loads + weight_loads:
+        load.start()
+    for pair in PAIRS:
+        state_ref[pair], sum_ref[pair] = unpack(packet_ref, pair, pair_diag(256, 128))
+        prev_ref[:, pair_lanes(pair)] = unpack_halo(packet_ref, 0, pair)
+        prev_ref[:, value_lanes(pair)] = unpack_halo(packet_ref, 1, pair)
+    back_ref[...] = jnp.zeros_like(back_ref)
+    for load in first_loads:
+        load.wait()
+
+    def block(step, _):
+        @pl.when(step == 1)
+        def _():
+            for load in later_loads:
+                load.wait()
+
+        here = pl.ds(pl.multiple_of(step * BLOCK, BLOCK), BLOCK)
+        only_here = pl.ds(step, 1)
         mixed = mixer_forward_block(
             step,
-            blocks * BLOCK,
+            rows,
             lengths_ref,
-            own_ref,
-            other_ref,
-            packet_ref,
+            own_ref.at[here],
+            other_ref.at[here],
             blend_own_ref,
             blend_other_ref,
-            state_out_ref,
-            prev_out_ref,
-            near_ref,
-            weights_ref,
-            features_ref,
-            sums_ref,
-            total_ref,
+            state_out_ref.at[only_here],
+            prev_out_ref.at[only_here],
+            near_ref.at[only_here],
+            weights_ref.at[only_here],
+            sums_ref.at[here],
+            total_ref.at[here],
             state_ref,
             sum_ref,
             prev_ref,
         )
-        here = pl.ds(pl.multiple_of(step * BLOCK, BLOCK), BLOCK)
-        mixed_out_ref[...] = mixed
         mixed_ref[here, :] = mixed
-        hidden = x_ref[...].astype(F32)
+        hidden = x_ref[here, :].astype(F32)
         hidden = hidden + nn(mixed[:, :heads], wa_own_ref[...]) + nn(mixed[:, heads:], wa_other_ref[...])
         r = lax.rsqrt(jnp.mean(hidden * hidden, axis=1, keepdims=True) + EPS)
         y = hidden * r
@@ -589,18 +650,49 @@
         normed = (y * gain_ref[...]).astype(BF)
         normed_ref[here, :] = normed
         normed_turned_ref[:, here] = normed.T
-        grad_ref[here, :] = cot_ref[...]
-        grad_turned_ref[:, here] = cot_ref[...].T
-
-    @pl.when(step == blocks)
-    def _():
-        for load in loads:
-            load.wait()
-
-    @pl.when(step >= blocks)
-    def _():
-        half = (step - blocks) // parts
-        place = (step - blocks) % parts
+        grad_turned_ref[:, here] = grad_ref[here, :].T
+        return 0
+
+    def some_blocks(step, _):
+        for sub in range(STEP_BLOCKS):
+            block(step * STEP_BLOCKS + sub, 0)
+        return 0
+
+    lax.fori_loop(0, blocks // STEP_BLOCKS, some_blocks, 0)
+    stores = [
+        copies.make(source, target)
+        for source, target in (
+            (mixed_ref, mixed_hbm),
+            (state_out_ref, state_hbm),
+            (prev_out_ref, prev_hbm),
+            (near_ref, near_hbm),
+            (weights_ref, weights_hbm),
+            (sums_ref, sums_hbm),
+            (total_ref, total_hbm),
+        )
+    ]
+    for store in stores:
+        store.start()
+    for load in weight_loads:
+        load.wait()
+    chunk_stores = []
+    for late in range(2 * parts):
+        half, place = late // parts, late % parts
+        out_target, in_target = ((out_own_hbm, in_own_hbm), (out_sent_hbm, in_sent_hbm))[half]
+        spots = [(0, out_target, units * side + chunk_units * place, chunk_units) for side in range(width // LANES)]
+        count = width * chunk_units // LANES
+        spots.append((1, in_target, count * place, count))
+        columns = pl.ds(late * chunk_units, chunk_units)
+        chunk_stores.append(
+            [
+                copies.make(stack_ref.at[half, kind, pl.ds(row, count), :], target.at[pl.ds(row, count), :])
+                for kind, target, row, count in spots
+            ]
+            + [copies.make(active_ref.at[:, columns], active_hbm.at[:, columns])]
+        )
+
+    def chunk(late, _):
+        half, place = late // parts, late % parts
         normed = normed_ref[...]
         grad = grad_ref[...]
         first = pl.multiple_of(place * chunk_units, chunk_units)
@@ -610,13 +702,14 @@
         us = [nn(normed, wi[:, span]) for span in spans]
         gacts = [nt(grad, wo[span, :]) for span in spans]
         gpres = []
-        for piece, span in enumerate(spans):
+        for piece in range(len(spans)):
             u = us[piece]
             square = u * u
             t = jnp.tanh(u * (GELU_A + (GELU_A * GELU_B) * square))
             gate = 0.5 + 0.5 * t
             active = (u * gate).astype(BF)
-            active_ref[:, span] = active
+            column = pl.multiple_of(late * chunk_units + LANES * piece, LANES)
+            active_ref[:, pl.ds(column, LANES)] = active
             slope = gate + (u * (0.5 - 0.5 * t * t)) * (GELU_A + (3.0 * GELU_A * GELU_B) * square)
             gpre = (gacts[piece] * slope).astype(BF)
             gpres.append(gpre)
@@ -628,51 +721,32 @@
             row = pl.multiple_of(width * spot, LANES)
             stack_ref[half, 1, pl.ds(row, width), :] = nn(normed_turned_ref[...], gpre).astype(BF)
         back_ref[...] += nt(jnp.concatenate(gpres, axis=1), wi)
-
-    stores = []
-    for late in range(2 * parts):
-        half, place = late // parts, late % parts
-        out_target, in_target = ((out_own_ref, in_own_ref), (out_sent_ref, in_sent_ref))[half]
-        spots = [(0, out_target, units * side + chunk_units * place, chunk_units) for side in range(width // LANES)]
-        rows = width * chunk_units // LANES
-        spots.append((1, in_target, rows * place, rows))
-        stores.append(
-            [
-                pltpu.make_async_copy(
-                    stack_ref.at[half, kind, pl.ds(row, count), :],
-                    target.at[pl.ds(row, count), :],
-                    store_sems.at[late, number],
-                )
-                for number, (kind, target, row, count) in enumerate(spots)
-            ]
-        )
-
-    for late in range(2 * parts):
-
-        @pl.when(step == blocks + late)
-        def _(late=late):
-            for store in stores[late]:
-                store.start()
-
-    @pl.when(step == blocks + 2 * parts - 1)
-    def _():
-        back, y = back_ref[...], y_ref[...]
-        scaled = back * gain_ref[...]
-        mean = jnp.mean(scaled * y, axis=1, keepdims=True)
-        ghid = grad_ref[...].astype(F32) + r_ref[:, :1] * (scaled - y * mean)
-        branch = ghid.astype(BF)
-        branch_ref[...] = branch
-        gmix_ref[:, :heads] = nt(branch, wa_own_ref[...]).astype(BF)
-        gmix_ref[:, heads:] = nt(branch, wa_other_ref[...]).astype(BF)
-        ggain_ref[...] = jnp.broadcast_to(jnp.sum(back * y, axis=0, keepdims=True), ggain_ref.shape)
-        gattn = tn(mixed_ref[...], branch).astype(BF)
-        for half, ref in enumerate((attn_own_ref, attn_sent_ref)):
-            for side in range(width // LANES):
-                lanes = slice(LANES * side, LANES * side + LANES)
-                ref[heads * side : heads * side + heads] = gattn[heads * half : heads * half + heads, lanes]
-        for some in stores:
-            for store in some:
-                store.wait()
+        for number, some in enumerate(chunk_stores):
+
+            @pl.when(late == number)
+            def _(some=some):
+                for store in some:
+                    store.start()
+
+        return 0
+
+    lax.fori_loop(0, 2 * parts, chunk, 0)
+    back, y = back_ref[...], y_ref[...]
+    scaled = back * gain_ref[...]
+    mean = jnp.mean(scaled * y, axis=1, keepdims=True)
+    ghid = grad_ref[...].astype(F32) + r_ref[:, :1] * (scaled - y * mean)
+    branch = ghid.astype(BF)
+    branch_ref[...] = branch
+    gmix_ref[:, :heads] = nt(branch, wa_own_ref[...]).astype(BF)
+    gmix_ref[:, heads:] = nt(branch, wa_other_ref[...]).astype(BF)
+    ggain_ref[...] = jnp.broadcast_to(jnp.sum(back * y, axis=0, keepdims=True), ggain_ref.shape)
+    gattn = tn(mixed_ref[...], branch).astype(BF)
+    for half, ref in enumerate((attn_own_ref, attn_sent_ref)):
+        for side in range(width // LANES):
+            lanes = slice(LANES * side, LANES * side + LANES)
+            ref[heads * side : heads * side + heads] = gattn[heads * half : heads * half + heads, lanes]
+    for store in stores + [store for some in chunk_stores for store in some]:
+        store.wait()
 
 
 def output_kernel(x_ref, mixed_ref, active_ref, wa_own_ref, wa_other_ref, wo_own_ref, wo_other_ref, out_ref):
@@ -686,87 +760,145 @@
 
 def finish_kernel(
     lengths_ref,
-    own_ref,
-    other_ref,
-    normed_ref,
-    packet_ref,
     gblend_ref,
     ggain_ref,
     gain_ref,
+    packet_hbm,
+    own_hbm,
+    other_hbm,
+    gk_hbm,
+    gv_hbm,
+    gq_hbm,
+    normed_hbm,
+    w_own_hbm,
+    w_other_hbm,
+    attn_own_hbm,
+    attn_sent_hbm,
+    gkv_hbm,
+    wgrad_own_hbm,
+    wgrad_sent_hbm,
+    packet_ref,
+    own_ref,
+    other_ref,
+    gk_ref,
+    gv_ref,
+    gq_ref,
+    normed_ref,
     w_own_ref,
     w_other_ref,
-    attn_own_ref,
-    attn_sent_ref,
-    *refs,
+    gkv_ref,
+    wgrad_own_ref,
+    wgrad_sent_ref,
+    sems,
 ):
-    gq_ref, gk_ref, gv_ref, gproj_ref, wgrad_own_ref, wgrad_sent_ref = refs
-
-    rows = own_ref.shape[0]
+    copies = Copies(sems)
+    rows, width = normed_ref.shape
+    cols = w_own_ref.shape[2]
+    wgrads = (wgrad_own_ref, wgrad_sent_ref)
+    attn_rows = attn_own_hbm.shape[0]
+    keys_values = slice(cols, 3 * cols)
+    loads = [
+        copies.make(source, target)
+        for source, target in (
+            (packet_hbm, packet_ref),
+            (own_hbm.at[:, keys_values], own_ref),
+            (gk_hbm, gk_ref),
+            (gv_hbm, gv_ref),
+            (other_hbm.at[:, keys_values], other_ref),
+            (normed_hbm, normed_ref),
+            (gq_hbm, gq_ref),
+            (w_own_hbm, w_own_ref),
+            (w_other_hbm, w_other_ref),
+            (attn_own_hbm, wgrad_own_ref.at[3 * width : 3 * width + attn_rows]),
+            (attn_sent_hbm, wgrad_sent_ref.at[3 * width : 3 * width + attn_rows]),
+        )
+    ]
+    gkv_stores, wgrad_stores = [], []
+    for half, target in enumerate((wgrad_own_hbm, wgrad_sent_hbm)):
+        lanes = slice(2 * cols * half, 2 * cols * half + 2 * cols)
+        gkv_stores.append(copies.make(gkv_ref.at[:, lanes], gkv_hbm.at[:, lanes]))
+        spans = [slice(width * kind, width * kind + width) for kind in range(3)]
+        spans.append(slice(3 * width, wgrads[half].shape[0]))
+        wgrad_stores.append([copies.make(wgrads[half].at[span], target.at[span]) for span in spans])
+    for load in loads:
+        load.start()
     live = lax.axis_index("tensor") == 0
     member_from = start_at(document_ends(lengths_ref, rows), rows - 1)
     member = (iota((rows, 1), 0) >= member_from) & live
     diag = pair_diag(256, 128)
-    for pair in range(4):
+    cut = rows - HALO
+    for load in loads[:4]:
+        load.wait()
+    for pair in PAIRS:
+        if pair == 2:
+            loads[4].wait()
         src = own_ref if pair < 2 else other_ref
         col = 128 * (pair % 2)
-        lanes = slice(128 * pair, 128 * pair + 128)
-        base = 768 * (pair // 2) + col
-        k = src[:, 256 + col : 384 + col].astype(F32)
-        v = src[:, 512 + col : 640 + col]
+        lanes = pair_lanes(pair)
+        k = src[:, col : col + 128].astype(F32)
+        v = src[:, cols + col : cols + col + 128]
         back, back_sum = unpack(packet_ref, pair, diag)
         back, back_sum = back.astype(BF), back_sum[0:1]
         t = jnp.tanh(k)
-        slope = jnp.exp(jnp.minimum(k, 0.0))
-        k_both = jnp.concatenate([first_feature(k), t.astype(BF)], axis=1)
+        raised = jnp.exp(jnp.minimum(k, 0.0))
+        k_both = jnp.concatenate([jnp.where(k > 0, k + 1.0, raised).astype(BF), t.astype(BF)], axis=1)
         dfeat = nt(v, back)
-        extra_k = (dfeat[:, :128] - back_sum) * slope + dfeat[:, 128:] * (1.0 - t * t)
+        extra_k = (dfeat[:, :128] - back_sum) * raised + dfeat[:, 128:] * (1.0 - t * t)
         extra_v = nn(k_both, back)
-        gk = gk_ref[:, lanes].astype(F32) + jnp.where(member, extra_k, 0.0)
-        gv = gv_ref[:, lanes].astype(F32) + jnp.where(member, extra_v, 0.0)
-        halo_k = jnp.where(live, unpack_halo(packet_ref, 0, pair).astype(F32), 0.0)
-        halo_v = jnp.where(live, unpack_halo(packet_ref, 1, pair).astype(F32), 0.0)
-        cut = rows - HALO
-        gproj_ref[:, base : base + 128] = gq_ref[:, lanes]
-        gproj_ref[:cut, base + 256 : base + 384] = gk[:cut].astype(BF)
-        gproj_ref[cut:, base + 256 : base + 384] = (gk[cut:] + halo_k).astype(BF)
-        gproj_ref[:cut, base + 512 : base + 640] = gv[:cut].astype(BF)
-        gproj_ref[cut:, base + 512 : base + 640] = (gv[cut:] + halo_v).astype(BF)
-    width = normed_ref.shape[1]
-    cols = w_own_ref.shape[2]
-    normed = normed_ref[...]
-    ones = jnp.ones((1, cols), F32)
+        for kind, (grad_ref, extra) in enumerate(((gk_ref, extra_k), (gv_ref, extra_v))):
+            grad = grad_ref[:, lanes].astype(F32) + jnp.where(member, extra, 0.0)
+            halo = jnp.where(live, unpack_halo(packet_ref, kind, pair).astype(F32), 0.0)
+            base = cols * (2 * (pair // 2) + kind) + col
+            gkv_ref[:cut, base : base + 128] = grad[:cut].astype(BF)
+            gkv_ref[cut:, base : base + 128] = (grad[cut:] + halo).astype(BF)
+        if pair % 2 == 1:
+            gkv_stores[pair // 2].start()
+    for load in loads[5:]:
+        load.wait()
+    normed = normed_ref[...].T
+    ones = jnp.ones((1, cols), BF)
     gain_grad = jnp.zeros((1, width), F32)
-    for half, (wgrad_ref, w_ref) in enumerate(((wgrad_own_ref, w_own_ref), (wgrad_sent_ref, w_other_ref))):
+    for half, (wgrad_ref, w_ref) in enumerate(zip(wgrads, (w_own_ref, w_other_ref))):
         for kind in range(3):
-            first = 3 * cols * half + cols * kind
-            wgrad = tn(normed, gproj_ref[:, first : first + cols])
+            if kind == 0:
+                grad = gq_ref[:, cols * half : cols * half + cols]
+            else:
+                first = cols * (2 * half + kind - 1)
+                grad = gkv_ref[:, first : first + cols]
+            wgrad = nn(normed, grad)
             wgrad_ref[width * kind : width * kind + width] = wgrad.astype(BF)
+            wgrad_stores[half][kind].start()
             products = wgrad * w_ref[kind].astype(F32)
             high = products.astype(BF)
             low = (products - high.astype(F32)).astype(BF)
-            gain_grad = gain_grad + nt(ones.astype(BF), high) + nt(ones.astype(BF), low)
+            gain_grad = gain_grad + nt(ones, high) + nt(ones, low)
     gain_grad = gain_grad / gain_ref[...]
-    for half, wgrad_ref in enumerate((wgrad_own_ref, wgrad_sent_ref)):
+    for half, wgrad_ref in enumerate(wgrads):
         blends = [
             jnp.concatenate([gblend_ref[kind, 2 * half + pair][0:1] for pair in range(2)], axis=1)
             for kind in range(2)
         ]
         gains = [gain_grad[:, :256], gain_grad[:, 256:], ggain_ref[0:1, :256], ggain_ref[0:1, 256:]]
         extra = jnp.concatenate(blends + gains + [jnp.zeros((10, 256), F32)], axis=0)
-        attn_ref = (attn_own_ref, attn_sent_ref)[half]
-        wgrad_ref[3 * width : 3 * width + attn_ref.shape[0]] = attn_ref[...]
-        base = 3 * width + attn_ref.shape[0]
+        base = 3 * width + attn_rows
         wgrad_ref[base : base + 16] = extra.astype(BF)
         wgrad_ref[base + 16 :] = jnp.zeros((EXTRA - 16, 256), BF)
-
-
-def input_grad_kernel(gproj_ref, x_ref, branch_ref, gain_ref, w_own_ref, w_other_ref, out_ref):
+        wgrad_stores[half][3].start()
+    for store in gkv_stores + wgrad_stores[0] + wgrad_stores[1]:
+        store.wait()
+
+
+def input_grad_kernel(gq_ref, gkv_ref, x_ref, branch_ref, gain_ref, w_own_ref, w_other_ref, out_ref):
     cols = w_own_ref.shape[2]
     gnormed = None
     for half, w_ref in enumerate((w_own_ref, w_other_ref)):
         for kind in range(3):
-            first = 3 * cols * half + cols * kind
-            term = nt(gproj_ref[:, first : first + cols], w_ref[kind])
+            if kind == 0:
+                grad = gq_ref[:, cols * half : cols * half + cols]
+            else:
+                first = cols * (2 * half + kind - 1)
+                grad = gkv_ref[:, first : first + cols]
+            term = nt(grad, w_ref[kind])
             gnormed = term if gnormed is None else gnormed + term
     x = x_ref[...].astype(F32)
     r = lax.rsqrt(jnp.mean(x * x, axis=1, keepdims=True) + EPS)
@@ -778,6 +910,13 @@
 
 def merged(low, mine, got):
     return jnp.where(low, mine, got), jnp.where(low, got, mine)
+
+
+def put_part_kernel(parts_ref, out_part_ref, in_part_ref, wo_ref, wi_ref):
+    wo_ref[...] = out_part_ref[...].astype(F32)
+    width = wi_ref.shape[0]
+    for side in range(wi_ref.shape[1] // LANES):
+        wi_ref[:, LANES * side : LANES * side + LANES] = in_part_ref[width * side : width * side + width].astype(F32)
 
 
 def put_rows(ref, first_row, lane, parts, first, count):
@@ -790,20 +929,70 @@
             ref[first_row + low - first : first_row + high - first, lane : lane + lanes] = values
 
 
-def feed_output_kernel(bits_ref, out_mine_ref, out_got_ref, in_mine_ref, in_got_ref, wo_ref, wi_ref):
-    units, width = wo_ref.shape
-    outs = merged(bits_ref[0] == 0, out_mine_ref[...], out_got_ref[...])
-    for side in range(width // LANES):
-        put_rows(wo_ref, 0, LANES * side, outs, units * side, units)
-    ins = merged(bits_ref[1] == 0, in_mine_ref[...], in_got_ref[...])
-    for place in range(units // LANES):
-        put_rows(wi_ref, 0, LANES * place, ins, width * place, width)
-
-
-def attention_output_kernel(
-    bits_ref, a_mine_ref, a_got_ref, b_mine_ref, b_got_ref, wq_ref, wa_ref, gain_one_ref, gain_two_ref, blend_ref
+def last_output_kernel(
+    bits_ref,
+    out_part_hbm,
+    in_part_hbm,
+    a_mine_hbm,
+    a_got_hbm,
+    b_mine_hbm,
+    b_got_hbm,
+    wo_before_hbm,
+    wi_before_hbm,
+    wo_hbm,
+    wi_hbm,
+    wq_ref,
+    wa_ref,
+    gain_one_ref,
+    gain_two_ref,
+    blend_ref,
+    out_part_ref,
+    in_part_ref,
+    a_mine_ref,
+    a_got_ref,
+    b_mine_ref,
+    b_got_ref,
+    wo_ref,
+    wi_ref,
+    sems,
 ):
-    heads, width = wa_ref.shape
+    copies = Copies(sems)
+    loads = [
+        copies.make(source, target)
+        for source, target in (
+            (out_part_hbm, out_part_ref),
+            (in_part_hbm, in_part_ref),
+            (a_mine_hbm, a_mine_ref),
+            (a_got_hbm, a_got_ref),
+            (b_mine_hbm, b_mine_ref),
+            (b_got_hbm, b_got_ref),
+        )
+    ]
+    for load in loads:
+        load.start()
+    wo_column = pl.multiple_of((1 - bits_ref[0]) * wo_ref.shape[1], LANES)
+    wi_column = pl.multiple_of((1 - bits_ref[1]) * wi_ref.shape[1], LANES)
+    middle = wo_ref.shape[0] // 2
+    stores = [
+        copies.make(wo_ref.at[span], wo_hbm.at[span, pl.ds(wo_column, wo_ref.shape[1])])
+        for span in (slice(0, middle), slice(middle, 2 * middle))
+    ]
+    for side in range(wi_ref.shape[1] // LANES):
+        lanes = slice(LANES * side, LANES * side + LANES)
+        target = wi_hbm.at[:, pl.ds(pl.multiple_of(wi_column + LANES * side, LANES), LANES)]
+        stores.append(copies.make(wi_ref.at[:, lanes], target))
+    for load in loads[:2]:
+        load.wait()
+    wo_ref[...] = out_part_ref[...].astype(F32)
+    for store in stores[:2]:
+        store.start()
+    width = wi_ref.shape[0]
+    for side in range(wi_ref.shape[1] // LANES):
+        wi_ref[:, LANES * side : LANES * side + LANES] = in_part_ref[width * side : width * side + width].astype(F32)
+        stores[2 + side].start()
+    for load in loads[2:]:
+        load.wait()
+    heads = wa_ref.shape[0]
     parts = merged(bits_ref[0] == 0, a_mine_ref[...], a_got_ref[...])
     parts += merged(bits_ref[1] == 0, b_mine_ref[...], b_got_ref[...])
     rows = a_mine_ref.shape[0]
@@ -815,6 +1004,8 @@
     gain_two_ref[...] = jnp.concatenate([rest[4:5], rest[5:6]], axis=1)
     sums = [jnp.sum(rest[:2, 64 * head : 64 * head + 64], axis=1, keepdims=True) for head in range(4)]
     blend_ref[...] = jnp.concatenate(sums, axis=1)
+    for store in stores:
+        store.wait()
 
 
 def flip(values, count, stride):
@@ -832,8 +1023,8 @@
 
 class Reduction:
     def __init__(self, stacks, count, whole_late=False):
-        self.stacks = [[(term, 0) for term in terms] for terms in stacks]
-        self.rows = [terms[0].shape[0] for terms in stacks]
+        self.stacks = [[(term, first) for term in terms] for terms, first, _ in stacks]
+        self.rows = [rows for _, _, rows in stacks]
         self.count = count
         strides = strides_of(count)
         self.orders = [strides, strides[1::-1] + strides[2:]]
@@ -975,6 +1166,7 @@
         cost_estimate=cost(5),
         name="norm_project",
     )(tokens, gain_one, wq_own)
+    normed, wi_other, wo_other, wa_other = tie(normed, wi_other, wo_other, wa_other)
     other, packet = pl.pallas_call(
         project_state_kernel,
         in_specs=[smem] + [pl.BlockSpec(memory_space=pltpu.VMEM)] * 3,
@@ -994,127 +1186,107 @@
     vmem = pl.BlockSpec(memory_space=pltpu.VMEM)
     stack_rows = units * width // LANES
     attn_rows = w_attn.shape[0] * width // LANES
-    anywhere = pl.BlockSpec(memory_space=pl.ANY)
-
-    def early(*shape):
-        return pl.BlockSpec(shape, lambda i: (jnp.minimum(i, blocks - 1),) + (0,) * (len(shape) - 1))
-
-    kept_blocks = [
-        ((blocks, 4, 256, 128), BF),
+    anywhere = pl.BlockSpec(memory_space=pltpu.HBM)
+
+    kept_shapes = [
+        ((blocks, 4, 128, 128), BF),
         ((blocks, HALO, 1024), BF),
         ((blocks, 4, BLOCK + HALO, 256), BF),
         ((blocks, 4, BLOCK, 256), BF),
-        ((blocks, 4, 2, BLOCK, 256), BF),
+        ((rows, width), BF),
+        ((rows, width), BF),
     ]
-    mixed, *outs = pl.pallas_call(
+    stored_shapes = [((rows, width), BF)] + kept_shapes + [((rows, 2 * units), BF)]
+    branch, gmix, ggain_mlp, *outs = pl.pallas_call(
         partial(layer_kernel, blocks, parts),
-        grid=(blocks + 2 * parts,),
-        in_specs=[
-            smem,
-            early(BLOCK, own_cols),
-            early(BLOCK, own_cols),
-            whole((PACKET, 128)),
-            smem,
-            smem,
-            early(BLOCK, width),
-            early(BLOCK, width),
-            whole((1, width)),
-            whole(w_attn.shape),
-            whole(w_attn.shape),
-        ]
-        + [anywhere] * 4,
-        out_specs=[early(BLOCK, width)]
-        + [early(1, *shape[1:]) for shape, _ in kept_blocks]
-        + [early(BLOCK, width)] * 2
-        + [
-            pl.BlockSpec((rows, units // parts), lambda i: (0, jnp.maximum(i - blocks, 0))),
-            whole((rows, width)),
-            whole((rows, width)),
-            whole((8, width)),
-            whole((attn_rows, LANES)),
-            whole((attn_rows, LANES)),
-        ]
-        + [anywhere] * 4,
-        out_shape=[jax.ShapeDtypeStruct((rows, width), BF)]
-        + [jax.ShapeDtypeStruct(shape, kind) for shape, kind in kept_blocks]
-        + [jax.ShapeDtypeStruct((rows, width), F32)] * 2
-        + [
-            jax.ShapeDtypeStruct((rows, 2 * units), BF),
+        in_specs=[smem] * 3 + [vmem] * 4 + [anywhere] * 8,
+        out_specs=[vmem] * 5 + [anywhere] * 12,
+        out_shape=[
             jax.ShapeDtypeStruct((rows, width), BF),
             jax.ShapeDtypeStruct((rows, width), BF),
             jax.ShapeDtypeStruct((8, width), F32),
             jax.ShapeDtypeStruct((attn_rows, LANES), BF),
             jax.ShapeDtypeStruct((attn_rows, LANES), BF),
         ]
+        + [jax.ShapeDtypeStruct(shape, kind) for shape, kind in stored_shapes]
         + [jax.ShapeDtypeStruct((stack_rows, LANES), BF)] * 4,
         scratch_shapes=[
+            pltpu.VMEM((rows, own_cols), BF),
+            pltpu.VMEM((rows, own_cols), BF),
+            pltpu.VMEM((rows, width), BF),
+            pltpu.VMEM((rows, width), BF),
+            pltpu.VMEM((2,) + w_in.shape, BF),
+            pltpu.VMEM((2,) + w_out.shape, BF),
+        ]
+        + [pltpu.VMEM(shape, kind) for shape, kind in stored_shapes]
+        + [
+            pltpu.VMEM((2, 2, stack_rows, LANES), BF),
             pltpu.VMEM((4, 256, 128), F32),
             pltpu.VMEM((4, 8, 128), F32),
             pltpu.VMEM((HALO, 1024), BF),
-            pltpu.VMEM((rows, width), BF),
             pltpu.VMEM((rows, width), F32),
             pltpu.VMEM((rows, 128), F32),
             pltpu.VMEM((rows, width), BF),
             pltpu.VMEM((width, rows), BF),
-            pltpu.VMEM((rows, width), BF),
             pltpu.VMEM((width, rows), BF),
             pltpu.VMEM((rows, width), F32),
-            pltpu.VMEM((2,) + w_in.shape, BF),
-            pltpu.VMEM((2,) + w_out.shape, BF),
-            pltpu.VMEM((2, 2, stack_rows, LANES), BF),
-            pltpu.SemaphoreType.DMA((4,)),
-            pltpu.SemaphoreType.DMA((2 * parts, 1 + width // LANES)),
+            pltpu.SemaphoreType.DMA((64,)),
         ],
-        compiler_params=params(60),
+        compiler_params=params(62),
         cost_estimate=cost(30),
         name="layer",
     )(
         lengths,
-        own,
-        other,
-        packet,
         blend,
         blend_other,
-        tokens,
-        cotangent,
+        packet,
         gain_two,
         w_attn,
         wa_other,
+        own,
+        other,
+        tokens,
+        cotangent,
         w_in,
         wi_other,
         w_out,
         wo_other,
     )
-    kept, outs = outs[:7], outs[7:]
-    active, branch, gmix, ggain_mlp, *attn_grads = outs[:6]
-    out_own, in_own, out_sent, in_sent = outs[6:]
-
-    feed_sum = Reduction([[out_own, swap(out_sent)], [in_own, swap(in_sent)]], count)
+    attn_grads, outs = outs[:2], outs[2:]
+    mixed, *kept = outs[:7]
+    active, out_own, in_own, out_sent, in_sent = outs[7:]
+
+    feed_sum = Reduction(
+        [([out_own, swap(out_sent)], 0, stack_rows), ([in_own, swap(in_sent)], 0, stack_rows)], count
+    )
     wanted = feed_sum.steps
     if wanted > 0:
         cuts = feed_sum.outgoing()
         gmix, *cuts = tie(gmix, *cuts)
         feed_sum.send(cuts)
 
+    steps = blocks // STEP_BLOCKS
+
     def back_block(*shape):
-        return pl.BlockSpec(shape, lambda i: (blocks - 1 - i,) + (0,) * (len(shape) - 1))
+        return pl.BlockSpec(
+            (shape[0] * STEP_BLOCKS,) + shape[1:], lambda i: (steps - 1 - i,) + (0,) * (len(shape) - 1)
+        )
 
     gq, gk, gv, packet_back, gblend = pl.pallas_call(
-        partial(mixer_backward_kernel, rows),
-        grid=(blocks,),
+        mixer_backward_kernel,
+        grid=(steps,),
         in_specs=[
+            smem,
+            smem,
             smem,
             back_block(BLOCK, own_cols),
             back_block(BLOCK, own_cols),
-            back_block(1, 4, 256, 128),
+            back_block(1, 4, 128, 128),
             back_block(1, HALO, 1024),
             back_block(1, 4, BLOCK + HALO, 256),
             back_block(1, 4, BLOCK, 256),
-            back_block(1, 4, 2, BLOCK, 256),
             back_block(BLOCK, width),
             back_block(BLOCK, width),
-            smem,
-            smem,
             back_block(BLOCK, width),
         ],
         out_specs=[back_block(BLOCK, width)] * 3 + [whole((PACKET, 128)), whole((2, 4, 8, 128))],
@@ -1128,7 +1300,7 @@
         compiler_params=params(60),
         cost_estimate=cost(20),
         name="mixer_backward",
-    )(lengths, own, other, *kept, blend, blend_other, gmix)
+    )(lengths, blend, blend_other, own, other, *kept, gmix)
     if wanted > 1:
         (packet_back,) = feed_sum.after(packet_back)
     packet_got = swap(packet_back)
@@ -1137,33 +1309,50 @@
         packet_got, *cuts = tie(packet_got, *cuts)
         feed_sum.send(cuts)
 
+    wq_shape = (3 * width + attn_rows + EXTRA, own_cols // 3)
+    kv_cols = 2 * own_cols // 3
     gproj, wq_mine, wq_sent = pl.pallas_call(
         finish_kernel,
-        in_specs=[smem] + [pl.BlockSpec(memory_space=pltpu.VMEM)] * 14,
+        in_specs=[smem] + [vmem] * 3 + [anywhere] * 11,
+        out_specs=[anywhere] * 3,
         out_shape=[
-            jax.ShapeDtypeStruct((rows, 2 * own_cols), BF),
-            jax.ShapeDtypeStruct((3 * width + attn_rows + EXTRA, own_cols // 3), BF),
-            jax.ShapeDtypeStruct((3 * width + attn_rows + EXTRA, own_cols // 3), BF),
+            jax.ShapeDtypeStruct((rows, 2 * kv_cols), BF),
+            jax.ShapeDtypeStruct(wq_shape, BF),
+            jax.ShapeDtypeStruct(wq_shape, BF),
+        ],
+        scratch_shapes=[
+            pltpu.VMEM((PACKET, 128), BF),
+            pltpu.VMEM((rows, kv_cols), BF),
+            pltpu.VMEM((rows, kv_cols), BF),
+        ]
+        + [pltpu.VMEM((rows, width), BF)] * 4
+        + [pltpu.VMEM(wq_own.shape, BF)] * 2
+        + [
+            pltpu.VMEM((rows, 2 * kv_cols), BF),
+            pltpu.VMEM(wq_shape, BF),
+            pltpu.VMEM(wq_shape, BF),
+            pltpu.SemaphoreType.DMA((24,)),
         ],
         compiler_params=params(60),
         cost_estimate=cost(8),
         name="finish",
     )(
         lengths,
-        own,
-        other,
-        normed,
-        packet_got,
         gblend,
         ggain_mlp,
         gain_one,
+        packet_got,
+        own,
+        other,
+        gk,
+        gv,
+        gq,
+        normed,
         wq_own,
         wq_other,
         *attn_grads,
-        gq,
-        gk,
-        gv,
     )
+
     def layer_output(active):
         return pl.pallas_call(
             output_kernel,
@@ -1183,7 +1372,8 @@
             input_grad_kernel,
             grid=(4,),
             in_specs=[
-                row_block(tall, 2 * own_cols),
+                row_block(tall, width),
+                row_block(tall, 2 * kv_cols),
                 row_block(tall, width),
                 row_block(tall, width),
                 whole((1, width)),
@@ -1195,13 +1385,13 @@
             compiler_params=params(60),
             cost_estimate=cost(7),
             name="input_grad",
-        )(gproj, tokens, branch, gain_one, wq_own, wq_other)
+        )(gq, gproj, tokens, branch, gain_one, wq_own, wq_other)
 
     if wanted > 1:
         (wq_sent,) = feed_sum.after(wq_sent)
     wq_got = swap(wq_sent)
     cut = wq_got.shape[0] // 2
-    wq_sum = Reduction([[wq_mine[:cut], wq_got[:cut]], [wq_mine[cut:], wq_got[cut:]]], count, True)
+    wq_sum = Reduction([([wq_mine, wq_got], 0, cut), ([wq_mine, wq_got], cut, cut)], count, True)
     beside = {0: lambda: input_gradient(gproj), 3: lambda: layer_output(active)}
     done = {}
     step = 0
@@ -1224,28 +1414,55 @@
             done[step] = beside[step]()
     grad_input, output = done[0], done[3]
 
+    out_mine, out_got, in_mine, in_got = feed_sum.parts()
+    bits = feed_sum.last_bits()
+    if wanted > 1:
+        out_mine, in_mine, *wq_sum.held = tie(out_mine, in_mine, *wq_sum.held)
+    grad_shapes = [jax.ShapeDtypeStruct(w_out.shape, F32), jax.ShapeDtypeStruct(w_in.shape, F32)]
     wo_grad, wi_grad = pl.pallas_call(
-        feed_output_kernel,
-        in_specs=[smem] + [vmem] * 4,
-        out_shape=[jax.ShapeDtypeStruct(w_out.shape, F32), jax.ShapeDtypeStruct(w_in.shape, F32)],
+        put_part_kernel,
+        grid_spec=pltpu.PrefetchScalarGridSpec(
+            num_scalar_prefetch=1,
+            grid=(1,),
+            in_specs=[whole(out_mine.shape), whole(in_mine.shape)],
+            out_specs=[
+                pl.BlockSpec((units, LANES), lambda i, places: (0, places[0])),
+                pl.BlockSpec((width, units // 2), lambda i, places: (0, places[1])),
+            ],
+        ),
+        out_shape=grad_shapes,
         compiler_params=params(60),
-        cost_estimate=cost(3),
-        name="feed_output",
-    )(feed_sum.last_bits(), *feed_sum.parts())
-    wq_grad, wa_grad, ggain_one, ggain_two, gblend_all = pl.pallas_call(
-        attention_output_kernel,
-        in_specs=[smem] + [vmem] * 4,
-        out_shape=[
+        cost_estimate=cost(2),
+        name="put_part",
+    )(bits, out_mine, in_mine)
+    if wanted > 1:
+        wo_grad, wi_grad, out_got, in_got = tie(wo_grad, wi_grad, out_got, in_got)
+        (wi_grad,) = wq_sum.after(wi_grad)
+    wq_parts = wq_sum.parts()
+    last_inputs = [out_got, in_got] + wq_parts
+    wo_grad, wi_grad, wq_grad, wa_grad, ggain_one, ggain_two, gblend_all = pl.pallas_call(
+        last_output_kernel,
+        in_specs=[smem] + [anywhere] * 8,
+        out_specs=[anywhere] * 2 + [vmem] * 5,
+        out_shape=grad_shapes
+        + [
             jax.ShapeDtypeStruct((3 * width, own_cols // 3), F32),
             jax.ShapeDtypeStruct(w_attn.shape, F32),
             jax.ShapeDtypeStruct((1, width), F32),
             jax.ShapeDtypeStruct((1, width), F32),
             jax.ShapeDtypeStruct(blend.shape, F32),
         ],
+        scratch_shapes=[pltpu.VMEM(part.shape, BF) for part in last_inputs]
+        + [
+            pltpu.VMEM((units, LANES), F32),
+            pltpu.VMEM((width, units // 2), F32),
+            pltpu.SemaphoreType.DMA((16,)),
+        ],
+        input_output_aliases={7: 0, 8: 1},
         compiler_params=params(60),
         cost_estimate=cost(3),
-        name="attention_output",
-    )(wq_sum.last_bits(), *wq_sum.parts())
+        name="last_output",
+    )(bits, *last_inputs, wo_grad, wi_grad)
 
     return (
         output,

time: 180 us -> 176 us (0.978)
  local copies, waits for them, and re-layouts: 8.17 us -> 4.24 us
  other arithmetic: 11.5 us -> 15.1 us
    convert_element_type x15 -> x12, other arithmetic: 9.61 us -> 12.5 us  [cut(): return total.astype(BF)]
    unnamed x44 -> x48, local copies, waits for them, and re-layouts: 6.76 us -> 4.22 us
  transfers between devices with their start and end apart: 32 -> 32, of which waited for: 15 -> 14; matrix products, arithmetic and copies ran while one was open for 5% -> 5% of each run, Pallas kernels for 29% -> 26%
where the time goes in v4:
time: 176 us; the launch traced here: 175 us
  Pallas kernels  87.2 us (50%)
  waiting for transfers between devices  35.3 us (20%)
  starting transfers between devices  31.9 us (18%)
  other arithmetic  15.1 us (9%)
  local copies, waits for them, and re-layouts  4.24 us (2%)
    pallas_call x1, Pallas kernels, body(): pl.pallas_call(partial(layer_kernel, blocks, parts), in_specs=[smem] * 3...  31.6 us
    ppermute x22, waiting for transfers between devices, flip(): lax.ppermute(values, 'dp', [(src, src ^ stride) for src in range(count)])  31.2 us
    ppermute x22, starting transfers between devices, flip(): lax.ppermute(values, 'dp', [(src, src ^ stride) for src in range(count)])  29.6 us
    pallas_call x1, Pallas kernels, body(): pl.pallas_call(mixer_backward_kernel, grid=(steps,), in_specs=[smem, smem...  15.6 us
    convert_element_type x12, other arithmetic, cut(): return total.astype(BF)  12.5 us
    pallas_call x1, Pallas kernels, body(): pl.pallas_call(finish_kernel, in_specs=[smem] + [vmem] * 3 + [anywhere] *...  9.27 us
    pallas_call x1, Pallas kernels, layer_output(): pl.pallas_call(output_kernel, grid=(4,), in_specs=[row_block(tall, width)...  7.1 us
    pallas_call x1, Pallas kernels, input_gradient(): pl.pallas_call(input_grad_kernel, grid=(4,), in_specs=[row_block(tall, wi...  6.32 us
  transfers between devices with their start and end apart: 32, of which 14 were waited for; matrix products, arithmetic and copies ran while one was open for 5% of the time, Pallas kernels for 26%

profile of v4, /device:TPU:0, one launch (start us, length us, event | category | flops | bytes accessed | tf_op | source)
XLA Modules:
  0.0 175.2 jit_solution(2055082839411599390)
XLA Ops:
  0.6 0.5 collective-permute-start.1
  1.2 0.4 collective-permute-start.4
  1.8 4.6 %norm_project.1 = (bf16[1024,512]{1,0:T(8,128)(2,1)}, bf16[1024,768]{1,0:T(8,128)(2,1)}) custom-call(bf16[1024,512]{1,0:T(8,128)(2,1)} %x_ref.5, f32[1,512]{1,0:T(1,128)} %bitcast.14, bf16[3,512,256]{2,1,0:T(8,128)(2,1)} %bitcast.11), custom_call_target="tpu_custom_call" | custom-call | flops 50000000 | bytes 1048576 | tf_op jit(solution)/shard_map/norm_project/pallas_call | solution.py:1159
  6.3 0.3 collective-permute-done.3.wa_other_ref
  6.7 1.0 copy-done
  7.7 4.9 %project_state.1 = (bf16[1024,768]{1,0:T(8,128)(2,1)}, bf16[832,128]{1,0:T(8,128)(2,1)}) custom-call(s32[1,6]{1,0:T(1,128)} %lengths_ref.7, bf16[1024,512]{1,0:T(8,128)(2,1)} %get-tuple-element.111.normed_ref.normed_hbm, bf16[3,512,256]{2,1,0:T(8,128)(2,1)} %copy-done, bf16[1024,768]{1,0:T(8,128)(2,1)} %get-tuple-element.109.own_ref.own_hbm.refs_0_), custom_call_target="tpu_custom_call" | custom-call | flops 50000000 | bytes 1048576 | tf_op jit(solution)/shard_map/project_state/pallas_call | solution.py:1170
  12.6 0.4 collective-permute-start.5
  13.1 1.0 collective-permute-done.blend_other_ref
  14.3 0.4 copy-done.23
  14.7 0.3 copy-done.21
  15.0 31.6 %layer.1 = (bf16[1024,512]{1,0:T(8,128)(2,1)}, bf16[1024,512]{1,0:T(8,128)(2,1)}, f32[8,512]{1,0:T(8,128)}, bf16[512,256]{1,0:T(8,128)(2,1)}, bf16[512,256]{1,0:...) custom-call(s32[1,6]{1,0:T(1,128)} %lengths_ref.7, ...), custom_call_target="tpu_custom_call" | custom-call | flops 300000000 | bytes 1048576 | tf_op jit(solution)/shard_map/layer/pallas_call | solution.py:1200
  46.6 0.4 collective-permute-start.6
  47.1 2.4 %collective-permute-done.6 = bf16[2048,256]{1,0:T(8,128)(2,1)S(1)} collective-permute-done((bf16[2048,256]{1,0:T(8,128)(2,1)}, bf16[2048,256]{1,0:T(8,128)(2,1)S(1)}, u32[]{:S(2)}, u32[]{:S(2)}) %collective-permute-start.6) | collective-permute-done | bytes 1048608 | tf_op jit(solution)/shard_map/ppermute | solution.py:1140
  49.5 1.5 add_convert_fusion.1
  51.1 1.1 add_convert_fusion
  52.2 2.8 %collective-permute-start.8 = (bf16[1024,256]{1,0:T(8,128)(2,1)S(1)}, bf16[1024,256]{1,0:T(8,128)(2,1)}, u32[]{:S(2)}, u32[]{:S(2)}) collective-permute-start(bf16[1024,256]{1,0:T(8,128)(2,1)S(1)} %add_convert_fusion.1), channel_id=1, source_target_pairs={{0,2},{2,0},{4,6},{6,4},{8,10},{10,8},{12,14},{14,12},{16,18},{18,... | collective-permute-start | bytes 1572872 | tf_op jit(solution)/shard_map/ppermute | solution.py:1012
  55.0 1.5 collective-permute-start.9
  56.5 15.6 %mixer_backward.1 = (bf16[1024,512]{1,0:T(8,128)(2,1)}, bf16[1024,512]{1,0:T(8,128)(2,1)}, bf16[1024,512]{1,0:T(8,128)(2,1)}, bf16[832,128]{1,0:T(8,128)(2,1)}, f32[2,4,8,128]{3,2,1,0:T(8,128)}) custom-call(s32[1,6]{1,0:T(1,128)} %lengths_ref.7, f32[2,4]{1,0:T(2,128)} %blend_own_ref.3, f32[2,4]{1,0:T(2,128)} %copy-done.23, ...), custom_call_target="tpu_custom_call" | custom-call | flops 200000000 | bytes 1048576 | tf_op jit(solution)/shard_map/mixer_backward/pallas_call | solution.py:1275
  72.3 1.3 add_convert_fusion.4
  73.9 0.7 copy-done.20
  74.6 0.5 collective-permute-start.11
  75.1 9.3 %finish.1 = (bf16[1024,1024]{1,0:T(8,128)(2,1)}, bf16[2112,256]{1,0:T(8,128)(2,1)}, bf16[2112,256]{1,0:T(8,128)(2,1)}) custom-call(s32[1,6]{1,0:T(1,128)} %lengths_ref.7, f32[2,4,8,128]{3,2,1,0:T(8,128)} %get-tuple-element.129.gblend_ref, f32[8,512]{1,0:T(8,128)} %get-tuple-element.130.ggain_ref, f32[1,512]{1,0:T(1,128)} %bitcast.15, ...), custom_call_target="tpu_custom_call" | custom-call | flops 80000000 | bytes 1048576 | tf_op jit(solution)/shard_map/finish/pallas_call | solution.py:1314
  84.5 0.7 copy-done.19
  85.2 1.2 add_convert_fusion.14
  86.3 1.0 add_convert_fusion.15
  87.4 0.7 pad_maximum_fusion.6
  88.1 0.9 add_convert_fusion.2
  89.1 2.0 %collective-permute-start.14 = (bf16[528,256]{1,0:T(8,128)(2,1)}, bf16[528,256]{1,0:T(8,128)(2,1)S(1)}, u32[]{:S(2)}, u32[]{:S(2)}) collective-permute-start(bf16[528,256]{1,0:T(8,128)(2,1)} %get-tuple-element.152), channel_id=1, source_target_pairs={{0,2},{2,0},{4,6},{6,4},{8,10},{10,8},{12,14},{14,12},{16,18},{18,... | collective-permute-start | bytes 811016 | tf_op jit(solution)/shard_map/ppermute | solution.py:1012
  91.0 1.5 collective-permute-start.15
  92.5 1.6 collective-permute-start.16
  94.1 6.3 %input_grad.1 = bf16[1024,512]{1,0:T(8,128)(2,1)} custom-call(bf16[1024,512]{1,0:T(8,128)(2,1)} %get-tuple-element.140.gq_hbm.gq_ref, bf16[1024,1024]{1,0:T(8,128)(2,1)} %get-tuple-element.154.gkv_ref, bf16[1024,512]{1,0:T(8,128)(2,1)} %x_ref.5, bf16[1024,512]{1,0:T(8,128)(2,1)} %get-tuple-element.155.branch_ref, f32[1,512]{1,0:T(1,128)} %bitcast.16, ...), custom_call_target="tpu_custom_call" | custom-call | flops 70000000 | bytes 1048576 | tf_op jit(solution)/shard_map/input_grad/pallas_call | solution.py:1371
  100.5 0.6 collective-permute-done.16
  101.0 1.2 add_convert_fusion.19
  102.2 0.7 pad_maximum_fusion.10
  102.9 1.7 add_convert_fusion.12
  104.6 2.6 %collective-permute-start.19 = (bf16[256,256]{1,0:T(8,128)(2,1)}, bf16[256,256]{1,0:T(8,128)(2,1)}, u32[]{:S(2)}, u32[]{:S(2)}) collective-permute-start(bf16[256,256]{1,0:T(8,128)(2,1)} %pad_maximum_fusion.10), channel_id=1, source_target_pairs={{0,16},{2,18},{4,20},{6,22},{8,24},{10,26},{12,28},{14,30},{16,0},... | collective-permute-start | bytes 393224 | tf_op jit(solution)/shard_map/ppermute | solution.py:1012
  107.2 0.5 collective-permute-start.17
  107.7 0.5 collective-permute-start.18
  108.2 5.0 %collective-permute-done.19 = bf16[256,256]{1,0:T(8,128)(2,1)} collective-permute-done((bf16[256,256]{1,0:T(8,128)(2,1)}, bf16[256,256]{1,0:T(8,128)(2,1)}, u32[]{:S(2)}, u32[]{:S(2)}) %collective-permute-start.19) | collective-permute-done | bytes 131104 | tf_op jit(solution)/shard_map/ppermute | solution.py:1012
  113.2 1.2 add_convert_fusion.17
  114.5 1.1 add_convert_fusion.11
  115.9 3.9 %collective-permute-start.20 = (bf16[528,256]{1,0:T(8,128)(2,1)S(1)}, bf16[528,256]{1,0:T(8,128)(2,1)S(1)}, u32[]{:S(2)}, u32[]{:S(2)}) collective-permute-start(bf16[528,256]{1,0:T(8,128)(2,1)S(1)} %pad_maximum_fusion.2), channel_id=1, source_target_pairs={{0,8},{2,10},{4,12},{6,14},{8,0},{10,2},{12,4},{14,6},{16,24},{18,... | collective-permute-start | bytes 811016 | tf_op jit(solution)/shard_map/ppermute | solution.py:1012
  119.8 4.3 %collective-permute-done.21 = bf16[256,256]{1,0:T(8,128)(2,1)S(1)} collective-permute-done((bf16[256,256]{1,0:T(8,128)(2,1)S(1)}, bf16[256,256]{1,0:T(8,128)(2,1)S(1)}, u32[]{:S(2)}, u32[]{:S(2)}) %collective-permute-start.21) | collective-permute-done | bytes 131104 | tf_op jit(solution)/shard_map/ppermute | solution.py:1012
  124.1 3.1 %collective-permute-done.20 = bf16[528,256]{1,0:T(8,128)(2,1)S(1)} collective-permute-done((bf16[528,256]{1,0:T(8,128)(2,1)S(1)}, bf16[528,256]{1,0:T(8,128)(2,1)S(1)}, u32[]{:S(2)}, u32[]{:S(2)}) %collective-permute-start.20) | collective-permute-done | bytes 270368 | tf_op jit(solution)/shard_map/ppermute | solution.py:1012
  127.3 0.4 collective-permute-start.23
  127.8 3.2 %collective-permute-start.22 = (bf16[528,256]{1,0:T(8,128)(2,1)S(1)}, bf16[528,256]{1,0:T(8,128)(2,1)S(1)}, u32[]{:S(2)}, u32[]{:S(2)}) collective-permute-start(bf16[528,256]{1,0:T(8,128)(2,1)S(1)} %pad_maximum_fusion.3), channel_id=1, source_target_pairs={{0,16},{2,18},{4,20},{6,22},{8,24},{10,26},{12,28},{14,30},{16,0},... | collective-permute-start | bytes 811016 | tf_op jit(solution)/shard_map/ppermute | solution.py:1012
  131.0 7.1 %layer_output.1 = bf16[1024,512]{1,0:T(8,128)(2,1)} custom-call(bf16[1024,512]{1,0:T(8,128)(2,1)} %x_ref.5, bf16[1024,512]{1,0:T(8,128)(2,1)} %get-tuple-element.170.mixed_ref, bf16[1024,2048]{1,0:T(8,128)(2,1)} %get-tuple-element.171.active_ref, bf16[256,512]{1,0:T(8,128)(2,1)} %wa_own_ref.3, bf16[256,512]{1,0:T(8,128)(2,1)} %copy-done.8, ...), custom_call_target="tpu_custom_call" | custom-call | flops 50000000 | bytes 1048576 | tf_op jit(solution)/shard_map/layer_output/pallas_call | solution.py:1357
  138.1 1.8 %collective-permute-done.23 = bf16[512,256]{1,0:T(8,128)(2,1)S(1)} collective-permute-done((bf16[512,256]{1,0:T(8,128)(2,1)S(1)}, bf16[512,256]{1,0:T(8,128)(2,1)S(1)}, u32[]{:S(2)}, u32[]{:S(2)}) %collective-permute-start.23) | collective-permute-done | bytes 262176 | tf_op jit(solution)/shard_map/ppermute | solution.py:1012
  140.0 2.1 %collective-permute-done.22 = bf16[528,256]{1,0:T(8,128)(2,1)S(1)} collective-permute-done((bf16[528,256]{1,0:T(8,128)(2,1)S(1)}, bf16[528,256]{1,0:T(8,128)(2,1)S(1)}, u32[]{:S(2)}, u32[]{:S(2)}) %collective-permute-start.22) | collective-permute-done | bytes 270368 | tf_op jit(solution)/shard_map/ppermute | solution.py:1012
  142.2 1.2 collective-permute-start.26
  143.4 0.9 collective-permute-start.24
  144.3 0.6 collective-permute-start.25
  144.9 1.5 collective-permute-start.27
  146.3 1.0 collective-permute-done.26
  147.3 6.8 %collective-permute-done.27 = bf16[264,256]{1,0:T(8,128)(2,1)S(1)} collective-permute-done((bf16[264,256]{1,0:T(8,128)(2,1)S(1)}, bf16[264,256]{1,0:T(8,128)(2,1)S(1)}, u32[]{:S(2)}, u32[]{:S(2)}) %collective-permute-start.27) | collective-permute-done | bytes 135200 | tf_op jit(solution)/shard_map/ppermute | solution.py:1012
  154.5 0.6 collective-permute-start.28
  155.2 1.2 collective-permute-start.29
  156.4 1.5 collective-permute-start.30
  157.9 0.8 collective-permute-start.31
  158.7 0.7 pad_add_fusion.parts_ref.bits_ref
  159.3 3.2 %put_part.1 = (f32[1024,512]{1,0:T(8,128)}, f32[512,1024]{1,0:T(8,128)}) custom-call(s32[2]{0:T(128)} %pad_add_fusion.parts_ref.bits_ref, bf16[1024,256]{1,0:T(8,128)(2,1)} %copy-done.2, bf16[1024,256]{1,0:T(8,128)(2,1)} %copy-done.3), custom_call_target="tpu_custom_call" | custom-call | flops 20000000 | bytes 1048576 | tf_op jit(solution)/shard_map/put_part/pallas_call | solution.py:1422
  162.6 6.6 %collective-permute-done.30.a_got_hbm = bf16[528,256]{1,0:T(8,128)(2,1)S(1)} collective-permute-done((bf16[528,256]{1,0:T(8,128)(2,1)S(1)}, bf16[528,256]{1,0:T(8,128)(2,1)S(1)}, u32[]{:S(2)}, u32[]{:S(2)}) %collective-permute-start.30) | collective-permute-done | bytes 270368 | tf_op jit(solution)/shard_map/ppermute | solution.py:1012
  169.2 0.7 copy-done.15
  170.3 4.7 %last_output.1 = (f32[1024,512]{1,0:T(8,128)}, f32[512,1024]{1,0:T(8,128)}, f32[1536,256]{1,0:T(8,128)}, f32[256,512]{1,0:T(8,128)}, f32[1,512]{1,0:T(1,128)}, /*index=5*/f32[1,512]{1,0:T(1,128)}, f32[2,4]{1,0:T(2,128)}) custom-call(s32[2]{0:T(128)} %pad_add_fusion.parts_ref.bits_ref, ...), custom_call_target="tpu_custom_call", output_to_operand_aliasing={{0}: (7, {}), {1}: (8, {})} | custom-call | flops 30000000 | bytes 1048576 | tf_op jit(solution)/shard_map/last_output/pallas_call | solution.py:1443
  (92 shorter events, 2.5 us)
Async XLA Ops:
  0.6 6.0 %collective-permute-start.1 = (bf16[512,1024]{1,0:T(8,128)(2,1)}, bf16[512,1024]{1,0:T(8,128)(2,1)S(1)}, u32[]{:S(2)}, u32[]{:S(2)}) collective-permute-start(bf16[512,1024]{1,0:T(8,128)(2,1)} %wi_own_hbm.1), channel_id=1, source_target_pairs={{0,1},{1,0},{2,3},{3,2},{4,5},{5,4},{6,7},{7,6},{8,9},{9,8},{10,11... | collective-permute-start | bytes 3145736 | tf_op jit(solution)/shard_map/ppermute | solution.py:1140
  1.2 5.5 %collective-permute-start.2 = (bf16[1024,512]{1,0:T(8,128)(2,1)}, bf16[1024,512]{1,0:T(8,128)(2,1)S(1)}, u32[]{:S(2)}, u32[]{:S(2)}) collective-permute-start(bf16[1024,512]{1,0:T(8,128)(2,1)} %wo_own_ref.1), channel_id=1, source_target_pairs={{0,1},{1,0},{2,3},{3,2},{4,5},{5,4},{6,7},{7,6},{8,9},{9,8},{10,11... | collective-permute-start | bytes 3145736 | tf_op jit(solution)/shard_map/ppermute | solution.py:1140
  1.2 5.4 %collective-permute-start.4 = (bf16[3,512,256]{2,1,0:T(8,128)(2,1)}, bf16[3,512,256]{2,1,0:T(8,128)(2,1)S(1)}, u32[]{:S(2)}, u32[]{:S(2)}) collective-permute-start(bf16[3,512,256]{2,1,0:T(8,128)(2,1)} %bitcast.10), channel_id=1, source_target_pairs={{0,1},{1,0},{2,3},{3,2},{4,5},{5,4},{6,7},{7,6},{8,9},{9,8},{10,11... | collective-permute-start | bytes 2359304 | tf_op jit(solution)/shard_map/ppermute | solution.py:1140
  1.7 5.0 %collective-permute-start.3 = (bf16[256,512]{1,0:T(8,128)(2,1)}, bf16[256,512]{1,0:T(8,128)(2,1)S(1)}, u32[]{:S(2)}, u32[]{:S(2)}) collective-permute-start(bf16[256,512]{1,0:T(8,128)(2,1)} %wa_own_ref.3), channel_id=1, source_target_pairs={{0,1},{1,0},{2,3},{3,2},{4,5},{5,4},{6,7},{7,6},{8,9},{9,8},{10,11... | collective-permute-start | bytes 786440 | tf_op jit(solution)/shard_map/ppermute | solution.py:1140
  6.7 5.9 %copy-start.8 = (bf16[256,512]{1,0:T(8,128)(2,1)}, bf16[256,512]{1,0:T(8,128)(2,1)S(1)}, u32[]{:S(2)}) copy-start(bf16[256,512]{1,0:T(8,128)(2,1)S(1)} %collective-permute-done.3.wa_other_ref) | copy-start | bytes 786436
  6.7 5.9 %copy-start.7 = (bf16[512,1024]{1,0:T(8,128)(2,1)}, bf16[512,1024]{1,0:T(8,128)(2,1)S(1)}, u32[]{:S(2)}) copy-start(bf16[512,1024]{1,0:T(8,128)(2,1)S(1)} %collective-permute-done.1.wi_other_hbm) | copy-start | bytes 3145732
  6.7 7.6 %copy-start.1 = (bf16[1024,512]{1,0:T(8,128)(2,1)}, bf16[1024,512]{1,0:T(8,128)(2,1)S(1)}, u32[]{:S(2)}) copy-start(bf16[1024,512]{1,0:T(8,128)(2,1)S(1)} %collective-permute-done.2.wo_other_hbm.wo_other_ref) | copy-start | bytes 3145732
  6.7 1.0 copy-start
  7.7 5.3 %copy-start.22 = (f32[2,4]{1,0:T(2,128)S(1)}, f32[2,4]{1,0:T(2,128)}, u32[]{:S(2)}) copy-start(f32[2,4]{1,0:T(2,128)} %blend_own_ref.3) | copy-start | bytes 100
  12.6 1.7 collective-permute-start.5
  13.0 1.1 collective-permute-start
  14.1 0.6 copy-start.23
  14.3 0.7 copy-start.21
  46.6 4.5 %copy-start.10 = (bf16[2048,256]{1,0:T(8,128)(2,1)S(1)}, bf16[2048,256]{1,0:T(8,128)(2,1)}, u32[]{:S(2)}) copy-start(bf16[2048,256]{1,0:T(8,128)(2,1)} %get-tuple-element.126) | copy-start | bytes 3145732
  46.6 2.9 %collective-permute-start.6 = (bf16[2048,256]{1,0:T(8,128)(2,1)}, bf16[2048,256]{1,0:T(8,128)(2,1)S(1)}, u32[]{:S(2)}, u32[]{:S(2)}) collective-permute-start(bf16[2048,256]{1,0:T(8,128)(2,1)} %get-tuple-element.125), channel_id=1, source_target_pairs={{0,1},{1,0},{2,3},{3,2},{4,5},{5,4},{6,7},{7,6},{8,9},{9,8},{10,11... | collective-permute-start | bytes 3145736 | tf_op jit(solution)/shard_map/ppermute | solution.py:1140
  47.0 4.0 %collective-permute-start.7 = (bf16[2048,256]{1,0:T(8,128)(2,1)}, bf16[2048,256]{1,0:T(8,128)(2,1)S(1)}, u32[]{:S(2)}, u32[]{:S(2)}) collective-permute-start(bf16[2048,256]{1,0:T(8,128)(2,1)} %get-tuple-element.127), channel_id=1, source_target_pairs={{0,1},{1,0},{2,3},{3,2},{4,5},{5,4},{6,7},{7,6},{8,9},{9,8},{10,11... | collective-permute-start | bytes 3145736 | tf_op jit(solution)/shard_map/ppermute | solution.py:1140
  49.5 22.7 %copy-start.11 = (bf16[2048,256]{1,0:T(8,128)(2,1)}, bf16[2048,256]{1,0:T(8,128)(2,1)S(1)}, u32[]{:S(2)}) copy-start(bf16[2048,256]{1,0:T(8,128)(2,1)S(1)} %collective-permute-done.6) | copy-start | bytes 3145732
  51.1 5.5 %copy-start.12 = (bf16[2048,256]{1,0:T(8,128)(2,1)}, bf16[2048,256]{1,0:T(8,128)(2,1)S(1)}, u32[]{:S(2)}) copy-start(bf16[2048,256]{1,0:T(8,128)(2,1)S(1)} %collective-permute-done.7) | copy-start | bytes 3145732
  52.2 20.0 %collective-permute-start.8 = (bf16[1024,256]{1,0:T(8,128)(2,1)S(1)}, bf16[1024,256]{1,0:T(8,128)(2,1)}, u32[]{:S(2)}, u32[]{:S(2)}) collective-permute-start(bf16[1024,256]{1,0:T(8,128)(2,1)S(1)} %add_convert_fusion.1), channel_id=1, source_target_pairs={{0,2},{2,0},{4,6},{6,4},{8,10},{10,8},{12,14},{14,12},{16,18},{18,... | collective-permute-start | bytes 1572872 | tf_op jit(solution)/shard_map/ppermute | solution.py:1012
  55.0 17.1 %collective-permute-start.9 = (bf16[1024,256]{1,0:T(8,128)(2,1)}, bf16[1024,256]{1,0:T(8,128)(2,1)}, u32[]{:S(2)}, u32[]{:S(2)}) collective-permute-start(bf16[1024,256]{1,0:T(8,128)(2,1)} %add_convert_fusion), channel_id=1, source_target_pairs={{0,4},{2,6},{4,0},{6,2},{8,12},{10,14},{12,8},{14,10},{16,20},{18,... | collective-permute-start | bytes 1572872 | tf_op jit(solution)/shard_map/ppermute | solution.py:1012
  56.5 15.7 %copy-start.9 = (bf16[2048,256]{1,0:T(8,128)(2,1)S(1)}, bf16[2048,256]{1,0:T(8,128)(2,1)}, u32[]{:S(2)}) copy-start(bf16[2048,256]{1,0:T(8,128)(2,1)} %get-tuple-element.124) | copy-start | bytes 3145732
  72.1 1.7 collective-permute-start.10
  73.9 0.7 copy-start.20
  74.6 9.8 %collective-permute-start.11 = (bf16[512,256]{1,0:T(8,128)(2,1)S(1)}, bf16[512,256]{1,0:T(8,128)(2,1)S(1)}, u32[]{:S(2)}, u32[]{:S(2)}) collective-permute-start(bf16[512,256]{1,0:T(8,128)(2,1)S(1)} %get-tuple-element.144), channel_id=1, source_target_pairs={{0,4},{2,6},{4,0},{6,2},{8,12},{10,14},{12,8},{14,10},{16,20},{18,... | collective-permute-start | bytes 786440 | tf_op jit(solution)/shard_map/ppermute | solution.py:1012
  75.1 9.4 %collective-permute-start.12 = (bf16[512,256]{1,0:T(8,128)(2,1)S(1)}, bf16[512,256]{1,0:T(8,128)(2,1)S(1)}, u32[]{:S(2)}, u32[]{:S(2)}) collective-permute-start(bf16[512,256]{1,0:T(8,128)(2,1)S(1)} %get-tuple-element.145), channel_id=1, source_target_pairs={{0,2},{2,0},{4,6},{6,4},{8,10},{10,8},{12,14},{14,12},{16,18},{18,... | collective-permute-start | bytes 786440 | tf_op jit(solution)/shard_map/ppermute | solution.py:1012
  84.4 3.7 %copy-start.6 = (bf16[2112,256]{1,0:T(8,128)(2,1)S(1)}, bf16[2112,256]{1,0:T(8,128)(2,1)}, u32[]{:S(2)}) copy-start(bf16[2112,256]{1,0:T(8,128)(2,1)} %get-tuple-element.143) | copy-start | bytes 3244036
  84.4 4.6 %copy-start.18 = (bf16[512,256]{1,0:T(8,128)(2,1)}, bf16[512,256]{1,0:T(8,128)(2,1)S(1)}, u32[]{:S(2)}) copy-start(bf16[512,256]{1,0:T(8,128)(2,1)S(1)} %collective-permute-done.11) | copy-start | bytes 786436
  84.4 0.7 copy-start.19
  85.2 3.0 %collective-permute-start.13 = (bf16[2112,256]{1,0:T(8,128)(2,1)}, bf16[2112,256]{1,0:T(8,128)(2,1)S(1)}, u32[]{:S(2)}, u32[]{:S(2)}) collective-permute-start(bf16[2112,256]{1,0:T(8,128)(2,1)} %get-tuple-element.147), channel_id=1, source_target_pairs={{0,1},{1,0},{2,3},{3,2},{4,5},{5,4},{6,7},{7,6},{8,9},{9,8},{10,11... | collective-permute-start | bytes 3244040 | tf_op jit(solution)/shard_map/ppermute | solution.py:1140
  89.1 11.4 %collective-permute-start.14 = (bf16[528,256]{1,0:T(8,128)(2,1)}, bf16[528,256]{1,0:T(8,128)(2,1)S(1)}, u32[]{:S(2)}, u32[]{:S(2)}) collective-permute-start(bf16[528,256]{1,0:T(8,128)(2,1)} %get-tuple-element.152), channel_id=1, source_target_pairs={{0,2},{2,0},{4,6},{6,4},{8,10},{10,8},{12,14},{14,12},{16,18},{18,... | collective-permute-start | bytes 811016 | tf_op jit(solution)/shard_map/ppermute | solution.py:1012
  91.0 9.4 %collective-permute-start.15 = (bf16[528,256]{1,0:T(8,128)(2,1)}, bf16[528,256]{1,0:T(8,128)(2,1)}, u32[]{:S(2)}, u32[]{:S(2)}) collective-permute-start(bf16[528,256]{1,0:T(8,128)(2,1)} %get-tuple-element.153), channel_id=1, source_target_pairs={{0,4},{2,6},{4,0},{6,2},{8,12},{10,14},{12,8},{14,10},{16,20},{18,... | collective-permute-start | bytes 811016 | tf_op jit(solution)/shard_map/ppermute | solution.py:1012
  92.5 8.5 %collective-permute-start.16 = (bf16[512,256]{1,0:T(8,128)(2,1)}, bf16[512,256]{1,0:T(8,128)(2,1)}, u32[]{:S(2)}, u32[]{:S(2)}) collective-permute-start(bf16[512,256]{1,0:T(8,128)(2,1)} %pad_maximum_fusion.6), channel_id=1, source_target_pairs={{0,8},{2,10},{4,12},{6,14},{8,0},{10,2},{12,4},{14,6},{16,24},{18,... | collective-permute-start | bytes 786440 | tf_op jit(solution)/shard_map/ppermute | solution.py:1012
  100.4 7.8 %copy-start.17 = (bf16[528,256]{1,0:T(8,128)(2,1)}, bf16[528,256]{1,0:T(8,128)(2,1)S(1)}, u32[]{:S(2)}) copy-start(bf16[528,256]{1,0:T(8,128)(2,1)S(1)} %collective-permute-done.14) | copy-start | bytes 811012
  104.6 8.6 %collective-permute-start.19 = (bf16[256,256]{1,0:T(8,128)(2,1)}, bf16[256,256]{1,0:T(8,128)(2,1)}, u32[]{:S(2)}, u32[]{:S(2)}) collective-permute-start(bf16[256,256]{1,0:T(8,128)(2,1)} %pad_maximum_fusion.10), channel_id=1, source_target_pairs={{0,16},{2,18},{4,20},{6,22},{8,24},{10,26},{12,28},{14,30},{16,0},... | collective-permute-start | bytes 393224 | tf_op jit(solution)/shard_map/ppermute | solution.py:1012
  107.2 7.3 %collective-permute-start.17 = (bf16[264,256]{1,0:T(8,128)(2,1)}, bf16[264,256]{1,0:T(8,128)(2,1)S(1)}, u32[]{:S(2)}, u32[]{:S(2)}) collective-permute-start(bf16[264,256]{1,0:T(8,128)(2,1)} %get-tuple-element.162), channel_id=1, source_target_pairs={{0,4},{2,6},{4,0},{6,2},{8,12},{10,14},{12,8},{14,10},{16,20},{18,... | collective-permute-start | bytes 405512 | tf_op jit(solution)/shard_map/ppermute | solution.py:1012
  107.7 6.8 %collective-permute-start.18 = (bf16[264,256]{1,0:T(8,128)(2,1)}, bf16[264,256]{1,0:T(8,128)(2,1)S(1)}, u32[]{:S(2)}, u32[]{:S(2)}) collective-permute-start(bf16[264,256]{1,0:T(8,128)(2,1)} %get-tuple-element.163), channel_id=1, source_target_pairs={{0,2},{2,0},{4,6},{6,4},{8,10},{10,8},{12,14},{14,12},{16,18},{18,... | collective-permute-start | bytes 405512 | tf_op jit(solution)/shard_map/ppermute | solution.py:1012
  115.7 8.4 %collective-permute-start.21 = (bf16[256,256]{1,0:T(8,128)(2,1)S(1)}, bf16[256,256]{1,0:T(8,128)(2,1)S(1)}, u32[]{:S(2)}, u32[]{:S(2)}) collective-permute-start(bf16[256,256]{1,0:T(8,128)(2,1)S(1)} %pad_maximum_fusion.11), channel_id=1, source_target_pairs={{0,16},{2,18},{4,20},{6,22},{8,24},{10,26},{12,28},{14,30},{16,0},... | collective-permute-start | bytes 393224 | tf_op jit(solution)/shard_map/ppermute | solution.py:1012
  115.9 11.4 %collective-permute-start.20 = (bf16[528,256]{1,0:T(8,128)(2,1)S(1)}, bf16[528,256]{1,0:T(8,128)(2,1)S(1)}, u32[]{:S(2)}, u32[]{:S(2)}) collective-permute-start(bf16[528,256]{1,0:T(8,128)(2,1)S(1)} %pad_maximum_fusion.2), channel_id=1, source_target_pairs={{0,8},{2,10},{4,12},{6,14},{8,0},{10,2},{12,4},{14,6},{16,24},{18,... | collective-permute-start | bytes 811016 | tf_op jit(solution)/shard_map/ppermute | solution.py:1012
  127.3 12.6 %collective-permute-start.23 = (bf16[512,256]{1,0:T(8,128)(2,1)S(1)}, bf16[512,256]{1,0:T(8,128)(2,1)S(1)}, u32[]{:S(2)}, u32[]{:S(2)}) collective-permute-start(bf16[512,256]{1,0:T(8,128)(2,1)S(1)} %pad_maximum_fusion.7), channel_id=1, source_target_pairs={{0,8},{2,10},{4,12},{6,14},{8,0},{10,2},{12,4},{14,6},{16,24},{18,... | collective-permute-start | bytes 786440 | tf_op jit(solution)/shard_map/ppermute | solution.py:1012
  127.8 14.4 %collective-permute-start.22 = (bf16[528,256]{1,0:T(8,128)(2,1)S(1)}, bf16[528,256]{1,0:T(8,128)(2,1)S(1)}, u32[]{:S(2)}, u32[]{:S(2)}) collective-permute-start(bf16[528,256]{1,0:T(8,128)(2,1)S(1)} %pad_maximum_fusion.3), channel_id=1, source_target_pairs={{0,16},{2,18},{4,20},{6,22},{8,24},{10,26},{12,28},{14,30},{16,0},... | collective-permute-start | bytes 811016 | tf_op jit(solution)/shard_map/ppermute | solution.py:1012
  142.2 5.1 %collective-permute-start.26 = (bf16[264,256]{1,0:T(8,128)(2,1)S(1)}, bf16[264,256]{1,0:T(8,128)(2,1)S(1)}, u32[]{:S(2)}, u32[]{:S(2)}) collective-permute-start(bf16[264,256]{1,0:T(8,128)(2,1)S(1)} %get-tuple-element.182), channel_id=1, source_target_pairs={{0,4},{2,6},{4,0},{6,2},{8,12},{10,14},{12,8},{14,10},{16,20},{18,... | collective-permute-start | bytes 405512 | tf_op jit(solution)/shard_map/ppermute | solution.py:1012
  143.4 10.8 %collective-permute-start.24 = (bf16[512,256]{1,0:T(8,128)(2,1)S(1)}, bf16[512,256]{1,0:T(8,128)(2,1)S(1)}, u32[]{:S(2)}, u32[]{:S(2)}) collective-permute-start(bf16[512,256]{1,0:T(8,128)(2,1)S(1)} %pad_maximum_fusion.8), channel_id=1, source_target_pairs={{0,4},{2,6},{4,0},{6,2},{8,12},{10,14},{12,8},{14,10},{16,20},{18,... | collective-permute-start | bytes 786440 | tf_op jit(solution)/shard_map/ppermute | solution.py:1012
  144.3 10.1 %collective-permute-start.25 = (bf16[512,256]{1,0:T(8,128)(2,1)S(1)}, bf16[512,256]{1,0:T(8,128)(2,1)S(1)}, u32[]{:S(2)}, u32[]{:S(2)}) collective-permute-start(bf16[512,256]{1,0:T(8,128)(2,1)S(1)} %pad_maximum_fusion.9), channel_id=1, source_target_pairs={{0,2},{2,0},{4,6},{6,4},{8,10},{10,8},{12,14},{14,12},{16,18},{18,... | collective-permute-start | bytes 786440 | tf_op jit(solution)/shard_map/ppermute | solution.py:1012
  144.9 9.2 %collective-permute-start.27 = (bf16[264,256]{1,0:T(8,128)(2,1)S(1)}, bf16[264,256]{1,0:T(8,128)(2,1)S(1)}, u32[]{:S(2)}, u32[]{:S(2)}) collective-permute-start(bf16[264,256]{1,0:T(8,128)(2,1)S(1)} %get-tuple-element.183), channel_id=1, source_target_pairs={{0,2},{2,0},{4,6},{6,4},{8,10},{10,8},{12,14},{14,12},{16,18},{18,... | collective-permute-start | bytes 405512 | tf_op jit(solution)/shard_map/ppermute | solution.py:1012
  154.1 2.2 %copy-start.4 = (bf16[528,256]{1,0:T(8,128)(2,1)}, bf16[528,256]{1,0:T(8,128)(2,1)S(1)}, u32[]{:S(2)}) copy-start(bf16[528,256]{1,0:T(8,128)(2,1)S(1)} %pad_maximum_fusion.4.a_mine_hbm) | copy-start | bytes 811012
  154.2 3.7 %copy-start.5 = (bf16[528,256]{1,0:T(8,128)(2,1)}, bf16[528,256]{1,0:T(8,128)(2,1)S(1)}, u32[]{:S(2)}) copy-start(bf16[528,256]{1,0:T(8,128)(2,1)S(1)} %pad_maximum_fusion.5.b_mine_hbm) | copy-start | bytes 811012
  154.4 5.0 %copy-start.2 = (bf16[1024,256]{1,0:T(8,128)(2,1)}, bf16[1024,256]{1,0:T(8,128)(2,1)S(1)}, u32[]{:S(2)}) copy-start(bf16[1024,256]{1,0:T(8,128)(2,1)S(1)} %pad_maximum_fusion.out_part_ref) | copy-start | bytes 1572868
  154.5 4.8 %copy-start.3 = (bf16[1024,256]{1,0:T(8,128)(2,1)}, bf16[1024,256]{1,0:T(8,128)(2,1)S(1)}, u32[]{:S(2)}) copy-start(bf16[1024,256]{1,0:T(8,128)(2,1)S(1)} %pad_maximum_fusion.1.in_part_ref) | copy-start | bytes 1572868
  154.5 14.6 %collective-permute-start.28 = (bf16[1024,256]{1,0:T(8,128)(2,1)S(1)}, bf16[1024,256]{1,0:T(8,128)(2,1)S(1)}, u32[]{:S(2)}, u32[]{:S(2)}) collective-permute-start(bf16[1024,256]{1,0:T(8,128)(2,1)S(1)} %pad_maximum_fusion.out_part_ref), channel_id=1, source_target_pairs={{0,2},{2,0},{4,6},{6,4},{8,10},{10,8},{12,14},{14,12},{16,18},{18,... | collective-permute-start | bytes 1572872 | tf_op jit(solution)/shard_map/ppermute | solution.py:1012
  155.2 14.0 %collective-permute-start.29 = (bf16[1024,256]{1,0:T(8,128)(2,1)S(1)}, bf16[1024,256]{1,0:T(8,128)(2,1)S(1)}, u32[]{:S(2)}, u32[]{:S(2)}) collective-permute-start(bf16[1024,256]{1,0:T(8,128)(2,1)S(1)} %pad_maximum_fusion.1.in_part_ref), channel_id=1, source_target_pairs={{0,4},{2,6},{4,0},{6,2},{8,12},{10,14},{12,8},{14,10},{16,20},{18,... | collective-permute-start | bytes 1572872 | tf_op jit(solution)/shard_map/ppermute | solution.py:1012
  156.4 12.8 %collective-permute-start.30 = (bf16[528,256]{1,0:T(8,128)(2,1)S(1)}, bf16[528,256]{1,0:T(8,128)(2,1)S(1)}, u32[]{:S(2)}, u32[]{:S(2)}) collective-permute-start(bf16[528,256]{1,0:T(8,128)(2,1)S(1)} %pad_maximum_fusion.4.a_mine_hbm), channel_id=1, source_target_pairs={{0,2},{2,0},{4,6},{6,4},{8,10},{10,8},{12,14},{14,12},{16,18},{18,... | collective-permute-start | bytes 811016 | tf_op jit(solution)/shard_map/ppermute | solution.py:1012
  157.9 11.3 %collective-permute-start.31 = (bf16[528,256]{1,0:T(8,128)(2,1)S(1)}, bf16[528,256]{1,0:T(8,128)(2,1)S(1)}, u32[]{:S(2)}, u32[]{:S(2)}) collective-permute-start(bf16[528,256]{1,0:T(8,128)(2,1)S(1)} %pad_maximum_fusion.5.b_mine_hbm), channel_id=1, source_target_pairs={{0,4},{2,6},{4,0},{6,2},{8,12},{10,14},{12,8},{14,10},{16,20},{18,... | collective-permute-start | bytes 811016 | tf_op jit(solution)/shard_map/ppermute | solution.py:1012
  169.1 0.7 copy-start.15
  169.1 0.8 copy-start.16
  169.2 1.0 copy-start.13
  169.2 1.1 copy-start.14

commit v5 on v4

--- a/solution.py
+++ b/solution.py
@@ -10,6 +10,7 @@
 BAND = 30
 HALO = 32
 EXTRA = 64
+LATE_TURN = 1
 BLOCK = 128
 EPS = 1e-06
 BF = jnp.bfloat16
@@ -912,13 +913,6 @@
     return jnp.where(low, mine, got), jnp.where(low, got, mine)
 
 
-def put_part_kernel(parts_ref, out_part_ref, in_part_ref, wo_ref, wi_ref):
-    wo_ref[...] = out_part_ref[...].astype(F32)
-    width = wi_ref.shape[0]
-    for side in range(wi_ref.shape[1] // LANES):
-        wi_ref[:, LANES * side : LANES * side + LANES] = in_part_ref[width * side : width * side + width].astype(F32)
-
-
 def put_rows(ref, first_row, lane, parts, first, count):
     rows = parts[0].shape[0]
     lanes = parts[0].shape[1]
@@ -929,70 +923,91 @@
             ref[first_row + low - first : first_row + high - first, lane : lane + lanes] = values
 
 
+def feed_output_kernel(
+    bits_ref,
+    out_mine_hbm,
+    in_mine_hbm,
+    out_got_hbm,
+    in_got_hbm,
+    wo_hbm,
+    wi_hbm,
+    out_mine_ref,
+    in_mine_ref,
+    out_got_ref,
+    in_got_ref,
+    wo_ref,
+    wi_ref,
+    sems,
+):
+    copies = Copies(sems)
+    parts = ((out_mine_ref, in_mine_ref), (out_got_ref, in_got_ref))
+    loads = [
+        copies.make(source, target)
+        for source, target in (
+            (out_mine_hbm, out_mine_ref),
+            (in_mine_hbm, in_mine_ref),
+            (out_got_hbm, out_got_ref),
+            (in_got_hbm, in_got_ref),
+        )
+    ]
+    for load in loads:
+        load.start()
+    units, wide = wo_ref.shape[1], wo_ref.shape[2]
+    width, span = wi_ref.shape[1], wi_ref.shape[2]
+    middle = units // 2
+    stores = []
+    for place, (out_part_ref, in_part_ref) in enumerate(parts):
+        wo_first = bits_ref[0] if place == 0 else 1 - bits_ref[0]
+        wi_first = bits_ref[1] if place == 0 else 1 - bits_ref[1]
+        loads[2 * place].wait()
+        wo_ref[place] = out_part_ref[...].astype(F32)
+        column = pl.multiple_of(wo_first * wide, LANES)
+        for rows in (slice(0, middle), slice(middle, units)):
+            stores.append(copies.make(wo_ref.at[place, rows], wo_hbm.at[rows, pl.ds(column, wide)]))
+            stores[-1].start()
+        loads[2 * place + 1].wait()
+        for side in range(span // LANES):
+            lanes = slice(LANES * side, LANES * side + LANES)
+            wi_ref[place, :, lanes] = in_part_ref[width * side : width * side + width].astype(F32)
+            column = pl.multiple_of(wi_first * span + LANES * side, LANES)
+            stores.append(copies.make(wi_ref.at[place, :, lanes], wi_hbm.at[:, pl.ds(column, LANES)]))
+            stores[-1].start()
+    for store in stores:
+        store.wait()
+
+
 def last_output_kernel(
     bits_ref,
-    out_part_hbm,
-    in_part_hbm,
     a_mine_hbm,
+    b_mine_hbm,
     a_got_hbm,
-    b_mine_hbm,
     b_got_hbm,
-    wo_before_hbm,
-    wi_before_hbm,
-    wo_hbm,
-    wi_hbm,
     wq_ref,
     wa_ref,
     gain_one_ref,
     gain_two_ref,
     blend_ref,
-    out_part_ref,
-    in_part_ref,
     a_mine_ref,
+    b_mine_ref,
     a_got_ref,
-    b_mine_ref,
     b_got_ref,
-    wo_ref,
-    wi_ref,
     sems,
 ):
     copies = Copies(sems)
     loads = [
         copies.make(source, target)
         for source, target in (
-            (out_part_hbm, out_part_ref),
-            (in_part_hbm, in_part_ref),
             (a_mine_hbm, a_mine_ref),
+            (b_mine_hbm, b_mine_ref),
             (a_got_hbm, a_got_ref),
-            (b_mine_hbm, b_mine_ref),
             (b_got_hbm, b_got_ref),
         )
     ]
     for load in loads:
         load.start()
-    wo_column = pl.multiple_of((1 - bits_ref[0]) * wo_ref.shape[1], LANES)
-    wi_column = pl.multiple_of((1 - bits_ref[1]) * wi_ref.shape[1], LANES)
-    middle = wo_ref.shape[0] // 2
-    stores = [
-        copies.make(wo_ref.at[span], wo_hbm.at[span, pl.ds(wo_column, wo_ref.shape[1])])
-        for span in (slice(0, middle), slice(middle, 2 * middle))
-    ]
-    for side in range(wi_ref.shape[1] // LANES):
-        lanes = slice(LANES * side, LANES * side + LANES)
-        target = wi_hbm.at[:, pl.ds(pl.multiple_of(wi_column + LANES * side, LANES), LANES)]
-        stores.append(copies.make(wi_ref.at[:, lanes], target))
-    for load in loads[:2]:
+    for load in loads:
         load.wait()
-    wo_ref[...] = out_part_ref[...].astype(F32)
-    for store in stores[:2]:
-        store.start()
-    width = wi_ref.shape[0]
-    for side in range(wi_ref.shape[1] // LANES):
-        wi_ref[:, LANES * side : LANES * side + LANES] = in_part_ref[width * side : width * side + width].astype(F32)
-        stores[2 + side].start()
-    for load in loads[2:]:
-        load.wait()
-    heads = wa_ref.shape[0]
+    heads, width = wa_ref.shape
     parts = merged(bits_ref[0] == 0, a_mine_ref[...], a_got_ref[...])
     parts += merged(bits_ref[1] == 0, b_mine_ref[...], b_got_ref[...])
     rows = a_mine_ref.shape[0]
@@ -1004,21 +1019,35 @@
     gain_two_ref[...] = jnp.concatenate([rest[4:5], rest[5:6]], axis=1)
     sums = [jnp.sum(rest[:2, 64 * head : 64 * head + 64], axis=1, keepdims=True) for head in range(4)]
     blend_ref[...] = jnp.concatenate(sums, axis=1)
-    for store in stores:
-        store.wait()
-
-
-def flip(values, count, stride):
-    return lax.ppermute(values, "dp", [(src, src ^ stride) for src in range(count)])
-
-
-def strides_of(count):
-    strides = []
+
+
+def steps_of(count, late_sizes):
+    steps = []
     stride = 1
     while stride < count:
-        strides.append(stride)
-        stride *= 2
-    return strides
+        left = count // stride
+        size = next(size for size in ((2,) if len(steps) < 2 else late_sizes) if left % size == 0)
+        steps.append((stride, size))
+        stride *= size
+    return steps
+
+
+def flip(values, count, step):
+    stride, _ = step
+    pairs = [(src, src + stride * (1 - 2 * ((src // stride) % 2))) for src in range(count)]
+    return lax.ppermute(values, "dp", pairs)
+
+
+def trade(values, count, step):
+    stride, size = step
+    groups = [
+        [first + stride * digit for digit in range(size)]
+        for first in range(count)
+        if (first // stride) % size == 0
+    ]
+    return lax.all_to_all(
+        values, "dp", split_axis=0, concat_axis=0, axis_index_groups=groups, tiled=True
+    )
 
 
 class Reduction:
@@ -1026,114 +1055,120 @@
         self.stacks = [[(term, first) for term in terms] for terms, first, _ in stacks]
         self.rows = [rows for _, _, rows in stacks]
         self.count = count
-        strides = strides_of(count)
-        self.orders = [strides, strides[1::-1] + strides[2:]]
-        self.steps = len(strides)
+        steps = steps_of(count, (2,) if whole_late else (4, 2))
+        self.orders = [steps, steps[1::-1] + steps[2:]]
+        self.whole_late = whole_late
+        self.left = min(2, len(steps)) if whole_late else len(steps)
         self.taken = 0
-        self.halved = min(2, self.steps) if whole_late else self.steps
         self.place = lax.axis_index("dp")
         self.held = None
-
-    def bit(self, stride):
-        return (self.place // stride) % 2
-
-    def after(self, *tokens):
-        if self.held is not None:
-            *self.gots, first, second = tie(*self.gots, *self.held)
-            self.held = [first, second]
-            return tokens
-        news = [terms[-1][0] for terms in self.stacks]
-        if news[0] is news[1]:
-            news = news[:1]
-        tied = tie(*news, *tokens)
-        for stack in range(2):
-            offset = self.stacks[stack][-1][1]
-            self.stacks[stack][-1] = (tied[min(stack, len(news) - 1)], offset)
-        return tied[len(news) :]
-
-    def cut(self, stack, rows, skip):
+        self.gots = []
+
+    def digit(self, step):
+        return (self.place // step[0]) % step[1]
+
+    def cut(self, stack, first, rows):
         total = None
         for term, offset in self.stacks[stack]:
-            part = lax.dynamic_slice_in_dim(term, offset + skip, rows, 0).astype(F32)
+            part = lax.dynamic_slice_in_dim(term, offset + first, rows, 0).astype(F32)
             total = part if total is None else total + part
         return total.astype(BF)
 
-    def outgoing(self):
-        cuts = []
-        for stack in range(2):
-            if self.taken < self.halved:
+    def after(self, *tokens):
+        count = len(self.gots)
+        tied = tie(*self.gots, *tokens)
+        self.gots = list(tied[:count])
+        return tied[count:]
+
+    def gathering(self):
+        return self.taken == len(self.orders[0])
+
+    def level(self):
+        return self.left - 1 if self.gathering() else self.taken
+
+    def cuts(self):
+        if self.gathering():
+            if self.held is None:
+                self.held = [self.cut(stack, 0, self.rows[stack]) for stack in range(2)]
+            if self.level() < 2:
+                return list(self.held)
+            both = jnp.concatenate(self.held, axis=0)
+            return [jnp.broadcast_to(both[None], (self.orders[0][self.level()][1],) + both.shape)]
+        if self.level() < 2:
+            cuts = []
+            for stack in range(2):
+                step = self.orders[stack][self.level()]
+                rows = self.rows[stack] // 2
+                cuts.append(self.cut(stack, (1 - self.digit(step)) * rows, rows))
+            return cuts
+        size = self.orders[0][self.level()][1]
+        wholes = [self.cut(stack, 0, self.rows[stack]) for stack in range(2)]
+        if self.whole_late:
+            self.sent = jnp.concatenate(wholes, axis=0)
+            return [self.sent]
+        return [jnp.concatenate([part.reshape(size, -1, part.shape[1]) for part in wholes], axis=1)]
+
+    def send(self, cuts):
+        steps = [order[self.level()] for order in self.orders]
+        if self.level() < 2:
+            self.gots = [flip(cut, self.count, step) for cut, step in zip(cuts, steps)]
+        elif self.whole_late:
+            self.sent = cuts[0]
+            self.gots = [flip(cuts[0], self.count, steps[0])]
+        else:
+            self.gots = [trade(cuts[0], self.count, steps[0])]
+
+    def take(self):
+        steps = [order[self.level()] for order in self.orders]
+        size = steps[0][1]
+        if self.gathering():
+            if self.level() < 2:
+                for stack in range(2):
+                    low = self.digit(steps[stack]) == 0
+                    mine, got = self.held[stack], self.gots[stack]
+                    self.held[stack] = jnp.concatenate(
+                        [jnp.where(low, mine, got), jnp.where(low, got, mine)], axis=0
+                    )
+            else:
+                first = self.held[0].shape[0]
+                (got,) = self.gots
+                self.held = [part.reshape(-1, part.shape[2]) for part in (got[:, :first], got[:, first:])]
+            self.left -= 1
+            self.gots = []
+            return
+        if self.level() < 2:
+            for stack in range(2):
                 self.rows[stack] //= 2
-                bit = self.bit(self.orders[stack][self.taken])
-                cuts.append(self.cut(stack, self.rows[stack], (1 - bit) * self.rows[stack]))
-            else:
-                cuts.append(self.cut(stack, self.rows[stack], 0))
-        return cuts if self.taken < 2 else [jnp.concatenate(cuts, axis=0)]
-
-    def send(self, cuts):
-        gots = [flip(cut, self.count, self.orders[stack][self.taken]) for stack, cut in enumerate(cuts)]
-        for stack in range(2):
-            skip = self.rows[0] if stack == 1 and len(cuts) == 1 else 0
-            got = gots[min(stack, len(cuts) - 1)]
-            if self.taken < self.halved:
-                bit = self.bit(self.orders[stack][self.taken])
-                kept = [(term, offset + bit * self.rows[stack]) for term, offset in self.stacks[stack]]
-            else:
-                kept = [(cuts[0], skip)]
-            self.stacks[stack] = kept + [(got, skip)]
+                offset = self.digit(steps[stack]) * self.rows[stack]
+                terms = [(term, first + offset) for term, first in self.stacks[stack]]
+                self.stacks[stack] = terms + [(self.gots[stack], 0)]
+        elif self.whole_late:
+            (got,) = self.gots
+            self.stacks = [[(self.sent, skip), (got, skip)] for skip in (0, self.rows[0])]
+        else:
+            (got,) = self.gots
+            self.rows = [rows // size for rows in self.rows]
+            flat = got.reshape(-1, got.shape[2])
+            for stack in range(2):
+                skip = self.rows[0] * stack
+                self.stacks[stack] = [(flat, sum(self.rows) * piece + skip) for piece in range(size)]
         self.taken += 1
-
-    def start_gather(self):
-        self.held = [self.cut(stack, self.rows[stack], 0) for stack in range(2)]
-
-    def gather_outgoing(self):
-        return list(self.held) if self.halved <= 2 else [jnp.concatenate(self.held, axis=0)]
-
-    def gather_send(self, cuts):
-        step = self.halved - 1
-        gots = [flip(cut, self.count, self.orders[stack][step]) for stack, cut in enumerate(cuts)]
-        if len(gots) == 1:
-            first = self.held[0].shape[0]
-            gots = [gots[0][:first], gots[0][first:]]
-        self.gots = gots
-        self.halved = step
-
-    def finished(self):
-        return self.taken == self.steps and (self.steps == 0 or (self.held is not None and self.halved == 0))
-
-    def next_cuts(self):
-        if self.taken < self.steps:
-            return self.outgoing()
-        if self.held is None:
-            self.start_gather()
-        return self.gather_outgoing()
-
-    def next_send(self, cuts):
-        if self.held is None:
-            self.send(cuts)
-        else:
-            self.gather_send(cuts)
-
-    def next_take(self):
-        if self.held is not None and self.halved > 0:
-            self.gather_take()
+        self.gots = []
+
+    def last(self):
+        return self.gathering() and self.left <= 1
 
     def last_bits(self):
-        return jnp.stack([self.bit(order[0]) if order else 0 * self.place for order in self.orders])
+        return jnp.stack([self.digit(order[0]) if order else 0 * self.place for order in self.orders])
 
     def parts(self):
-        if self.steps > 0:
+        if self.orders[0]:
             return [self.held[0], self.gots[0], self.held[1], self.gots[1]]
         halves = []
-        for held in [self.cut(stack, self.rows[stack], 0) for stack in range(2)]:
+        for held in [self.cut(stack, 0, self.rows[stack]) for stack in range(2)]:
             middle = held.shape[0] // 2
             halves += [held[:middle], held[middle:]]
         return halves
-
-    def gather_take(self):
-        for stack in range(2):
-            low = self.bit(self.orders[stack][self.halved]) == 0
-            mine, got = self.held[stack], self.gots[stack]
-            self.held[stack] = jnp.concatenate([jnp.where(low, mine, got), jnp.where(low, got, mine)], axis=0)
 
 
 def swap(values):
@@ -1259,10 +1294,9 @@
     feed_sum = Reduction(
         [([out_own, swap(out_sent)], 0, stack_rows), ([in_own, swap(in_sent)], 0, stack_rows)], count
     )
-    wanted = feed_sum.steps
+    wanted = len(feed_sum.orders[0])
     if wanted > 0:
-        cuts = feed_sum.outgoing()
-        gmix, *cuts = tie(gmix, *cuts)
+        gmix, *cuts = tie(gmix, *feed_sum.cuts())
         feed_sum.send(cuts)
 
     steps = blocks // STEP_BLOCKS
@@ -1303,10 +1337,10 @@
     )(lengths, blend, blend_other, own, other, *kept, gmix)
     if wanted > 1:
         (packet_back,) = feed_sum.after(packet_back)
+        feed_sum.take()
     packet_got = swap(packet_back)
     if wanted > 1:
-        cuts = feed_sum.outgoing()
-        packet_got, *cuts = tie(packet_got, *cuts)
+        packet_got, *cuts = tie(packet_got, *feed_sum.cuts())
         feed_sum.send(cuts)
 
     wq_shape = (3 * width + attn_rows + EXTRA, own_cols // 3)
@@ -1389,80 +1423,78 @@
 
     if wanted > 1:
         (wq_sent,) = feed_sum.after(wq_sent)
+        feed_sum.take()
     wq_got = swap(wq_sent)
     cut = wq_got.shape[0] // 2
     wq_sum = Reduction([([wq_mine, wq_got], 0, cut), ([wq_mine, wq_got], cut, cut)], count, True)
-    beside = {0: lambda: input_gradient(gproj), 3: lambda: layer_output(active)}
-    done = {}
-    step = 0
-    while not (feed_sum.finished() and wq_sum.finished()):
-        running = [reduction for reduction in (wq_sum, feed_sum) if not reduction.finished()]
-        cuts = [reduction.next_cuts() for reduction in running]
-        flat = list(tie(*[cut for some in cuts for cut in some], gproj, active))
-        active, gproj = flat.pop(), flat.pop()
-        for reduction, some in zip(running, cuts):
-            reduction.next_send([flat.pop(0) for _ in some])
-        if step in beside:
-            done[step] = beside[step]()
-            for reduction in running:
-                (done[step],) = reduction.after(done[step])
-        for reduction in running:
-            reduction.next_take()
-        step += 1
-    for step in beside:
-        if step not in done:
-            done[step] = beside[step]()
-    grad_input, output = done[0], done[3]
+    if wanted == 3:
+        feed_cuts, wq_cuts = feed_sum.cuts(), wq_sum.cuts()
+        gproj, *cuts = tie(gproj, *wq_cuts, *feed_cuts)
+        wq_sum.send(cuts[: len(wq_cuts)])
+        feed_sum.send(cuts[len(wq_cuts) :])
+        grad_input = input_gradient(gproj)
+        (grad_input,) = wq_sum.after(grad_input)
+        turns = ((wq_sum,), (feed_sum, wq_sum), (feed_sum, wq_sum), (feed_sum,), (wq_sum,), (wq_sum,))
+        for turn, reductions in enumerate(turns):
+            if turn == len(turns) - 1:
+                wq_sum.gots = list(feed_sum.after(*wq_sum.gots))
+            some = []
+            for reduction in reductions:
+                reduction.take()
+                some.append(reduction.cuts())
+            active, *cuts = tie(active, *[cut for own_cuts in some for cut in own_cuts])
+            for reduction, own_cuts in zip(reductions, some):
+                reduction.send([cuts.pop(0) for _ in own_cuts])
+            if turn == LATE_TURN:
+                output = layer_output(active)
+                (output,) = feed_sum.after(output)
+                (output,) = wq_sum.after(output)
+    else:
+        grad_input, output = input_gradient(gproj), layer_output(active)
+        for reduction in (feed_sum, wq_sum):
+            while reduction.orders[0] and not (reduction.last() and reduction.gots and reduction.held is not None):
+                if reduction.gots:
+                    reduction.take()
+                reduction.send(reduction.cuts())
 
     out_mine, out_got, in_mine, in_got = feed_sum.parts()
     bits = feed_sum.last_bits()
+    feed_parts = [out_mine, in_mine, out_got, in_got]
+    wo_grad, wi_grad = pl.pallas_call(
+        feed_output_kernel,
+        in_specs=[smem] + [anywhere] * 4,
+        out_specs=[anywhere] * 2,
+        out_shape=[jax.ShapeDtypeStruct(w_out.shape, F32), jax.ShapeDtypeStruct(w_in.shape, F32)],
+        scratch_shapes=[pltpu.VMEM(part.shape, BF) for part in feed_parts]
+        + [
+            pltpu.VMEM((2, units, LANES), F32),
+            pltpu.VMEM((2, width, units // 2), F32),
+            pltpu.SemaphoreType.DMA((16,)),
+        ],
+        compiler_params=params(60),
+        cost_estimate=cost(3),
+        name="feed_output",
+    )(bits, *feed_parts)
     if wanted > 1:
-        out_mine, in_mine, *wq_sum.held = tie(out_mine, in_mine, *wq_sum.held)
-    grad_shapes = [jax.ShapeDtypeStruct(w_out.shape, F32), jax.ShapeDtypeStruct(w_in.shape, F32)]
-    wo_grad, wi_grad = pl.pallas_call(
-        put_part_kernel,
-        grid_spec=pltpu.PrefetchScalarGridSpec(
-            num_scalar_prefetch=1,
-            grid=(1,),
-            in_specs=[whole(out_mine.shape), whole(in_mine.shape)],
-            out_specs=[
-                pl.BlockSpec((units, LANES), lambda i, places: (0, places[0])),
-                pl.BlockSpec((width, units // 2), lambda i, places: (0, places[1])),
-            ],
-        ),
-        out_shape=grad_shapes,
-        compiler_params=params(60),
-        cost_estimate=cost(2),
-        name="put_part",
-    )(bits, out_mine, in_mine)
-    if wanted > 1:
-        wo_grad, wi_grad, out_got, in_got = tie(wo_grad, wi_grad, out_got, in_got)
         (wi_grad,) = wq_sum.after(wi_grad)
-    wq_parts = wq_sum.parts()
-    last_inputs = [out_got, in_got] + wq_parts
-    wo_grad, wi_grad, wq_grad, wa_grad, ggain_one, ggain_two, gblend_all = pl.pallas_call(
+    a_mine, a_got, b_mine, b_got = wq_sum.parts()
+    wq_parts = [a_mine, b_mine, a_got, b_got]
+    wq_grad, wa_grad, ggain_one, ggain_two, gblend_all = pl.pallas_call(
         last_output_kernel,
-        in_specs=[smem] + [anywhere] * 8,
-        out_specs=[anywhere] * 2 + [vmem] * 5,
-        out_shape=grad_shapes
-        + [
+        in_specs=[smem] + [anywhere] * 4,
+        out_specs=[vmem] * 5,
+        out_shape=[
             jax.ShapeDtypeStruct((3 * width, own_cols // 3), F32),
             jax.ShapeDtypeStruct(w_attn.shape, F32),
             jax.ShapeDtypeStruct((1, width), F32),
             jax.ShapeDtypeStruct((1, width), F32),
             jax.ShapeDtypeStruct(blend.shape, F32),
         ],
-        scratch_shapes=[pltpu.VMEM(part.shape, BF) for part in last_inputs]
-        + [
-            pltpu.VMEM((units, LANES), F32),
-            pltpu.VMEM((width, units // 2), F32),
-            pltpu.SemaphoreType.DMA((16,)),
-        ],
-        input_output_aliases={7: 0, 8: 1},
+        scratch_shapes=[pltpu.VMEM(part.shape, BF) for part in wq_parts] + [pltpu.SemaphoreType.DMA((4,))],
         compiler_params=params(60),
         cost_estimate=cost(3),
         name="last_output",
-    )(bits, *last_inputs, wo_grad, wi_grad)
+    )(bits, *wq_parts)
 
     return (
         output,

time: 176 us -> 170 us (0.966)
  waiting for transfers between devices: 35.3 us -> 29.1 us
  starting transfers between devices: 31.9 us -> 36.7 us
  other arithmetic: 15.1 us -> 12.1 us
    all_to_all x0 -> x2, starting transfers between devices: none -> 9.66 us  [trade(): lax.all_to_all(values, 'dp', split_axis=0, concat_axis=0, axis_index_grou...]
    ppermute x22 -> x18, waiting for transfers between devices: 31.2 us -> 22.7 us  [flip(): return lax.ppermute(values, 'dp', pairs)]
    ppermute x22 -> x18, starting transfers between devices: 29.6 us -> 24.3 us  [flip(): return lax.ppermute(values, 'dp', pairs)]
    all_to_all x0 -> x2, waiting for transfers between devices: none -> 2.54 us  [trade(): lax.all_to_all(values, 'dp', split_axis=0, concat_axis=0, axis_index_grou...]
    convert_element_type x12 -> x11, other arithmetic: 12.5 us -> 10.3 us  [cut(): return total.astype(BF)]
    unnamed x48 -> x42, local copies, waits for them, and re-layouts: 4.22 us -> 3.12 us
  transfers between devices with their start and end apart: 32 -> 30, of which waited for: 14 -> 12; matrix products, arithmetic and copies ran while one was open for 5% -> 6% of each run, Pallas kernels for 26% -> 28%
where the time goes in v5:
time: 170 us
  Pallas kernels  86.5 us (51%)
  starting transfers between devices  36.7 us (22%)
  waiting for transfers between devices  29.1 us (17%)
  other arithmetic  12.1 us (7%)
  local copies, waits for them, and re-layouts  3.98 us (2%)
    pallas_call x1, Pallas kernels, body(): pl.pallas_call(partial(layer_kernel, blocks, parts), in_specs=[smem] * 3...  31.5 us
    ppermute x18, starting transfers between devices, flip(): return lax.ppermute(values, 'dp', pairs)  24.3 us
    ppermute x18, waiting for transfers between devices, flip(): return lax.ppermute(values, 'dp', pairs)  22.7 us
    pallas_call x1, Pallas kernels, body(): pl.pallas_call(mixer_backward_kernel, grid=(steps,), in_specs=[smem, smem...  15.5 us
    convert_element_type x11, other arithmetic, cut(): return total.astype(BF)  10.3 us
    all_to_all x2, starting transfers between devices, trade(): lax.all_to_all(values, 'dp', split_axis=0, concat_axis=0, axis_index_grou...  9.66 us
    pallas_call x1, Pallas kernels, body(): pl.pallas_call(finish_kernel, in_specs=[smem] + [vmem] * 3 + [anywhere] *...  9.27 us
    pallas_call x1, Pallas kernels, layer_output(): pl.pallas_call(output_kernel, grid=(4,), in_specs=[row_block(tall, width)...  7.1 us
  transfers between devices with their start and end apart: 30, of which 12 were waited for; matrix products, arithmetic and copies ran while one was open for 6% of the time, Pallas kernels for 28%

profile of v5, /device:TPU:0, one launch (start us, length us, event | category | flops | bytes accessed | tf_op | source)
XLA Modules:
  0.0 169.6 jit_solution(16757494360278169798)
XLA Ops:
  0.6 0.5 collective-permute-start.1
  1.2 0.4 collective-permute-start.4
  1.8 4.6 %norm_project.1 = (bf16[1024,512]{1,0:T(8,128)(2,1)}, bf16[1024,768]{1,0:T(8,128)(2,1)}) custom-call(bf16[1024,512]{1,0:T(8,128)(2,1)} %x_ref.5, f32[1,512]{1,0:T(1,128)} %bitcast.28, bf16[3,512,256]{2,1,0:T(8,128)(2,1)} %bitcast.20), custom_call_target="tpu_custom_call" | custom-call | flops 50000000 | bytes 1048576 | tf_op jit(solution)/shard_map/norm_project/pallas_call | solution.py:1194
  6.3 0.3 collective-permute-done.3.wa_other_ref
  6.7 0.9 copy-done
  7.6 4.9 %project_state.1 = (bf16[1024,768]{1,0:T(8,128)(2,1)}, bf16[832,128]{1,0:T(8,128)(2,1)}) custom-call(s32[1,6]{1,0:T(1,128)} %lengths_ref.7, bf16[1024,512]{1,0:T(8,128)(2,1)} %get-tuple-element.95.normed_ref.normed_hbm, bf16[3,512,256]{2,1,0:T(8,128)(2,1)} %copy-done, bf16[1024,768]{1,0:T(8,128)(2,1)} %get-tuple-element.96.own_ref.own_hbm.refs_0_), custom_call_target="tpu_custom_call" | custom-call | flops 50000000 | bytes 1048576 | tf_op jit(solution)/shard_map/project_state/pallas_call | solution.py:1205
  12.6 0.4 collective-permute-start.5
  13.0 0.1 collective-permute-start
  13.1 1.0 collective-permute-done.blend_other_ref
  14.1 0.2 collective-permute-done.5.packet_ref
  14.3 0.4 copy-done.20
  14.7 0.3 copy-done.18
  15.0 31.5 %layer.1 = (bf16[1024,512]{1,0:T(8,128)(2,1)}, bf16[1024,512]{1,0:T(8,128)(2,1)}, f32[8,512]{1,0:T(8,128)}, bf16[512,256]{1,0:T(8,128)(2,1)}, bf16[512,256]{1,0:...) custom-call(s32[1,6]{1,0:T(1,128)} %lengths_ref.7, ...), custom_call_target="tpu_custom_call" | custom-call | flops 300000000 | bytes 1048576 | tf_op jit(solution)/shard_map/layer/pallas_call | solution.py:1235
  46.5 0.4 collective-permute-start.7
  47.0 0.1 collective-permute-start.6
  47.1 2.4 %collective-permute-done.7 = bf16[2048,256]{1,0:T(8,128)(2,1)S(1)} collective-permute-done((bf16[2048,256]{1,0:T(8,128)(2,1)}, bf16[2048,256]{1,0:T(8,128)(2,1)S(1)}, u32[]{:S(2)}, u32[]{:S(2)}) %collective-permute-start.7) | collective-permute-done | bytes 1048608 | tf_op jit(solution)/shard_map/ppermute | solution.py:1175
  49.5 2.3 %add_convert_fusion = bf16[1024,256]{1,0:T(8,128)(2,1)} fusion(bf16[2048,256]{1,0:T(8,128)(2,1)S(1)} %collective-permute-done.7, s32[]{:T(128)S(6)} %select_n.196, bf16[2048,256]{1,0:T(8,128)(2,1)} %get-tuple-element.112), kind=kLoop, calls=%fused_computation | loop fusion | flops 1048576 | bytes 1572868 | tf_op jit(solution)/shard_map/convert_element_type | solution.py:1075
  51.8 1.1 add_convert_fusion.1
  52.9 2.9 %collective-permute-start.8 = (bf16[1024,256]{1,0:T(8,128)(2,1)}, bf16[1024,256]{1,0:T(8,128)(2,1)}, u32[]{:S(2)}, u32[]{:S(2)}) collective-permute-start(bf16[1024,256]{1,0:T(8,128)(2,1)} %add_convert_fusion.1), channel_id=1, source_target_pairs={{0,2},{2,0},{4,6},{6,4},{8,10},{10,8},{12,14},{14,12},{16,18},{18,... | collective-permute-start | bytes 1572872 | tf_op jit(solution)/shard_map/ppermute | solution.py:1038
  55.7 1.5 collective-permute-start.9
  57.3 15.5 %mixer_backward.1 = (bf16[1024,512]{1,0:T(8,128)(2,1)}, bf16[1024,512]{1,0:T(8,128)(2,1)}, bf16[1024,512]{1,0:T(8,128)(2,1)}, bf16[832,128]{1,0:T(8,128)(2,1)}, f32[2,4,8,128]{3,2,1,0:T(8,128)}) custom-call(s32[1,6]{1,0:T(1,128)} %lengths_ref.7, f32[2,4]{1,0:T(2,128)} %blend_own_ref.3, f32[2,4]{1,0:T(2,128)} %copy-done.20, ...), custom_call_target="tpu_custom_call" | custom-call | flops 200000000 | bytes 1048576 | tf_op jit(solution)/shard_map/mixer_backward/pallas_call | solution.py:1309
  72.9 1.1 add_convert_fusion.6
  74.0 1.1 add_convert_fusion.7
  75.1 0.6 collective-permute-start.11
  75.7 0.1 collective-permute-start.12
  75.8 9.3 %finish.1 = (bf16[1024,1024]{1,0:T(8,128)(2,1)}, bf16[2112,256]{1,0:T(8,128)(2,1)}, bf16[2112,256]{1,0:T(8,128)(2,1)}) custom-call(s32[1,6]{1,0:T(1,128)} %lengths_ref.7, f32[2,4,8,128]{3,2,1,0:T(8,128)} %get-tuple-element.115.gblend_ref, f32[8,512]{1,0:T(8,128)} %get-tuple-element.116.ggain_ref, f32[1,512]{1,0:T(1,128)} %bitcast.29, ...), custom_call_target="tpu_custom_call" | custom-call | flops 80000000 | bytes 1048576 | tf_op jit(solution)/shard_map/finish/pallas_call | solution.py:1348
  85.1 0.7 copy-done.16
  85.8 0.5 collective-permute-start.13
  86.3 1.7 add_convert_fusion.4
  88.0 0.8 pad_maximum_fusion
  88.8 0.9 add_convert_fusion.2
  89.7 1.8 %collective-permute-start.14 = (bf16[528,256]{1,0:T(8,128)(2,1)}, bf16[528,256]{1,0:T(8,128)(2,1)S(1)}, u32[]{:S(2)}, u32[]{:S(2)}) collective-permute-start(bf16[528,256]{1,0:T(8,128)(2,1)} %get-tuple-element.137), channel_id=1, source_target_pairs={{0,2},{2,0},{4,6},{6,4},{8,10},{10,8},{12,14},{14,12},{16,18},{18,... | collective-permute-start | bytes 811016 | tf_op jit(solution)/shard_map/ppermute | solution.py:1038
  91.6 1.5 collective-permute-start.15
  93.1 4.9 %all-to-all-start = ((bf16[4,256,256]{2,1,0:T(8,128)(2,1)}), bf16[4,256,256]{2,1,0:T(8,128)(2,1)S(1)}, u32[]{:S(2)}, u32[]{:S(2)}) async-start(bf16[4,256,256]{2,1,0:T(8,128)(2,1)} %pad_maximum_fusion), calls=%async_computation | async-start | bytes 1048576 | tf_op jit(solution)/shard_map/all_to_all | solution.py:1048
  97.9 6.3 %input_grad.1 = bf16[1024,512]{1,0:T(8,128)(2,1)} custom-call(bf16[1024,512]{1,0:T(8,128)(2,1)} %get-tuple-element.126.gq_hbm.gq_ref, bf16[1024,1024]{1,0:T(8,128)(2,1)} %get-tuple-element.139.gkv_ref, bf16[1024,512]{1,0:T(8,128)(2,1)} %x_ref.5, bf16[1024,512]{1,0:T(8,128)(2,1)} %get-tuple-element.140.branch_ref, f32[1,512]{1,0:T(1,128)} %bitcast.30, ...), custom_call_target="tpu_custom_call" | custom-call | flops 70000000 | bytes 1048576 | tf_op jit(solution)/shard_map/input_grad/pallas_call | solution.py:1405
  104.3 0.8 add_convert_fusion.14
  105.1 0.5 collective-permute-start.16
  105.6 0.5 collective-permute-start.17
  106.1 4.3 %collective-permute-done.16 = bf16[264,256]{1,0:T(8,128)(2,1)} collective-permute-done((bf16[264,256]{1,0:T(8,128)(2,1)}, bf16[264,256]{1,0:T(8,128)(2,1)}, u32[]{:S(2)}, u32[]{:S(2)}) %collective-permute-start.16) | collective-permute-done | bytes 135200 | tf_op jit(solution)/shard_map/ppermute | solution.py:1038
  110.4 0.3 collective-permute-done.17
  110.7 1.1 add_convert_fusion.13
  111.9 0.3 all-to-all-done
  112.3 0.8 broadcast_in_dim.2
  113.1 4.8 %all-to-all-start.1 = ((bf16[4,256,256]{2,1,0:T(8,128)(2,1)}), bf16[4,256,256]{2,1,0:T(8,128)(2,1)S(1)}, u32[]{:S(2)}, u32[]{:S(2)}) async-start(bf16[4,256,256]{2,1,0:T(8,128)(2,1)} %broadcast_in_dim.2), calls=%async_computation.1 | async-start | bytes 1048576 | tf_op jit(solution)/shard_map/all_to_all | solution.py:1048
  117.9 2.0 %collective-permute-start.18 = (bf16[528,256]{1,0:T(8,128)(2,1)S(1)}, bf16[528,256]{1,0:T(8,128)(2,1)S(1)}, u32[]{:S(2)}, u32[]{:S(2)}) collective-permute-start(bf16[528,256]{1,0:T(8,128)(2,1)S(1)} %pad_maximum_fusion.3), channel_id=1, source_target_pairs={{0,8},{2,10},{4,12},{6,14},{8,0},{10,2},{12,4},{14,6},{16,24},{18,... | collective-permute-start | bytes 811016 | tf_op jit(solution)/shard_map/ppermute | solution.py:1038
  119.9 7.1 %layer_output.1 = bf16[1024,512]{1,0:T(8,128)(2,1)} custom-call(bf16[1024,512]{1,0:T(8,128)(2,1)} %x_ref.5, bf16[1024,512]{1,0:T(8,128)(2,1)} %get-tuple-element.149.mixed_ref, bf16[1024,2048]{1,0:T(8,128)(2,1)} %get-tuple-element.150.active_ref, bf16[256,512]{1,0:T(8,128)(2,1)} %wa_own_ref.3, bf16[256,512]{1,0:T(8,128)(2,1)} %copy-done.8, ...), custom_call_target="tpu_custom_call" | custom-call | flops 50000000 | bytes 1048576 | tf_op jit(solution)/shard_map/layer_output/pallas_call | solution.py:1391
  127.0 2.2 %all-to-all-done.1 = bf16[4,256,256]{2,1,0:T(8,128)(2,1)S(1)} async-done(((bf16[4,256,256]{2,1,0:T(8,128)(2,1)}), bf16[4,256,256]{2,1,0:T(8,128)(2,1)S(1)}, u32[]{:S(2)}, u32[]{:S(2)}) %all-to-all-start.1) | async-done | bytes 524320 | tf_op jit(solution)/shard_map/all_to_all | solution.py:1048
  129.2 3.4 %collective-permute-done.18 = bf16[528,256]{1,0:T(8,128)(2,1)S(1)} collective-permute-done((bf16[528,256]{1,0:T(8,128)(2,1)S(1)}, bf16[528,256]{1,0:T(8,128)(2,1)S(1)}, u32[]{:S(2)}, u32[]{:S(2)}) %collective-permute-start.18) | collective-permute-done | bytes 270368 | tf_op jit(solution)/shard_map/ppermute | solution.py:1038
  132.8 0.6 collective-permute-start.21
  133.4 2.5 %collective-permute-start.19 = (bf16[528,256]{1,0:T(8,128)(2,1)S(1)}, bf16[528,256]{1,0:T(8,128)(2,1)S(1)}, u32[]{:S(2)}, u32[]{:S(2)}) collective-permute-start(bf16[528,256]{1,0:T(8,128)(2,1)S(1)} %pad_maximum_fusion.4), channel_id=1, source_target_pairs={{0,16},{2,18},{4,20},{6,22},{8,24},{10,26},{12,28},{14,30},{16,0},... | collective-permute-start | bytes 811016 | tf_op jit(solution)/shard_map/ppermute | solution.py:1038
  135.8 1.4 collective-permute-start.20
  137.2 2.0 %collective-permute-done.21 = bf16[512,256]{1,0:T(8,128)(2,1)S(1)} collective-permute-done((bf16[512,256]{1,0:T(8,128)(2,1)S(1)}, bf16[512,256]{1,0:T(8,128)(2,1)S(1)}, u32[]{:S(2)}, u32[]{:S(2)}) %collective-permute-start.21) | collective-permute-done | bytes 262176 | tf_op jit(solution)/shard_map/ppermute | solution.py:1038
  139.3 3.7 %collective-permute-done.20 = bf16[512,256]{1,0:T(8,128)(2,1)S(1)} collective-permute-done((bf16[512,256]{1,0:T(8,128)(2,1)S(1)}, bf16[512,256]{1,0:T(8,128)(2,1)S(1)}, u32[]{:S(2)}, u32[]{:S(2)}) %collective-permute-start.20) | collective-permute-done | bytes 262176 | tf_op jit(solution)/shard_map/ppermute | solution.py:1038
  143.2 2.5 %collective-permute-start.22 = (bf16[1024,256]{1,0:T(8,128)(2,1)S(1)}, bf16[1024,256]{1,0:T(8,128)(2,1)S(1)}, u32[]{:S(2)}, u32[]{:S(2)}) collective-permute-start(bf16[1024,256]{1,0:T(8,128)(2,1)S(1)} %pad_maximum_fusion.1.out_mine_hbm), channel_id=1, source_target_pairs={{0,2},{2,0},{4,6},{6,4},{8,10},{10,8},{12,14},{14,12},{16,18},{18,... | collective-permute-start | bytes 1572872 | tf_op jit(solution)/shard_map/ppermute | solution.py:1038
  145.6 1.5 collective-permute-start.23
  147.2 0.6 collective-permute-start.24
  147.8 1.2 collective-permute-start.25
  149.0 9.0 %collective-permute-done.24 = bf16[264,256]{1,0:T(8,128)(2,1)S(1)} collective-permute-done((bf16[264,256]{1,0:T(8,128)(2,1)S(1)}, bf16[264,256]{1,0:T(8,128)(2,1)S(1)}, u32[]{:S(2)}, u32[]{:S(2)}) %collective-permute-start.24) | collective-permute-done | bytes 135200 | tf_op jit(solution)/shard_map/ppermute | solution.py:1038
  158.1 0.5 collective-permute-start.26
  158.6 2.1 %collective-permute-start.27 = (bf16[528,256]{1,0:T(8,128)(2,1)S(1)}, bf16[528,256]{1,0:T(8,128)(2,1)S(1)}, u32[]{:S(2)}, u32[]{:S(2)}) collective-permute-start(bf16[528,256]{1,0:T(8,128)(2,1)S(1)} %pad_maximum_fusion.6.b_mine_hbm), channel_id=1, source_target_pairs={{0,4},{2,6},{4,0},{6,2},{8,12},{10,14},{12,8},{14,10},{16,20},{18,... | collective-permute-start | bytes 811016 | tf_op jit(solution)/shard_map/ppermute | solution.py:1038
  160.7 0.7 pad_add_fusion.bits_ref
  161.4 3.9 %feed_output.1 = (f32[1024,512]{1,0:T(8,128)}, f32[512,1024]{1,0:T(8,128)}) custom-call(s32[2]{0:T(128)} %pad_add_fusion.bits_ref, bf16[1024,256]{1,0:T(8,128)(2,1)} %copy-done.3, bf16[1024,256]{1,0:T(8,128)(2,1)} %copy-done.2, bf16[1024,256]{1,0:T(8,128)(2,1)} %copy-done.12, bf16[1024,256]{1,0:T(8,128)(2,1)} %copy-done.13), custom_call_target="tpu_custom_call" | custom-call | flops 30000000 | bytes 1048576 | tf_op jit(solution)/shard_map/feed_output/pallas_call | solution.py:1463
  165.4 0.7 copy-done.14
  166.1 3.3 %last_output.1 = (f32[1536,256]{1,0:T(8,128)}, f32[256,512]{1,0:T(8,128)}, f32[1,512]{1,0:T(1,128)}, f32[1,512]{1,0:T(1,128)}, f32[2,4]{1,0:T(2,128)}) custom-call(s32[2]{0:T(128)} %pad_add_fusion.bits_ref, bf16[528,256]{1,0:T(8,128)(2,1)} %copy-done.5, bf16[528,256]{1,0:T(8,128)(2,1)} %copy-done.4, bf16[528,256]{1,0:T(8,128)(2,1)} %copy-done.14, ...), custom_call_target="tpu_custom_call" | custom-call | flops 30000000 | bytes 1048576 | tf_op jit(solution)/shard_map/last_output/pallas_call | solution.py:1482
  (73 shorter events, 1.0 us)
Async XLA Ops:
  0.6 6.0 %collective-permute-start.1 = (bf16[512,1024]{1,0:T(8,128)(2,1)}, bf16[512,1024]{1,0:T(8,128)(2,1)S(1)}, u32[]{:S(2)}, u32[]{:S(2)}) collective-permute-start(bf16[512,1024]{1,0:T(8,128)(2,1)} %wi_own_hbm.1), channel_id=1, source_target_pairs={{0,1},{1,0},{2,3},{3,2},{4,5},{5,4},{6,7},{7,6},{8,9},{9,8},{10,11... | collective-permute-start | bytes 3145736 | tf_op jit(solution)/shard_map/ppermute | solution.py:1175
  1.2 5.5 %collective-permute-start.2 = (bf16[1024,512]{1,0:T(8,128)(2,1)}, bf16[1024,512]{1,0:T(8,128)(2,1)S(1)}, u32[]{:S(2)}, u32[]{:S(2)}) collective-permute-start(bf16[1024,512]{1,0:T(8,128)(2,1)} %wo_own_ref.1), channel_id=1, source_target_pairs={{0,1},{1,0},{2,3},{3,2},{4,5},{5,4},{6,7},{7,6},{8,9},{9,8},{10,11... | collective-permute-start | bytes 3145736 | tf_op jit(solution)/shard_map/ppermute | solution.py:1175
  1.2 5.4 %collective-permute-start.4 = (bf16[3,512,256]{2,1,0:T(8,128)(2,1)}, bf16[3,512,256]{2,1,0:T(8,128)(2,1)S(1)}, u32[]{:S(2)}, u32[]{:S(2)}) collective-permute-start(bf16[3,512,256]{2,1,0:T(8,128)(2,1)} %bitcast.19), channel_id=1, source_target_pairs={{0,1},{1,0},{2,3},{3,2},{4,5},{5,4},{6,7},{7,6},{8,9},{9,8},{10,11... | collective-permute-start | bytes 2359304 | tf_op jit(solution)/shard_map/ppermute | solution.py:1175
  1.7 5.0 %collective-permute-start.3 = (bf16[256,512]{1,0:T(8,128)(2,1)}, bf16[256,512]{1,0:T(8,128)(2,1)S(1)}, u32[]{:S(2)}, u32[]{:S(2)}) collective-permute-start(bf16[256,512]{1,0:T(8,128)(2,1)} %wa_own_ref.3), channel_id=1, source_target_pairs={{0,1},{1,0},{2,3},{3,2},{4,5},{5,4},{6,7},{7,6},{8,9},{9,8},{10,11... | collective-permute-start | bytes 786440 | tf_op jit(solution)/shard_map/ppermute | solution.py:1175
  6.7 5.9 %copy-start.8 = (bf16[256,512]{1,0:T(8,128)(2,1)}, bf16[256,512]{1,0:T(8,128)(2,1)S(1)}, u32[]{:S(2)}) copy-start(bf16[256,512]{1,0:T(8,128)(2,1)S(1)} %collective-permute-done.3.wa_other_ref) | copy-start | bytes 786436
  6.7 5.9 %copy-start.7 = (bf16[512,1024]{1,0:T(8,128)(2,1)}, bf16[512,1024]{1,0:T(8,128)(2,1)S(1)}, u32[]{:S(2)}) copy-start(bf16[512,1024]{1,0:T(8,128)(2,1)S(1)} %collective-permute-done.1.wi_other_hbm) | copy-start | bytes 3145732
  6.7 7.6 %copy-start.1 = (bf16[1024,512]{1,0:T(8,128)(2,1)}, bf16[1024,512]{1,0:T(8,128)(2,1)S(1)}, u32[]{:S(2)}) copy-start(bf16[1024,512]{1,0:T(8,128)(2,1)S(1)} %collective-permute-done.2.wo_other_hbm.wo_other_ref) | copy-start | bytes 3145732
  6.7 0.9 copy-start
  7.6 5.4 %copy-start.19 = (f32[2,4]{1,0:T(2,128)S(1)}, f32[2,4]{1,0:T(2,128)}, u32[]{:S(2)}) copy-start(f32[2,4]{1,0:T(2,128)} %blend_own_ref.3) | copy-start | bytes 100
  12.6 1.7 %collective-permute-start.5 = (bf16[832,128]{1,0:T(8,128)(2,1)}, bf16[832,128]{1,0:T(8,128)(2,1)S(1)}, u32[]{:S(2)}, u32[]{:S(2)}) collective-permute-start(bf16[832,128]{1,0:T(8,128)(2,1)} %get-tuple-element.97), channel_id=1, source_target_pairs={{0,1},{1,0},{2,3},{3,2},{4,5},{5,4},{6,7},{7,6},{8,9},{9,8},{10,11... | collective-permute-start | bytes 638984 | tf_op jit(solution)/shard_map/ppermute | solution.py:1175
  13.0 1.1 collective-permute-start
  14.1 0.6 copy-start.20
  14.3 0.7 copy-start.18
  46.5 5.3 %copy-start.9 = (bf16[2048,256]{1,0:T(8,128)(2,1)S(1)}, bf16[2048,256]{1,0:T(8,128)(2,1)}, u32[]{:S(2)}) copy-start(bf16[2048,256]{1,0:T(8,128)(2,1)} %get-tuple-element.110) | copy-start | bytes 3145732
  46.5 2.9 %collective-permute-start.7 = (bf16[2048,256]{1,0:T(8,128)(2,1)}, bf16[2048,256]{1,0:T(8,128)(2,1)S(1)}, u32[]{:S(2)}, u32[]{:S(2)}) collective-permute-start(bf16[2048,256]{1,0:T(8,128)(2,1)} %get-tuple-element.113), channel_id=1, source_target_pairs={{0,1},{1,0},{2,3},{3,2},{4,5},{5,4},{6,7},{7,6},{8,9},{9,8},{10,11... | collective-permute-start | bytes 3145736 | tf_op jit(solution)/shard_map/ppermute | solution.py:1175
  47.0 4.8 %collective-permute-start.6 = (bf16[2048,256]{1,0:T(8,128)(2,1)}, bf16[2048,256]{1,0:T(8,128)(2,1)S(1)}, u32[]{:S(2)}, u32[]{:S(2)}) collective-permute-start(bf16[2048,256]{1,0:T(8,128)(2,1)} %get-tuple-element.111), channel_id=1, source_target_pairs={{0,1},{1,0},{2,3},{3,2},{4,5},{5,4},{6,7},{7,6},{8,9},{9,8},{10,11... | collective-permute-start | bytes 3145736 | tf_op jit(solution)/shard_map/ppermute | solution.py:1175
  49.5 23.4 %copy-start.10 = (bf16[2048,256]{1,0:T(8,128)(2,1)}, bf16[2048,256]{1,0:T(8,128)(2,1)S(1)}, u32[]{:S(2)}) copy-start(bf16[2048,256]{1,0:T(8,128)(2,1)S(1)} %collective-permute-done.7) | copy-start | bytes 3145732
  51.8 22.2 %copy-start.11 = (bf16[2048,256]{1,0:T(8,128)(2,1)}, bf16[2048,256]{1,0:T(8,128)(2,1)S(1)}, u32[]{:S(2)}) copy-start(bf16[2048,256]{1,0:T(8,128)(2,1)S(1)} %collective-permute-done.6) | copy-start | bytes 3145732
  52.9 19.9 %collective-permute-start.8 = (bf16[1024,256]{1,0:T(8,128)(2,1)}, bf16[1024,256]{1,0:T(8,128)(2,1)}, u32[]{:S(2)}, u32[]{:S(2)}) collective-permute-start(bf16[1024,256]{1,0:T(8,128)(2,1)} %add_convert_fusion.1), channel_id=1, source_target_pairs={{0,2},{2,0},{4,6},{6,4},{8,10},{10,8},{12,14},{14,12},{16,18},{18,... | collective-permute-start | bytes 1572872 | tf_op jit(solution)/shard_map/ppermute | solution.py:1038
  55.7 17.0 %collective-permute-start.9 = (bf16[1024,256]{1,0:T(8,128)(2,1)}, bf16[1024,256]{1,0:T(8,128)(2,1)}, u32[]{:S(2)}, u32[]{:S(2)}) collective-permute-start(bf16[1024,256]{1,0:T(8,128)(2,1)} %add_convert_fusion), channel_id=1, source_target_pairs={{0,4},{2,6},{4,0},{6,2},{8,12},{10,14},{12,8},{14,10},{16,20},{18,... | collective-permute-start | bytes 1572872 | tf_op jit(solution)/shard_map/ppermute | solution.py:1038
  72.8 2.3 %collective-permute-start.10 = (bf16[832,128]{1,0:T(8,128)(2,1)}, bf16[832,128]{1,0:T(8,128)(2,1)S(1)}, u32[]{:S(2)}, u32[]{:S(2)}) collective-permute-start(bf16[832,128]{1,0:T(8,128)(2,1)} %get-tuple-element.120), channel_id=1, source_target_pairs={{0,1},{1,0},{2,3},{3,2},{4,5},{5,4},{6,7},{7,6},{8,9},{9,8},{10,11... | collective-permute-start | bytes 638984 | tf_op jit(solution)/shard_map/ppermute | solution.py:1175
  75.1 0.7 copy-start.17
  75.1 10.0 %collective-permute-start.11 = (bf16[512,256]{1,0:T(8,128)(2,1)S(1)}, bf16[512,256]{1,0:T(8,128)(2,1)S(1)}, u32[]{:S(2)}, u32[]{:S(2)}) collective-permute-start(bf16[512,256]{1,0:T(8,128)(2,1)S(1)} %add_convert_fusion.7), channel_id=1, source_target_pairs={{0,4},{2,6},{4,0},{6,2},{8,12},{10,14},{12,8},{14,10},{16,20},{18,... | collective-permute-start | bytes 786440 | tf_op jit(solution)/shard_map/ppermute | solution.py:1038
  75.7 9.4 %collective-permute-start.12 = (bf16[512,256]{1,0:T(8,128)(2,1)S(1)}, bf16[512,256]{1,0:T(8,128)(2,1)S(1)}, u32[]{:S(2)}, u32[]{:S(2)}) collective-permute-start(bf16[512,256]{1,0:T(8,128)(2,1)S(1)} %add_convert_fusion.6), channel_id=1, source_target_pairs={{0,2},{2,0},{4,6},{6,4},{8,10},{10,8},{12,14},{14,12},{16,18},{18,... | collective-permute-start | bytes 786440 | tf_op jit(solution)/shard_map/ppermute | solution.py:1038
  85.1 0.7 copy-start.16
  85.8 3.0 %collective-permute-start.13 = (bf16[2112,256]{1,0:T(8,128)(2,1)}, bf16[2112,256]{1,0:T(8,128)(2,1)S(1)}, u32[]{:S(2)}, u32[]{:S(2)}) collective-permute-start(bf16[2112,256]{1,0:T(8,128)(2,1)} %get-tuple-element.133), channel_id=1, source_target_pairs={{0,1},{1,0},{2,3},{3,2},{4,5},{5,4},{6,7},{7,6},{8,9},{9,8},{10,11... | collective-permute-start | bytes 3244040 | tf_op jit(solution)/shard_map/ppermute | solution.py:1175
  86.3 2.5 %copy-start.6 = (bf16[2112,256]{1,0:T(8,128)(2,1)S(1)}, bf16[2112,256]{1,0:T(8,128)(2,1)}, u32[]{:S(2)}) copy-start(bf16[2112,256]{1,0:T(8,128)(2,1)} %get-tuple-element.129) | copy-start | bytes 3244036
  89.7 14.5 %collective-permute-start.14 = (bf16[528,256]{1,0:T(8,128)(2,1)}, bf16[528,256]{1,0:T(8,128)(2,1)S(1)}, u32[]{:S(2)}, u32[]{:S(2)}) collective-permute-start(bf16[528,256]{1,0:T(8,128)(2,1)} %get-tuple-element.137), channel_id=1, source_target_pairs={{0,2},{2,0},{4,6},{6,4},{8,10},{10,8},{12,14},{14,12},{16,18},{18,... | collective-permute-start | bytes 811016 | tf_op jit(solution)/shard_map/ppermute | solution.py:1038
  91.6 12.7 %collective-permute-start.15 = (bf16[528,256]{1,0:T(8,128)(2,1)}, bf16[528,256]{1,0:T(8,128)(2,1)S(1)}, u32[]{:S(2)}, u32[]{:S(2)}) collective-permute-start(bf16[528,256]{1,0:T(8,128)(2,1)} %get-tuple-element.138), channel_id=1, source_target_pairs={{0,4},{2,6},{4,0},{6,2},{8,12},{10,14},{12,8},{14,10},{16,20},{18,... | collective-permute-start | bytes 811016 | tf_op jit(solution)/shard_map/ppermute | solution.py:1038
  93.1 19.1 %all-to-all-start = ((bf16[4,256,256]{2,1,0:T(8,128)(2,1)}), bf16[4,256,256]{2,1,0:T(8,128)(2,1)S(1)}, u32[]{:S(2)}, u32[]{:S(2)}) async-start(bf16[4,256,256]{2,1,0:T(8,128)(2,1)} %pad_maximum_fusion), calls=%async_computation | async-start | bytes 1048576 | tf_op jit(solution)/shard_map/all_to_all | solution.py:1048
  105.1 5.3 %collective-permute-start.16 = (bf16[264,256]{1,0:T(8,128)(2,1)}, bf16[264,256]{1,0:T(8,128)(2,1)}, u32[]{:S(2)}, u32[]{:S(2)}) collective-permute-start(bf16[264,256]{1,0:T(8,128)(2,1)} %get-tuple-element.145), channel_id=1, source_target_pairs={{0,4},{2,6},{4,0},{6,2},{8,12},{10,14},{12,8},{14,10},{16,20},{18,... | collective-permute-start | bytes 405512 | tf_op jit(solution)/shard_map/ppermute | solution.py:1038
  105.6 5.1 %collective-permute-start.17 = (bf16[264,256]{1,0:T(8,128)(2,1)S(1)}, bf16[264,256]{1,0:T(8,128)(2,1)}, u32[]{:S(2)}, u32[]{:S(2)}) collective-permute-start(bf16[264,256]{1,0:T(8,128)(2,1)S(1)} %get-tuple-element.146), channel_id=1, source_target_pairs={{0,2},{2,0},{4,6},{6,4},{8,10},{10,8},{12,14},{14,12},{16,18},{18,... | collective-permute-start | bytes 405512 | tf_op jit(solution)/shard_map/ppermute | solution.py:1038
  113.1 16.1 %all-to-all-start.1 = ((bf16[4,256,256]{2,1,0:T(8,128)(2,1)}), bf16[4,256,256]{2,1,0:T(8,128)(2,1)S(1)}, u32[]{:S(2)}, u32[]{:S(2)}) async-start(bf16[4,256,256]{2,1,0:T(8,128)(2,1)} %broadcast_in_dim.2), calls=%async_computation.1 | async-start | bytes 1048576 | tf_op jit(solution)/shard_map/all_to_all | solution.py:1048
  117.9 14.7 %collective-permute-start.18 = (bf16[528,256]{1,0:T(8,128)(2,1)S(1)}, bf16[528,256]{1,0:T(8,128)(2,1)S(1)}, u32[]{:S(2)}, u32[]{:S(2)}) collective-permute-start(bf16[528,256]{1,0:T(8,128)(2,1)S(1)} %pad_maximum_fusion.3), channel_id=1, source_target_pairs={{0,8},{2,10},{4,12},{6,14},{8,0},{10,2},{12,4},{14,6},{16,24},{18,... | collective-permute-start | bytes 811016 | tf_op jit(solution)/shard_map/ppermute | solution.py:1038
  132.8 6.4 %collective-permute-start.21 = (bf16[512,256]{1,0:T(8,128)(2,1)S(1)}, bf16[512,256]{1,0:T(8,128)(2,1)S(1)}, u32[]{:S(2)}, u32[]{:S(2)}) collective-permute-start(bf16[512,256]{1,0:T(8,128)(2,1)S(1)} %bitcast.27), channel_id=1, source_target_pairs={{0,2},{2,0},{4,6},{6,4},{8,10},{10,8},{12,14},{14,12},{16,18},{18,... | collective-permute-start | bytes 786440 | tf_op jit(solution)/shard_map/ppermute | solution.py:1038
  133.4 13.8 %collective-permute-start.19 = (bf16[528,256]{1,0:T(8,128)(2,1)S(1)}, bf16[528,256]{1,0:T(8,128)(2,1)S(1)}, u32[]{:S(2)}, u32[]{:S(2)}) collective-permute-start(bf16[528,256]{1,0:T(8,128)(2,1)S(1)} %pad_maximum_fusion.4), channel_id=1, source_target_pairs={{0,16},{2,18},{4,20},{6,22},{8,24},{10,26},{12,28},{14,30},{16,0},... | collective-permute-start | bytes 811016 | tf_op jit(solution)/shard_map/ppermute | solution.py:1038
  135.8 7.2 %collective-permute-start.20 = (bf16[512,256]{1,0:T(8,128)(2,1)S(1)}, bf16[512,256]{1,0:T(8,128)(2,1)S(1)}, u32[]{:S(2)}, u32[]{:S(2)}) collective-permute-start(bf16[512,256]{1,0:T(8,128)(2,1)S(1)} %bitcast.26), channel_id=1, source_target_pairs={{0,4},{2,6},{4,0},{6,2},{8,12},{10,14},{12,8},{14,10},{16,20},{18,... | collective-permute-start | bytes 786440 | tf_op jit(solution)/shard_map/ppermute | solution.py:1038
  139.3 18.7 %copy-start.2 = (bf16[1024,256]{1,0:T(8,128)(2,1)}, bf16[1024,256]{1,0:T(8,128)(2,1)S(1)}, u32[]{:S(2)}) copy-start(bf16[1024,256]{1,0:T(8,128)(2,1)S(1)} %pad_maximum_fusion.2.in_mine_hbm) | copy-start | bytes 1572868
  143.2 18.2 %copy-start.3 = (bf16[1024,256]{1,0:T(8,128)(2,1)}, bf16[1024,256]{1,0:T(8,128)(2,1)S(1)}, u32[]{:S(2)}) copy-start(bf16[1024,256]{1,0:T(8,128)(2,1)S(1)} %pad_maximum_fusion.1.out_mine_hbm) | copy-start | bytes 1572868
  143.2 14.8 %collective-permute-start.22 = (bf16[1024,256]{1,0:T(8,128)(2,1)S(1)}, bf16[1024,256]{1,0:T(8,128)(2,1)S(1)}, u32[]{:S(2)}, u32[]{:S(2)}) collective-permute-start(bf16[1024,256]{1,0:T(8,128)(2,1)S(1)} %pad_maximum_fusion.1.out_mine_hbm), channel_id=1, source_target_pairs={{0,2},{2,0},{4,6},{6,4},{8,10},{10,8},{12,14},{14,12},{16,18},{18,... | collective-permute-start | bytes 1572872 | tf_op jit(solution)/shard_map/ppermute | solution.py:1038
  145.6 12.3 %collective-permute-start.23 = (bf16[1024,256]{1,0:T(8,128)(2,1)S(1)}, bf16[1024,256]{1,0:T(8,128)(2,1)S(1)}, u32[]{:S(2)}, u32[]{:S(2)}) collective-permute-start(bf16[1024,256]{1,0:T(8,128)(2,1)S(1)} %pad_maximum_fusion.2.in_mine_hbm), channel_id=1, source_target_pairs={{0,4},{2,6},{4,0},{6,2},{8,12},{10,14},{12,8},{14,10},{16,20},{18,... | collective-permute-start | bytes 1572872 | tf_op jit(solution)/shard_map/ppermute | solution.py:1038
  147.2 10.7 %collective-permute-start.24 = (bf16[264,256]{1,0:T(8,128)(2,1)S(1)}, bf16[264,256]{1,0:T(8,128)(2,1)S(1)}, u32[]{:S(2)}, u32[]{:S(2)}) collective-permute-start(bf16[264,256]{1,0:T(8,128)(2,1)S(1)} %get-tuple-element.161), channel_id=1, source_target_pairs={{0,4},{2,6},{4,0},{6,2},{8,12},{10,14},{12,8},{14,10},{16,20},{18,... | collective-permute-start | bytes 405512 | tf_op jit(solution)/shard_map/ppermute | solution.py:1038
  147.8 10.1 %collective-permute-start.25 = (bf16[264,256]{1,0:T(8,128)(2,1)S(1)}, bf16[264,256]{1,0:T(8,128)(2,1)S(1)}, u32[]{:S(2)}, u32[]{:S(2)}) collective-permute-start(bf16[264,256]{1,0:T(8,128)(2,1)S(1)} %get-tuple-element.162), channel_id=1, source_target_pairs={{0,2},{2,0},{4,6},{6,4},{8,10},{10,8},{12,14},{14,12},{16,18},{18,... | collective-permute-start | bytes 405512 | tf_op jit(solution)/shard_map/ppermute | solution.py:1038
  157.9 3.4 %copy-start.12 = (bf16[1024,256]{1,0:T(8,128)(2,1)}, bf16[1024,256]{1,0:T(8,128)(2,1)S(1)}, u32[]{:S(2)}) copy-start(bf16[1024,256]{1,0:T(8,128)(2,1)S(1)} %collective-permute-done.22.out_got_hbm) | copy-start | bytes 1572868
  158.0 3.4 %copy-start.13 = (bf16[1024,256]{1,0:T(8,128)(2,1)}, bf16[1024,256]{1,0:T(8,128)(2,1)S(1)}, u32[]{:S(2)}) copy-start(bf16[1024,256]{1,0:T(8,128)(2,1)S(1)} %collective-permute-done.23.in_got_hbm) | copy-start | bytes 1572868
  158.1 7.3 %copy-start.4 = (bf16[528,256]{1,0:T(8,128)(2,1)}, bf16[528,256]{1,0:T(8,128)(2,1)S(1)}, u32[]{:S(2)}) copy-start(bf16[528,256]{1,0:T(8,128)(2,1)S(1)} %pad_maximum_fusion.6.b_mine_hbm) | copy-start | bytes 811012
  158.1 7.3 %copy-start.5 = (bf16[528,256]{1,0:T(8,128)(2,1)}, bf16[528,256]{1,0:T(8,128)(2,1)S(1)}, u32[]{:S(2)}) copy-start(bf16[528,256]{1,0:T(8,128)(2,1)S(1)} %pad_maximum_fusion.5.a_mine_hbm) | copy-start | bytes 811012
  158.1 7.2 %collective-permute-start.26 = (bf16[528,256]{1,0:T(8,128)(2,1)S(1)}, bf16[528,256]{1,0:T(8,128)(2,1)S(1)}, u32[]{:S(2)}, u32[]{:S(2)}) collective-permute-start(bf16[528,256]{1,0:T(8,128)(2,1)S(1)} %pad_maximum_fusion.5.a_mine_hbm), channel_id=1, source_target_pairs={{0,2},{2,0},{4,6},{6,4},{8,10},{10,8},{12,14},{14,12},{16,18},{18,... | collective-permute-start | bytes 811016 | tf_op jit(solution)/shard_map/ppermute | solution.py:1038
  158.6 6.7 %collective-permute-start.27 = (bf16[528,256]{1,0:T(8,128)(2,1)S(1)}, bf16[528,256]{1,0:T(8,128)(2,1)S(1)}, u32[]{:S(2)}, u32[]{:S(2)}) collective-permute-start(bf16[528,256]{1,0:T(8,128)(2,1)S(1)} %pad_maximum_fusion.6.b_mine_hbm), channel_id=1, source_target_pairs={{0,4},{2,6},{4,0},{6,2},{8,12},{10,14},{12,8},{14,10},{16,20},{18,... | collective-permute-start | bytes 811016 | tf_op jit(solution)/shard_map/ppermute | solution.py:1038
  165.3 0.7 copy-start.14
  165.3 0.8 copy-start.15

commit v6 on v5

--- a/solution.py
+++ b/solution.py
@@ -10,7 +10,7 @@
 BAND = 30
 HALO = 32
 EXTRA = 64
-LATE_TURN = 1
+LATE_TURN = 2
 BLOCK = 128
 EPS = 1e-06
 BF = jnp.bfloat16
@@ -1428,13 +1428,16 @@
     cut = wq_got.shape[0] // 2
     wq_sum = Reduction([([wq_mine, wq_got], 0, cut), ([wq_mine, wq_got], cut, cut)], count, True)
     if wanted == 3:
-        feed_cuts, wq_cuts = feed_sum.cuts(), wq_sum.cuts()
-        gproj, *cuts = tie(gproj, *wq_cuts, *feed_cuts)
-        wq_sum.send(cuts[: len(wq_cuts)])
-        feed_sum.send(cuts[len(wq_cuts) :])
+        feed_cuts = feed_sum.cuts()
+        wq_cuts = wq_sum.cuts()
+        gproj, *feed_cuts = tie(gproj, *feed_cuts)
+        feed_sum.send(feed_cuts)
+        gproj, *wq_cuts = tie(gproj, *wq_cuts)
+        wq_sum.send(wq_cuts)
         grad_input = input_gradient(gproj)
         (grad_input,) = wq_sum.after(grad_input)
-        turns = ((wq_sum,), (feed_sum, wq_sum), (feed_sum, wq_sum), (feed_sum,), (wq_sum,), (wq_sum,))
+        (grad_input,) = feed_sum.after(grad_input)
+        turns = ((wq_sum,), (feed_sum,), (wq_sum,), (feed_sum, wq_sum), (feed_sum,), (wq_sum,), (wq_sum,))
         for turn, reductions in enumerate(turns):
             if turn == len(turns) - 1:
                 wq_sum.gots = list(feed_sum.after(*wq_sum.gots))

time: 170 us -> 167 us (0.982)
  starting transfers between devices: 36.7 us -> 33.5 us
    ppermute x18, starting transfers between devices: 24.3 us -> 22.1 us  [flip(): return lax.ppermute(values, 'dp', pairs)]
  transfers between devices with their start and end apart: 30 -> 30, of which waited for: 12 -> 15; matrix products, arithmetic and copies ran while one was open for 6% -> 6% of each run, Pallas kernels for 28% -> 28%
where the time goes in v6:
time: 167 us; the launch traced here: 166 us
  Pallas kernels  86.6 us (52%)
  starting transfers between devices  33.5 us (20%)
  waiting for transfers between devices  29.5 us (18%)
  other arithmetic  11.9 us (7%)
  local copies, waits for them, and re-layouts  3.24 us (2%)
    pallas_call x1, Pallas kernels, body(): pl.pallas_call(partial(layer_kernel, blocks, parts), in_specs=[smem] * 3...  31.5 us
    ppermute x18, waiting for transfers between devices, flip(): return lax.ppermute(values, 'dp', pairs)  22.3 us
    ppermute x18, starting transfers between devices, flip(): return lax.ppermute(values, 'dp', pairs)  22.1 us
    pallas_call x1, Pallas kernels, body(): pl.pallas_call(mixer_backward_kernel, grid=(steps,), in_specs=[smem, smem...  15.6 us
    convert_element_type x11, other arithmetic, cut(): return total.astype(BF)  10.2 us
    pallas_call x1, Pallas kernels, body(): pl.pallas_call(finish_kernel, in_specs=[smem] + [vmem] * 3 + [anywhere] *...  9.27 us
    all_to_all x2, starting transfers between devices, trade(): lax.all_to_all(values, 'dp', split_axis=0, concat_axis=0, axis_index_grou...  8.58 us
    pallas_call x1, Pallas kernels, layer_output(): pl.pallas_call(output_kernel, grid=(4,), in_specs=[row_block(tall, width)...  7.1 us
  transfers between devices with their start and end apart: 30, of which 15 were waited for; matrix products, arithmetic and copies ran while one was open for 6% of the time, Pallas kernels for 28%

profile of v6, /device:TPU:0, one launch (start us, length us, event | category | flops | bytes accessed | tf_op | source)
XLA Modules:
  0.0 166.0 jit_solution(8337279919195540056)
XLA Ops:
  0.6 0.5 collective-permute-start.1
  1.2 0.4 collective-permute-start.4
  1.8 4.6 %norm_project.1 = (bf16[1024,512]{1,0:T(8,128)(2,1)}, bf16[1024,768]{1,0:T(8,128)(2,1)}) custom-call(bf16[1024,512]{1,0:T(8,128)(2,1)} %x_ref.5, f32[1,512]{1,0:T(1,128)} %bitcast.28, bf16[3,512,256]{2,1,0:T(8,128)(2,1)} %bitcast.20), custom_call_target="tpu_custom_call" | custom-call | flops 50000000 | bytes 1048576 | tf_op jit(solution)/shard_map/norm_project/pallas_call | solution.py:1194
  6.3 0.3 collective-permute-done.3.wa_other_ref
  6.7 0.9 copy-done
  7.6 4.9 %project_state.1 = (bf16[1024,768]{1,0:T(8,128)(2,1)}, bf16[832,128]{1,0:T(8,128)(2,1)}) custom-call(s32[1,6]{1,0:T(1,128)} %lengths_ref.7, bf16[1024,512]{1,0:T(8,128)(2,1)} %get-tuple-element.99.normed_ref.normed_hbm, bf16[3,512,256]{2,1,0:T(8,128)(2,1)} %copy-done, bf16[1024,768]{1,0:T(8,128)(2,1)} %get-tuple-element.100.own_ref.own_hbm.refs_0_), custom_call_target="tpu_custom_call" | custom-call | flops 50000000 | bytes 1048576 | tf_op jit(solution)/shard_map/project_state/pallas_call | solution.py:1205
  12.6 0.4 collective-permute-start.5
  13.0 0.1 collective-permute-start
  13.1 1.0 collective-permute-done.blend_other_ref
  14.1 0.2 collective-permute-done.5.packet_ref
  14.3 0.4 copy-done.21
  14.7 0.3 copy-done.18
  15.0 31.5 %layer.1 = (bf16[1024,512]{1,0:T(8,128)(2,1)}, bf16[1024,512]{1,0:T(8,128)(2,1)}, f32[8,512]{1,0:T(8,128)}, bf16[512,256]{1,0:T(8,128)(2,1)}, bf16[512,256]{1,0:...) custom-call(s32[1,6]{1,0:T(1,128)} %lengths_ref.7, ...), custom_call_target="tpu_custom_call" | custom-call | flops 300000000 | bytes 1048576 | tf_op jit(solution)/shard_map/layer/pallas_call | solution.py:1235
  46.5 0.4 collective-permute-start.7
  47.1 2.4 %collective-permute-done.7 = bf16[2048,256]{1,0:T(8,128)(2,1)S(1)} collective-permute-done((bf16[2048,256]{1,0:T(8,128)(2,1)}, bf16[2048,256]{1,0:T(8,128)(2,1)S(1)}, u32[]{:S(2)}, u32[]{:S(2)}) %collective-permute-start.7) | collective-permute-done | bytes 1048608 | tf_op jit(solution)/shard_map/ppermute | solution.py:1175
  49.5 2.3 %add_convert_fusion = bf16[1024,256]{1,0:T(8,128)(2,1)} fusion(bf16[2048,256]{1,0:T(8,128)(2,1)S(1)} %collective-permute-done.7, s32[]{:T(128)S(6)} %select_n.196, bf16[2048,256]{1,0:T(8,128)(2,1)} %get-tuple-element.116), kind=kLoop, calls=%fused_computation | loop fusion | flops 1048576 | bytes 1572868 | tf_op jit(solution)/shard_map/convert_element_type | solution.py:1075
  51.8 1.1 add_convert_fusion.1
  52.9 2.9 %collective-permute-start.8 = (bf16[1024,256]{1,0:T(8,128)(2,1)}, bf16[1024,256]{1,0:T(8,128)(2,1)}, u32[]{:S(2)}, u32[]{:S(2)}) collective-permute-start(bf16[1024,256]{1,0:T(8,128)(2,1)} %add_convert_fusion.1), channel_id=1, source_target_pairs={{0,2},{2,0},{4,6},{6,4},{8,10},{10,8},{12,14},{14,12},{16,18},{18,... | collective-permute-start | bytes 1572872 | tf_op jit(solution)/shard_map/ppermute | solution.py:1038
  55.8 1.5 collective-permute-start.9
  57.3 15.6 %mixer_backward.1 = (bf16[1024,512]{1,0:T(8,128)(2,1)}, bf16[1024,512]{1,0:T(8,128)(2,1)}, bf16[1024,512]{1,0:T(8,128)(2,1)}, bf16[832,128]{1,0:T(8,128)(2,1)}, f32[2,4,8,128]{3,2,1,0:T(8,128)}) custom-call(s32[1,6]{1,0:T(1,128)} %lengths_ref.7, f32[2,4]{1,0:T(2,128)} %blend_own_ref.3, f32[2,4]{1,0:T(2,128)} %copy-done.21, ...), custom_call_target="tpu_custom_call" | custom-call | flops 200000000 | bytes 1048576 | tf_op jit(solution)/shard_map/mixer_backward/pallas_call | solution.py:1309
  73.0 1.1 add_convert_fusion.6
  74.1 1.1 add_convert_fusion.7
  75.2 0.6 collective-permute-start.11
  75.9 9.3 %finish.1 = (bf16[1024,1024]{1,0:T(8,128)(2,1)}, bf16[2112,256]{1,0:T(8,128)(2,1)}, bf16[2112,256]{1,0:T(8,128)(2,1)}) custom-call(s32[1,6]{1,0:T(1,128)} %lengths_ref.7, f32[2,4,8,128]{3,2,1,0:T(8,128)} %get-tuple-element.119.gblend_ref, f32[8,512]{1,0:T(8,128)} %get-tuple-element.120.ggain_ref, f32[1,512]{1,0:T(1,128)} %bitcast.29, ...), custom_call_target="tpu_custom_call" | custom-call | flops 80000000 | bytes 1048576 | tf_op jit(solution)/shard_map/finish/pallas_call | solution.py:1348
  85.2 0.5 collective-permute-start.13
  85.7 1.5 add_convert_fusion.4
  87.3 0.8 pad_maximum_fusion
  88.1 4.9 %all-to-all-start = ((bf16[4,256,256]{2,1,0:T(8,128)(2,1)}), bf16[4,256,256]{2,1,0:T(8,128)(2,1)S(1)}, u32[]{:S(2)}, u32[]{:S(2)}) async-start(bf16[4,256,256]{2,1,0:T(8,128)(2,1)} %pad_maximum_fusion), calls=%async_computation | async-start | bytes 1048576 | tf_op jit(solution)/shard_map/all_to_all | solution.py:1048
  93.0 0.9 add_convert_fusion.2
  93.9 1.5 collective-permute-start.14
  95.4 1.5 collective-permute-start.15
  96.9 6.3 %input_grad.1 = bf16[1024,512]{1,0:T(8,128)(2,1)} custom-call(bf16[1024,512]{1,0:T(8,128)(2,1)} %get-tuple-element.130.gq_hbm.gq_ref, bf16[1024,1024]{1,0:T(8,128)(2,1)} %get-tuple-element.144.gkv_ref, bf16[1024,512]{1,0:T(8,128)(2,1)} %x_ref.5, bf16[1024,512]{1,0:T(8,128)(2,1)} %get-tuple-element.145.branch_ref, f32[1,512]{1,0:T(1,128)} %bitcast.30, ...), custom_call_target="tpu_custom_call" | custom-call | flops 70000000 | bytes 1048576 | tf_op jit(solution)/shard_map/input_grad/pallas_call | solution.py:1405
  103.3 0.7 collective-permute-done.15
  103.9 0.8 add_convert_fusion.14
  104.7 3.4 %all-to-all-done = bf16[4,256,256]{2,1,0:T(8,128)(2,1)S(1)} async-done(((bf16[4,256,256]{2,1,0:T(8,128)(2,1)}), bf16[4,256,256]{2,1,0:T(8,128)(2,1)S(1)}, u32[]{:S(2)}, u32[]{:S(2)}) %all-to-all-start) | async-done | bytes 524320 | tf_op jit(solution)/shard_map/all_to_all | solution.py:1048
  108.2 0.8 broadcast_in_dim.2
  109.0 3.7 %all-to-all-start.1 = ((bf16[4,256,256]{2,1,0:T(8,128)(2,1)}), bf16[4,256,256]{2,1,0:T(8,128)(2,1)S(1)}, u32[]{:S(2)}, u32[]{:S(2)}) async-start(bf16[4,256,256]{2,1,0:T(8,128)(2,1)} %broadcast_in_dim.2), calls=%async_computation.1 | async-start | bytes 1048576 | tf_op jit(solution)/shard_map/all_to_all | solution.py:1048
  112.7 1.6 collective-permute-start.16
  114.3 1.5 collective-permute-start.17
  115.8 2.3 %collective-permute-done.16 = bf16[264,256]{1,0:T(8,128)(2,1)} collective-permute-done((bf16[264,256]{1,0:T(8,128)(2,1)}, bf16[264,256]{1,0:T(8,128)(2,1)}, u32[]{:S(2)}, u32[]{:S(2)}) %collective-permute-start.16) | collective-permute-done | bytes 135200 | tf_op jit(solution)/shard_map/ppermute | solution.py:1038
  118.1 1.3 collective-permute-done.17
  119.4 1.1 add_convert_fusion.13
  120.6 1.8 %collective-permute-start.18 = (bf16[528,256]{1,0:T(8,128)(2,1)S(1)}, bf16[528,256]{1,0:T(8,128)(2,1)S(1)}, u32[]{:S(2)}, u32[]{:S(2)}) collective-permute-start(bf16[528,256]{1,0:T(8,128)(2,1)S(1)} %pad_maximum_fusion.3), channel_id=1, source_target_pairs={{0,8},{2,10},{4,12},{6,14},{8,0},{10,2},{12,4},{14,6},{16,24},{18,... | collective-permute-start | bytes 811016 | tf_op jit(solution)/shard_map/ppermute | solution.py:1038
  122.3 7.1 %layer_output.1 = bf16[1024,512]{1,0:T(8,128)(2,1)} custom-call(bf16[1024,512]{1,0:T(8,128)(2,1)} %x_ref.5, bf16[1024,512]{1,0:T(8,128)(2,1)} %get-tuple-element.157.mixed_ref, bf16[1024,2048]{1,0:T(8,128)(2,1)} %get-tuple-element.158.active_ref, bf16[256,512]{1,0:T(8,128)(2,1)} %wa_own_ref.3, bf16[256,512]{1,0:T(8,128)(2,1)} %copy-done.8, ...), custom_call_target="tpu_custom_call" | custom-call | flops 50000000 | bytes 1048576 | tf_op jit(solution)/shard_map/layer_output/pallas_call | solution.py:1391
  129.4 0.2 collective-permute-done.18
  129.8 1.6 collective-permute-start.21
  131.3 2.2 %collective-permute-start.19 = (bf16[528,256]{1,0:T(8,128)(2,1)S(1)}, bf16[528,256]{1,0:T(8,128)(2,1)S(1)}, u32[]{:S(2)}, u32[]{:S(2)}) collective-permute-start(bf16[528,256]{1,0:T(8,128)(2,1)S(1)} %pad_maximum_fusion.4), channel_id=1, source_target_pairs={{0,16},{2,18},{4,20},{6,22},{8,24},{10,26},{12,28},{14,30},{16,0},... | collective-permute-start | bytes 811016 | tf_op jit(solution)/shard_map/ppermute | solution.py:1038
  133.5 1.0 collective-permute-start.20
  134.5 1.8 %collective-permute-done.21 = bf16[512,256]{1,0:T(8,128)(2,1)S(1)} collective-permute-done((bf16[512,256]{1,0:T(8,128)(2,1)S(1)}, bf16[512,256]{1,0:T(8,128)(2,1)S(1)}, u32[]{:S(2)}, u32[]{:S(2)}) %collective-permute-start.21) | collective-permute-done | bytes 262176 | tf_op jit(solution)/shard_map/ppermute | solution.py:1038
  136.4 3.9 %collective-permute-done.20 = bf16[512,256]{1,0:T(8,128)(2,1)S(1)} collective-permute-done((bf16[512,256]{1,0:T(8,128)(2,1)S(1)}, bf16[512,256]{1,0:T(8,128)(2,1)S(1)}, u32[]{:S(2)}, u32[]{:S(2)}) %collective-permute-start.20) | collective-permute-done | bytes 262176 | tf_op jit(solution)/shard_map/ppermute | solution.py:1038
  140.4 0.1 collective-permute-start.22
  140.6 1.0 collective-permute-start.23
  141.6 2.9 %collective-permute-done.19 = bf16[528,256]{1,0:T(8,128)(2,1)S(1)} collective-permute-done((bf16[528,256]{1,0:T(8,128)(2,1)S(1)}, bf16[528,256]{1,0:T(8,128)(2,1)S(1)}, u32[]{:S(2)}, u32[]{:S(2)}) %collective-permute-start.19) | collective-permute-done | bytes 270368 | tf_op jit(solution)/shard_map/ppermute | solution.py:1038
  144.5 0.9 collective-permute-start.24
  145.4 0.5 collective-permute-start.25
  145.9 8.6 %collective-permute-done.24 = bf16[264,256]{1,0:T(8,128)(2,1)S(1)} collective-permute-done((bf16[264,256]{1,0:T(8,128)(2,1)S(1)}, bf16[264,256]{1,0:T(8,128)(2,1)S(1)}, u32[]{:S(2)}, u32[]{:S(2)}) %collective-permute-start.24) | collective-permute-done | bytes 135200 | tf_op jit(solution)/shard_map/ppermute | solution.py:1038
  154.7 0.6 collective-permute-start.26
  155.3 1.3 collective-permute-start.27
  156.6 0.6 pad_add_fusion.bits_ref
  157.2 3.9 %feed_output.1 = (f32[1024,512]{1,0:T(8,128)}, f32[512,1024]{1,0:T(8,128)}) custom-call(s32[2]{0:T(128)} %pad_add_fusion.bits_ref, bf16[1024,256]{1,0:T(8,128)(2,1)} %copy-done.3, bf16[1024,256]{1,0:T(8,128)(2,1)} %copy-done.2, bf16[1024,256]{1,0:T(8,128)(2,1)} %copy-done.13, bf16[1024,256]{1,0:T(8,128)(2,1)} %copy-done.14), custom_call_target="tpu_custom_call" | custom-call | flops 30000000 | bytes 1048576 | tf_op jit(solution)/shard_map/feed_output/pallas_call | solution.py:1466
  161.3 0.5 collective-permute-done.27.b_got_hbm
  161.8 0.2 copy-done.15
  162.0 0.5 copy-done.16
  162.4 3.3 %last_output.1 = (f32[1536,256]{1,0:T(8,128)}, f32[256,512]{1,0:T(8,128)}, f32[1,512]{1,0:T(1,128)}, f32[1,512]{1,0:T(1,128)}, f32[2,4]{1,0:T(2,128)}) custom-call(s32[2]{0:T(128)} %pad_add_fusion.bits_ref, bf16[528,256]{1,0:T(8,128)(2,1)} %copy-done.5, bf16[528,256]{1,0:T(8,128)(2,1)} %copy-done.4, bf16[528,256]{1,0:T(8,128)(2,1)} %copy-done.15, ...), custom_call_target="tpu_custom_call" | custom-call | flops 30000000 | bytes 1048576 | tf_op jit(solution)/shard_map/last_output/pallas_call | solution.py:1485
  (75 shorter events, 1.3 us)
Async XLA Ops:
  0.6 6.0 %collective-permute-start.1 = (bf16[512,1024]{1,0:T(8,128)(2,1)}, bf16[512,1024]{1,0:T(8,128)(2,1)S(1)}, u32[]{:S(2)}, u32[]{:S(2)}) collective-permute-start(bf16[512,1024]{1,0:T(8,128)(2,1)} %wi_own_hbm.1), channel_id=1, source_target_pairs={{0,1},{1,0},{2,3},{3,2},{4,5},{5,4},{6,7},{7,6},{8,9},{9,8},{10,11... | collective-permute-start | bytes 3145736 | tf_op jit(solution)/shard_map/ppermute | solution.py:1175
  1.2 5.5 %collective-permute-start.2 = (bf16[1024,512]{1,0:T(8,128)(2,1)}, bf16[1024,512]{1,0:T(8,128)(2,1)S(1)}, u32[]{:S(2)}, u32[]{:S(2)}) collective-permute-start(bf16[1024,512]{1,0:T(8,128)(2,1)} %wo_own_ref.1), channel_id=1, source_target_pairs={{0,1},{1,0},{2,3},{3,2},{4,5},{5,4},{6,7},{7,6},{8,9},{9,8},{10,11... | collective-permute-start | bytes 3145736 | tf_op jit(solution)/shard_map/ppermute | solution.py:1175
  1.2 5.4 %collective-permute-start.4 = (bf16[3,512,256]{2,1,0:T(8,128)(2,1)}, bf16[3,512,256]{2,1,0:T(8,128)(2,1)S(1)}, u32[]{:S(2)}, u32[]{:S(2)}) collective-permute-start(bf16[3,512,256]{2,1,0:T(8,128)(2,1)} %bitcast.19), channel_id=1, source_target_pairs={{0,1},{1,0},{2,3},{3,2},{4,5},{5,4},{6,7},{7,6},{8,9},{9,8},{10,11... | collective-permute-start | bytes 2359304 | tf_op jit(solution)/shard_map/ppermute | solution.py:1175
  1.7 5.0 %collective-permute-start.3 = (bf16[256,512]{1,0:T(8,128)(2,1)}, bf16[256,512]{1,0:T(8,128)(2,1)S(1)}, u32[]{:S(2)}, u32[]{:S(2)}) collective-permute-start(bf16[256,512]{1,0:T(8,128)(2,1)} %wa_own_ref.3), channel_id=1, source_target_pairs={{0,1},{1,0},{2,3},{3,2},{4,5},{5,4},{6,7},{7,6},{8,9},{9,8},{10,11... | collective-permute-start | bytes 786440 | tf_op jit(solution)/shard_map/ppermute | solution.py:1175
  6.7 5.9 %copy-start.8 = (bf16[256,512]{1,0:T(8,128)(2,1)}, bf16[256,512]{1,0:T(8,128)(2,1)S(1)}, u32[]{:S(2)}) copy-start(bf16[256,512]{1,0:T(8,128)(2,1)S(1)} %collective-permute-done.3.wa_other_ref) | copy-start | bytes 786436
  6.7 5.9 %copy-start.7 = (bf16[512,1024]{1,0:T(8,128)(2,1)}, bf16[512,1024]{1,0:T(8,128)(2,1)S(1)}, u32[]{:S(2)}) copy-start(bf16[512,1024]{1,0:T(8,128)(2,1)S(1)} %collective-permute-done.1.wi_other_hbm) | copy-start | bytes 3145732
  6.7 7.6 %copy-start.1 = (bf16[1024,512]{1,0:T(8,128)(2,1)}, bf16[1024,512]{1,0:T(8,128)(2,1)S(1)}, u32[]{:S(2)}) copy-start(bf16[1024,512]{1,0:T(8,128)(2,1)S(1)} %collective-permute-done.2.wo_other_hbm.wo_other_ref) | copy-start | bytes 3145732
  6.7 0.9 copy-start
  7.6 5.4 %copy-start.20 = (f32[2,4]{1,0:T(2,128)S(1)}, f32[2,4]{1,0:T(2,128)}, u32[]{:S(2)}) copy-start(f32[2,4]{1,0:T(2,128)} %blend_own_ref.3) | copy-start | bytes 100
  12.6 1.7 %collective-permute-start.5 = (bf16[832,128]{1,0:T(8,128)(2,1)}, bf16[832,128]{1,0:T(8,128)(2,1)S(1)}, u32[]{:S(2)}, u32[]{:S(2)}) collective-permute-start(bf16[832,128]{1,0:T(8,128)(2,1)} %get-tuple-element.101), channel_id=1, source_target_pairs={{0,1},{1,0},{2,3},{3,2},{4,5},{5,4},{6,7},{7,6},{8,9},{9,8},{10,11... | collective-permute-start | bytes 638984 | tf_op jit(solution)/shard_map/ppermute | solution.py:1175
  13.0 1.1 collective-permute-start
  14.1 0.6 copy-start.21
  14.3 0.7 copy-start.18
  46.5 5.3 %copy-start.9 = (bf16[2048,256]{1,0:T(8,128)(2,1)S(1)}, bf16[2048,256]{1,0:T(8,128)(2,1)}, u32[]{:S(2)}) copy-start(bf16[2048,256]{1,0:T(8,128)(2,1)} %get-tuple-element.114) | copy-start | bytes 3145732
  46.5 2.9 %collective-permute-start.7 = (bf16[2048,256]{1,0:T(8,128)(2,1)}, bf16[2048,256]{1,0:T(8,128)(2,1)S(1)}, u32[]{:S(2)}, u32[]{:S(2)}) collective-permute-start(bf16[2048,256]{1,0:T(8,128)(2,1)} %get-tuple-element.117), channel_id=1, source_target_pairs={{0,1},{1,0},{2,3},{3,2},{4,5},{5,4},{6,7},{7,6},{8,9},{9,8},{10,11... | collective-permute-start | bytes 3145736 | tf_op jit(solution)/shard_map/ppermute | solution.py:1175
  47.0 4.8 %collective-permute-start.6 = (bf16[2048,256]{1,0:T(8,128)(2,1)}, bf16[2048,256]{1,0:T(8,128)(2,1)S(1)}, u32[]{:S(2)}, u32[]{:S(2)}) collective-permute-start(bf16[2048,256]{1,0:T(8,128)(2,1)} %get-tuple-element.115), channel_id=1, source_target_pairs={{0,1},{1,0},{2,3},{3,2},{4,5},{5,4},{6,7},{7,6},{8,9},{9,8},{10,11... | collective-permute-start | bytes 3145736 | tf_op jit(solution)/shard_map/ppermute | solution.py:1175
  49.5 23.5 %copy-start.11 = (bf16[2048,256]{1,0:T(8,128)(2,1)}, bf16[2048,256]{1,0:T(8,128)(2,1)S(1)}, u32[]{:S(2)}) copy-start(bf16[2048,256]{1,0:T(8,128)(2,1)S(1)} %collective-permute-done.7) | copy-start | bytes 3145732
  51.8 5.5 %copy-start.12 = (bf16[2048,256]{1,0:T(8,128)(2,1)}, bf16[2048,256]{1,0:T(8,128)(2,1)S(1)}, u32[]{:S(2)}) copy-start(bf16[2048,256]{1,0:T(8,128)(2,1)S(1)} %collective-permute-done.6) | copy-start | bytes 3145732
  52.9 20.0 %collective-permute-start.8 = (bf16[1024,256]{1,0:T(8,128)(2,1)}, bf16[1024,256]{1,0:T(8,128)(2,1)}, u32[]{:S(2)}, u32[]{:S(2)}) collective-permute-start(bf16[1024,256]{1,0:T(8,128)(2,1)} %add_convert_fusion.1), channel_id=1, source_target_pairs={{0,2},{2,0},{4,6},{6,4},{8,10},{10,8},{12,14},{14,12},{16,18},{18,... | collective-permute-start | bytes 1572872 | tf_op jit(solution)/shard_map/ppermute | solution.py:1038
  55.8 17.1 %collective-permute-start.9 = (bf16[1024,256]{1,0:T(8,128)(2,1)}, bf16[1024,256]{1,0:T(8,128)(2,1)}, u32[]{:S(2)}, u32[]{:S(2)}) collective-permute-start(bf16[1024,256]{1,0:T(8,128)(2,1)} %add_convert_fusion), channel_id=1, source_target_pairs={{0,4},{2,6},{4,0},{6,2},{8,12},{10,14},{12,8},{14,10},{16,20},{18,... | collective-permute-start | bytes 1572872 | tf_op jit(solution)/shard_map/ppermute | solution.py:1038
  57.3 15.7 %copy-start.10 = (bf16[2048,256]{1,0:T(8,128)(2,1)S(1)}, bf16[2048,256]{1,0:T(8,128)(2,1)}, u32[]{:S(2)}) copy-start(bf16[2048,256]{1,0:T(8,128)(2,1)} %get-tuple-element.116) | copy-start | bytes 3145732
  72.9 2.3 %collective-permute-start.10 = (bf16[832,128]{1,0:T(8,128)(2,1)}, bf16[832,128]{1,0:T(8,128)(2,1)S(1)}, u32[]{:S(2)}, u32[]{:S(2)}) collective-permute-start(bf16[832,128]{1,0:T(8,128)(2,1)} %get-tuple-element.124), channel_id=1, source_target_pairs={{0,1},{1,0},{2,3},{3,2},{4,5},{5,4},{6,7},{7,6},{8,9},{9,8},{10,11... | collective-permute-start | bytes 638984 | tf_op jit(solution)/shard_map/ppermute | solution.py:1175
  75.2 0.7 copy-start.17
  75.2 10.0 %collective-permute-start.11 = (bf16[512,256]{1,0:T(8,128)(2,1)S(1)}, bf16[512,256]{1,0:T(8,128)(2,1)S(1)}, u32[]{:S(2)}, u32[]{:S(2)}) collective-permute-start(bf16[512,256]{1,0:T(8,128)(2,1)S(1)} %add_convert_fusion.7), channel_id=1, source_target_pairs={{0,4},{2,6},{4,0},{6,2},{8,12},{10,14},{12,8},{14,10},{16,20},{18,... | collective-permute-start | bytes 786440 | tf_op jit(solution)/shard_map/ppermute | solution.py:1038
  75.8 9.4 %collective-permute-start.12 = (bf16[512,256]{1,0:T(8,128)(2,1)S(1)}, bf16[512,256]{1,0:T(8,128)(2,1)}, u32[]{:S(2)}, u32[]{:S(2)}) collective-permute-start(bf16[512,256]{1,0:T(8,128)(2,1)S(1)} %add_convert_fusion.6), channel_id=1, source_target_pairs={{0,2},{2,0},{4,6},{6,4},{8,10},{10,8},{12,14},{14,12},{16,18},{18,... | collective-permute-start | bytes 786440 | tf_op jit(solution)/shard_map/ppermute | solution.py:1038
  85.2 7.8 %collective-permute-start.13 = (bf16[2112,256]{1,0:T(8,128)(2,1)}, bf16[2112,256]{1,0:T(8,128)(2,1)S(1)}, u32[]{:S(2)}, u32[]{:S(2)}) collective-permute-start(bf16[2112,256]{1,0:T(8,128)(2,1)} %get-tuple-element.137), channel_id=1, source_target_pairs={{0,1},{1,0},{2,3},{3,2},{4,5},{5,4},{6,7},{7,6},{8,9},{9,8},{10,11... | collective-permute-start | bytes 3244040 | tf_op jit(solution)/shard_map/ppermute | solution.py:1175
  87.3 5.7 %copy-start.6 = (bf16[2112,256]{1,0:T(8,128)(2,1)S(1)}, bf16[2112,256]{1,0:T(8,128)(2,1)}, u32[]{:S(2)}) copy-start(bf16[2112,256]{1,0:T(8,128)(2,1)} %get-tuple-element.133) | copy-start | bytes 3244036
  88.1 20.0 %all-to-all-start = ((bf16[4,256,256]{2,1,0:T(8,128)(2,1)}), bf16[4,256,256]{2,1,0:T(8,128)(2,1)S(1)}, u32[]{:S(2)}, u32[]{:S(2)}) async-start(bf16[4,256,256]{2,1,0:T(8,128)(2,1)} %pad_maximum_fusion), calls=%async_computation | async-start | bytes 1048576 | tf_op jit(solution)/shard_map/all_to_all | solution.py:1048
  93.9 9.3 %collective-permute-start.14 = (bf16[528,256]{1,0:T(8,128)(2,1)}, bf16[528,256]{1,0:T(8,128)(2,1)S(1)}, u32[]{:S(2)}, u32[]{:S(2)}) collective-permute-start(bf16[528,256]{1,0:T(8,128)(2,1)} %get-tuple-element.142), channel_id=1, source_target_pairs={{0,2},{2,0},{4,6},{6,4},{8,10},{10,8},{12,14},{14,12},{16,18},{18,... | collective-permute-start | bytes 811016 | tf_op jit(solution)/shard_map/ppermute | solution.py:1038
  95.4 8.5 %collective-permute-start.15 = (bf16[528,256]{1,0:T(8,128)(2,1)}, bf16[528,256]{1,0:T(8,128)(2,1)S(1)}, u32[]{:S(2)}, u32[]{:S(2)}) collective-permute-start(bf16[528,256]{1,0:T(8,128)(2,1)} %get-tuple-element.143), channel_id=1, source_target_pairs={{0,4},{2,6},{4,0},{6,2},{8,12},{10,14},{12,8},{14,10},{16,20},{18,... | collective-permute-start | bytes 811016 | tf_op jit(solution)/shard_map/ppermute | solution.py:1038
  108.2 6.1 %copy-start.19 = (bf16[264,256]{1,0:T(8,128)(2,1)S(1)}, bf16[264,256]{1,0:T(8,128)(2,1)}, u32[]{:S(2)}) copy-start(bf16[264,256]{1,0:T(8,128)(2,1)} %get-tuple-element.154) | copy-start | bytes 405508
  109.0 20.4 %all-to-all-start.1 = ((bf16[4,256,256]{2,1,0:T(8,128)(2,1)}), bf16[4,256,256]{2,1,0:T(8,128)(2,1)S(1)}, u32[]{:S(2)}, u32[]{:S(2)}) async-start(bf16[4,256,256]{2,1,0:T(8,128)(2,1)} %broadcast_in_dim.2), calls=%async_computation.1 | async-start | bytes 1048576 | tf_op jit(solution)/shard_map/all_to_all | solution.py:1048
  112.7 5.4 %collective-permute-start.16 = (bf16[264,256]{1,0:T(8,128)(2,1)}, bf16[264,256]{1,0:T(8,128)(2,1)}, u32[]{:S(2)}, u32[]{:S(2)}) collective-permute-start(bf16[264,256]{1,0:T(8,128)(2,1)} %get-tuple-element.153), channel_id=1, source_target_pairs={{0,4},{2,6},{4,0},{6,2},{8,12},{10,14},{12,8},{14,10},{16,20},{18,... | collective-permute-start | bytes 405512 | tf_op jit(solution)/shard_map/ppermute | solution.py:1038
  114.3 5.1 %collective-permute-start.17 = (bf16[264,256]{1,0:T(8,128)(2,1)S(1)}, bf16[264,256]{1,0:T(8,128)(2,1)}, u32[]{:S(2)}, u32[]{:S(2)}) collective-permute-start(bf16[264,256]{1,0:T(8,128)(2,1)S(1)} %copy-done.19), channel_id=1, source_target_pairs={{0,2},{2,0},{4,6},{6,4},{8,10},{10,8},{12,14},{14,12},{16,18},{18,... | collective-permute-start | bytes 405512 | tf_op jit(solution)/shard_map/ppermute | solution.py:1038
  120.6 9.0 %collective-permute-start.18 = (bf16[528,256]{1,0:T(8,128)(2,1)S(1)}, bf16[528,256]{1,0:T(8,128)(2,1)S(1)}, u32[]{:S(2)}, u32[]{:S(2)}) collective-permute-start(bf16[528,256]{1,0:T(8,128)(2,1)S(1)} %pad_maximum_fusion.3), channel_id=1, source_target_pairs={{0,8},{2,10},{4,12},{6,14},{8,0},{10,2},{12,4},{14,6},{16,24},{18,... | collective-permute-start | bytes 811016 | tf_op jit(solution)/shard_map/ppermute | solution.py:1038
  129.8 6.5 %collective-permute-start.21 = (bf16[512,256]{1,0:T(8,128)(2,1)S(1)}, bf16[512,256]{1,0:T(8,128)(2,1)S(1)}, u32[]{:S(2)}, u32[]{:S(2)}) collective-permute-start(bf16[512,256]{1,0:T(8,128)(2,1)S(1)} %bitcast.27), channel_id=1, source_target_pairs={{0,2},{2,0},{4,6},{6,4},{8,10},{10,8},{12,14},{14,12},{16,18},{18,... | collective-permute-start | bytes 786440 | tf_op jit(solution)/shard_map/ppermute | solution.py:1038
  131.3 13.1 %collective-permute-start.19 = (bf16[528,256]{1,0:T(8,128)(2,1)S(1)}, bf16[528,256]{1,0:T(8,128)(2,1)S(1)}, u32[]{:S(2)}, u32[]{:S(2)}) collective-permute-start(bf16[528,256]{1,0:T(8,128)(2,1)S(1)} %pad_maximum_fusion.4), channel_id=1, source_target_pairs={{0,16},{2,18},{4,20},{6,22},{8,24},{10,26},{12,28},{14,30},{16,0},... | collective-permute-start | bytes 811016 | tf_op jit(solution)/shard_map/ppermute | solution.py:1038
  133.5 6.8 %collective-permute-start.20 = (bf16[512,256]{1,0:T(8,128)(2,1)S(1)}, bf16[512,256]{1,0:T(8,128)(2,1)S(1)}, u32[]{:S(2)}, u32[]{:S(2)}) collective-permute-start(bf16[512,256]{1,0:T(8,128)(2,1)S(1)} %bitcast.26), channel_id=1, source_target_pairs={{0,4},{2,6},{4,0},{6,2},{8,12},{10,14},{12,8},{14,10},{16,20},{18,... | collective-permute-start | bytes 786440 | tf_op jit(solution)/shard_map/ppermute | solution.py:1038
  136.4 18.2 %copy-start.2 = (bf16[1024,256]{1,0:T(8,128)(2,1)}, bf16[1024,256]{1,0:T(8,128)(2,1)S(1)}, u32[]{:S(2)}) copy-start(bf16[1024,256]{1,0:T(8,128)(2,1)S(1)} %pad_maximum_fusion.2.in_mine_hbm) | copy-start | bytes 1572868
  140.4 16.8 %copy-start.3 = (bf16[1024,256]{1,0:T(8,128)(2,1)}, bf16[1024,256]{1,0:T(8,128)(2,1)S(1)}, u32[]{:S(2)}) copy-start(bf16[1024,256]{1,0:T(8,128)(2,1)S(1)} %pad_maximum_fusion.1.out_mine_hbm) | copy-start | bytes 1572868
  140.4 14.1 %collective-permute-start.22 = (bf16[1024,256]{1,0:T(8,128)(2,1)S(1)}, bf16[1024,256]{1,0:T(8,128)(2,1)S(1)}, u32[]{:S(2)}, u32[]{:S(2)}) collective-permute-start(bf16[1024,256]{1,0:T(8,128)(2,1)S(1)} %pad_maximum_fusion.1.out_mine_hbm), channel_id=1, source_target_pairs={{0,2},{2,0},{4,6},{6,4},{8,10},{10,8},{12,14},{14,12},{16,18},{18,... | collective-permute-start | bytes 1572872 | tf_op jit(solution)/shard_map/ppermute | solution.py:1038
  140.6 14.0 %collective-permute-start.23 = (bf16[1024,256]{1,0:T(8,128)(2,1)S(1)}, bf16[1024,256]{1,0:T(8,128)(2,1)S(1)}, u32[]{:S(2)}, u32[]{:S(2)}) collective-permute-start(bf16[1024,256]{1,0:T(8,128)(2,1)S(1)} %pad_maximum_fusion.2.in_mine_hbm), channel_id=1, source_target_pairs={{0,4},{2,6},{4,0},{6,2},{8,12},{10,14},{12,8},{14,10},{16,20},{18,... | collective-permute-start | bytes 1572872 | tf_op jit(solution)/shard_map/ppermute | solution.py:1038
  144.5 10.1 %collective-permute-start.24 = (bf16[264,256]{1,0:T(8,128)(2,1)S(1)}, bf16[264,256]{1,0:T(8,128)(2,1)S(1)}, u32[]{:S(2)}, u32[]{:S(2)}) collective-permute-start(bf16[264,256]{1,0:T(8,128)(2,1)S(1)} %get-tuple-element.169), channel_id=1, source_target_pairs={{0,4},{2,6},{4,0},{6,2},{8,12},{10,14},{12,8},{14,10},{16,20},{18,... | collective-permute-start | bytes 405512 | tf_op jit(solution)/shard_map/ppermute | solution.py:1038
  145.4 9.1 %collective-permute-start.25 = (bf16[264,256]{1,0:T(8,128)(2,1)S(1)}, bf16[264,256]{1,0:T(8,128)(2,1)S(1)}, u32[]{:S(2)}, u32[]{:S(2)}) collective-permute-start(bf16[264,256]{1,0:T(8,128)(2,1)S(1)} %get-tuple-element.170), channel_id=1, source_target_pairs={{0,2},{2,0},{4,6},{6,4},{8,10},{10,8},{12,14},{14,12},{16,18},{18,... | collective-permute-start | bytes 405512 | tf_op jit(solution)/shard_map/ppermute | solution.py:1038
  154.5 2.6 %copy-start.13 = (bf16[1024,256]{1,0:T(8,128)(2,1)}, bf16[1024,256]{1,0:T(8,128)(2,1)S(1)}, u32[]{:S(2)}) copy-start(bf16[1024,256]{1,0:T(8,128)(2,1)S(1)} %collective-permute-done.22.out_got_hbm) | copy-start | bytes 1572868
  154.6 2.6 %copy-start.14 = (bf16[1024,256]{1,0:T(8,128)(2,1)}, bf16[1024,256]{1,0:T(8,128)(2,1)S(1)}, u32[]{:S(2)}) copy-start(bf16[1024,256]{1,0:T(8,128)(2,1)S(1)} %collective-permute-done.23.in_got_hbm) | copy-start | bytes 1572868
  154.7 7.1 %copy-start.4 = (bf16[528,256]{1,0:T(8,128)(2,1)}, bf16[528,256]{1,0:T(8,128)(2,1)S(1)}, u32[]{:S(2)}) copy-start(bf16[528,256]{1,0:T(8,128)(2,1)S(1)} %pad_maximum_fusion.6.b_mine_hbm) | copy-start | bytes 811012
  154.7 7.0 %copy-start.5 = (bf16[528,256]{1,0:T(8,128)(2,1)}, bf16[528,256]{1,0:T(8,128)(2,1)S(1)}, u32[]{:S(2)}) copy-start(bf16[528,256]{1,0:T(8,128)(2,1)S(1)} %pad_maximum_fusion.5.a_mine_hbm) | copy-start | bytes 811012
  154.7 6.5 %collective-permute-start.26 = (bf16[528,256]{1,0:T(8,128)(2,1)S(1)}, bf16[528,256]{1,0:T(8,128)(2,1)S(1)}, u32[]{:S(2)}, u32[]{:S(2)}) collective-permute-start(bf16[528,256]{1,0:T(8,128)(2,1)S(1)} %pad_maximum_fusion.5.a_mine_hbm), channel_id=1, source_target_pairs={{0,2},{2,0},{4,6},{6,4},{8,10},{10,8},{12,14},{14,12},{16,18},{18,... | collective-permute-start | bytes 811016 | tf_op jit(solution)/shard_map/ppermute | solution.py:1038
  155.3 6.5 %collective-permute-start.27 = (bf16[528,256]{1,0:T(8,128)(2,1)S(1)}, bf16[528,256]{1,0:T(8,128)(2,1)S(1)}, u32[]{:S(2)}, u32[]{:S(2)}) collective-permute-start(bf16[528,256]{1,0:T(8,128)(2,1)S(1)} %pad_maximum_fusion.6.b_mine_hbm), channel_id=1, source_target_pairs={{0,4},{2,6},{4,0},{6,2},{8,12},{10,14},{12,8},{14,10},{16,20},{18,... | collective-permute-start | bytes 811016 | tf_op jit(solution)/shard_map/ppermute | solution.py:1038
  161.3 0.7 copy-start.15
  161.7 0.7 copy-start.16

commit v7 on v6

--- a/solution.py
+++ b/solution.py
@@ -125,7 +125,7 @@
 def unpack(packet_ref, pair, diag):
     base = 144 * pair
     state = unpacked_state(packet_ref[base : base + 128].astype(F32), diag)
-    return state, packet_ref[base + 128 : base + 136].astype(F32)
+    return state, packet_ref[base + 128 : base + 144].astype(F32)[:8]
 
 
 def unpack_halo(packet_ref, kind, pair):

time: 167 us -> 167 us (level)
  no operation moved by 1% of the time
where the time goes in v7:
time: 167 us; the launch traced here: 166 us
  Pallas kernels  86.6 us (52%)
  starting transfers between devices  33.5 us (20%)
  waiting for transfers between devices  29.5 us (18%)
  other arithmetic  11.9 us (7%)
  local copies, waits for them, and re-layouts  3.24 us (2%)
    pallas_call x1, Pallas kernels, body(): pl.pallas_call(partial(layer_kernel, blocks, parts), in_specs=[smem] * 3...  31.5 us
    ppermute x18, waiting for transfers between devices, flip(): return lax.ppermute(values, 'dp', pairs)  22.3 us
    ppermute x18, starting transfers between devices, flip(): return lax.ppermute(values, 'dp', pairs)  22.1 us
    pallas_call x1, Pallas kernels, body(): pl.pallas_call(mixer_backward_kernel, grid=(steps,), in_specs=[smem, smem...  15.6 us
    convert_element_type x11, other arithmetic, cut(): return total.astype(BF)  10.2 us
    pallas_call x1, Pallas kernels, body(): pl.pallas_call(finish_kernel, in_specs=[smem] + [vmem] * 3 + [anywhere] *...  9.27 us
    all_to_all x2, starting transfers between devices, trade(): lax.all_to_all(values, 'dp', split_axis=0, concat_axis=0, axis_index_grou...  8.58 us
    pallas_call x1, Pallas kernels, layer_output(): pl.pallas_call(output_kernel, grid=(4,), in_specs=[row_block(tall, width)...  7.1 us
  transfers between devices with their start and end apart: 30, of which 15 were waited for; matrix products, arithmetic and copies ran while one was open for 6% of the time, Pallas kernels for 28%

profile of v7, /device:TPU:0, one launch (start us, length us, event | category | flops | bytes accessed | tf_op | source)
XLA Modules:
  0.0 166.0 jit_solution(8337279919195540056)
XLA Ops:
  0.6 0.5 collective-permute-start.1
  1.2 0.4 collective-permute-start.4
  1.8 4.6 %norm_project.1 = (bf16[1024,512]{1,0:T(8,128)(2,1)}, bf16[1024,768]{1,0:T(8,128)(2,1)}) custom-call(bf16[1024,512]{1,0:T(8,128)(2,1)} %x_ref.5, f32[1,512]{1,0:T(1,128)} %bitcast.28, bf16[3,512,256]{2,1,0:T(8,128)(2,1)} %bitcast.20), custom_call_target="tpu_custom_call" | custom-call | flops 50000000 | bytes 1048576 | tf_op jit(solution)/shard_map/norm_project/pallas_call | solution.py:1194
  6.3 0.3 collective-permute-done.3.wa_other_ref
  6.7 0.9 copy-done
  7.6 4.9 %project_state.1 = (bf16[1024,768]{1,0:T(8,128)(2,1)}, bf16[832,128]{1,0:T(8,128)(2,1)}) custom-call(s32[1,6]{1,0:T(1,128)} %lengths_ref.7, bf16[1024,512]{1,0:T(8,128)(2,1)} %get-tuple-element.99.normed_ref.normed_hbm, bf16[3,512,256]{2,1,0:T(8,128)(2,1)} %copy-done, bf16[1024,768]{1,0:T(8,128)(2,1)} %get-tuple-element.100.own_ref.own_hbm.refs_0_), custom_call_target="tpu_custom_call" | custom-call | flops 50000000 | bytes 1048576 | tf_op jit(solution)/shard_map/project_state/pallas_call | solution.py:1205
  12.6 0.4 collective-permute-start.5
  13.0 0.1 collective-permute-start
  13.1 1.0 collective-permute-done.blend_other_ref
  14.1 0.2 collective-permute-done.5.packet_ref
  14.3 0.4 copy-done.21
  14.7 0.3 copy-done.18
  15.0 31.5 %layer.1 = (bf16[1024,512]{1,0:T(8,128)(2,1)}, bf16[1024,512]{1,0:T(8,128)(2,1)}, f32[8,512]{1,0:T(8,128)}, bf16[512,256]{1,0:T(8,128)(2,1)}, bf16[512,256]{1,0:...) custom-call(s32[1,6]{1,0:T(1,128)} %lengths_ref.7, ...), custom_call_target="tpu_custom_call" | custom-call | flops 300000000 | bytes 1048576 | tf_op jit(solution)/shard_map/layer/pallas_call | solution.py:1235
  46.5 0.4 collective-permute-start.7
  47.1 2.4 %collective-permute-done.7 = bf16[2048,256]{1,0:T(8,128)(2,1)S(1)} collective-permute-done((bf16[2048,256]{1,0:T(8,128)(2,1)}, bf16[2048,256]{1,0:T(8,128)(2,1)S(1)}, u32[]{:S(2)}, u32[]{:S(2)}) %collective-permute-start.7) | collective-permute-done | bytes 1048608 | tf_op jit(solution)/shard_map/ppermute | solution.py:1175
  49.5 2.3 %add_convert_fusion = bf16[1024,256]{1,0:T(8,128)(2,1)} fusion(bf16[2048,256]{1,0:T(8,128)(2,1)S(1)} %collective-permute-done.7, s32[]{:T(128)S(6)} %select_n.196, bf16[2048,256]{1,0:T(8,128)(2,1)} %get-tuple-element.116), kind=kLoop, calls=%fused_computation | loop fusion | flops 1048576 | bytes 1572868 | tf_op jit(solution)/shard_map/convert_element_type | solution.py:1075
  51.8 1.1 add_convert_fusion.1
  52.9 2.9 %collective-permute-start.8 = (bf16[1024,256]{1,0:T(8,128)(2,1)}, bf16[1024,256]{1,0:T(8,128)(2,1)}, u32[]{:S(2)}, u32[]{:S(2)}) collective-permute-start(bf16[1024,256]{1,0:T(8,128)(2,1)} %add_convert_fusion.1), channel_id=1, source_target_pairs={{0,2},{2,0},{4,6},{6,4},{8,10},{10,8},{12,14},{14,12},{16,18},{18,... | collective-permute-start | bytes 1572872 | tf_op jit(solution)/shard_map/ppermute | solution.py:1038
  55.8 1.5 collective-permute-start.9
  57.3 15.6 %mixer_backward.1 = (bf16[1024,512]{1,0:T(8,128)(2,1)}, bf16[1024,512]{1,0:T(8,128)(2,1)}, bf16[1024,512]{1,0:T(8,128)(2,1)}, bf16[832,128]{1,0:T(8,128)(2,1)}, f32[2,4,8,128]{3,2,1,0:T(8,128)}) custom-call(s32[1,6]{1,0:T(1,128)} %lengths_ref.7, f32[2,4]{1,0:T(2,128)} %blend_own_ref.3, f32[2,4]{1,0:T(2,128)} %copy-done.21, ...), custom_call_target="tpu_custom_call" | custom-call | flops 200000000 | bytes 1048576 | tf_op jit(solution)/shard_map/mixer_backward/pallas_call | solution.py:1309
  73.0 1.1 add_convert_fusion.6
  74.1 1.1 add_convert_fusion.7
  75.2 0.6 collective-permute-start.11
  75.9 9.3 %finish.1 = (bf16[1024,1024]{1,0:T(8,128)(2,1)}, bf16[2112,256]{1,0:T(8,128)(2,1)}, bf16[2112,256]{1,0:T(8,128)(2,1)}) custom-call(s32[1,6]{1,0:T(1,128)} %lengths_ref.7, f32[2,4,8,128]{3,2,1,0:T(8,128)} %get-tuple-element.119.gblend_ref, f32[8,512]{1,0:T(8,128)} %get-tuple-element.120.ggain_ref, f32[1,512]{1,0:T(1,128)} %bitcast.29, ...), custom_call_target="tpu_custom_call" | custom-call | flops 80000000 | bytes 1048576 | tf_op jit(solution)/shard_map/finish/pallas_call | solution.py:1348
  85.2 0.5 collective-permute-start.13
  85.7 1.5 add_convert_fusion.4
  87.3 0.8 pad_maximum_fusion
  88.1 4.9 %all-to-all-start = ((bf16[4,256,256]{2,1,0:T(8,128)(2,1)}), bf16[4,256,256]{2,1,0:T(8,128)(2,1)S(1)}, u32[]{:S(2)}, u32[]{:S(2)}) async-start(bf16[4,256,256]{2,1,0:T(8,128)(2,1)} %pad_maximum_fusion), calls=%async_computation | async-start | bytes 1048576 | tf_op jit(solution)/shard_map/all_to_all | solution.py:1048
  93.0 0.9 add_convert_fusion.2
  93.9 1.5 collective-permute-start.14
  95.4 1.5 collective-permute-start.15
  96.9 6.3 %input_grad.1 = bf16[1024,512]{1,0:T(8,128)(2,1)} custom-call(bf16[1024,512]{1,0:T(8,128)(2,1)} %get-tuple-element.130.gq_hbm.gq_ref, bf16[1024,1024]{1,0:T(8,128)(2,1)} %get-tuple-element.144.gkv_ref, bf16[1024,512]{1,0:T(8,128)(2,1)} %x_ref.5, bf16[1024,512]{1,0:T(8,128)(2,1)} %get-tuple-element.145.branch_ref, f32[1,512]{1,0:T(1,128)} %bitcast.30, ...), custom_call_target="tpu_custom_call" | custom-call | flops 70000000 | bytes 1048576 | tf_op jit(solution)/shard_map/input_grad/pallas_call | solution.py:1405
  103.3 0.7 collective-permute-done.15
  103.9 0.8 add_convert_fusion.14
  104.7 3.4 %all-to-all-done = bf16[4,256,256]{2,1,0:T(8,128)(2,1)S(1)} async-done(((bf16[4,256,256]{2,1,0:T(8,128)(2,1)}), bf16[4,256,256]{2,1,0:T(8,128)(2,1)S(1)}, u32[]{:S(2)}, u32[]{:S(2)}) %all-to-all-start) | async-done | bytes 524320 | tf_op jit(solution)/shard_map/all_to_all | solution.py:1048
  108.2 0.8 broadcast_in_dim.2
  109.0 3.7 %all-to-all-start.1 = ((bf16[4,256,256]{2,1,0:T(8,128)(2,1)}), bf16[4,256,256]{2,1,0:T(8,128)(2,1)S(1)}, u32[]{:S(2)}, u32[]{:S(2)}) async-start(bf16[4,256,256]{2,1,0:T(8,128)(2,1)} %broadcast_in_dim.2), calls=%async_computation.1 | async-start | bytes 1048576 | tf_op jit(solution)/shard_map/all_to_all | solution.py:1048
  112.7 1.6 collective-permute-start.16
  114.3 1.5 collective-permute-start.17
  115.8 2.3 %collective-permute-done.16 = bf16[264,256]{1,0:T(8,128)(2,1)} collective-permute-done((bf16[264,256]{1,0:T(8,128)(2,1)}, bf16[264,256]{1,0:T(8,128)(2,1)}, u32[]{:S(2)}, u32[]{:S(2)}) %collective-permute-start.16) | collective-permute-done | bytes 135200 | tf_op jit(solution)/shard_map/ppermute | solution.py:1038
  118.1 1.3 collective-permute-done.17
  119.4 1.1 add_convert_fusion.13
  120.6 1.8 %collective-permute-start.18 = (bf16[528,256]{1,0:T(8,128)(2,1)S(1)}, bf16[528,256]{1,0:T(8,128)(2,1)S(1)}, u32[]{:S(2)}, u32[]{:S(2)}) collective-permute-start(bf16[528,256]{1,0:T(8,128)(2,1)S(1)} %pad_maximum_fusion.3), channel_id=1, source_target_pairs={{0,8},{2,10},{4,12},{6,14},{8,0},{10,2},{12,4},{14,6},{16,24},{18,... | collective-permute-start | bytes 811016 | tf_op jit(solution)/shard_map/ppermute | solution.py:1038
  122.3 7.1 %layer_output.1 = bf16[1024,512]{1,0:T(8,128)(2,1)} custom-call(bf16[1024,512]{1,0:T(8,128)(2,1)} %x_ref.5, bf16[1024,512]{1,0:T(8,128)(2,1)} %get-tuple-element.157.mixed_ref, bf16[1024,2048]{1,0:T(8,128)(2,1)} %get-tuple-element.158.active_ref, bf16[256,512]{1,0:T(8,128)(2,1)} %wa_own_ref.3, bf16[256,512]{1,0:T(8,128)(2,1)} %copy-done.8, ...), custom_call_target="tpu_custom_call" | custom-call | flops 50000000 | bytes 1048576 | tf_op jit(solution)/shard_map/layer_output/pallas_call | solution.py:1391
  129.4 0.2 collective-permute-done.18
  129.8 1.6 collective-permute-start.21
  131.3 2.2 %collective-permute-start.19 = (bf16[528,256]{1,0:T(8,128)(2,1)S(1)}, bf16[528,256]{1,0:T(8,128)(2,1)S(1)}, u32[]{:S(2)}, u32[]{:S(2)}) collective-permute-start(bf16[528,256]{1,0:T(8,128)(2,1)S(1)} %pad_maximum_fusion.4), channel_id=1, source_target_pairs={{0,16},{2,18},{4,20},{6,22},{8,24},{10,26},{12,28},{14,30},{16,0},... | collective-permute-start | bytes 811016 | tf_op jit(solution)/shard_map/ppermute | solution.py:1038
  133.5 1.0 collective-permute-start.20
  134.5 1.8 %collective-permute-done.21 = bf16[512,256]{1,0:T(8,128)(2,1)S(1)} collective-permute-done((bf16[512,256]{1,0:T(8,128)(2,1)S(1)}, bf16[512,256]{1,0:T(8,128)(2,1)S(1)}, u32[]{:S(2)}, u32[]{:S(2)}) %collective-permute-start.21) | collective-permute-done | bytes 262176 | tf_op jit(solution)/shard_map/ppermute | solution.py:1038
  136.4 3.9 %collective-permute-done.20 = bf16[512,256]{1,0:T(8,128)(2,1)S(1)} collective-permute-done((bf16[512,256]{1,0:T(8,128)(2,1)S(1)}, bf16[512,256]{1,0:T(8,128)(2,1)S(1)}, u32[]{:S(2)}, u32[]{:S(2)}) %collective-permute-start.20) | collective-permute-done | bytes 262176 | tf_op jit(solution)/shard_map/ppermute | solution.py:1038
  140.4 0.1 collective-permute-start.22
  140.6 1.0 collective-permute-start.23
  141.6 2.9 %collective-permute-done.19 = bf16[528,256]{1,0:T(8,128)(2,1)S(1)} collective-permute-done((bf16[528,256]{1,0:T(8,128)(2,1)S(1)}, bf16[528,256]{1,0:T(8,128)(2,1)S(1)}, u32[]{:S(2)}, u32[]{:S(2)}) %collective-permute-start.19) | collective-permute-done | bytes 270368 | tf_op jit(solution)/shard_map/ppermute | solution.py:1038
  144.5 0.9 collective-permute-start.24
  145.4 0.5 collective-permute-start.25
  145.9 8.6 %collective-permute-done.24 = bf16[264,256]{1,0:T(8,128)(2,1)S(1)} collective-permute-done((bf16[264,256]{1,0:T(8,128)(2,1)S(1)}, bf16[264,256]{1,0:T(8,128)(2,1)S(1)}, u32[]{:S(2)}, u32[]{:S(2)}) %collective-permute-start.24) | collective-permute-done | bytes 135200 | tf_op jit(solution)/shard_map/ppermute | solution.py:1038
  154.7 0.6 collective-permute-start.26
  155.3 1.3 collective-permute-start.27
  156.6 0.6 pad_add_fusion.bits_ref
  157.2 3.9 %feed_output.1 = (f32[1024,512]{1,0:T(8,128)}, f32[512,1024]{1,0:T(8,128)}) custom-call(s32[2]{0:T(128)} %pad_add_fusion.bits_ref, bf16[1024,256]{1,0:T(8,128)(2,1)} %copy-done.3, bf16[1024,256]{1,0:T(8,128)(2,1)} %copy-done.2, bf16[1024,256]{1,0:T(8,128)(2,1)} %copy-done.13, bf16[1024,256]{1,0:T(8,128)(2,1)} %copy-done.14), custom_call_target="tpu_custom_call" | custom-call | flops 30000000 | bytes 1048576 | tf_op jit(solution)/shard_map/feed_output/pallas_call | solution.py:1466
  161.3 0.5 collective-permute-done.27.b_got_hbm
  161.8 0.2 copy-done.15
  162.0 0.5 copy-done.16
  162.4 3.3 %last_output.1 = (f32[1536,256]{1,0:T(8,128)}, f32[256,512]{1,0:T(8,128)}, f32[1,512]{1,0:T(1,128)}, f32[1,512]{1,0:T(1,128)}, f32[2,4]{1,0:T(2,128)}) custom-call(s32[2]{0:T(128)} %pad_add_fusion.bits_ref, bf16[528,256]{1,0:T(8,128)(2,1)} %copy-done.5, bf16[528,256]{1,0:T(8,128)(2,1)} %copy-done.4, bf16[528,256]{1,0:T(8,128)(2,1)} %copy-done.15, ...), custom_call_target="tpu_custom_call" | custom-call | flops 30000000 | bytes 1048576 | tf_op jit(solution)/shard_map/last_output/pallas_call | solution.py:1485
  (75 shorter events, 1.3 us)
Async XLA Ops:
  0.6 6.0 %collective-permute-start.1 = (bf16[512,1024]{1,0:T(8,128)(2,1)}, bf16[512,1024]{1,0:T(8,128)(2,1)S(1)}, u32[]{:S(2)}, u32[]{:S(2)}) collective-permute-start(bf16[512,1024]{1,0:T(8,128)(2,1)} %wi_own_hbm.1), channel_id=1, source_target_pairs={{0,1},{1,0},{2,3},{3,2},{4,5},{5,4},{6,7},{7,6},{8,9},{9,8},{10,11... | collective-permute-start | bytes 3145736 | tf_op jit(solution)/shard_map/ppermute | solution.py:1175
  1.2 5.5 %collective-permute-start.2 = (bf16[1024,512]{1,0:T(8,128)(2,1)}, bf16[1024,512]{1,0:T(8,128)(2,1)S(1)}, u32[]{:S(2)}, u32[]{:S(2)}) collective-permute-start(bf16[1024,512]{1,0:T(8,128)(2,1)} %wo_own_ref.1), channel_id=1, source_target_pairs={{0,1},{1,0},{2,3},{3,2},{4,5},{5,4},{6,7},{7,6},{8,9},{9,8},{10,11... | collective-permute-start | bytes 3145736 | tf_op jit(solution)/shard_map/ppermute | solution.py:1175
  1.2 5.4 %collective-permute-start.4 = (bf16[3,512,256]{2,1,0:T(8,128)(2,1)}, bf16[3,512,256]{2,1,0:T(8,128)(2,1)S(1)}, u32[]{:S(2)}, u32[]{:S(2)}) collective-permute-start(bf16[3,512,256]{2,1,0:T(8,128)(2,1)} %bitcast.19), channel_id=1, source_target_pairs={{0,1},{1,0},{2,3},{3,2},{4,5},{5,4},{6,7},{7,6},{8,9},{9,8},{10,11... | collective-permute-start | bytes 2359304 | tf_op jit(solution)/shard_map/ppermute | solution.py:1175
  1.7 5.0 %collective-permute-start.3 = (bf16[256,512]{1,0:T(8,128)(2,1)}, bf16[256,512]{1,0:T(8,128)(2,1)S(1)}, u32[]{:S(2)}, u32[]{:S(2)}) collective-permute-start(bf16[256,512]{1,0:T(8,128)(2,1)} %wa_own_ref.3), channel_id=1, source_target_pairs={{0,1},{1,0},{2,3},{3,2},{4,5},{5,4},{6,7},{7,6},{8,9},{9,8},{10,11... | collective-permute-start | bytes 786440 | tf_op jit(solution)/shard_map/ppermute | solution.py:1175
  6.7 5.9 %copy-start.8 = (bf16[256,512]{1,0:T(8,128)(2,1)}, bf16[256,512]{1,0:T(8,128)(2,1)S(1)}, u32[]{:S(2)}) copy-start(bf16[256,512]{1,0:T(8,128)(2,1)S(1)} %collective-permute-done.3.wa_other_ref) | copy-start | bytes 786436
  6.7 5.9 %copy-start.7 = (bf16[512,1024]{1,0:T(8,128)(2,1)}, bf16[512,1024]{1,0:T(8,128)(2,1)S(1)}, u32[]{:S(2)}) copy-start(bf16[512,1024]{1,0:T(8,128)(2,1)S(1)} %collective-permute-done.1.wi_other_hbm) | copy-start | bytes 3145732
  6.7 7.6 %copy-start.1 = (bf16[1024,512]{1,0:T(8,128)(2,1)}, bf16[1024,512]{1,0:T(8,128)(2,1)S(1)}, u32[]{:S(2)}) copy-start(bf16[1024,512]{1,0:T(8,128)(2,1)S(1)} %collective-permute-done.2.wo_other_hbm.wo_other_ref) | copy-start | bytes 3145732
  6.7 0.9 copy-start
  7.6 5.4 %copy-start.20 = (f32[2,4]{1,0:T(2,128)S(1)}, f32[2,4]{1,0:T(2,128)}, u32[]{:S(2)}) copy-start(f32[2,4]{1,0:T(2,128)} %blend_own_ref.3) | copy-start | bytes 100
  12.6 1.7 %collective-permute-start.5 = (bf16[832,128]{1,0:T(8,128)(2,1)}, bf16[832,128]{1,0:T(8,128)(2,1)S(1)}, u32[]{:S(2)}, u32[]{:S(2)}) collective-permute-start(bf16[832,128]{1,0:T(8,128)(2,1)} %get-tuple-element.101), channel_id=1, source_target_pairs={{0,1},{1,0},{2,3},{3,2},{4,5},{5,4},{6,7},{7,6},{8,9},{9,8},{10,11... | collective-permute-start | bytes 638984 | tf_op jit(solution)/shard_map/ppermute | solution.py:1175
  13.0 1.1 collective-permute-start
  14.1 0.6 copy-start.21
  14.3 0.7 copy-start.18
  46.5 5.3 %copy-start.9 = (bf16[2048,256]{1,0:T(8,128)(2,1)S(1)}, bf16[2048,256]{1,0:T(8,128)(2,1)}, u32[]{:S(2)}) copy-start(bf16[2048,256]{1,0:T(8,128)(2,1)} %get-tuple-element.114) | copy-start | bytes 3145732
  46.5 2.9 %collective-permute-start.7 = (bf16[2048,256]{1,0:T(8,128)(2,1)}, bf16[2048,256]{1,0:T(8,128)(2,1)S(1)}, u32[]{:S(2)}, u32[]{:S(2)}) collective-permute-start(bf16[2048,256]{1,0:T(8,128)(2,1)} %get-tuple-element.117), channel_id=1, source_target_pairs={{0,1},{1,0},{2,3},{3,2},{4,5},{5,4},{6,7},{7,6},{8,9},{9,8},{10,11... | collective-permute-start | bytes 3145736 | tf_op jit(solution)/shard_map/ppermute | solution.py:1175
  47.0 4.8 %collective-permute-start.6 = (bf16[2048,256]{1,0:T(8,128)(2,1)}, bf16[2048,256]{1,0:T(8,128)(2,1)S(1)}, u32[]{:S(2)}, u32[]{:S(2)}) collective-permute-start(bf16[2048,256]{1,0:T(8,128)(2,1)} %get-tuple-element.115), channel_id=1, source_target_pairs={{0,1},{1,0},{2,3},{3,2},{4,5},{5,4},{6,7},{7,6},{8,9},{9,8},{10,11... | collective-permute-start | bytes 3145736 | tf_op jit(solution)/shard_map/ppermute | solution.py:1175
  49.5 23.5 %copy-start.11 = (bf16[2048,256]{1,0:T(8,128)(2,1)}, bf16[2048,256]{1,0:T(8,128)(2,1)S(1)}, u32[]{:S(2)}) copy-start(bf16[2048,256]{1,0:T(8,128)(2,1)S(1)} %collective-permute-done.7) | copy-start | bytes 3145732
  51.8 5.5 %copy-start.12 = (bf16[2048,256]{1,0:T(8,128)(2,1)}, bf16[2048,256]{1,0:T(8,128)(2,1)S(1)}, u32[]{:S(2)}) copy-start(bf16[2048,256]{1,0:T(8,128)(2,1)S(1)} %collective-permute-done.6) | copy-start | bytes 3145732
  52.9 20.0 %collective-permute-start.8 = (bf16[1024,256]{1,0:T(8,128)(2,1)}, bf16[1024,256]{1,0:T(8,128)(2,1)}, u32[]{:S(2)}, u32[]{:S(2)}) collective-permute-start(bf16[1024,256]{1,0:T(8,128)(2,1)} %add_convert_fusion.1), channel_id=1, source_target_pairs={{0,2},{2,0},{4,6},{6,4},{8,10},{10,8},{12,14},{14,12},{16,18},{18,... | collective-permute-start | bytes 1572872 | tf_op jit(solution)/shard_map/ppermute | solution.py:1038
  55.8 17.1 %collective-permute-start.9 = (bf16[1024,256]{1,0:T(8,128)(2,1)}, bf16[1024,256]{1,0:T(8,128)(2,1)}, u32[]{:S(2)}, u32[]{:S(2)}) collective-permute-start(bf16[1024,256]{1,0:T(8,128)(2,1)} %add_convert_fusion), channel_id=1, source_target_pairs={{0,4},{2,6},{4,0},{6,2},{8,12},{10,14},{12,8},{14,10},{16,20},{18,... | collective-permute-start | bytes 1572872 | tf_op jit(solution)/shard_map/ppermute | solution.py:1038
  57.3 15.7 %copy-start.10 = (bf16[2048,256]{1,0:T(8,128)(2,1)S(1)}, bf16[2048,256]{1,0:T(8,128)(2,1)}, u32[]{:S(2)}) copy-start(bf16[2048,256]{1,0:T(8,128)(2,1)} %get-tuple-element.116) | copy-start | bytes 3145732
  72.9 2.3 %collective-permute-start.10 = (bf16[832,128]{1,0:T(8,128)(2,1)}, bf16[832,128]{1,0:T(8,128)(2,1)S(1)}, u32[]{:S(2)}, u32[]{:S(2)}) collective-permute-start(bf16[832,128]{1,0:T(8,128)(2,1)} %get-tuple-element.124), channel_id=1, source_target_pairs={{0,1},{1,0},{2,3},{3,2},{4,5},{5,4},{6,7},{7,6},{8,9},{9,8},{10,11... | collective-permute-start | bytes 638984 | tf_op jit(solution)/shard_map/ppermute | solution.py:1175
  75.2 0.7 copy-start.17
  75.2 10.0 %collective-permute-start.11 = (bf16[512,256]{1,0:T(8,128)(2,1)S(1)}, bf16[512,256]{1,0:T(8,128)(2,1)S(1)}, u32[]{:S(2)}, u32[]{:S(2)}) collective-permute-start(bf16[512,256]{1,0:T(8,128)(2,1)S(1)} %add_convert_fusion.7), channel_id=1, source_target_pairs={{0,4},{2,6},{4,0},{6,2},{8,12},{10,14},{12,8},{14,10},{16,20},{18,... | collective-permute-start | bytes 786440 | tf_op jit(solution)/shard_map/ppermute | solution.py:1038
  75.8 9.4 %collective-permute-start.12 = (bf16[512,256]{1,0:T(8,128)(2,1)S(1)}, bf16[512,256]{1,0:T(8,128)(2,1)}, u32[]{:S(2)}, u32[]{:S(2)}) collective-permute-start(bf16[512,256]{1,0:T(8,128)(2,1)S(1)} %add_convert_fusion.6), channel_id=1, source_target_pairs={{0,2},{2,0},{4,6},{6,4},{8,10},{10,8},{12,14},{14,12},{16,18},{18,... | collective-permute-start | bytes 786440 | tf_op jit(solution)/shard_map/ppermute | solution.py:1038
  85.2 7.8 %collective-permute-start.13 = (bf16[2112,256]{1,0:T(8,128)(2,1)}, bf16[2112,256]{1,0:T(8,128)(2,1)S(1)}, u32[]{:S(2)}, u32[]{:S(2)}) collective-permute-start(bf16[2112,256]{1,0:T(8,128)(2,1)} %get-tuple-element.137), channel_id=1, source_target_pairs={{0,1},{1,0},{2,3},{3,2},{4,5},{5,4},{6,7},{7,6},{8,9},{9,8},{10,11... | collective-permute-start | bytes 3244040 | tf_op jit(solution)/shard_map/ppermute | solution.py:1175
  87.3 5.7 %copy-start.6 = (bf16[2112,256]{1,0:T(8,128)(2,1)S(1)}, bf16[2112,256]{1,0:T(8,128)(2,1)}, u32[]{:S(2)}) copy-start(bf16[2112,256]{1,0:T(8,128)(2,1)} %get-tuple-element.133) | copy-start | bytes 3244036
  88.1 20.0 %all-to-all-start = ((bf16[4,256,256]{2,1,0:T(8,128)(2,1)}), bf16[4,256,256]{2,1,0:T(8,128)(2,1)S(1)}, u32[]{:S(2)}, u32[]{:S(2)}) async-start(bf16[4,256,256]{2,1,0:T(8,128)(2,1)} %pad_maximum_fusion), calls=%async_computation | async-start | bytes 1048576 | tf_op jit(solution)/shard_map/all_to_all | solution.py:1048
  93.9 9.3 %collective-permute-start.14 = (bf16[528,256]{1,0:T(8,128)(2,1)}, bf16[528,256]{1,0:T(8,128)(2,1)S(1)}, u32[]{:S(2)}, u32[]{:S(2)}) collective-permute-start(bf16[528,256]{1,0:T(8,128)(2,1)} %get-tuple-element.142), channel_id=1, source_target_pairs={{0,2},{2,0},{4,6},{6,4},{8,10},{10,8},{12,14},{14,12},{16,18},{18,... | collective-permute-start | bytes 811016 | tf_op jit(solution)/shard_map/ppermute | solution.py:1038
  95.4 8.5 %collective-permute-start.15 = (bf16[528,256]{1,0:T(8,128)(2,1)}, bf16[528,256]{1,0:T(8,128)(2,1)S(1)}, u32[]{:S(2)}, u32[]{:S(2)}) collective-permute-start(bf16[528,256]{1,0:T(8,128)(2,1)} %get-tuple-element.143), channel_id=1, source_target_pairs={{0,4},{2,6},{4,0},{6,2},{8,12},{10,14},{12,8},{14,10},{16,20},{18,... | collective-permute-start | bytes 811016 | tf_op jit(solution)/shard_map/ppermute | solution.py:1038
  108.2 6.1 %copy-start.19 = (bf16[264,256]{1,0:T(8,128)(2,1)S(1)}, bf16[264,256]{1,0:T(8,128)(2,1)}, u32[]{:S(2)}) copy-start(bf16[264,256]{1,0:T(8,128)(2,1)} %get-tuple-element.154) | copy-start | bytes 405508
  109.0 20.4 %all-to-all-start.1 = ((bf16[4,256,256]{2,1,0:T(8,128)(2,1)}), bf16[4,256,256]{2,1,0:T(8,128)(2,1)S(1)}, u32[]{:S(2)}, u32[]{:S(2)}) async-start(bf16[4,256,256]{2,1,0:T(8,128)(2,1)} %broadcast_in_dim.2), calls=%async_computation.1 | async-start | bytes 1048576 | tf_op jit(solution)/shard_map/all_to_all | solution.py:1048
  112.7 5.4 %collective-permute-start.16 = (bf16[264,256]{1,0:T(8,128)(2,1)}, bf16[264,256]{1,0:T(8,128)(2,1)}, u32[]{:S(2)}, u32[]{:S(2)}) collective-permute-start(bf16[264,256]{1,0:T(8,128)(2,1)} %get-tuple-element.153), channel_id=1, source_target_pairs={{0,4},{2,6},{4,0},{6,2},{8,12},{10,14},{12,8},{14,10},{16,20},{18,... | collective-permute-start | bytes 405512 | tf_op jit(solution)/shard_map/ppermute | solution.py:1038
  114.3 5.1 %collective-permute-start.17 = (bf16[264,256]{1,0:T(8,128)(2,1)S(1)}, bf16[264,256]{1,0:T(8,128)(2,1)}, u32[]{:S(2)}, u32[]{:S(2)}) collective-permute-start(bf16[264,256]{1,0:T(8,128)(2,1)S(1)} %copy-done.19), channel_id=1, source_target_pairs={{0,2},{2,0},{4,6},{6,4},{8,10},{10,8},{12,14},{14,12},{16,18},{18,... | collective-permute-start | bytes 405512 | tf_op jit(solution)/shard_map/ppermute | solution.py:1038
  120.6 9.0 %collective-permute-start.18 = (bf16[528,256]{1,0:T(8,128)(2,1)S(1)}, bf16[528,256]{1,0:T(8,128)(2,1)S(1)}, u32[]{:S(2)}, u32[]{:S(2)}) collective-permute-start(bf16[528,256]{1,0:T(8,128)(2,1)S(1)} %pad_maximum_fusion.3), channel_id=1, source_target_pairs={{0,8},{2,10},{4,12},{6,14},{8,0},{10,2},{12,4},{14,6},{16,24},{18,... | collective-permute-start | bytes 811016 | tf_op jit(solution)/shard_map/ppermute | solution.py:1038
  129.8 6.5 %collective-permute-start.21 = (bf16[512,256]{1,0:T(8,128)(2,1)S(1)}, bf16[512,256]{1,0:T(8,128)(2,1)S(1)}, u32[]{:S(2)}, u32[]{:S(2)}) collective-permute-start(bf16[512,256]{1,0:T(8,128)(2,1)S(1)} %bitcast.27), channel_id=1, source_target_pairs={{0,2},{2,0},{4,6},{6,4},{8,10},{10,8},{12,14},{14,12},{16,18},{18,... | collective-permute-start | bytes 786440 | tf_op jit(solution)/shard_map/ppermute | solution.py:1038
  131.3 13.1 %collective-permute-start.19 = (bf16[528,256]{1,0:T(8,128)(2,1)S(1)}, bf16[528,256]{1,0:T(8,128)(2,1)S(1)}, u32[]{:S(2)}, u32[]{:S(2)}) collective-permute-start(bf16[528,256]{1,0:T(8,128)(2,1)S(1)} %pad_maximum_fusion.4), channel_id=1, source_target_pairs={{0,16},{2,18},{4,20},{6,22},{8,24},{10,26},{12,28},{14,30},{16,0},... | collective-permute-start | bytes 811016 | tf_op jit(solution)/shard_map/ppermute | solution.py:1038
  133.5 6.8 %collective-permute-start.20 = (bf16[512,256]{1,0:T(8,128)(2,1)S(1)}, bf16[512,256]{1,0:T(8,128)(2,1)S(1)}, u32[]{:S(2)}, u32[]{:S(2)}) collective-permute-start(bf16[512,256]{1,0:T(8,128)(2,1)S(1)} %bitcast.26), channel_id=1, source_target_pairs={{0,4},{2,6},{4,0},{6,2},{8,12},{10,14},{12,8},{14,10},{16,20},{18,... | collective-permute-start | bytes 786440 | tf_op jit(solution)/shard_map/ppermute | solution.py:1038
  136.4 18.2 %copy-start.2 = (bf16[1024,256]{1,0:T(8,128)(2,1)}, bf16[1024,256]{1,0:T(8,128)(2,1)S(1)}, u32[]{:S(2)}) copy-start(bf16[1024,256]{1,0:T(8,128)(2,1)S(1)} %pad_maximum_fusion.2.in_mine_hbm) | copy-start | bytes 1572868
  140.4 16.8 %copy-start.3 = (bf16[1024,256]{1,0:T(8,128)(2,1)}, bf16[1024,256]{1,0:T(8,128)(2,1)S(1)}, u32[]{:S(2)}) copy-start(bf16[1024,256]{1,0:T(8,128)(2,1)S(1)} %pad_maximum_fusion.1.out_mine_hbm) | copy-start | bytes 1572868
  140.4 14.1 %collective-permute-start.22 = (bf16[1024,256]{1,0:T(8,128)(2,1)S(1)}, bf16[1024,256]{1,0:T(8,128)(2,1)S(1)}, u32[]{:S(2)}, u32[]{:S(2)}) collective-permute-start(bf16[1024,256]{1,0:T(8,128)(2,1)S(1)} %pad_maximum_fusion.1.out_mine_hbm), channel_id=1, source_target_pairs={{0,2},{2,0},{4,6},{6,4},{8,10},{10,8},{12,14},{14,12},{16,18},{18,... | collective-permute-start | bytes 1572872 | tf_op jit(solution)/shard_map/ppermute | solution.py:1038
  140.6 14.0 %collective-permute-start.23 = (bf16[1024,256]{1,0:T(8,128)(2,1)S(1)}, bf16[1024,256]{1,0:T(8,128)(2,1)S(1)}, u32[]{:S(2)}, u32[]{:S(2)}) collective-permute-start(bf16[1024,256]{1,0:T(8,128)(2,1)S(1)} %pad_maximum_fusion.2.in_mine_hbm), channel_id=1, source_target_pairs={{0,4},{2,6},{4,0},{6,2},{8,12},{10,14},{12,8},{14,10},{16,20},{18,... | collective-permute-start | bytes 1572872 | tf_op jit(solution)/shard_map/ppermute | solution.py:1038
  144.5 10.1 %collective-permute-start.24 = (bf16[264,256]{1,0:T(8,128)(2,1)S(1)}, bf16[264,256]{1,0:T(8,128)(2,1)S(1)}, u32[]{:S(2)}, u32[]{:S(2)}) collective-permute-start(bf16[264,256]{1,0:T(8,128)(2,1)S(1)} %get-tuple-element.169), channel_id=1, source_target_pairs={{0,4},{2,6},{4,0},{6,2},{8,12},{10,14},{12,8},{14,10},{16,20},{18,... | collective-permute-start | bytes 405512 | tf_op jit(solution)/shard_map/ppermute | solution.py:1038
  145.4 9.1 %collective-permute-start.25 = (bf16[264,256]{1,0:T(8,128)(2,1)S(1)}, bf16[264,256]{1,0:T(8,128)(2,1)S(1)}, u32[]{:S(2)}, u32[]{:S(2)}) collective-permute-start(bf16[264,256]{1,0:T(8,128)(2,1)S(1)} %get-tuple-element.170), channel_id=1, source_target_pairs={{0,2},{2,0},{4,6},{6,4},{8,10},{10,8},{12,14},{14,12},{16,18},{18,... | collective-permute-start | bytes 405512 | tf_op jit(solution)/shard_map/ppermute | solution.py:1038
  154.5 2.6 %copy-start.13 = (bf16[1024,256]{1,0:T(8,128)(2,1)}, bf16[1024,256]{1,0:T(8,128)(2,1)S(1)}, u32[]{:S(2)}) copy-start(bf16[1024,256]{1,0:T(8,128)(2,1)S(1)} %collective-permute-done.22.out_got_hbm) | copy-start | bytes 1572868
  154.6 2.6 %copy-start.14 = (bf16[1024,256]{1,0:T(8,128)(2,1)}, bf16[1024,256]{1,0:T(8,128)(2,1)S(1)}, u32[]{:S(2)}) copy-start(bf16[1024,256]{1,0:T(8,128)(2,1)S(1)} %collective-permute-done.23.in_got_hbm) | copy-start | bytes 1572868
  154.7 7.1 %copy-start.4 = (bf16[528,256]{1,0:T(8,128)(2,1)}, bf16[528,256]{1,0:T(8,128)(2,1)S(1)}, u32[]{:S(2)}) copy-start(bf16[528,256]{1,0:T(8,128)(2,1)S(1)} %pad_maximum_fusion.6.b_mine_hbm) | copy-start | bytes 811012
  154.7 7.0 %copy-start.5 = (bf16[528,256]{1,0:T(8,128)(2,1)}, bf16[528,256]{1,0:T(8,128)(2,1)S(1)}, u32[]{:S(2)}) copy-start(bf16[528,256]{1,0:T(8,128)(2,1)S(1)} %pad_maximum_fusion.5.a_mine_hbm) | copy-start | bytes 811012
  154.7 6.5 %collective-permute-start.26 = (bf16[528,256]{1,0:T(8,128)(2,1)S(1)}, bf16[528,256]{1,0:T(8,128)(2,1)S(1)}, u32[]{:S(2)}, u32[]{:S(2)}) collective-permute-start(bf16[528,256]{1,0:T(8,128)(2,1)S(1)} %pad_maximum_fusion.5.a_mine_hbm), channel_id=1, source_target_pairs={{0,2},{2,0},{4,6},{6,4},{8,10},{10,8},{12,14},{14,12},{16,18},{18,... | collective-permute-start | bytes 811016 | tf_op jit(solution)/shard_map/ppermute | solution.py:1038
  155.3 6.5 %collective-permute-start.27 = (bf16[528,256]{1,0:T(8,128)(2,1)S(1)}, bf16[528,256]{1,0:T(8,128)(2,1)S(1)}, u32[]{:S(2)}, u32[]{:S(2)}) collective-permute-start(bf16[528,256]{1,0:T(8,128)(2,1)S(1)} %pad_maximum_fusion.6.b_mine_hbm), channel_id=1, source_target_pairs={{0,4},{2,6},{4,0},{6,2},{8,12},{10,14},{12,8},{14,10},{16,20},{18,... | collective-permute-start | bytes 811016 | tf_op jit(solution)/shard_map/ppermute | solution.py:1038
  161.3 0.7 copy-start.15
  161.7 0.7 copy-start.16
